TPU v7x, 32 devices: a whole 2x2x4 slice. The times are simulated.
32 devices in a mesh: seq: 4 (over z), head: 2 (over x), dp: 4 (over y, core).
Axes of the slice: x: 2, y: 2, z: 4, core: 2. Of those that a mesh axis runs over, the one named last changes fastest.
Arguments:
- events: bfloat16 [12288, 1024], P(('dp', 'seq'), 'head'), parts along dimension 0
- w_proj: bfloat16 [4, 1024, 1024], P(None, None, 'head'), may hold values from -0.1875 to 0.1875
- w_out: bfloat16 [1024, 1024], P(None, 'head'), may hold values from -0.1875 to 0.1875
- block_target: int32 [768], P('dp'), parts along dimension 0, may hold values from 0 to 191, as said below
- user_lengths: int32 [12], P('dp'), parts along dimension 0, may hold values from 1 to 2880, 3072 in all
Outputs:
- layer_out: bfloat16 [12288, 1024], P(('dp', 'seq'), 'head'), parts along dimension 0
There are 4 independent parts, one for each index of `dp`. A program takes and returns all parts, laid end to end along the dimension named above; an argument that names none is the same for every part. Nothing has to cross between parts.
Inputs may be any that keep to these rules, and one draw needn't show every extreme that they name: block_target is a permutation of 0 to 191; each aligned range of 12 values lies wholly in one aligned group of 48 entries (one log shard); each such group holds exactly 12 values in each aligned range of 48 values, and exactly 12 values v with (v mod 48) // 12 = i for each i below 4. `user_lengths`: the lengths sum to 3072.
All inputs are finite; a program needn't handle non-finite values.
Results may differ from a plain program's by a relative error of at most 0.0077.
Values may be sent and summed in bfloat16 or wider, within the bound.
No kernel may reach another device: no remote copies, remote signals or barrier semaphores. Data moves between devices by JAX's collectives and lax.ppermute only.
A program may use at most 64 MiB of HBM per device.

v0:
```python
import jax
import jax.numpy as jnp
from jax import lax
from jax.sharding import PartitionSpec as P

D = 1024
DH = 64
RB = 16


eps_norm = 1e-05


def from_behind(block, axis, distance):
    devices = range(lax.axis_size(axis))
    route = [((i - distance) % len(devices), i) for i in devices]
    return lax.ppermute(block, axis, route)


def user_index(positions, user_ends):
    return jnp.sum((positions[:, None] >= user_ends[None, :]).astype(jnp.int32), axis=1)


def body(events, w_proj, w_out, block_target, user_lengths):
    rows_here = events.shape[0]
    col_width = events.shape[1]
    seq_count = lax.axis_size("seq")
    seq_index = lax.axis_index("seq")
    block_count = rows_here // RB
    per_owner = block_count // seq_count

    def window_position(shard, local):
        return shard * rows_here + local

    owners = block_target // block_count
    slots = block_target % block_count
    my_owners = lax.dynamic_slice_in_dim(owners, seq_index * block_count, block_count)
    send_order = jnp.argsort(my_owners, stable=True)
    outgoing = events.reshape(block_count, RB, col_width)[send_order]
    outgoing = outgoing.reshape(seq_count, per_owner, RB, col_width)
    incoming = lax.all_to_all(outgoing, "seq", split_axis=0, concat_axis=0, tiled=True)
    arrived = jnp.argsort(jnp.where(owners == seq_index, 0, 1), stable=True)[:block_count]
    slot_ids = slots[arrived]
    placed = incoming.reshape(block_count, RB, col_width)[jnp.argsort(slot_ids)]
    ordered = placed.reshape(rows_here, col_width)
    widened = ordered.astype(jnp.float32)
    row_sum, row_squares = lax.psum(
        (jnp.sum(widened, axis=1), jnp.sum(widened * widened, axis=1)), "head"
    )
    mean_value = row_sum / D
    square_mean = row_squares / D
    normed = (
        (widened - mean_value[:, None])
        * lax.rsqrt(square_mean - mean_value * mean_value + eps_norm)[:, None]
    ).astype(jnp.bfloat16)
    weight_rows = w_proj
    projected = jnp.einsum(
        "ln,jnc->jlc",
        lax.all_gather(normed, "head", axis=1, tiled=True),
        weight_rows,
        preferred_element_type=jnp.float32,
    )
    activated = jax.nn.silu(projected).astype(jnp.bfloat16)
    gate_rows = activated[0]
    value_rows = activated[1]
    query_rows = activated[2]
    key_rows = activated[3]
    user_ends = jnp.cumsum(user_lengths)
    head_count = col_width // DH
    query_heads = query_rows.reshape(rows_here, head_count, DH)
    local_rows = jnp.arange(rows_here, dtype=jnp.int32)
    query_pos = window_position(seq_index, local_rows)
    query_users = user_index(query_pos, user_ends)
    zero_sum = jnp.zeros((rows_here, col_width), jnp.float32)

    def key_term(key_piece, value_piece, key_pos):
        row_count = key_piece.shape[0]
        key_heads = key_piece.reshape(row_count, head_count, DH)
        value_heads = value_piece.reshape(row_count, head_count, DH)
        key_users = user_index(key_pos, user_ends)
        allowed = (key_pos[None, :] <= query_pos[:, None]) & (
            key_users[None, :] == query_users[:, None]
        )
        scores = jnp.einsum(
            "lhd,nhd->hln", query_heads, key_heads, preferred_element_type=jnp.float32
        )
        weights = jnp.where(allowed[None], jax.nn.silu(scores), 0.0).astype(jnp.bfloat16)
        summed = jnp.einsum(
            "hln,nhd->lhd", weights, value_heads, preferred_element_type=jnp.float32
        )
        return summed.reshape(rows_here, col_width)

    def guarded_term(key_piece, value_piece, key_pos):
        return key_term(key_piece, value_piece, key_pos)

    def sweep_piece(running, key_piece, value_piece, key_pos):
        row_count = key_piece.shape[0]
        block_rows = min(row_count, 1024)
        rounds = row_count // block_rows

        def visit_block(partial_sum, inputs):
            key_block, value_block, block_pos = inputs
            return (partial_sum + guarded_term(key_block, value_block, block_pos), None)

        key_stack = key_piece.reshape(rounds, block_rows, col_width)
        value_stack = value_piece.reshape(rounds, block_rows, col_width)
        pos_stack = key_pos.reshape(rounds, block_rows)
        running, _ = lax.scan(visit_block, running, (key_stack, value_stack, pos_stack))
        return running

    stacked = jnp.stack([key_rows, value_rows])
    own_block = sweep_piece(zero_sum, key_rows, value_rows, query_pos)

    def relay_step(offset, loop_state):
        running, carried = loop_state
        carried = from_behind(carried, "seq", 1)
        source_shard = (seq_index - offset + seq_count) % seq_count
        running = sweep_piece(
            running, carried[0], carried[1], window_position(source_shard, local_rows)
        )
        return (running, carried)

    attended, _ = lax.fori_loop(1, seq_count, relay_step, (own_block, stacked))
    att_sum, att_squares = lax.psum(
        (jnp.sum(attended, axis=1), jnp.sum(attended * attended, axis=1)), "head"
    )
    att_mean = att_sum / D
    att_square_mean = att_squares / D
    scaled = (attended - att_mean[:, None]) * lax.rsqrt(
        att_square_mean - att_mean * att_mean + eps_norm
    )[:, None]
    gated_rows = (scaled * gate_rows.astype(jnp.float32)).astype(jnp.bfloat16)
    weight_rows = w_out
    projected_out = jnp.dot(
        lax.all_gather(gated_rows, "head", axis=1, tiled=True),
        weight_rows,
        preferred_element_type=jnp.float32,
    )
    finished = (widened + projected_out).astype(jnp.bfloat16)
    return finished


def solution(mesh):
    placed = (P(("dp", "seq"), "head"), P(None, None, "head"), P(None, "head"), P("dp"), P("dp"))
    return jax.shard_map(
        body, mesh=mesh, in_specs=placed, out_specs=P(("dp", "seq"), "head"), check_vma=False
    )
```

profile of v0, /device:TPU:8, one launch (start us, length us, event | category | flops | bytes accessed | tf_op | source)
XLA Modules:
  0.0 296.4 jit_solution(12151734962270498540)
XLA Ops:
  6.5 0.8 compare_select_fusion.3
  7.4 2.0 sort.51
  9.5 2.7 gather_fusion
  12.1 5.3 %all-to-all-start = ((bf16[4,12,16,512]{3,2,1,0:T(8,128)(2,1)}), bf16[4,12,16,512]{3,2,1,0:T(8,128)(2,1)S(1)}, u32[]{:S(2)}, u32[]{:S(2)}) async-start(bf16[4,12,16,512]{3,2,1,0:T(8,128)(2,1)} %bitcast.1), calls=%async_computation | async-start | bytes 1572864 | tf_op jit(solution)/shard_map/all_to_all | solution.py:41
  17.4 3.2 %sort.52 = (s32[192]{0:T(256)}, s32[192]{0:T(256)S(1)}) sort(s32[192]{0:T(256)S(1)} %get-tuple-element.349, s32[192]{0:T(256)S(1)} %iota.23), dimensions={0}, to_apply=%region_1.2 | sort | flops 1536 | bytes 3072 | tf_op jit(solution)/shard_map/jit(argsort)/sort | solution.py:42
  20.6 0.8 gather_fusion.1
  21.4 2.1 sort.53
  23.6 10.7 %all-to-all-done = bf16[4,12,16,512]{3,2,1,0:T(8,128)(2,1)S(1)} async-done(((bf16[4,12,16,512]{3,2,1,0:T(8,128)(2,1)}), bf16[4,12,16,512]{3,2,1,0:T(8,128)(2,1)S(1)}, u32[]{:S(2)}, u32[]{:S(2)}) %all-to-all-start) | async-done | bytes 786464 | tf_op jit(solution)/shard_map/all_to_all | solution.py:41
  34.3 0.6 gather_fusion.2
  34.9 0.4 convert_reduce_fusion.1
  35.5 5.0 %all-reduce.1 = (f32[768]{0:T(1024)S(1)}, f32[768]{0:T(1024)S(1)}) all-reduce(f32[768]{0:T(1024)S(1)} %reduce_sum.74, f32[768]{0:T(1024)S(1)} %reduce_sum.72), channel_id=1, replica_groups=mesh['seq'=4,'head'=2,'dp'=4] {'head'}, use_global_device_ids=true, to_apply=%region_6.7 | all-reduce | flops 1536 | bytes 12288 | tf_op jit(solution)/shard_map/psum | solution.py:47
  40.5 1.2 fusion.20
  42.0 1.3 compare_and_fusion.1
  43.4 27.5 %all-gather.3.cloned.1.call-done = bf16[768,1024]{1,0:T(8,128)(2,1)} async-done(((bf16[768,512]{1,0:T(8,128)(2,1)}), bf16[768,1024]{1,0:T(8,128)(2,1)}) %all-gather.3.cloned.1.call-update) | async-done | bytes 1572880 | tf_op jit(solution)/shard_map/all_gather | solution.py:59
  70.9 6.9 %fusion.13 = bf16[4,768,512]{1,2,0:T(8,128)(2,1)S(1)} fusion(bf16[4,1024,512]{2,1,0:T(8,128)(2,1)} %param.8, bf16[768,1024]{1,0:T(8,128)(2,1)} %all-gather.3.cloned.1.call-done), kind=kOutput, calls=%fused_computation.22 | convolution fusion | flops 3229089792 | bytes 8912896 | tf_op jit(solution)/shard_map/ln,jnc->jlc/dot_general | solution.py:57
  77.9 1.5 copy-done.4
  79.4 1.3 pad_maximum_fusion
  80.7 10.4 %fusion.9 = f32[8,64,768]{2,1,0:T(8,128)} fusion(bf16[768,8,64]{0,2,1:T(8,128)(2,1)S(1)} %bitcast.73, pred[768,768]{1,0:T(8,128)(4,1)} %compare_and_fusion.1, bf16[768,8,64]{0,2,1:T(8,128)(2,1)S(1)} %bitcast.74, bf16[768,8,64]{0,2,1:T(8,128)(2,1)S(1)} %bitcast.72), kind=kOutput, calls=%fused_computation.16 | convolution fusion | flops 1236271104 | bytes 4521984 | tf_op jit(solution)/shard_map/while/body/eval_jaxpr/hln,nhd->lhd/dot_general | solution.py:88
  91.1 158.5 %while.30 = (s32[]{:T(128)}, f32[768,512]{0,1:T(8,128)}, bf16[2,768,512]{1,2,0:T(8,128)(2,1)}, s32[]{:T(128)}, s32[3]{0:T(128)S(1)}, /*index=5*/s32[768]{0:T(102...) while((s32[]{:T(128)}, f32[768,512]{0,1:T(8,128)}, ...), condition=%wide.region_11.12_spmd.clone, body=%wide.region_9.11_spmd.clone.sunk | while | flops 1238441472 | bytes 28729728 | solution.py:123
  91.1 1.5 collective-permute-start
  92.7 1.4 compare_and_fusion.3
  94.1 33.4 %collective-permute-done = bf16[2,768,512]{1,2,0:T(8,128)(2,1)S(1)} collective-permute-done((bf16[2,768,512]{1,2,0:T(8,128)(2,1)}, bf16[2,768,512]{1,2,0:T(8,128)(2,1)S(1)}, u32[]{:S(2)}, u32[]{:S(2)}) %collective-permute-start) | collective-permute-done | bytes 1572896 | tf_op jit(solution)/shard_map/while/body/eval_jaxpr/ppermute | solution.py:17
  127.4 1.0 fusion.44
  128.4 10.7 %fusion.45 = f32[8,768,64]{1,2,0:T(8,128)} fusion(bf16[768,8,64]{0,2,1:T(8,128)(2,1)} %bitcast.70, pred[768,768]{1,0:T(8,128)(4,1)} %compare_and_fusion.3, bf16[768,8,64]{0,2,1:T(8,128)(2,1)} %copy-done.5, bf16[768,8,64]{0,2,1:T(8,128)(2,1)S(1)} %bitcast.69), kind=kOutput, calls=%fused_computation.6.clone.1 | convolution fusion | flops 1236271104 | bytes 4521984 | tf_op jit(solution)/shard_map/while/body/eval_jaxpr/while/body/eval_jaxpr/hln,nhd->lhd/dot_general | solution.py:88
  139.1 3.2 %bitcast_add_fusion.3 = f32[768,512]{0,1:T(8,128)} fusion(f32[768,512]{0,1:T(8,128)} %get-tuple-element.434, f32[8,768,64]{1,2,0:T(8,128)} %fusion.45), kind=kLoop, calls=%fused_computation.9.clone.1 | loop fusion | flops 393216 | bytes 4718592 | tf_op jit(solution)/shard_map/while/body/eval_jaxpr/while/body/eval_jaxpr/add | solution.py:103
  142.3 1.2 copy.18
  143.5 0.5 copy-done.6
  144.0 1.5 collective-permute-start
  145.6 1.4 compare_and_fusion.3
  147.0 33.1 %collective-permute-done = bf16[2,768,512]{1,2,0:T(8,128)(2,1)S(1)} collective-permute-done((bf16[2,768,512]{1,2,0:T(8,128)(2,1)}, bf16[2,768,512]{1,2,0:T(8,128)(2,1)S(1)}, u32[]{:S(2)}, u32[]{:S(2)}) %collective-permute-start) | collective-permute-done | bytes 1572896 | tf_op jit(solution)/shard_map/while/body/eval_jaxpr/ppermute | solution.py:17
  180.1 1.0 fusion.44
  181.1 10.7 %fusion.45 = f32[8,768,64]{1,2,0:T(8,128)} fusion(bf16[768,8,64]{0,2,1:T(8,128)(2,1)} %bitcast.70, pred[768,768]{1,0:T(8,128)(4,1)} %compare_and_fusion.3, bf16[768,8,64]{0,2,1:T(8,128)(2,1)} %copy-done.5, bf16[768,8,64]{0,2,1:T(8,128)(2,1)S(1)} %bitcast.69), kind=kOutput, calls=%fused_computation.6.clone.1 | convolution fusion | flops 1236271104 | bytes 4521984 | tf_op jit(solution)/shard_map/while/body/eval_jaxpr/while/body/eval_jaxpr/hln,nhd->lhd/dot_general | solution.py:88
  191.8 3.2 %bitcast_add_fusion.3 = f32[768,512]{0,1:T(8,128)} fusion(f32[768,512]{0,1:T(8,128)} %get-tuple-element.434, f32[8,768,64]{1,2,0:T(8,128)} %fusion.45), kind=kLoop, calls=%fused_computation.9.clone.1 | loop fusion | flops 393216 | bytes 4718592 | tf_op jit(solution)/shard_map/while/body/eval_jaxpr/while/body/eval_jaxpr/add | solution.py:103
  195.0 1.2 copy.18
  196.2 0.5 copy-done.6
  196.7 0.9 collective-permute-start
  197.6 1.4 compare_and_fusion.3
  199.0 34.0 %collective-permute-done = bf16[2,768,512]{1,2,0:T(8,128)(2,1)S(1)} collective-permute-done((bf16[2,768,512]{1,2,0:T(8,128)(2,1)}, bf16[2,768,512]{1,2,0:T(8,128)(2,1)S(1)}, u32[]{:S(2)}, u32[]{:S(2)}) %collective-permute-start) | collective-permute-done | bytes 1572896 | tf_op jit(solution)/shard_map/while/body/eval_jaxpr/ppermute | solution.py:17
  233.0 1.0 fusion.44
  234.0 10.7 %fusion.45 = f32[8,768,64]{1,2,0:T(8,128)} fusion(bf16[768,8,64]{0,2,1:T(8,128)(2,1)} %bitcast.70, pred[768,768]{1,0:T(8,128)(4,1)} %compare_and_fusion.3, bf16[768,8,64]{0,2,1:T(8,128)(2,1)} %copy-done.5, bf16[768,8,64]{0,2,1:T(8,128)(2,1)S(1)} %bitcast.69), kind=kOutput, calls=%fused_computation.6.clone.1 | convolution fusion | flops 1236271104 | bytes 4521984 | tf_op jit(solution)/shard_map/while/body/eval_jaxpr/while/body/eval_jaxpr/hln,nhd->lhd/dot_general | solution.py:88
  244.7 3.2 %bitcast_add_fusion.3 = f32[768,512]{0,1:T(8,128)} fusion(f32[768,512]{0,1:T(8,128)} %get-tuple-element.434, f32[8,768,64]{1,2,0:T(8,128)} %fusion.45), kind=kLoop, calls=%fused_computation.9.clone.1 | loop fusion | flops 393216 | bytes 4718592 | tf_op jit(solution)/shard_map/while/body/eval_jaxpr/while/body/eval_jaxpr/add | solution.py:103
  247.9 1.2 copy.18
  249.1 0.5 copy-done.6
  249.6 1.7 fusion.24
  251.3 5.0 %all-reduce = (f32[768]{0:T(1024)S(1)}, f32[768]{0:T(1024)S(1)}) all-reduce(f32[768]{0:T(1024)S(1)} %get-tuple-element.326, f32[768]{0:T(1024)S(1)} %get-tuple-element.325), channel_id=1, replica_groups=mesh['seq'=4,'head'=2,'dp'=4] {'head'}, use_global_device_ids=true, to_apply=%region_15.16 | all-reduce | flops 1536 | bytes 12288 | tf_op jit(solution)/shard_map/psum | solution.py:124
  256.3 2.3 fusion.16
  258.7 27.6 %all-gather.5.cloned.1.call-done = bf16[768,1024]{0,1:T(8,128)(2,1)} async-done(((bf16[768,512]{0,1:T(8,128)(2,1)}), bf16[768,1024]{0,1:T(8,128)(2,1)}) %all-gather.5.cloned.1.call-update) | async-done | bytes 1572880 | tf_op jit(solution)/shard_map/all_gather | solution.py:135
  286.3 3.3 %fusion.21 = bf16[768,512]{1,0:T(8,128)(2,1)} fusion(bf16[48,16,512]{2,1,0:T(8,128)(2,1)S(1)} %copy-done.3, bf16[768,1024]{0,1:T(8,128)(2,1)} %all-gather.5.cloned.1.call-done, bf16[1024,512]{1,0:T(8,128)(2,1)S(1)} %copy-done), kind=kOutput, calls=%fused_computation.36 | convolution fusion | flops 806486016 | bytes 4194304 | tf_op jit(solution)/shard_map/dot_general | solution.py:134
  (48 shorter events, 1.1 us)
Async XLA Ops:
  6.5 279.7 %copy-start = (bf16[1024,512]{1,0:T(8,128)(2,1)S(1)}, bf16[1024,512]{1,0:T(8,128)(2,1)}, u32[]{:S(2)}) copy-start(bf16[1024,512]{1,0:T(8,128)(2,1)} %param.9) | copy-start | bytes 3145732
  12.1 22.2 %all-to-all-start = ((bf16[4,12,16,512]{3,2,1,0:T(8,128)(2,1)}), bf16[4,12,16,512]{3,2,1,0:T(8,128)(2,1)S(1)}, u32[]{:S(2)}, u32[]{:S(2)}) async-start(bf16[4,12,16,512]{3,2,1,0:T(8,128)(2,1)} %bitcast.1), calls=%async_computation | async-start | bytes 1572864 | tf_op jit(solution)/shard_map/all_to_all | solution.py:41
  17.4 53.5 %all-gather.3.cloned.1.call-start = ((), (), s32[]{:S(2)}) async-start(), calls=%async_computation.1 | async-start | bytes 2359296 | tf_op jit(solution)/shard_map/all_gather | solution.py:59
  34.9 6.8 %copy-start.2 = (bf16[48,16,512]{2,1,0:T(8,128)(2,1)}, bf16[48,16,512]{2,1,0:T(8,128)(2,1)S(1)}, u32[]{:S(2)}) copy-start(bf16[48,16,512]{2,1,0:T(8,128)(2,1)S(1)} %gather_fusion.2) | copy-start | bytes 2359300
  34.9 6.8 %copy-start.7 = (s32[3]{0:T(128)S(1)}, s32[3]{0:T(128)}, u32[]{:S(2)}) copy-start(s32[3]{0:T(128)} %param.11) | copy-start | bytes 40
  41.7 244.6 %all-gather.5.cloned.1.call-start = ((), (), s32[]{:S(2)}) async-start(), calls=%async_computation.2 | async-start | bytes 2359296 | tf_op jit(solution)/shard_map/all_gather | solution.py:135
  77.8 1.7 copy-start.4
  91.1 3.0 %copy-start.5 = (bf16[768,8,64]{0,2,1:T(8,128)(2,1)}, bf16[768,8,64]{0,2,1:T(8,128)(2,1)S(1)}, u32[]{:S(2)}) copy-start(bf16[768,8,64]{0,2,1:T(8,128)(2,1)S(1)} %get-tuple-element.452) | copy-start | bytes 2359300 | tf_op jit(solution)/shard_map/while
  91.1 36.3 %collective-permute-start = (bf16[2,768,512]{1,2,0:T(8,128)(2,1)}, bf16[2,768,512]{1,2,0:T(8,128)(2,1)S(1)}, u32[]{:S(2)}, u32[]{:S(2)}) collective-permute-start(bf16[2,768,512]{1,2,0:T(8,128)(2,1)} %get-tuple-element.435), channel_id=1, source_target_pairs={{24,0},{0,8},{8,16},{16,24},{25,1},{1,9},{9,17},{17,25},{26,2},{2,... | collective-permute-start | bytes 4718600 | tf_op jit(solution)/shard_map/while/body/eval_jaxpr/ppermute | solution.py:17
  142.3 1.7 copy-start.6
  144.0 3.0 %copy-start.5 = (bf16[768,8,64]{0,2,1:T(8,128)(2,1)}, bf16[768,8,64]{0,2,1:T(8,128)(2,1)S(1)}, u32[]{:S(2)}) copy-start(bf16[768,8,64]{0,2,1:T(8,128)(2,1)S(1)} %get-tuple-element.452) | copy-start | bytes 2359300 | tf_op jit(solution)/shard_map/while
  144.0 36.1 %collective-permute-start = (bf16[2,768,512]{1,2,0:T(8,128)(2,1)}, bf16[2,768,512]{1,2,0:T(8,128)(2,1)S(1)}, u32[]{:S(2)}, u32[]{:S(2)}) collective-permute-start(bf16[2,768,512]{1,2,0:T(8,128)(2,1)} %get-tuple-element.435), channel_id=1, source_target_pairs={{24,0},{0,8},{8,16},{16,24},{25,1},{1,9},{9,17},{17,25},{26,2},{2,... | collective-permute-start | bytes 4718600 | tf_op jit(solution)/shard_map/while/body/eval_jaxpr/ppermute | solution.py:17
  195.0 1.7 copy-start.6
  196.7 2.4 copy-start.5
  196.7 36.3 %collective-permute-start = (bf16[2,768,512]{1,2,0:T(8,128)(2,1)}, bf16[2,768,512]{1,2,0:T(8,128)(2,1)S(1)}, u32[]{:S(2)}, u32[]{:S(2)}) collective-permute-start(bf16[2,768,512]{1,2,0:T(8,128)(2,1)} %get-tuple-element.435), channel_id=1, source_target_pairs={{24,0},{0,8},{8,16},{16,24},{25,1},{1,9},{9,17},{17,25},{26,2},{2,... | collective-permute-start | bytes 4718600 | tf_op jit(solution)/shard_map/while/body/eval_jaxpr/ppermute | solution.py:17
  247.9 1.7 copy-start.6
  249.6 6.7 %copy-start.1 = (f32[768,512]{0,1:T(8,128)S(1)}, f32[768,512]{0,1:T(8,128)}, u32[]{:S(2)}) copy-start(f32[768,512]{0,1:T(8,128)} %get-tuple-element.304) | copy-start | bytes 4718596
  256.3 30.0 %copy-start.3 = (bf16[48,16,512]{2,1,0:T(8,128)(2,1)S(1)}, bf16[48,16,512]{2,1,0:T(8,128)(2,1)}, u32[]{:S(2)}) copy-start(bf16[48,16,512]{2,1,0:T(8,128)(2,1)} %copy-done.2) | copy-start | bytes 2359300
Sparse Core Ops, SparseCore 0:
  41.8 29.0 all-gather.2
  258.8 27.4 all-gather.4
where the time goes:
time: 299 us; the launch traced here: 296 us
  waiting for transfers between devices  166 us (56%)
  matrix products  52.7 us (18%)
  other arithmetic  30.8 us (10%)
  local copies, waits for them, and re-layouts  13.9 us (5%)
  between operations  13.5 us (5%)
  blocking collectives  9.99 us (3%)
  starting transfers between devices  9.21 us (3%)
    ppermute x3, waiting for transfers between devices, from_behind(): return lax.ppermute(block, axis, route)  100 us
    dot_general x4, matrix products, key_term(): jnp.einsum('hln,nhd->lhd', weights, value_heads, preferred_element_type=j...  42.5 us
    all_gather x1, waiting for transfers between devices, body(): lax.all_gather(gated_rows, 'head', axis=1, tiled=True)  27.6 us
    all_gather x1, waiting for transfers between devices, body(): lax.all_gather(normed, 'head', axis=1, tiled=True)  27.5 us
    all_to_all x1, waiting for transfers between devices, body(): lax.all_to_all(outgoing, 'seq', split_axis=0, concat_axis=0, tiled=True)  10.7 us
    add x3, other arithmetic, visit_block(): return (partial_sum + guarded_term(key_block, value_block, block_pos), None)  9.61 us
    dot_general x1, matrix products, body(): jnp.einsum('ln,jnc->jlc', lax.all_gather(normed, 'head', axis=1, tiled=Tr...  6.85 us
  transfers between devices with their start and end apart: 6, of which 6 were waited for; matrix products, arithmetic and copies ran while one was open for 4% of the time, Pallas kernels for 0%

commit v1 on v0

--- a/solution.py
+++ b/solution.py
@@ -1,6 +1,8 @@
 import jax
 import jax.numpy as jnp
 from jax import lax
+from jax.experimental import pallas as pl
+from jax.experimental.pallas import tpu as pltpu
 from jax.sharding import PartitionSpec as P
 
 D = 1024
@@ -140,7 +142,454 @@
     return finished
 
 
+def team_plan(mesh):
+    return jax.sharding.Mesh(
+        mesh.devices.reshape(2, 2, 2, mesh.devices.shape[2] // 2, 2),
+        ("half", "zlo", "head", "y", "core"),
+    )
+
+
+ROUTE = ("half", "zlo", "head", "core")
+
+
+def route(rule):
+    pairs = []
+    for half in range(2):
+        for zlo in range(2):
+            for head in range(2):
+                for core in range(2):
+                    to = rule(half, zlo, head, core)
+                    if to is not None:
+                        pairs.append(
+                            (
+                                ((half * 2 + zlo) * 2 + head) * 2 + core,
+                                ((to[0] * 2 + to[1]) * 2 + to[2]) * 2 + to[3],
+                            )
+                        )
+    return pairs
+
+
+def move(value, rule):
+    return lax.ppermute(value, ROUTE, route(rule))
+
+
+def to_partner(half, zlo, head, core):
+    if core == half:
+        return (half, 1 - zlo, head, 1 - half)
+    return None
+
+
+def to_other_team(half, zlo, head, core):
+    if core == half:
+        return None
+    other = 1 - half
+    inner = (zlo ^ half) == 1
+    return (other, 1 - other, head, other if inner else 1 - other)
+
+
+def inner_to_outer(half, zlo, head, core):
+    if (zlo ^ half) == 1:
+        return (half, 1 - zlo, head, core)
+    return None
+
+
+def across(select):
+    def rule(half, zlo, head, core):
+        if select(half, zlo, head, core):
+            return (half, zlo, 1 - head, core)
+        return None
+
+    return rule
+
+
+def other_core(half, zlo, head, core):
+    return (half, zlo, head, 1 - core)
+
+
+def project_kernel(info, own_a, own_b, other_a, other_b, w_ref, mine_ref, sib_ref, own_v, other_v, sems):
+    rows = own_v.shape[0]
+    width = own_v.shape[1]
+    first = info[0] == 0
+
+    @pl.when(first)
+    def _():
+        pltpu.make_async_copy(own_a, own_v, sems.at[0]).start()
+        pltpu.make_async_copy(other_a, other_v, sems.at[1]).start()
+
+    @pl.when(jnp.logical_not(first))
+    def _():
+        pltpu.make_async_copy(own_b, own_v, sems.at[0]).start()
+        pltpu.make_async_copy(other_b, other_v, sems.at[1]).start()
+
+    pltpu.make_async_copy(own_a, own_v, sems.at[0]).wait()
+    pltpu.make_async_copy(other_a, other_v, sems.at[1]).wait()
+    own_rows = pl.multiple_of(info[1] * width, width)
+    other_rows = pl.multiple_of(info[2] * width, width)
+    low_core = info[3] == 0
+    step = 128
+
+    @pl.loop(0, rows // step)
+    def _(i):
+        at = pl.ds(pl.multiple_of(i * step, step), step)
+        a = own_v[at, :].astype(jnp.float32)
+        b = other_v[at, :].astype(jnp.float32)
+        mean = (jnp.sum(a, axis=1, keepdims=True) + jnp.sum(b, axis=1, keepdims=True)) / (2 * width)
+        square = (
+            jnp.sum(a * a, axis=1, keepdims=True) + jnp.sum(b * b, axis=1, keepdims=True)
+        ) / (2 * width)
+        scale = lax.rsqrt(square - mean * mean + eps_norm)
+        a = ((a - mean) * scale).astype(jnp.bfloat16)
+        b = ((b - mean) * scale).astype(jnp.bfloat16)
+        for j in range(4):
+            z = jnp.dot(
+                a, w_ref[j, pl.ds(own_rows, width), :], preferred_element_type=jnp.float32
+            ) + jnp.dot(
+                b, w_ref[j, pl.ds(other_rows, width), :], preferred_element_type=jnp.float32
+            )
+            t = 0.5 * z
+            act = (t + t * jnp.tanh(t)).astype(jnp.bfloat16)
+            low, high = act[:, :128], act[:, 128:]
+            cols = pl.ds(j * 128, 128)
+            mine_ref[at, cols] = jnp.where(low_core, low, high)
+            sib_ref[at, cols] = jnp.where(low_core, high, low)
+
+
+def project(info, own_a, own_b, other_a, other_b, w, zlo):
+    rows, width = own_a.shape
+    anywhere = pl.BlockSpec(memory_space=pl.ANY)
+    out = jax.ShapeDtypeStruct((rows, 512), jnp.bfloat16)
+    return pl.pallas_call(
+        project_kernel,
+        out_shape=(out, out),
+        in_specs=[pl.BlockSpec(memory_space=pltpu.SMEM)] + [anywhere] * 4 + [pl.BlockSpec(memory_space=pltpu.VMEM)],
+        out_specs=(pl.BlockSpec(memory_space=pltpu.VMEM),) * 2,
+        scratch_shapes=[
+            pltpu.VMEM((rows, width), jnp.bfloat16),
+            pltpu.VMEM((rows, width), jnp.bfloat16),
+            pltpu.SemaphoreType.DMA((2,)),
+        ],
+        compiler_params=pltpu.CompilerParams(vmem_limit_bytes=40 * 1024 * 1024),
+        cost_estimate=pl.CostEstimate(
+            flops=2 * rows * D * 1024, bytes_accessed=rows * D * 4 + w.size * 2, transcendentals=rows * 1024
+        ),
+    )(info, own_a, own_b, other_a, other_b, w)
+
+
+TQ = 256
+TK = 512
+
+
+def attend_kernel(info, targets, lengths, *refs):
+    pieces, (att_ref, u_ref, stat_ref, q_s, v0, v1, k_s, k0, k1) = refs[:-9], refs[-9:]
+    seq = att_ref.shape[0]
+    lane = lax.broadcasted_iota(jnp.int32, (RB, 128), 1)
+    low = lane < DH
+    zero = jnp.zeros((RB, 128), jnp.bfloat16)
+
+    for n, piece in enumerate(pieces):
+        base = info[n]
+
+        @pl.loop(0, piece.shape[0] // RB, unroll=4)
+        def _(b):
+            frm = pl.ds(pl.multiple_of(b * RB, RB), RB)
+            to = pl.ds(pl.multiple_of(targets[base + b] * RB, RB), RB)
+            u_ref[to, :] = piece[frm, 0:128]
+            v = piece[frm, 128:256]
+            v0[to, :] = jnp.where(low, v, zero)
+            v1[to, :] = jnp.where(low, zero, v)
+            q_s[to, :] = piece[frm, 256:384] * 0.5
+            k_s[to, :] = piece[frm, 384:512]
+
+    row = lax.broadcasted_iota(jnp.int32, (128, 256), 0)
+
+    @pl.loop(0, seq // 256)
+    def _(i):
+        at = pl.ds(pl.multiple_of(i * 256, 256), 256)
+        kt = k_s[at, :].T
+        k0[:, at] = jnp.where(row < DH, kt, jnp.zeros_like(kt))
+        k1[:, at] = jnp.where(row < DH, jnp.zeros_like(kt), kt)
+
+    ends = []
+    total = jnp.int32(0)
+    for i in range(lengths.shape[0]):
+        total = total + lengths[i]
+        ends.append(total)
+
+    def start_of(p):
+        best = p * 0
+        for e in ends:
+            best = jnp.where(p >= e, e, best)
+        return best
+
+    @pl.loop(0, seq // TQ)
+    def _(qi):
+        q0 = qi * TQ
+        at = pl.ds(pl.multiple_of(q0, TQ), TQ)
+        q = q_s[at, :]
+
+        def tile(j, acc, masked):
+            ks = pl.ds(pl.multiple_of(j * TK, TK), TK)
+            if masked:
+                qp = q0 + lax.broadcasted_iota(jnp.int32, (TQ, 1), 0)
+                kp = j * TK + lax.broadcasted_iota(jnp.int32, (1, TK), 1)
+                ok = (kp <= qp) & (kp >= start_of(qp))
+            for kt, vv in ((k0, v0), (k1, v1)):
+                t = jnp.dot(q, kt[:, ks], preferred_element_type=jnp.float32)
+                w = t + t * jnp.tanh(t)
+                if masked:
+                    w = jnp.where(ok, w, 0.0)
+                acc = acc + jnp.dot(
+                    w.astype(jnp.bfloat16), vv[ks, :], preferred_element_type=jnp.float32
+                )
+            return acc
+
+        lo = start_of(q0) // TK
+        last = start_of(q0 + TQ - 1)
+        hi = (q0 + TQ + TK - 1) // TK
+        diag = q0 // TK
+        mid = jnp.minimum((last + TK - 1) // TK, diag)
+        mid = jnp.maximum(mid, lo)
+        acc = jnp.zeros((TQ, 128), jnp.float32)
+        acc = lax.fori_loop(lo, mid, lambda j, c: tile(j, c, True), acc)
+        acc = lax.fori_loop(mid, diag, lambda j, c: tile(j, c, False), acc)
+        acc = lax.fori_loop(jnp.maximum(mid, diag), hi, lambda j, c: tile(j, c, True), acc)
+        att_ref[at, :] = acc
+        flip = acc.T
+        stat_ref[0:1, at] = jnp.sum(flip, axis=0, keepdims=True)
+        stat_ref[1:2, at] = jnp.sum(flip * flip, axis=0, keepdims=True)
+
+
+def attend(info, targets, lengths, pieces):
+    seq = sum(p.shape[0] for p in pieces)
+    smem = pl.BlockSpec(memory_space=pltpu.SMEM)
+    vmem = pl.BlockSpec(memory_space=pltpu.VMEM)
+    return pl.pallas_call(
+        attend_kernel,
+        out_shape=(
+            jax.ShapeDtypeStruct((seq, 128), jnp.float32),
+            jax.ShapeDtypeStruct((seq, 128), jnp.bfloat16),
+            jax.ShapeDtypeStruct((2, seq), jnp.float32),
+        ),
+        in_specs=[smem] * 3 + [vmem] * len(pieces),
+        out_specs=(vmem,) * 3,
+        scratch_shapes=[pltpu.VMEM((seq, 128), jnp.bfloat16)] * 4
+        + [pltpu.VMEM((128, seq), jnp.bfloat16)] * 2,
+        compiler_params=pltpu.CompilerParams(vmem_limit_bytes=40 * 1024 * 1024),
+        cost_estimate=pl.CostEstimate(
+            flops=2 * seq * seq * 128, bytes_accessed=seq * 128 * 14, transcendentals=seq * seq
+        ),
+    )(info, targets, lengths, *pieces)
+
+
+def gate_kernel(info, att_ref, u_ref, stat_ref, *outs):
+    rows = outs[0].shape[0]
+    step = 256
+    for k, out in enumerate(outs):
+        block = lax.rem(info[0] + k, len(outs))
+
+        @pl.loop(0, rows // step)
+        def _(i):
+            at = pl.ds(pl.multiple_of(block * rows + i * step, step), step)
+            mean = stat_ref[0:1, at] / D
+            square = stat_ref[1:2, at] / D
+            scale = lax.rsqrt(square - mean * mean + eps_norm)
+            mean = jnp.broadcast_to(mean, (128, step)).T
+            scale = jnp.broadcast_to(scale, (128, step)).T
+            gated = ((att_ref[at, :] - mean) * scale) * u_ref[at, :].astype(jnp.float32)
+            out[pl.ds(pl.multiple_of(i * step, step), step), :] = gated.astype(jnp.bfloat16)
+
+
+def gate(info, att, u, stat, count):
+    rows = att.shape[0] // count
+    vmem = pl.BlockSpec(memory_space=pltpu.VMEM)
+    out = jax.ShapeDtypeStruct((rows, 128), jnp.bfloat16)
+    return pl.pallas_call(
+        gate_kernel,
+        out_shape=(out,) * count,
+        in_specs=[pl.BlockSpec(memory_space=pltpu.SMEM)] + [vmem] * 3,
+        out_specs=(vmem,) * count,
+        compiler_params=pltpu.CompilerParams(vmem_limit_bytes=40 * 1024 * 1024),
+        cost_estimate=pl.CostEstimate(flops=att.size * 8, bytes_accessed=att.size * 8, transcendentals=0),
+    )(info, att, u, stat)
+
+
+def outgoing_kernel(info, targets, events_ref, out_ref):
+    count = out_ref.shape[0]
+    blocks = events_ref.shape[0] // RB
+    base = info[0] * blocks
+
+    def step(b, filled):
+        owner = targets[base + b] // blocks
+        place = jnp.int32(0)
+        for k in range(count):
+            place = jnp.where(owner == k, filled[k], place)
+        frm = pl.ds(pl.multiple_of(b * RB, RB), RB)
+        to = pl.ds(pl.multiple_of(place * RB, RB), RB)
+        out_ref[pl.ds(owner, 1), to, :] = events_ref[frm, :][None]
+        return tuple(filled[k] + (owner == k).astype(jnp.int32) for k in range(count))
+
+    lax.fori_loop(0, blocks, step, (jnp.int32(0),) * count)
+
+
+def outgoing(info, targets, events, count):
+    smem = pl.BlockSpec(memory_space=pltpu.SMEM)
+    vmem = pl.BlockSpec(memory_space=pltpu.VMEM)
+    return pl.pallas_call(
+        outgoing_kernel,
+        out_shape=jax.ShapeDtypeStruct((count, events.shape[0] // count, events.shape[1]), events.dtype),
+        in_specs=[smem, smem, vmem],
+        out_specs=vmem,
+        cost_estimate=pl.CostEstimate(flops=0, bytes_accessed=events.size * 4, transcendentals=0),
+    )(info, targets, events)
+
+
+def place_kernel(info, targets, in_ref, out_ref):
+    blocks = out_ref.shape[0] // RB
+
+    def step(g, filled):
+        t = targets[g]
+        mine = t // blocks == info[0]
+
+        @pl.when(mine)
+        def _():
+            frm = pl.ds(pl.multiple_of(filled * RB, RB), RB)
+            to = pl.ds(pl.multiple_of(lax.rem(t, blocks) * RB, RB), RB)
+            out_ref[to, :] = in_ref[frm, :]
+
+        return filled + mine.astype(jnp.int32)
+
+    lax.fori_loop(0, targets.shape[0], step, jnp.int32(0))
+
+
+def place(info, targets, incoming):
+    smem = pl.BlockSpec(memory_space=pltpu.SMEM)
+    vmem = pl.BlockSpec(memory_space=pltpu.VMEM)
+    return pl.pallas_call(
+        place_kernel,
+        out_shape=jax.ShapeDtypeStruct(incoming.shape, incoming.dtype),
+        in_specs=[smem, smem, vmem],
+        out_specs=vmem,
+        cost_estimate=pl.CostEstimate(flops=0, bytes_accessed=incoming.size * 4, transcendentals=0),
+    )(info, targets, incoming)
+
+
+def finish_kernel(info, res_ref, w_ref, *refs):
+    pieces, out_ref = refs[:-1], refs[-1]
+    step = 256
+    rows = res_ref.shape[0]
+
+    @pl.loop(0, rows // step)
+    def _(i):
+        at = pl.ds(pl.multiple_of(i * step, step), step)
+        acc = res_ref[at, :].astype(jnp.float32)
+        for n, piece in enumerate(pieces):
+            feats = pl.ds(pl.multiple_of(info[n] * 128, 128), 128)
+            acc = acc + jnp.dot(piece[at, :], w_ref[feats, :], preferred_element_type=jnp.float32)
+        out_ref[at, :] = acc.astype(out_ref.dtype)
+
+
+def finish(info, residual, w_out, pieces):
+    vmem = pl.BlockSpec(memory_space=pltpu.VMEM)
+    return pl.pallas_call(
+        finish_kernel,
+        out_shape=jax.ShapeDtypeStruct(residual.shape, jnp.bfloat16),
+        in_specs=[pl.BlockSpec(memory_space=pltpu.SMEM)] + [vmem] * (2 + len(pieces)),
+        out_specs=vmem,
+        cost_estimate=pl.CostEstimate(
+            flops=2 * residual.size * D, bytes_accessed=residual.size * 4 + w_out.size * 2, transcendentals=0
+        ),
+    )(info, residual, w_out, *pieces)
+
+
+def team_body(events, w_proj, w_out, block_target, user_lengths):
+    half, zlo = lax.axis_index("half"), lax.axis_index("zlo")
+    head, core = lax.axis_index("head"), lax.axis_index("core")
+    z = half * 2 + zlo
+    foreign = core ^ half
+    outer = 1 - (zlo ^ half)
+    rows = events.shape[0]
+    blocks = rows // RB
+    targets_here = block_target
+    other_ints = move(jnp.concatenate([block_target, user_lengths]), other_core)
+    targets = jnp.where(foreign == 0, block_target, other_ints[: block_target.shape[0]])
+    lengths = jnp.where(foreign == 0, user_lengths, other_ints[block_target.shape[0] :])
+    w_mine = lax.dynamic_slice_in_dim(w_proj, zlo * 256, 256, axis=2)
+
+    x_own = move(events, across(lambda half, zlo, head, core: core == half))
+    partner = move(events, to_partner)
+    parts = 2
+    span = rows // parts
+    remote = [move(events[i * span : (i + 1) * span], to_other_team) for i in range(parts)]
+    x_partner = move(partner, across(lambda half, zlo, head, core: core != half))
+    relayed = [move(r, inner_to_outer) for r in remote]
+    x_inner = [move(r, across(lambda half, zlo, head, core: (zlo ^ half) == 1)) for r in remote]
+    x_outer = [move(r, across(lambda half, zlo, head, core: (zlo ^ half) == 0)) for r in relayed]
+
+    def ints(*values):
+        return jnp.stack([jnp.asarray(v, jnp.int32) for v in values])
+
+    mine1, sib1 = project(
+        ints(foreign, head, 1 - head, core), events, partner, x_own, x_partner, w_mine, zlo
+    )
+    got1 = move(sib1, other_core)
+    mine, got = [mine1], [got1]
+    for i in range(parts):
+        m, s = project(
+            ints(outer, head, 1 - head, core), remote[i], relayed[i], x_inner[i], x_outer[i], w_mine, zlo
+        )
+        mine.append(m)
+        got.append(move(s, other_core))
+
+    near = half + 1
+    near = jnp.where(half == 0, 2, 1)
+    far = jnp.where(half == 0, 3, 0)
+    slot1 = jnp.where(foreign == 0, z, z ^ 1)
+    slot2 = jnp.where(foreign == 0, near, far)
+    sib_slot1 = jnp.where(foreign == 0, z ^ 1, z)
+    sib_slot2 = jnp.where(foreign == 0, far, near)
+    part_blocks = span // RB
+    starts = [slot1 * blocks]
+    starts += [slot2 * blocks + i * part_blocks for i in range(parts)]
+    starts += [sib_slot1 * blocks]
+    starts += [sib_slot2 * blocks + i * part_blocks for i in range(parts)]
+    att, u, stat = attend(ints(*starts), targets, lengths, mine + got)
+
+    send = outgoing(ints(z), targets_here, events, 4)
+    came = lax.all_to_all(send, ("half", "zlo"), split_axis=0, concat_axis=0, tiled=True)
+    residual = place(ints(z), targets_here, came.reshape(rows, events.shape[1]))
+
+    stat = lax.psum(stat, ("zlo", "head", "core"))
+    me = zlo * 2 + core
+    gated = gate(ints(me), att, u, stat, 4)
+
+    def to_block(k):
+        def rule(half, zlo, head, core):
+            j = (zlo * 2 + core + k) % 4
+            return (j // 2, j % 2, head, half)
+
+        return rule
+
+    pieces, feats = [], []
+    for k in range(4):
+        piece = move(gated[k], to_block(k))
+        source = lax.rem(z - k + 4, 4)
+        pieces += [piece, move(piece, across(lambda *p: True))]
+        feats += [head * 4 + source, (1 - head) * 4 + source]
+    return finish(ints(*feats), residual, w_out, pieces)
+
+
 def solution(mesh):
+    sizes = dict(mesh.shape)
+    if sizes["seq"] == 4 and sizes["head"] == 2 and sizes["dp"] % 2 == 0:
+        rows = P(("y", "core", "half", "zlo"), "head")
+        part = P(("y", "core"))
+        return jax.shard_map(
+            team_body,
+            mesh=team_plan(mesh),
+            in_specs=(rows, P(None, None, "head"), P(None, "head"), part, part),
+            out_specs=rows,
+            check_vma=False,
+        )
     placed = (P(("dp", "seq"), "head"), P(None, None, "head"), P(None, "head"), P("dp"), P("dp"))
     return jax.shard_map(
         body, mesh=mesh, in_specs=placed, out_specs=P(("dp", "seq"), "head"), check_vma=False

time: 299 us -> 163 us (0.55)
  waiting for transfers between devices: 166 us -> 30.8 us
  Pallas kernels: 0 us -> 58.1 us
  matrix products: 52.7 us -> 0 us
  starting transfers between devices: 9.21 us -> 43.3 us
  other arithmetic: 30.8 us -> 0.3 us
  blocking collectives: 9.99 us -> 24.7 us
  between operations: 13.5 us -> 0.28 us
  local copies, waits for them, and re-layouts: 13.9 us -> 4.41 us
    ppermute x3 -> x23, waiting for transfers between devices: 100 us -> 30.8 us  [move(): return lax.ppermute(value, ROUTE, route(rule))]
    pallas_call x0 -> x8, Pallas kernels: none -> 58.1 us  [the longest x1 30.3 us: attend(): pl.pallas_call(attend_kernel, out_shape=(jax.ShapeDtypeStruct((seq, 128),...]
    all_gather x2 -> x0, waiting for transfers between devices: 55.1 us -> none  [the longest x1 27.6 us: body(): lax.all_gather(gated_rows, 'head', axis=1, tiled=True)]
    dot_general x6 -> x0, matrix products: 52.7 us -> none  [the longest x4 42.5 us: key_term(): jnp.einsum('hln,nhd->lhd', weights, value_heads, preferred_element_type=j...]
    ppermute x3 -> x23, starting transfers between devices: 3.85 us -> 39.1 us  [move(): return lax.ppermute(value, ROUTE, route(rule))]
    psum x2 -> x1, blocking collectives: 9.99 us -> 24.7 us  [team_body(): stat = lax.psum(stat, ('zlo', 'head', 'core'))]
    all_to_all x1, waiting for transfers between devices: 10.7 us -> 0.01 us  [team_body(): lax.all_to_all(send, ('half', 'zlo'), split_axis=0, concat_axis=0, tiled=...]
    add x7 -> x0, other arithmetic: 9.62 us -> none  [the longest x3 9.61 us: visit_block(): return (partial_sum + guarded_term(key_block, value_block, block_pos), None)]
  transfers between devices with their start and end apart: 6 -> 24, of which waited for: 6 -> 9; matrix products, arithmetic and copies ran while one was open for 4% -> 2% of each run, Pallas kernels for 0% -> 33%
where the time goes in v1:
time: 163 us; the launch traced here: 162 us
  Pallas kernels  58.1 us (36%)
  starting transfers between devices  43.3 us (27%)
  waiting for transfers between devices  30.8 us (19%)
  blocking collectives  24.7 us (15%)
  local copies, waits for them, and re-layouts  4.41 us (3%)
    ppermute x23, starting transfers between devices, move(): return lax.ppermute(value, ROUTE, route(rule))  39.1 us
    ppermute x23, waiting for transfers between devices, move(): return lax.ppermute(value, ROUTE, route(rule))  30.8 us
    pallas_call x1, Pallas kernels, attend(): pl.pallas_call(attend_kernel, out_shape=(jax.ShapeDtypeStruct((seq, 128),...  30.3 us
    psum x1, blocking collectives, team_body(): stat = lax.psum(stat, ('zlo', 'head', 'core'))  24.7 us
    pallas_call x3, Pallas kernels, project(): pl.pallas_call(project_kernel, out_shape=(out, out), in_specs=[pl.BlockSp...  11.3 us
    pallas_call x1, Pallas kernels, place(): pl.pallas_call(place_kernel, out_shape=jax.ShapeDtypeStruct(incoming.shap...  6.8 us
    pallas_call x1, Pallas kernels, finish(): pl.pallas_call(finish_kernel, out_shape=jax.ShapeDtypeStruct(residual.sha...  4.85 us
    all_to_all x1, starting transfers between devices, team_body(): lax.all_to_all(send, ('half', 'zlo'), split_axis=0, concat_axis=0, tiled=...  4.19 us
  transfers between devices with their start and end apart: 24, of which 9 were waited for; matrix products, arithmetic and copies ran while one was open for 2% of the time, Pallas kernels for 33%

profile of v1, /device:TPU:8, one launch (start us, length us, event | category | flops | bytes accessed | tf_op | source)
XLA Modules:
  0.0 161.9 jit_solution(16037810019895707329)
XLA Ops:
  0.0 2.2 %collective-permute-start.1 = (bf16[768,512]{1,0:T(8,128)(2,1)}, bf16[768,512]{1,0:T(8,128)(2,1)}, u32[]{:S(2)}, u32[]{:S(2)}) collective-permute-start(bf16[768,512]{1,0:T(8,128)(2,1)} %own_a.1), channel_id=1, source_target_pairs={{0,9},{4,13},{8,1},{12,5},{17,24},{21,28},{25,16},{29,20},{2,11},{... | collective-permute-start | bytes 2359304 | tf_op jit(solution)/shard_map/ppermute | solution.py:173
  2.2 1.2 fusion
  3.4 1.3 collective-permute-start.4
  4.7 3.9 %collective-permute-start.2 = (bf16[768,512]{1,0:T(8,128)(2,1)}, bf16[768,512]{1,0:T(8,128)(2,1)}, u32[]{:S(2)}, u32[]{:S(2)}) collective-permute-start(bf16[768,512]{1,0:T(8,128)(2,1)} %own_a.1), channel_id=1, source_target_pairs={{0,4},{4,0},{8,12},{12,8},{17,21},{21,17},{25,29},{29,25},{2,6},{6... | collective-permute-start | bytes 2359304 | tf_op jit(solution)/shard_map/ppermute | solution.py:173
  8.6 1.3 collective-permute-start.8
  9.9 1.2 collective-permute-done.1.own_b
  11.1 1.5 collective-permute-start.3
  12.6 4.7 %collective-permute-done.4.own_a = bf16[384,512]{1,0:T(8,128)(2,1)} collective-permute-done((bf16[384,512]{1,0:T(8,128)(2,1)S(1)}, bf16[384,512]{1,0:T(8,128)(2,1)}, u32[]{:S(2)}, u32[]{:S(2)}) %collective-permute-start.4) | collective-permute-done | bytes 393248 | tf_op jit(solution)/shard_map/ppermute | solution.py:173
  17.4 5.1 %collective-permute-start.5 = (bf16[384,512]{1,0:T(8,128)(2,1)}, bf16[384,512]{1,0:T(8,128)(2,1)}, u32[]{:S(2)}, u32[]{:S(2)}) collective-permute-start(bf16[384,512]{1,0:T(8,128)(2,1)} %collective-permute-done.4.own_a), channel_id=1, source_target_pairs={{8,0},{9,1},{12,4},{13,5},{16,24},{17,25},{20,28},{21,29},{10,2},{... | collective-permute-start | bytes 1179656 | tf_op jit(solution)/shard_map/ppermute | solution.py:173
  22.5 3.0 %collective-permute-done.8.own_a = bf16[384,512]{1,0:T(8,128)(2,1)S(1)} collective-permute-done((bf16[384,512]{1,0:T(8,128)(2,1)S(1)}, bf16[384,512]{1,0:T(8,128)(2,1)S(1)}, u32[]{:S(2)}, u32[]{:S(2)}) %collective-permute-start.8) | collective-permute-done | bytes 393248 | tf_op jit(solution)/shard_map/ppermute | solution.py:173
  25.4 2.0 %collective-permute-start.9 = (bf16[384,512]{1,0:T(8,128)(2,1)S(1)}, bf16[384,512]{1,0:T(8,128)(2,1)}, u32[]{:S(2)}, u32[]{:S(2)}) collective-permute-start(bf16[384,512]{1,0:T(8,128)(2,1)S(1)} %collective-permute-done.8.own_a), channel_id=1, source_target_pairs={{8,0},{9,1},{12,4},{13,5},{16,24},{17,25},{20,28},{21,29},{10,2},{... | collective-permute-start | bytes 1179656 | tf_op jit(solution)/shard_map/ppermute | solution.py:173
  27.5 3.2 %shard_map.55 = bf16[4,192,512]{2,1,0:T(8,128)(2,1)} custom-call(s32[1]{0:T(128)} %bitcast.8.info, s32[192]{0:T(256)} %targets.3, bf16[768,512]{1,0:T(8,128)(2,1)} %own_a.1), custom_call_target="tpu_custom_call" | custom-call | bytes 1572864 | tf_op jit(solution)/shard_map/pallas_call | solution.py:437
  30.7 4.2 %all-to-all-start = ((bf16[4,192,512]{2,1,0:T(8,128)(2,1)}), bf16[4,192,512]{2,1,0:T(8,128)(2,1)}, u32[]{:S(2)}, u32[]{:S(2)}) async-start(bf16[4,192,512]{2,1,0:T(8,128)(2,1)} %shard_map.55), calls=%async_computation | async-start | bytes 1572864 | tf_op jit(solution)/shard_map/all_to_all | solution.py:558
  34.9 1.8 %constant_dynamic-slice_fusion.w_ref = bf16[4,1024,256]{2,1,0:T(8,128)(2,1)S(1)} fusion(bf16[4,1024,512]{2,1,0:T(8,128)(2,1)} %param.6, s32[]{:T(128)S(6)} %select_n.50), kind=kLoop, calls=%fused_computation.5 | loop fusion | bytes 4194308 | tf_op jit(solution)/shard_map/dynamic_slice | solution.py:516
  36.7 3.7 %collective-permute-start.6 = (bf16[384,512]{1,0:T(8,128)(2,1)}, bf16[384,512]{1,0:T(8,128)(2,1)}, u32[]{:S(2)}, u32[]{:S(2)}) collective-permute-start(bf16[384,512]{1,0:T(8,128)(2,1)} %collective-permute-done.4.own_a), channel_id=1, source_target_pairs={{8,12},{9,13},{12,8},{13,9},{16,20},{17,21},{20,16},{21,17},{10,14... | collective-permute-start | bytes 1179656 | tf_op jit(solution)/shard_map/ppermute | solution.py:173
  40.4 1.4 collective-permute-start.7
  41.8 0.1 add_add_fusion.info
  41.9 0.1 stack.101.info
  42.0 2.3 %collective-permute-start.10 = (bf16[384,512]{1,0:T(8,128)(2,1)S(1)}, bf16[384,512]{1,0:T(8,128)(2,1)S(1)}, u32[]{:S(2)}, u32[]{:S(2)}) collective-permute-start(bf16[384,512]{1,0:T(8,128)(2,1)S(1)} %collective-permute-done.8.own_a), channel_id=1, source_target_pairs={{8,12},{9,13},{12,8},{13,9},{16,20},{17,21},{20,16},{21,17},{10,14... | collective-permute-start | bytes 1179656 | tf_op jit(solution)/shard_map/ppermute | solution.py:173
  44.3 0.7 collective-permute-start.11
  45.0 5.2 %shard_map.57 = (bf16[768,512]{1,0:T(8,128)(2,1)S(1)}, bf16[768,512]{1,0:T(8,128)(2,1)S(1)}) custom-call(s32[4]{0:T(128)S(1)} %add_add_fusion.info, bf16[768,512]{1,0:T(8,128)(2,1)S(1)} %copy-done, bf16[768,512]{1,0:T(8,128)(2,1)} %collective-permute-done.1.own_b, bf16[768,512]{1,0:T(8,128)(2,1)} %collective-permute-done.2.other_a, ...), custom_call_target="tpu_custom_call" | custom-call | flops 1610612736 | bytes 5242880 | tf_op jit(solution)/shard_map/pallas_call | solution.py:261
  50.2 1.0 collective-permute-start.12
  51.2 0.1 add_add_fusion.1.info
  51.2 0.1 pad_add_fusion
  51.4 3.4 %shard_map.58 = (bf16[384,512]{1,0:T(8,128)(2,1)S(1)}, bf16[384,512]{1,0:T(8,128)(2,1)S(1)}) custom-call(s32[4]{0:T(128)S(1)} %add_add_fusion.1.info, bf16[384,512]{1,0:T(8,128)(2,1)} %collective-permute-done.4.own_a, bf16[384,512]{1,0:T(8,128)(2,1)} %collective-permute-done.5.own_b, bf16[384,512]{1,0:T(8,128)(2,1)} %collective-permute-done.6.other_a, ...), custom_call_target="tpu_custom_call" | custom-call | flops 805306368 | bytes 3670016 | tf_op jit(solution)/shard_map/pallas_call | solution.py:261
  54.8 0.6 collective-permute-start.13
  55.3 3.3 %collective-permute-done.10.other_a = bf16[384,512]{1,0:T(8,128)(2,1)S(1)} collective-permute-done((bf16[384,512]{1,0:T(8,128)(2,1)S(1)}, bf16[384,512]{1,0:T(8,128)(2,1)S(1)}, u32[]{:S(2)}, u32[]{:S(2)}) %collective-permute-start.10) | collective-permute-done | bytes 393248 | tf_op jit(solution)/shard_map/ppermute | solution.py:173
  58.7 2.7 %shard_map.59 = (bf16[384,512]{1,0:T(8,128)(2,1)S(1)}, bf16[384,512]{1,0:T(8,128)(2,1)S(1)}) custom-call(s32[4]{0:T(128)S(1)} %add_add_fusion.1.info, bf16[384,512]{1,0:T(8,128)(2,1)S(1)} %collective-permute-done.8.own_a, bf16[384,512]{1,0:T(8,128)(2,1)} %collective-permute-done.9.own_b, bf16[384,512]{1,0:T(8,128)(2,1)S(1)} %collective-permute-done.10.other_a, ...), custom_call_target="tpu_custom_call" | custom-call | flops 805306368 | bytes 3670016 | tf_op jit(solution)/shard_map/pallas_call | solution.py:261
  61.4 0.1 broadcast_select_fusion.lengths
  61.5 1.6 collective-permute-done.14.refs_5_
  63.1 30.3 %shard_map.60 = (f32[3072,128]{1,0:T(8,128)S(1)}, bf16[3072,128]{1,0:T(8,128)(2,1)S(1)}, f32[2,3072]{1,0:T(2,128)S(1)}) custom-call(s32[6]{0:T(128)S(1)} %stack.101.info, s32[192]{0:T(256)S(1)} %slice_select_fusion.targets, s32[3]{0:T(128)S(1)} %broadcast_select_fusion.lengths, bf16[768,512]{1,0:T(8,128)(2,1)S(1)} %get-tuple-element.18.refs_0_, ...), custom_call_target="tpu_custom_call" | custom-call | flops 2415919104 | bytes 5505024 | tf_op jit(solution)/shard_map/pallas_call | solution.py:366
  93.5 24.7 %psum.7.stat_ref = f32[2,3072]{1,0:T(2,128)S(1)} all-reduce(f32[2,3072]{1,0:T(2,128)S(1)} %get-tuple-element.26), channel_id=1, replica_groups=mesh['half'=2,'zlo'=2,'head'=2,'y'=2,'core'=2] {'zlo','head','core'}, use_global_device_ids=true, to_apply=%region_0.1 | all-reduce | flops 6144 | bytes 49152 | tf_op jit(solution)/shard_map/psum | solution.py:561
  118.2 1.7 %shard_map.61 = (bf16[768,128]{1,0:T(8,128)(2,1)S(1)}, bf16[768,128]{1,0:T(8,128)(2,1)S(1)}, bf16[768,128]{1,0:T(8,128)(2,1)S(1)}, bf16[768,128]{1,0:T(8,128)(2,1)S(1)}) custom-call(s32[1]{0:T(128)} %bitcast.10.info, f32[3072,128]{1,0:T(8,128)S(1)} %get-tuple-element.24.att_ref, bf16[3072,128]{1,0:T(8,128)(2,1)S(1)} %get-tuple-element.25.u_ref, ...), custom_call_target="tpu_custom_call" | custom-call | flops 3145728 | bytes 3145728 | tf_op jit(solution)/shard_map/pallas_call | solution.py:406
  119.9 4.7 %collective-permute-start.15 = (bf16[768,128]{1,0:T(8,128)(2,1)S(1)}, bf16[768,128]{1,0:T(8,128)(2,1)S(1)}, u32[]{:S(2)}, u32[]{:S(2)}) collective-permute-start(bf16[768,128]{1,0:T(8,128)(2,1)S(1)} %get-tuple-element.27), channel_id=1, source_target_pairs={{0,0},{1,8},{4,4},{5,12},{8,16},{9,24},{12,20},{13,28},{16,1},{17,... | collective-permute-start | bytes 589832 | tf_op jit(solution)/shard_map/ppermute | solution.py:173
  124.6 1.9 %collective-permute-start.17 = (bf16[768,128]{1,0:T(8,128)(2,1)S(1)}, bf16[768,128]{1,0:T(8,128)(2,1)S(1)}, u32[]{:S(2)}, u32[]{:S(2)}) collective-permute-start(bf16[768,128]{1,0:T(8,128)(2,1)S(1)} %get-tuple-element.28), channel_id=1, source_target_pairs={{0,8},{1,16},{4,12},{5,20},{8,24},{9,0},{12,28},{13,4},{16,9},{17,... | collective-permute-start | bytes 589832 | tf_op jit(solution)/shard_map/ppermute | solution.py:173
  126.5 2.1 %collective-permute-start.19 = (bf16[768,128]{1,0:T(8,128)(2,1)S(1)}, bf16[768,128]{1,0:T(8,128)(2,1)S(1)}, u32[]{:S(2)}, u32[]{:S(2)}) collective-permute-start(bf16[768,128]{1,0:T(8,128)(2,1)S(1)} %get-tuple-element.29), channel_id=1, source_target_pairs={{0,16},{1,24},{4,20},{5,28},{8,0},{9,8},{12,4},{13,12},{16,17},{17... | collective-permute-start | bytes 589832 | tf_op jit(solution)/shard_map/ppermute | solution.py:173
  128.6 0.7 collective-permute-start.21
  129.3 1.2 collective-permute-done.15.refs_0_
  130.4 0.5 collective-permute-start.16
  131.0 10.4 %collective-permute-done.17.refs_2_ = bf16[768,128]{1,0:T(8,128)(2,1)S(1)} collective-permute-done((bf16[768,128]{1,0:T(8,128)(2,1)S(1)}, bf16[768,128]{1,0:T(8,128)(2,1)S(1)}, u32[]{:S(2)}, u32[]{:S(2)}) %collective-permute-start.17) | collective-permute-done | bytes 196640 | tf_op jit(solution)/shard_map/ppermute | solution.py:173
  141.4 2.0 %collective-permute-start.20 = (bf16[768,128]{1,0:T(8,128)(2,1)S(1)}, bf16[768,128]{1,0:T(8,128)(2,1)S(1)}, u32[]{:S(2)}, u32[]{:S(2)}) collective-permute-start(bf16[768,128]{1,0:T(8,128)(2,1)S(1)} %collective-permute-done.19.refs_4_), channel_id=1, source_target_pairs={{0,4},{1,5},{4,0},{5,1},{8,12},{9,13},{12,8},{13,9},{16,20},{17,21... | collective-permute-start | bytes 589832 | tf_op jit(solution)/shard_map/ppermute | solution.py:173
  143.4 0.1 collective-permute-start.22
  143.5 0.7 stack.92.info
  144.1 6.8 %shard_map.56.res_ref = bf16[768,512]{1,0:T(8,128)(2,1)} custom-call(s32[1]{0:T(128)} %bitcast.8.info, s32[192]{0:T(256)} %targets.3, bf16[768,512]{1,0:T(8,128)(2,1)} %bitcast.9.in_ref), custom_call_target="tpu_custom_call" | custom-call | bytes 1572864 | tf_op jit(solution)/shard_map/pallas_call | solution.py:467
  151.0 2.4 %collective-permute-done.20.refs_5_ = bf16[768,128]{1,0:T(8,128)(2,1)S(1)} collective-permute-done((bf16[768,128]{1,0:T(8,128)(2,1)S(1)}, bf16[768,128]{1,0:T(8,128)(2,1)S(1)}, u32[]{:S(2)}, u32[]{:S(2)}) %collective-permute-start.20) | collective-permute-done | bytes 196640 | tf_op jit(solution)/shard_map/ppermute | solution.py:173
  153.4 3.0 %collective-permute-done.22.refs_7_ = bf16[768,128]{1,0:T(8,128)(2,1)S(1)} collective-permute-done((bf16[768,128]{1,0:T(8,128)(2,1)S(1)}, bf16[768,128]{1,0:T(8,128)(2,1)S(1)}, u32[]{:S(2)}, u32[]{:S(2)}) %collective-permute-start.22) | collective-permute-done | bytes 196640 | tf_op jit(solution)/shard_map/ppermute | solution.py:173
  156.4 0.7 copy-done.8
  157.1 4.9 %shard_map.62 = bf16[768,512]{1,0:T(8,128)(2,1)} custom-call(s32[8]{0:T(128)} %stack.92.info, bf16[768,512]{1,0:T(8,128)(2,1)} %shard_map.56.res_ref, bf16[1024,512]{1,0:T(8,128)(2,1)} %w_ref.1, bf16[768,128]{1,0:T(8,128)(2,1)} %copy-done.1, bf16[768,128]{1,0:T(8,128)(2,1)} %copy-done.5, bf16[768,128]{1,0:T(8,128)(2,1)} %copy-done.2, ...), custom_call_target="tpu_custom_call" | custom-call | flops 805306368 | bytes 2621440 | tf_op jit(solution)/shard_map/pallas_call | solution.py:493
  (40 shorter events, 0.2 us)
Async XLA Ops:
  0.0 11.1 %collective-permute-start.1 = (bf16[768,512]{1,0:T(8,128)(2,1)}, bf16[768,512]{1,0:T(8,128)(2,1)}, u32[]{:S(2)}, u32[]{:S(2)}) collective-permute-start(bf16[768,512]{1,0:T(8,128)(2,1)} %own_a.1), channel_id=1, source_target_pairs={{0,9},{4,13},{8,1},{12,5},{17,24},{21,28},{25,16},{29,20},{2,11},{... | collective-permute-start | bytes 2359304 | tf_op jit(solution)/shard_map/ppermute | solution.py:173
  3.4 14.0 %collective-permute-start.4 = (bf16[384,512]{1,0:T(8,128)(2,1)S(1)}, bf16[384,512]{1,0:T(8,128)(2,1)}, u32[]{:S(2)}, u32[]{:S(2)}) collective-permute-start(bf16[384,512]{1,0:T(8,128)(2,1)S(1)} %get-tuple-element.32), channel_id=1, source_target_pairs={{1,16},{5,20},{9,17},{13,21},{16,8},{20,12},{24,9},{28,13},{3,18},... | collective-permute-start | bytes 1179656 | tf_op jit(solution)/shard_map/ppermute | solution.py:173
  4.7 37.3 %collective-permute-start.2 = (bf16[768,512]{1,0:T(8,128)(2,1)}, bf16[768,512]{1,0:T(8,128)(2,1)}, u32[]{:S(2)}, u32[]{:S(2)}) collective-permute-start(bf16[768,512]{1,0:T(8,128)(2,1)} %own_a.1), channel_id=1, source_target_pairs={{0,4},{4,0},{8,12},{12,8},{17,21},{21,17},{25,29},{29,25},{2,6},{6... | collective-permute-start | bytes 2359304 | tf_op jit(solution)/shard_map/ppermute | solution.py:173
  8.6 16.8 %collective-permute-start.8 = (bf16[384,512]{1,0:T(8,128)(2,1)S(1)}, bf16[384,512]{1,0:T(8,128)(2,1)S(1)}, u32[]{:S(2)}, u32[]{:S(2)}) collective-permute-start(bf16[384,512]{1,0:T(8,128)(2,1)S(1)} %get-tuple-element.31), channel_id=1, source_target_pairs={{1,16},{5,20},{9,17},{13,21},{16,8},{20,12},{24,9},{28,13},{3,18},... | collective-permute-start | bytes 1179656 | tf_op jit(solution)/shard_map/ppermute | solution.py:173
  11.1 33.9 %collective-permute-start.3 = (bf16[768,512]{1,0:T(8,128)(2,1)}, bf16[768,512]{1,0:T(8,128)(2,1)}, u32[]{:S(2)}, u32[]{:S(2)}) collective-permute-start(bf16[768,512]{1,0:T(8,128)(2,1)} %collective-permute-done.1.own_b), channel_id=1, source_target_pairs={{1,5},{5,1},{9,13},{13,9},{16,20},{20,16},{24,28},{28,24},{3,7},{7... | collective-permute-start | bytes 2359304 | tf_op jit(solution)/shard_map/ppermute | solution.py:173
  17.4 23.0 %collective-permute-start.5 = (bf16[384,512]{1,0:T(8,128)(2,1)}, bf16[384,512]{1,0:T(8,128)(2,1)}, u32[]{:S(2)}, u32[]{:S(2)}) collective-permute-start(bf16[384,512]{1,0:T(8,128)(2,1)} %collective-permute-done.4.own_a), channel_id=1, source_target_pairs={{8,0},{9,1},{12,4},{13,5},{16,24},{17,25},{20,28},{21,29},{10,2},{... | collective-permute-start | bytes 1179656 | tf_op jit(solution)/shard_map/ppermute | solution.py:173
  25.4 18.9 %collective-permute-start.9 = (bf16[384,512]{1,0:T(8,128)(2,1)S(1)}, bf16[384,512]{1,0:T(8,128)(2,1)}, u32[]{:S(2)}, u32[]{:S(2)}) collective-permute-start(bf16[384,512]{1,0:T(8,128)(2,1)S(1)} %collective-permute-done.8.own_a), channel_id=1, source_target_pairs={{8,0},{9,1},{12,4},{13,5},{16,24},{17,25},{20,28},{21,29},{10,2},{... | collective-permute-start | bytes 1179656 | tf_op jit(solution)/shard_map/ppermute | solution.py:173
  30.7 113.5 %all-to-all-start = ((bf16[4,192,512]{2,1,0:T(8,128)(2,1)}), bf16[4,192,512]{2,1,0:T(8,128)(2,1)}, u32[]{:S(2)}, u32[]{:S(2)}) async-start(bf16[4,192,512]{2,1,0:T(8,128)(2,1)} %shard_map.55), calls=%async_computation | async-start | bytes 1572864 | tf_op jit(solution)/shard_map/all_to_all | solution.py:558
  34.9 10.1 %copy-start = (bf16[768,512]{1,0:T(8,128)(2,1)S(1)}, bf16[768,512]{1,0:T(8,128)(2,1)}, u32[]{:S(2)}) copy-start(bf16[768,512]{1,0:T(8,128)(2,1)} %own_a.1) | copy-start | bytes 2359300
  36.7 14.6 %collective-permute-start.6 = (bf16[384,512]{1,0:T(8,128)(2,1)}, bf16[384,512]{1,0:T(8,128)(2,1)}, u32[]{:S(2)}, u32[]{:S(2)}) collective-permute-start(bf16[384,512]{1,0:T(8,128)(2,1)} %collective-permute-done.4.own_a), channel_id=1, source_target_pairs={{8,12},{9,13},{12,8},{13,9},{16,20},{17,21},{20,16},{21,17},{10,14... | collective-permute-start | bytes 1179656 | tf_op jit(solution)/shard_map/ppermute | solution.py:173
  40.4 11.0 %collective-permute-start.7 = (bf16[384,512]{1,0:T(8,128)(2,1)}, bf16[384,512]{1,0:T(8,128)(2,1)}, u32[]{:S(2)}, u32[]{:S(2)}) collective-permute-start(bf16[384,512]{1,0:T(8,128)(2,1)} %collective-permute-done.5.own_b), channel_id=1, source_target_pairs={{0,4},{1,5},{4,0},{5,1},{24,28},{25,29},{28,24},{29,25},{2,6},{3,7... | collective-permute-start | bytes 1179656 | tf_op jit(solution)/shard_map/ppermute | solution.py:173
  41.9 9.3 %copy-start.9 = (s32[192]{0:T(256)S(1)}, s32[192]{0:T(256)}, u32[]{:S(2)}) copy-start(s32[192]{0:T(256)} %targets.3) | copy-start | bytes 2308
  41.9 9.3 %copy-start.10 = (s32[3]{0:T(128)S(1)}, s32[3]{0:T(128)}, u32[]{:S(2)}) copy-start(s32[3]{0:T(128)} %param.9) | copy-start | bytes 40
  42.0 16.7 %collective-permute-start.10 = (bf16[384,512]{1,0:T(8,128)(2,1)S(1)}, bf16[384,512]{1,0:T(8,128)(2,1)S(1)}, u32[]{:S(2)}, u32[]{:S(2)}) collective-permute-start(bf16[384,512]{1,0:T(8,128)(2,1)S(1)} %collective-permute-done.8.own_a), channel_id=1, source_target_pairs={{8,12},{9,13},{12,8},{13,9},{16,20},{17,21},{20,16},{21,17},{10,14... | collective-permute-start | bytes 1179656 | tf_op jit(solution)/shard_map/ppermute | solution.py:173
  44.3 14.4 %collective-permute-start.11 = (bf16[384,512]{1,0:T(8,128)(2,1)}, bf16[384,512]{1,0:T(8,128)(2,1)S(1)}, u32[]{:S(2)}, u32[]{:S(2)}) collective-permute-start(bf16[384,512]{1,0:T(8,128)(2,1)} %collective-permute-done.9.own_b), channel_id=1, source_target_pairs={{0,4},{1,5},{4,0},{5,1},{24,28},{25,29},{28,24},{29,25},{2,6},{3,7... | collective-permute-start | bytes 1179656 | tf_op jit(solution)/shard_map/ppermute | solution.py:173
  50.2 12.9 %collective-permute-start.12 = (bf16[768,512]{1,0:T(8,128)(2,1)S(1)}, bf16[768,512]{1,0:T(8,128)(2,1)S(1)}, u32[]{:S(2)}, u32[]{:S(2)}) collective-permute-start(bf16[768,512]{1,0:T(8,128)(2,1)S(1)} %get-tuple-element.21), channel_id=1, source_target_pairs={{0,1},{1,0},{4,5},{5,4},{8,9},{9,8},{12,13},{13,12},{16,17},{17,16... | collective-permute-start | bytes 2359304 | tf_op jit(solution)/shard_map/ppermute | solution.py:173
  51.3 10.1 %collective-permute-start = (s32[195]{0:T(256)S(1)}, s32[195]{0:T(256)S(1)}, u32[]{:S(2)}, u32[]{:S(2)}) collective-permute-start(s32[195]{0:T(256)S(1)} %pad_add_fusion), channel_id=1, source_target_pairs={{0,1},{1,0},{4,5},{5,4},{8,9},{9,8},{12,13},{13,12},{16,17},{17,16... | collective-permute-start | bytes 2348 | tf_op jit(solution)/shard_map/ppermute | solution.py:173
  54.8 6.7 %collective-permute-start.13 = (bf16[384,512]{1,0:T(8,128)(2,1)S(1)}, bf16[384,512]{1,0:T(8,128)(2,1)S(1)}, u32[]{:S(2)}, u32[]{:S(2)}) collective-permute-start(bf16[384,512]{1,0:T(8,128)(2,1)S(1)} %get-tuple-element.22), channel_id=1, source_target_pairs={{0,1},{1,0},{4,5},{5,4},{8,9},{9,8},{12,13},{13,12},{16,17},{17,16... | collective-permute-start | bytes 1179656 | tf_op jit(solution)/shard_map/ppermute | solution.py:173
  61.3 1.8 %collective-permute-start.14 = (bf16[384,512]{1,0:T(8,128)(2,1)S(1)}, bf16[384,512]{1,0:T(8,128)(2,1)S(1)}, u32[]{:S(2)}, u32[]{:S(2)}) collective-permute-start(bf16[384,512]{1,0:T(8,128)(2,1)S(1)} %get-tuple-element.23), channel_id=1, source_target_pairs={{0,1},{1,0},{4,5},{5,4},{8,9},{9,8},{12,13},{13,12},{16,17},{17,16... | collective-permute-start | bytes 1179656 | tf_op jit(solution)/shard_map/ppermute | solution.py:173
  119.9 10.6 %collective-permute-start.15 = (bf16[768,128]{1,0:T(8,128)(2,1)S(1)}, bf16[768,128]{1,0:T(8,128)(2,1)S(1)}, u32[]{:S(2)}, u32[]{:S(2)}) collective-permute-start(bf16[768,128]{1,0:T(8,128)(2,1)S(1)} %get-tuple-element.27), channel_id=1, source_target_pairs={{0,0},{1,8},{4,4},{5,12},{8,16},{9,24},{12,20},{13,28},{16,1},{17,... | collective-permute-start | bytes 589832 | tf_op jit(solution)/shard_map/ppermute | solution.py:173
  124.6 16.8 %collective-permute-start.17 = (bf16[768,128]{1,0:T(8,128)(2,1)S(1)}, bf16[768,128]{1,0:T(8,128)(2,1)S(1)}, u32[]{:S(2)}, u32[]{:S(2)}) collective-permute-start(bf16[768,128]{1,0:T(8,128)(2,1)S(1)} %get-tuple-element.28), channel_id=1, source_target_pairs={{0,8},{1,16},{4,12},{5,20},{8,24},{9,0},{12,28},{13,4},{16,9},{17,... | collective-permute-start | bytes 589832 | tf_op jit(solution)/shard_map/ppermute | solution.py:173
  126.5 14.8 %collective-permute-start.19 = (bf16[768,128]{1,0:T(8,128)(2,1)S(1)}, bf16[768,128]{1,0:T(8,128)(2,1)S(1)}, u32[]{:S(2)}, u32[]{:S(2)}) collective-permute-start(bf16[768,128]{1,0:T(8,128)(2,1)S(1)} %get-tuple-element.29), channel_id=1, source_target_pairs={{0,16},{1,24},{4,20},{5,28},{8,0},{9,8},{12,4},{13,12},{16,17},{17... | collective-permute-start | bytes 589832 | tf_op jit(solution)/shard_map/ppermute | solution.py:173
  128.6 14.8 %collective-permute-start.21 = (bf16[768,128]{1,0:T(8,128)(2,1)S(1)}, bf16[768,128]{1,0:T(8,128)(2,1)S(1)}, u32[]{:S(2)}, u32[]{:S(2)}) collective-permute-start(bf16[768,128]{1,0:T(8,128)(2,1)S(1)} %get-tuple-element.30), channel_id=1, source_target_pairs={{0,24},{1,0},{4,28},{5,4},{8,8},{9,16},{12,12},{13,20},{16,25},{17... | collective-permute-start | bytes 589832 | tf_op jit(solution)/shard_map/ppermute | solution.py:173
  130.4 25.9 %copy-start.1 = (bf16[768,128]{1,0:T(8,128)(2,1)}, bf16[768,128]{1,0:T(8,128)(2,1)S(1)}, u32[]{:S(2)}) copy-start(bf16[768,128]{1,0:T(8,128)(2,1)S(1)} %collective-permute-done.15.refs_0_) | copy-start | bytes 589828
  130.4 20.5 %collective-permute-start.16 = (bf16[768,128]{1,0:T(8,128)(2,1)S(1)}, bf16[768,128]{1,0:T(8,128)(2,1)S(1)}, u32[]{:S(2)}, u32[]{:S(2)}) collective-permute-start(bf16[768,128]{1,0:T(8,128)(2,1)S(1)} %collective-permute-done.15.refs_0_), channel_id=1, source_target_pairs={{0,4},{1,5},{4,0},{5,1},{8,12},{9,13},{12,8},{13,9},{16,20},{17,21... | collective-permute-start | bytes 589832 | tf_op jit(solution)/shard_map/ppermute | solution.py:173
  141.3 15.0 %copy-start.2 = (bf16[768,128]{1,0:T(8,128)(2,1)}, bf16[768,128]{1,0:T(8,128)(2,1)S(1)}, u32[]{:S(2)}) copy-start(bf16[768,128]{1,0:T(8,128)(2,1)S(1)} %collective-permute-done.17.refs_2_) | copy-start | bytes 589828
  141.4 9.6 %collective-permute-start.18 = (bf16[768,128]{1,0:T(8,128)(2,1)S(1)}, bf16[768,128]{1,0:T(8,128)(2,1)S(1)}, u32[]{:S(2)}, u32[]{:S(2)}) collective-permute-start(bf16[768,128]{1,0:T(8,128)(2,1)S(1)} %collective-permute-done.17.refs_2_), channel_id=1, source_target_pairs={{0,4},{1,5},{4,0},{5,1},{8,12},{9,13},{12,8},{13,9},{16,20},{17,21... | collective-permute-start | bytes 589832 | tf_op jit(solution)/shard_map/ppermute | solution.py:173
  141.4 15.0 %copy-start.3 = (bf16[768,128]{1,0:T(8,128)(2,1)}, bf16[768,128]{1,0:T(8,128)(2,1)S(1)}, u32[]{:S(2)}) copy-start(bf16[768,128]{1,0:T(8,128)(2,1)S(1)} %collective-permute-done.19.refs_4_) | copy-start | bytes 589828
  141.4 12.0 %collective-permute-start.20 = (bf16[768,128]{1,0:T(8,128)(2,1)S(1)}, bf16[768,128]{1,0:T(8,128)(2,1)S(1)}, u32[]{:S(2)}, u32[]{:S(2)}) collective-permute-start(bf16[768,128]{1,0:T(8,128)(2,1)S(1)} %collective-permute-done.19.refs_4_), channel_id=1, source_target_pairs={{0,4},{1,5},{4,0},{5,1},{8,12},{9,13},{12,8},{13,9},{16,20},{17,21... | collective-permute-start | bytes 589832 | tf_op jit(solution)/shard_map/ppermute | solution.py:173
  143.4 13.0 %copy-start.4 = (bf16[768,128]{1,0:T(8,128)(2,1)}, bf16[768,128]{1,0:T(8,128)(2,1)S(1)}, u32[]{:S(2)}) copy-start(bf16[768,128]{1,0:T(8,128)(2,1)S(1)} %collective-permute-done.21.refs_6_) | copy-start | bytes 589828
  143.4 12.9 %collective-permute-start.22 = (bf16[768,128]{1,0:T(8,128)(2,1)S(1)}, bf16[768,128]{1,0:T(8,128)(2,1)S(1)}, u32[]{:S(2)}, u32[]{:S(2)}) collective-permute-start(bf16[768,128]{1,0:T(8,128)(2,1)S(1)} %collective-permute-done.21.refs_6_), channel_id=1, source_target_pairs={{0,4},{1,5},{4,0},{5,1},{8,12},{9,13},{12,8},{13,9},{16,20},{17,21... | collective-permute-start | bytes 589832 | tf_op jit(solution)/shard_map/ppermute | solution.py:173
  150.9 5.4 %copy-start.5 = (bf16[768,128]{1,0:T(8,128)(2,1)}, bf16[768,128]{1,0:T(8,128)(2,1)S(1)}, u32[]{:S(2)}) copy-start(bf16[768,128]{1,0:T(8,128)(2,1)S(1)} %collective-permute-done.16.refs_1_) | copy-start | bytes 589828
  150.9 5.4 %copy-start.6 = (bf16[768,128]{1,0:T(8,128)(2,1)}, bf16[768,128]{1,0:T(8,128)(2,1)S(1)}, u32[]{:S(2)}) copy-start(bf16[768,128]{1,0:T(8,128)(2,1)S(1)} %collective-permute-done.18.refs_3_) | copy-start | bytes 589828
  153.4 3.0 %copy-start.7 = (bf16[768,128]{1,0:T(8,128)(2,1)}, bf16[768,128]{1,0:T(8,128)(2,1)S(1)}, u32[]{:S(2)}) copy-start(bf16[768,128]{1,0:T(8,128)(2,1)S(1)} %collective-permute-done.20.refs_5_) | copy-start | bytes 589828
  156.4 0.7 copy-start.8

commit v2 on v1

--- a/solution.py
+++ b/solution.py
@@ -275,21 +275,20 @@
     )(info, own_a, own_b, other_a, other_b, w)
 
 
-TQ = 256
+TQ = 1536
 TK = 512
+SUB = 256
+DSUB = 256
 
 
 def attend_kernel(info, targets, lengths, *refs):
-    pieces, (att_ref, u_ref, stat_ref, q_s, v0, v1, k_s, k0, k1) = refs[:-9], refs[-9:]
+    pieces, (att_ref, u_ref, stat_ref, q_s, v0, v1, k0, k1) = refs[:-8], refs[-8:]
     seq = att_ref.shape[0]
-    lane = lax.broadcasted_iota(jnp.int32, (RB, 128), 1)
-    low = lane < DH
+    low = lax.broadcasted_iota(jnp.int32, (RB, 128), 1) < DH
     zero = jnp.zeros((RB, 128), jnp.bfloat16)
-
     for n, piece in enumerate(pieces):
         base = info[n]
-
-        @pl.loop(0, piece.shape[0] // RB, unroll=4)
+        @pl.loop(0, piece.shape[0] // RB, unroll=8)
         def _(b):
             frm = pl.ds(pl.multiple_of(b * RB, RB), RB)
             to = pl.ds(pl.multiple_of(targets[base + b] * RB, RB), RB)
@@ -298,90 +297,79 @@
             v0[to, :] = jnp.where(low, v, zero)
             v1[to, :] = jnp.where(low, zero, v)
             q_s[to, :] = piece[frm, 256:384] * 0.5
-            k_s[to, :] = piece[frm, 384:512]
-
-    row = lax.broadcasted_iota(jnp.int32, (128, 256), 0)
-
-    @pl.loop(0, seq // 256)
-    def _(i):
-        at = pl.ds(pl.multiple_of(i * 256, 256), 256)
-        kt = k_s[at, :].T
-        k0[:, at] = jnp.where(row < DH, kt, jnp.zeros_like(kt))
-        k1[:, at] = jnp.where(row < DH, jnp.zeros_like(kt), kt)
-
+            k = piece[frm, 384:512]
+            k0[to, :] = jnp.where(low, k, zero)
+            k1[to, :] = jnp.where(low, zero, k)
     ends = []
     total = jnp.int32(0)
     for i in range(lengths.shape[0]):
         total = total + lengths[i]
         ends.append(total)
-
     def start_of(p):
         best = p * 0
         for e in ends:
             best = jnp.where(p >= e, e, best)
         return best
-
+    def term(q0, rows, k0_at, keys, first, causal):
+        at = pl.ds(pl.multiple_of(q0, 256), rows)
+        q = q_s[at, :]
+        total = None
+        for s in range(keys // SUB):
+            ks = pl.ds(pl.multiple_of(k0_at + s * SUB, SUB), SUB)
+            if first is not None:
+                kp = k0_at + s * SUB + lax.broadcasted_iota(jnp.int32, (1, SUB), 1)
+                ok = kp >= first
+                if causal:
+                    ok = ok & (kp <= q0 + lax.broadcasted_iota(jnp.int32, (rows, 1), 0))
+            for kk, vv in ((k0, v0), (k1, v1)):
+                t = lax.dot_general(q, kk[ks, :], (((1,), (1,)), ((), ())), preferred_element_type=jnp.float32)
+                w = t + t * jnp.tanh(t)
+                if first is not None:
+                    w = jnp.where(ok, w, 0.0)
+                d = jnp.dot(w.astype(jnp.bfloat16), vv[ks, :], preferred_element_type=jnp.float32)
+                total = d if total is None else total + d
+        att_ref[at, :] += total
     @pl.loop(0, seq // TQ)
     def _(qi):
         q0 = qi * TQ
         at = pl.ds(pl.multiple_of(q0, TQ), TQ)
-        q = q_s[at, :]
-
-        def tile(j, acc, masked):
-            ks = pl.ds(pl.multiple_of(j * TK, TK), TK)
-            if masked:
-                qp = q0 + lax.broadcasted_iota(jnp.int32, (TQ, 1), 0)
-                kp = j * TK + lax.broadcasted_iota(jnp.int32, (1, TK), 1)
-                ok = (kp <= qp) & (kp >= start_of(qp))
-            for kt, vv in ((k0, v0), (k1, v1)):
-                t = jnp.dot(q, kt[:, ks], preferred_element_type=jnp.float32)
-                w = t + t * jnp.tanh(t)
-                if masked:
-                    w = jnp.where(ok, w, 0.0)
-                acc = acc + jnp.dot(
-                    w.astype(jnp.bfloat16), vv[ks, :], preferred_element_type=jnp.float32
-                )
-            return acc
-
+        att_ref[at, :] = jnp.zeros((TQ, 128), jnp.float32)
+        first = start_of(q0 + lax.broadcasted_iota(jnp.int32, (TQ, 1), 0))
+        diag = q0 // TK
         lo = start_of(q0) // TK
-        last = start_of(q0 + TQ - 1)
-        hi = (q0 + TQ + TK - 1) // TK
-        diag = q0 // TK
-        mid = jnp.minimum((last + TK - 1) // TK, diag)
+        mid = jnp.minimum((start_of(q0 + TQ - 1) + TK - 1) // TK, diag)
         mid = jnp.maximum(mid, lo)
-        acc = jnp.zeros((TQ, 128), jnp.float32)
-        acc = lax.fori_loop(lo, mid, lambda j, c: tile(j, c, True), acc)
-        acc = lax.fori_loop(mid, diag, lambda j, c: tile(j, c, False), acc)
-        acc = lax.fori_loop(jnp.maximum(mid, diag), hi, lambda j, c: tile(j, c, True), acc)
-        att_ref[at, :] = acc
-        flip = acc.T
-        stat_ref[0:1, at] = jnp.sum(flip, axis=0, keepdims=True)
-        stat_ref[1:2, at] = jnp.sum(flip * flip, axis=0, keepdims=True)
-
-
+        @pl.loop(lo, mid)
+        def _(j):
+            term(q0, TQ, j * TK, TK, first, False)
+        @pl.loop(mid, diag)
+        def _(j):
+            term(q0, TQ, j * TK, TK, None, False)
+        for s in range(TQ // DSUB):
+            term(q0 + s * DSUB, TQ - s * DSUB, q0 + s * DSUB, DSUB, first[s * DSUB :], True)
+        for s in range(TQ // 256):
+            part = pl.ds(pl.multiple_of(q0 + s * 256, 256), 256)
+            flip = att_ref[part, :].T
+            stat_ref[0:1, part] = jnp.sum(flip, axis=0, keepdims=True)
+            stat_ref[1:2, part] = jnp.sum(flip * flip, axis=0, keepdims=True)
 def attend(info, targets, lengths, pieces):
     seq = sum(p.shape[0] for p in pieces)
     smem = pl.BlockSpec(memory_space=pltpu.SMEM)
     vmem = pl.BlockSpec(memory_space=pltpu.VMEM)
     return pl.pallas_call(
         attend_kernel,
-        out_shape=(
-            jax.ShapeDtypeStruct((seq, 128), jnp.float32),
-            jax.ShapeDtypeStruct((seq, 128), jnp.bfloat16),
-            jax.ShapeDtypeStruct((2, seq), jnp.float32),
-        ),
-        in_specs=[smem] * 3 + [vmem] * len(pieces),
-        out_specs=(vmem,) * 3,
-        scratch_shapes=[pltpu.VMEM((seq, 128), jnp.bfloat16)] * 4
-        + [pltpu.VMEM((128, seq), jnp.bfloat16)] * 2,
-        compiler_params=pltpu.CompilerParams(vmem_limit_bytes=40 * 1024 * 1024),
+        out_shape=(jax.ShapeDtypeStruct((seq, 128), jnp.float32), jax.ShapeDtypeStruct((seq, 128), jnp.bfloat16), jax.ShapeDtypeStruct((2, seq), jnp.float32)),
+        in_specs=[smem] * 3 + [vmem] * len(pieces), out_specs=(vmem,) * 3,
+        scratch_shapes=[pltpu.VMEM((seq, 128), jnp.bfloat16)] * 5,
+        compiler_params=pltpu.CompilerParams(vmem_limit_bytes=50 * 1024 * 1024),
         cost_estimate=pl.CostEstimate(
             flops=2 * seq * seq * 128, bytes_accessed=seq * 128 * 14, transcendentals=seq * seq
         ),
     )(info, targets, lengths, *pieces)
 
 
-def gate_kernel(info, att_ref, u_ref, stat_ref, *outs):
+def gate_kernel(info, att_ref, u_ref, *refs):
+    stats, outs = refs[:4], refs[4:]
     rows = outs[0].shape[0]
     step = 256
     for k, out in enumerate(outs):
@@ -390,8 +378,11 @@
         @pl.loop(0, rows // step)
         def _(i):
             at = pl.ds(pl.multiple_of(block * rows + i * step, step), step)
-            mean = stat_ref[0:1, at] / D
-            square = stat_ref[1:2, at] / D
+            sums = stats[0][:, at]
+            for other in stats[1:]:
+                sums = sums + other[:, at]
+            mean = sums[0:1] / D
+            square = sums[1:2] / D
             scale = lax.rsqrt(square - mean * mean + eps_norm)
             mean = jnp.broadcast_to(mean, (128, step)).T
             scale = jnp.broadcast_to(scale, (128, step)).T
@@ -399,106 +390,76 @@
             out[pl.ds(pl.multiple_of(i * step, step), step), :] = gated.astype(jnp.bfloat16)
 
 
-def gate(info, att, u, stat, count):
+def gate(info, att, u, stats, count):
     rows = att.shape[0] // count
     vmem = pl.BlockSpec(memory_space=pltpu.VMEM)
     out = jax.ShapeDtypeStruct((rows, 128), jnp.bfloat16)
     return pl.pallas_call(
         gate_kernel,
         out_shape=(out,) * count,
-        in_specs=[pl.BlockSpec(memory_space=pltpu.SMEM)] + [vmem] * 3,
+        in_specs=[pl.BlockSpec(memory_space=pltpu.SMEM)] + [vmem] * (2 + len(stats)),
         out_specs=(vmem,) * count,
         compiler_params=pltpu.CompilerParams(vmem_limit_bytes=40 * 1024 * 1024),
         cost_estimate=pl.CostEstimate(flops=att.size * 8, bytes_accessed=att.size * 8, transcendentals=0),
-    )(info, att, u, stat)
-
-
-def outgoing_kernel(info, targets, events_ref, out_ref):
+    )(info, att, u, *stats)
+
+
+def outgoing_kernel(info, targets, events_ref, after_ref, out_ref):
     count = out_ref.shape[0]
     blocks = events_ref.shape[0] // RB
     base = info[0] * blocks
 
-    def step(b, filled):
-        owner = targets[base + b] // blocks
-        place = jnp.int32(0)
-        for k in range(count):
-            place = jnp.where(owner == k, filled[k], place)
+    @pl.loop(0, blocks, unroll=4)
+    def _(b):
+        t = targets[base + b]
         frm = pl.ds(pl.multiple_of(b * RB, RB), RB)
-        to = pl.ds(pl.multiple_of(place * RB, RB), RB)
-        out_ref[pl.ds(owner, 1), to, :] = events_ref[frm, :][None]
-        return tuple(filled[k] + (owner == k).astype(jnp.int32) for k in range(count))
-
-    lax.fori_loop(0, blocks, step, (jnp.int32(0),) * count)
-
-
-def outgoing(info, targets, events, count):
+        to = pl.ds(pl.multiple_of(lax.rem(t, blocks // count) * RB, RB), RB)
+        out_ref[pl.ds(t // blocks, 1), to, :] = events_ref[frm, :][None]
+
+
+def outgoing(info, targets, events, after, count):
     smem = pl.BlockSpec(memory_space=pltpu.SMEM)
     vmem = pl.BlockSpec(memory_space=pltpu.VMEM)
     return pl.pallas_call(
         outgoing_kernel,
         out_shape=jax.ShapeDtypeStruct((count, events.shape[0] // count, events.shape[1]), events.dtype),
-        in_specs=[smem, smem, vmem],
+        in_specs=[smem, smem, vmem, pl.BlockSpec(memory_space=pl.ANY)],
         out_specs=vmem,
         cost_estimate=pl.CostEstimate(flops=0, bytes_accessed=events.size * 4, transcendentals=0),
-    )(info, targets, events)
-
-
-def place_kernel(info, targets, in_ref, out_ref):
-    blocks = out_ref.shape[0] // RB
-
-    def step(g, filled):
-        t = targets[g]
-        mine = t // blocks == info[0]
-
-        @pl.when(mine)
-        def _():
-            frm = pl.ds(pl.multiple_of(filled * RB, RB), RB)
-            to = pl.ds(pl.multiple_of(lax.rem(t, blocks) * RB, RB), RB)
-            out_ref[to, :] = in_ref[frm, :]
-
-        return filled + mine.astype(jnp.int32)
-
-    lax.fori_loop(0, targets.shape[0], step, jnp.int32(0))
-
-
-def place(info, targets, incoming):
+    )(info, targets, events, after)
+
+
+def finish_kernel(info, quarter, res_ref, w_ref, *refs):
+    pieces, out_ref = refs[:-1], refs[-1]
+    count, step = res_ref.shape[0], res_ref.shape[1]
+
+    @pl.loop(0, count)
+    def _(i):
+        at = pl.ds(pl.multiple_of(quarter[i] * step, step), step)
+        acc = res_ref[i].astype(jnp.float32)
+        for n in range(0, len(pieces), 2):
+            two = (n, n + 1)
+            left = jnp.concatenate([pieces[m][at, :] for m in two], axis=1)
+            right = jnp.concatenate(
+                [w_ref[pl.ds(pl.multiple_of(info[m] * 128, 128), 128), :] for m in two], axis=0
+            )
+            acc = acc + jnp.dot(left, right, preferred_element_type=jnp.float32)
+        out_ref[at, :] = acc.astype(out_ref.dtype)
+
+
+def finish(info, quarter, residual, w_out, pieces):
     smem = pl.BlockSpec(memory_space=pltpu.SMEM)
     vmem = pl.BlockSpec(memory_space=pltpu.VMEM)
-    return pl.pallas_call(
-        place_kernel,
-        out_shape=jax.ShapeDtypeStruct(incoming.shape, incoming.dtype),
-        in_specs=[smem, smem, vmem],
-        out_specs=vmem,
-        cost_estimate=pl.CostEstimate(flops=0, bytes_accessed=incoming.size * 4, transcendentals=0),
-    )(info, targets, incoming)
-
-
-def finish_kernel(info, res_ref, w_ref, *refs):
-    pieces, out_ref = refs[:-1], refs[-1]
-    step = 256
-    rows = res_ref.shape[0]
-
-    @pl.loop(0, rows // step)
-    def _(i):
-        at = pl.ds(pl.multiple_of(i * step, step), step)
-        acc = res_ref[at, :].astype(jnp.float32)
-        for n, piece in enumerate(pieces):
-            feats = pl.ds(pl.multiple_of(info[n] * 128, 128), 128)
-            acc = acc + jnp.dot(piece[at, :], w_ref[feats, :], preferred_element_type=jnp.float32)
-        out_ref[at, :] = acc.astype(out_ref.dtype)
-
-
-def finish(info, residual, w_out, pieces):
-    vmem = pl.BlockSpec(memory_space=pltpu.VMEM)
+    rows = residual.shape[0] * residual.shape[1]
     return pl.pallas_call(
         finish_kernel,
-        out_shape=jax.ShapeDtypeStruct(residual.shape, jnp.bfloat16),
-        in_specs=[pl.BlockSpec(memory_space=pltpu.SMEM)] + [vmem] * (2 + len(pieces)),
+        out_shape=jax.ShapeDtypeStruct((rows, residual.shape[2]), jnp.bfloat16),
+        in_specs=[smem] * 2 + [vmem] * (2 + len(pieces)),
         out_specs=vmem,
         cost_estimate=pl.CostEstimate(
             flops=2 * residual.size * D, bytes_accessed=residual.size * 4 + w_out.size * 2, transcendentals=0
         ),
-    )(info, residual, w_out, *pieces)
+    )(info, quarter, residual, w_out, *pieces)
 
 
 def team_body(events, w_proj, w_out, block_target, user_lengths):
@@ -519,7 +480,12 @@
     partner = move(events, to_partner)
     parts = 2
     span = rows // parts
-    remote = [move(events[i * span : (i + 1) * span], to_other_team) for i in range(parts)]
+    remote = []
+    for i in range(parts):
+        chunk = events[i * span : (i + 1) * span]
+        if remote:
+            chunk, _ = lax.optimization_barrier((chunk, remote[-1]))
+        remote.append(move(chunk, to_other_team))
     x_partner = move(partner, across(lambda half, zlo, head, core: core != half))
     relayed = [move(r, inner_to_outer) for r in remote]
     x_inner = [move(r, across(lambda half, zlo, head, core: (zlo ^ half) == 1)) for r in remote]
@@ -554,13 +520,21 @@
     starts += [sib_slot2 * blocks + i * part_blocks for i in range(parts)]
     att, u, stat = attend(ints(*starts), targets, lengths, mine + got)
 
-    send = outgoing(ints(z), targets_here, events, 4)
-    came = lax.all_to_all(send, ("half", "zlo"), split_axis=0, concat_axis=0, tiled=True)
-    residual = place(ints(z), targets_here, came.reshape(rows, events.shape[1]))
-
-    stat = lax.psum(stat, ("zlo", "head", "core"))
+    send = outgoing(ints(z), targets_here, events, mine[-1], 4)
+    residual = lax.all_to_all(send, ("half", "zlo"), split_axis=0, concat_axis=0, tiled=True)
+    by_shard = targets_here.reshape(4, blocks)
+    quarter = jnp.max(
+        jnp.where(by_shard // blocks == z, by_shard % blocks // (blocks // 4), 0), axis=1
+    )
+
+    stat = stat + move(stat, other_core)
+    stats = [stat]
+    for dz, dx in ((0, 1), (1, 0), (1, 1)):
+        stats.append(
+            move(stat, lambda half, zlo, head, core, dz=dz, dx=dx: (half, zlo ^ dz, head ^ dx, core))
+        )
     me = zlo * 2 + core
-    gated = gate(ints(me), att, u, stat, 4)
+    gated = gate(ints(me), att, u, stats, 4)
 
     def to_block(k):
         def rule(half, zlo, head, core):
@@ -575,7 +549,7 @@
         source = lax.rem(z - k + 4, 4)
         pieces += [piece, move(piece, across(lambda *p: True))]
         feats += [head * 4 + source, (1 - head) * 4 + source]
-    return finish(ints(*feats), residual, w_out, pieces)
+    return finish(ints(*feats), quarter, residual, w_out, pieces)
 
 
 def solution(mesh):

time: 163 us -> 139 us (0.85)
  blocking collectives: 24.7 us -> 0 us
  Pallas kernels: 58.1 us -> 39.4 us
  waiting for transfers between devices: 30.8 us -> 41.9 us
  starting transfers between devices: 43.3 us -> 48.5 us
  local copies, waits for them, and re-layouts: 4.41 us -> 7.53 us
    psum x1 -> x0, blocking collectives: 24.7 us -> none  [team_body(): stat = lax.psum(stat, ('zlo', 'head', 'core'))]
    pallas_call x1, Pallas kernels: 30.3 us -> 17.1 us  [attend(): pl.pallas_call(attend_kernel, out_shape=(jax.ShapeDtypeStruct((seq, 128),...]
    ppermute x23 -> x27, waiting for transfers between devices: 30.8 us -> 41.9 us  [move(): return lax.ppermute(value, ROUTE, route(rule))]
    pallas_call x2 -> x1, Pallas kernels: 11.7 us -> 4.29 us  [finish(): pl.pallas_call(finish_kernel, out_shape=jax.ShapeDtypeStruct((rows, resid...]
    all_to_all x1, starting transfers between devices: 4.19 us -> 7.58 us  [team_body(): lax.all_to_all(send, ('half', 'zlo'), split_axis=0, concat_axis=0, tiled=...]
    unnamed x22 -> x38, local copies, waits for them, and re-layouts: 0.7 us -> 3.64 us
    pallas_call x3, Pallas kernels: 11.3 us -> 13.7 us  [project(): pl.pallas_call(project_kernel, out_shape=(out, out), in_specs=[pl.BlockSp...]
    ppermute x23 -> x27, starting transfers between devices: 39.1 us -> 40.9 us  [move(): return lax.ppermute(value, ROUTE, route(rule))]
  transfers between devices with their start and end apart: 24 -> 28, of which waited for: 9 -> 12; matrix products, arithmetic and copies ran while one was open for 2% -> 4% of each run, Pallas kernels for 33% -> 25%
where the time goes in v2:
time: 139 us
  starting transfers between devices  48.5 us (35%)
  waiting for transfers between devices  41.9 us (30%)
  Pallas kernels  39.4 us (28%)
  local copies, waits for them, and re-layouts  7.53 us (5%)
    ppermute x27, waiting for transfers between devices, move(): return lax.ppermute(value, ROUTE, route(rule))  41.9 us
    ppermute x27, starting transfers between devices, move(): return lax.ppermute(value, ROUTE, route(rule))  40.9 us
    pallas_call x1, Pallas kernels, attend(): pl.pallas_call(attend_kernel, out_shape=(jax.ShapeDtypeStruct((seq, 128),...  17.1 us
    pallas_call x3, Pallas kernels, project(): pl.pallas_call(project_kernel, out_shape=(out, out), in_specs=[pl.BlockSp...  13.7 us
    all_to_all x1, starting transfers between devices, team_body(): lax.all_to_all(send, ('half', 'zlo'), split_axis=0, concat_axis=0, tiled=...  7.58 us
    pallas_call x1, Pallas kernels, finish(): pl.pallas_call(finish_kernel, out_shape=jax.ShapeDtypeStruct((rows, resid...  4.29 us
    unnamed x38, local copies, waits for them, and re-layouts  3.64 us
  transfers between devices with their start and end apart: 28, of which 12 were waited for; matrix products, arithmetic and copies ran while one was open for 4% of the time, Pallas kernels for 25%

profile of v2, /device:TPU:8, one launch (start us, length us, event | category | flops | bytes accessed | tf_op | source)
XLA Modules:
  0.0 138.7 jit_solution(6231998835406535034)
XLA Ops:
  0.0 2.2 %collective-permute-start.6 = (bf16[768,512]{1,0:T(8,128)(2,1)}, bf16[768,512]{1,0:T(8,128)(2,1)}, u32[]{:S(2)}, u32[]{:S(2)}) collective-permute-start(bf16[768,512]{1,0:T(8,128)(2,1)} %own_a.1), channel_id=1, source_target_pairs={{0,9},{4,13},{8,1},{12,5},{17,24},{21,28},{25,16},{29,20},{2,11},{... | collective-permute-start | bytes 2359304 | tf_op jit(solution)/shard_map/ppermute | solution.py:173
  2.2 1.2 fusion.4
  3.4 1.3 collective-permute-start
  4.7 3.9 %collective-permute-start.7 = (bf16[768,512]{1,0:T(8,128)(2,1)}, bf16[768,512]{1,0:T(8,128)(2,1)}, u32[]{:S(2)}, u32[]{:S(2)}) collective-permute-start(bf16[768,512]{1,0:T(8,128)(2,1)} %own_a.1), channel_id=1, source_target_pairs={{0,4},{4,0},{8,12},{12,8},{17,21},{21,17},{25,29},{29,25},{2,6},{6... | collective-permute-start | bytes 2359304 | tf_op jit(solution)/shard_map/ppermute | solution.py:173
  8.6 8.5 %collective-permute-done.own_a = bf16[384,512]{1,0:T(8,128)(2,1)} collective-permute-done((bf16[384,512]{1,0:T(8,128)(2,1)S(1)}, bf16[384,512]{1,0:T(8,128)(2,1)}, u32[]{:S(2)}, u32[]{:S(2)}) %collective-permute-start) | collective-permute-done | bytes 393248 | tf_op jit(solution)/shard_map/ppermute | solution.py:173
  17.1 1.3 collective-permute-start.1
  18.4 1.6 %collective-permute-start.8 = (bf16[768,512]{1,0:T(8,128)(2,1)}, bf16[768,512]{1,0:T(8,128)(2,1)}, u32[]{:S(2)}, u32[]{:S(2)}) collective-permute-start(bf16[768,512]{1,0:T(8,128)(2,1)} %collective-permute-done.6.own_b), channel_id=1, source_target_pairs={{1,5},{5,1},{9,13},{13,9},{16,20},{20,16},{24,28},{28,24},{3,7},{7... | collective-permute-start | bytes 2359304 | tf_op jit(solution)/shard_map/ppermute | solution.py:173
  20.0 2.0 %collective-permute-start.9 = (bf16[384,512]{1,0:T(8,128)(2,1)}, bf16[384,512]{1,0:T(8,128)(2,1)}, u32[]{:S(2)}, u32[]{:S(2)}) collective-permute-start(bf16[384,512]{1,0:T(8,128)(2,1)} %collective-permute-done.own_a), channel_id=1, source_target_pairs={{8,0},{9,1},{12,4},{13,5},{16,24},{17,25},{20,28},{21,29},{10,2},{... | collective-permute-start | bytes 1179656 | tf_op jit(solution)/shard_map/ppermute | solution.py:173
  22.0 9.0 %collective-permute-done.1.own_a = bf16[384,512]{1,0:T(8,128)(2,1)S(1)} collective-permute-done((bf16[384,512]{1,0:T(8,128)(2,1)S(1)}, bf16[384,512]{1,0:T(8,128)(2,1)S(1)}, u32[]{:S(2)}, u32[]{:S(2)}) %collective-permute-start.1) | collective-permute-done | bytes 393248 | tf_op jit(solution)/shard_map/ppermute | solution.py:173
  31.0 2.1 %collective-permute-start.2 = (bf16[384,512]{1,0:T(8,128)(2,1)S(1)}, bf16[384,512]{1,0:T(8,128)(2,1)}, u32[]{:S(2)}, u32[]{:S(2)}) collective-permute-start(bf16[384,512]{1,0:T(8,128)(2,1)S(1)} %collective-permute-done.1.own_a), channel_id=1, source_target_pairs={{8,0},{9,1},{12,4},{13,5},{16,24},{17,25},{20,28},{21,29},{10,2},{... | collective-permute-start | bytes 1179656 | tf_op jit(solution)/shard_map/ppermute | solution.py:173
  33.0 1.8 %constant_dynamic-slice_fusion.w_ref = bf16[4,1024,256]{2,1,0:T(8,128)(2,1)S(1)} fusion(bf16[4,1024,512]{2,1,0:T(8,128)(2,1)} %param.6, s32[]{:T(128)S(6)} %select_n.62), kind=kLoop, calls=%fused_computation.17 | loop fusion | bytes 4194308 | tf_op jit(solution)/shard_map/dynamic_slice | solution.py:477
  34.8 3.7 %collective-permute-start.10 = (bf16[384,512]{1,0:T(8,128)(2,1)}, bf16[384,512]{1,0:T(8,128)(2,1)}, u32[]{:S(2)}, u32[]{:S(2)}) collective-permute-start(bf16[384,512]{1,0:T(8,128)(2,1)} %collective-permute-done.own_a), channel_id=1, source_target_pairs={{8,12},{9,13},{12,8},{13,9},{16,20},{17,21},{20,16},{21,17},{10,14... | collective-permute-start | bytes 1179656 | tf_op jit(solution)/shard_map/ppermute | solution.py:173
  38.5 1.4 %collective-permute-start.11 = (bf16[384,512]{1,0:T(8,128)(2,1)}, bf16[384,512]{1,0:T(8,128)(2,1)}, u32[]{:S(2)}, u32[]{:S(2)}) collective-permute-start(bf16[384,512]{1,0:T(8,128)(2,1)} %collective-permute-done.9.own_b), channel_id=1, source_target_pairs={{0,4},{1,5},{4,0},{5,1},{24,28},{25,29},{28,24},{29,25},{2,6},{3,7... | collective-permute-start | bytes 1179656 | tf_op jit(solution)/shard_map/ppermute | solution.py:173
  40.1 2.3 %collective-permute-start.3 = (bf16[384,512]{1,0:T(8,128)(2,1)S(1)}, bf16[384,512]{1,0:T(8,128)(2,1)S(1)}, u32[]{:S(2)}, u32[]{:S(2)}) collective-permute-start(bf16[384,512]{1,0:T(8,128)(2,1)S(1)} %collective-permute-done.1.own_a), channel_id=1, source_target_pairs={{8,12},{9,13},{12,8},{13,9},{16,20},{17,21},{20,16},{21,17},{10,14... | collective-permute-start | bytes 1179656 | tf_op jit(solution)/shard_map/ppermute | solution.py:173
  42.5 0.7 collective-permute-start.4
  43.2 6.1 %shard_map.57 = (bf16[768,512]{1,0:T(8,128)(2,1)S(1)}, bf16[768,512]{1,0:T(8,128)(2,1)}) custom-call(s32[4]{0:T(128)S(1)} %add_add_fusion.1.info, bf16[768,512]{1,0:T(8,128)(2,1)S(1)} %copy-done, bf16[768,512]{1,0:T(8,128)(2,1)} %collective-permute-done.6.own_b, bf16[768,512]{1,0:T(8,128)(2,1)} %collective-permute-done.7.other_a, ...), custom_call_target="tpu_custom_call" | custom-call | flops 1610612736 | bytes 5242880 | tf_op jit(solution)/shard_map/pallas_call | solution.py:261
  49.5 0.5 collective-permute-start.5
  50.0 4.1 %shard_map.58 = (bf16[384,512]{1,0:T(8,128)(2,1)S(1)}, bf16[384,512]{1,0:T(8,128)(2,1)}) custom-call(s32[4]{0:T(128)S(1)} %add_add_fusion.info, bf16[384,512]{1,0:T(8,128)(2,1)} %collective-permute-done.own_a, bf16[384,512]{1,0:T(8,128)(2,1)} %collective-permute-done.9.own_b, bf16[384,512]{1,0:T(8,128)(2,1)} %collective-permute-done.10.other_a, ...), custom_call_target="tpu_custom_call" | custom-call | flops 805306368 | bytes 3670016 | tf_op jit(solution)/shard_map/pallas_call | solution.py:261
  54.2 0.7 copy-done.4
  55.4 3.4 %shard_map.55 = (bf16[384,512]{1,0:T(8,128)(2,1)S(1)}, bf16[384,512]{1,0:T(8,128)(2,1)}) custom-call(s32[4]{0:T(128)S(1)} %add_add_fusion.info, bf16[384,512]{1,0:T(8,128)(2,1)S(1)} %collective-permute-done.1.own_a, bf16[384,512]{1,0:T(8,128)(2,1)} %collective-permute-done.2.own_b, bf16[384,512]{1,0:T(8,128)(2,1)S(1)} %collective-permute-done.3.other_a, ...), custom_call_target="tpu_custom_call" | custom-call | flops 805306368 | bytes 3670016 | tf_op jit(solution)/shard_map/pallas_call | solution.py:261
  58.9 0.8 copy-done.2
  59.8 2.6 %shard_map.56 = bf16[4,192,512]{2,1,0:T(8,128)(2,1)} custom-call(s32[1]{0:T(128)} %bitcast.8.info, s32[192]{0:T(256)} %targets.1, bf16[768,512]{1,0:T(8,128)(2,1)} %own_a.1, bf16[384,512]{1,0:T(8,128)(2,1)} %copy-done.2), custom_call_target="tpu_custom_call" | custom-call | bytes 1572864 | tf_op jit(solution)/shard_map/pallas_call | solution.py:423
  62.4 7.6 %all-to-all-start = ((bf16[4,192,512]{2,1,0:T(8,128)(2,1)}), bf16[4,192,512]{2,1,0:T(8,128)(2,1)}, u32[]{:S(2)}, u32[]{:S(2)}) async-start(bf16[4,192,512]{2,1,0:T(8,128)(2,1)} %shard_map.56), calls=%async_computation | async-start | bytes 1572864 | tf_op jit(solution)/shard_map/all_to_all | solution.py:524
  70.1 17.1 %shard_map.59 = (f32[3072,128]{1,0:T(8,128)}, bf16[3072,128]{1,0:T(8,128)(2,1)S(1)}, f32[2,3072]{1,0:T(2,128)S(1)}) custom-call(s32[6]{0:T(128)S(1)} %stack.105.info, s32[192]{0:T(256)S(1)} %get-tuple-element.35.targets, s32[3]{0:T(128)S(1)} %broadcast_select_fusion.lengths, bf16[768,512]{1,0:T(8,128)(2,1)S(1)} %copy-done.7, bf16[384,512]{1,0:T(8,128)(2,1)S(1)} %copy-done.5, ...), custom_call_target="tpu_custom_call" | custom-call | flops 2415919104 | bytes 5505024 | tf_op jit(solution)/shard_map/pallas_call | solution.py:359
  87.2 1.2 collective-permute-done.15
  88.4 0.6 collective-permute-start.16
  89.3 2.7 %collective-permute-start.18 = (f32[2,3072]{1,0:T(2,128)S(1)}, f32[2,3072]{1,0:T(2,128)S(1)}, u32[]{:S(2)}, u32[]{:S(2)}) collective-permute-start(f32[2,3072]{1,0:T(2,128)S(1)} %add.89.refs_0_), channel_id=1, source_target_pairs={{0,12},{1,13},{4,8},{5,9},{8,4},{9,5},{12,0},{13,1},{16,28},{17,29... | collective-permute-start | bytes 73736 | tf_op jit(solution)/shard_map/ppermute | solution.py:173
  92.3 0.6 collective-permute-done.17.refs_2_
  93.0 1.1 collective-permute-done.18.refs_3_
  94.1 1.4 %copy-done.1 = f32[3072,128]{1,0:T(8,128)S(1)} copy-done((f32[3072,128]{1,0:T(8,128)S(1)}, f32[3072,128]{1,0:T(8,128)}, u32[]{:S(2)}) %copy-start.1) | copy-done | bytes 1572888
  95.5 1.7 %shard_map.60 = (bf16[768,128]{1,0:T(8,128)(2,1)S(1)}, bf16[768,128]{1,0:T(8,128)(2,1)S(1)}, bf16[768,128]{1,0:T(8,128)(2,1)S(1)}, bf16[768,128]{1,0:T(8,128)(2,1)S(1)}) custom-call(s32[1]{0:T(128)} %bitcast.13.info, f32[3072,128]{1,0:T(8,128)S(1)} %copy-done.1, bf16[3072,128]{1,0:T(8,128)(2,1)S(1)} %get-tuple-element.27.u_ref, f32[2,3072]{1,0:T(2,128)S(1)} %add.89.refs_0_, ...), custom_call_target="tpu_custom_call" | custom-call | flops 3145728 | bytes 3145728 | tf_op jit(solution)/shard_map/pallas_call | solution.py:397
  97.2 4.6 %collective-permute-start.19 = (bf16[768,128]{1,0:T(8,128)(2,1)S(1)}, bf16[768,128]{1,0:T(8,128)(2,1)S(1)}, u32[]{:S(2)}, u32[]{:S(2)}) collective-permute-start(bf16[768,128]{1,0:T(8,128)(2,1)S(1)} %get-tuple-element.29), channel_id=1, source_target_pairs={{0,0},{1,8},{4,4},{5,12},{8,16},{9,24},{12,20},{13,28},{16,1},{17,... | collective-permute-start | bytes 589832 | tf_op jit(solution)/shard_map/ppermute | solution.py:173
  101.8 1.9 %collective-permute-start.21 = (bf16[768,128]{1,0:T(8,128)(2,1)S(1)}, bf16[768,128]{1,0:T(8,128)(2,1)S(1)}, u32[]{:S(2)}, u32[]{:S(2)}) collective-permute-start(bf16[768,128]{1,0:T(8,128)(2,1)S(1)} %get-tuple-element.30), channel_id=1, source_target_pairs={{0,8},{1,16},{4,12},{5,20},{8,24},{9,0},{12,28},{13,4},{16,9},{17,... | collective-permute-start | bytes 589832 | tf_op jit(solution)/shard_map/ppermute | solution.py:173
  103.7 2.1 %collective-permute-start.23 = (bf16[768,128]{1,0:T(8,128)(2,1)S(1)}, bf16[768,128]{1,0:T(8,128)(2,1)S(1)}, u32[]{:S(2)}, u32[]{:S(2)}) collective-permute-start(bf16[768,128]{1,0:T(8,128)(2,1)S(1)} %get-tuple-element.31), channel_id=1, source_target_pairs={{0,16},{1,24},{4,20},{5,28},{8,0},{9,8},{12,4},{13,12},{16,17},{17... | collective-permute-start | bytes 589832 | tf_op jit(solution)/shard_map/ppermute | solution.py:173
  105.8 0.7 collective-permute-start.25
  106.4 2.8 %collective-permute-done.19.refs_0_ = bf16[768,128]{1,0:T(8,128)(2,1)S(1)} collective-permute-done((bf16[768,128]{1,0:T(8,128)(2,1)S(1)}, bf16[768,128]{1,0:T(8,128)(2,1)S(1)}, u32[]{:S(2)}, u32[]{:S(2)}) %collective-permute-start.19) | collective-permute-done | bytes 196640 | tf_op jit(solution)/shard_map/ppermute | solution.py:173
  109.3 1.5 %collective-permute-start.20 = (bf16[768,128]{1,0:T(8,128)(2,1)S(1)}, bf16[768,128]{1,0:T(8,128)(2,1)S(1)}, u32[]{:S(2)}, u32[]{:S(2)}) collective-permute-start(bf16[768,128]{1,0:T(8,128)(2,1)S(1)} %collective-permute-done.19.refs_0_), channel_id=1, source_target_pairs={{0,4},{1,5},{4,0},{5,1},{8,12},{9,13},{12,8},{13,9},{16,20},{17,21... | collective-permute-start | bytes 589832 | tf_op jit(solution)/shard_map/ppermute | solution.py:173
  110.8 8.3 %collective-permute-done.21.refs_2_ = bf16[768,128]{1,0:T(8,128)(2,1)S(1)} collective-permute-done((bf16[768,128]{1,0:T(8,128)(2,1)S(1)}, bf16[768,128]{1,0:T(8,128)(2,1)S(1)}, u32[]{:S(2)}, u32[]{:S(2)}) %collective-permute-start.21) | collective-permute-done | bytes 196640 | tf_op jit(solution)/shard_map/ppermute | solution.py:173
  119.1 1.5 %collective-permute-start.22 = (bf16[768,128]{1,0:T(8,128)(2,1)S(1)}, bf16[768,128]{1,0:T(8,128)(2,1)S(1)}, u32[]{:S(2)}, u32[]{:S(2)}) collective-permute-start(bf16[768,128]{1,0:T(8,128)(2,1)S(1)} %collective-permute-done.21.refs_2_), channel_id=1, source_target_pairs={{0,4},{1,5},{4,0},{5,1},{8,12},{9,13},{12,8},{13,9},{16,20},{17,21... | collective-permute-start | bytes 589832 | tf_op jit(solution)/shard_map/ppermute | solution.py:173
  120.6 0.5 collective-permute-start.24
  121.2 1.5 %collective-permute-start.26 = (bf16[768,128]{1,0:T(8,128)(2,1)S(1)}, bf16[768,128]{1,0:T(8,128)(2,1)S(1)}, u32[]{:S(2)}, u32[]{:S(2)}) collective-permute-start(bf16[768,128]{1,0:T(8,128)(2,1)S(1)} %collective-permute-done.25.refs_6_), channel_id=1, source_target_pairs={{0,4},{1,5},{4,0},{5,1},{8,12},{9,13},{12,8},{13,9},{16,20},{17,21... | collective-permute-start | bytes 589832 | tf_op jit(solution)/shard_map/ppermute | solution.py:173
  122.7 0.6 stack.91.info
  123.5 0.7 fusion.2.quarter
  124.2 2.7 %collective-permute-done.22.refs_3_ = bf16[768,128]{1,0:T(8,128)(2,1)S(1)} collective-permute-done((bf16[768,128]{1,0:T(8,128)(2,1)S(1)}, bf16[768,128]{1,0:T(8,128)(2,1)S(1)}, u32[]{:S(2)}, u32[]{:S(2)}) %collective-permute-start.22) | collective-permute-done | bytes 196640 | tf_op jit(solution)/shard_map/ppermute | solution.py:173
  127.0 4.2 %collective-permute-done.24.refs_5_ = bf16[768,128]{1,0:T(8,128)(2,1)S(1)} collective-permute-done((bf16[768,128]{1,0:T(8,128)(2,1)S(1)}, bf16[768,128]{1,0:T(8,128)(2,1)S(1)}, u32[]{:S(2)}, u32[]{:S(2)}) %collective-permute-start.24) | collective-permute-done | bytes 196640 | tf_op jit(solution)/shard_map/ppermute | solution.py:173
  131.2 2.5 %collective-permute-done.26.refs_7_ = bf16[768,128]{1,0:T(8,128)(2,1)S(1)} collective-permute-done((bf16[768,128]{1,0:T(8,128)(2,1)S(1)}, bf16[768,128]{1,0:T(8,128)(2,1)S(1)}, u32[]{:S(2)}, u32[]{:S(2)}) %collective-permute-start.26) | collective-permute-done | bytes 196640 | tf_op jit(solution)/shard_map/ppermute | solution.py:173
  133.7 0.7 copy-done.15
  134.4 4.3 %shard_map.61 = bf16[768,512]{1,0:T(8,128)(2,1)} custom-call(s32[8]{0:T(128)} %stack.91.info, s32[4]{0:T(128)} %fusion.2.quarter, bf16[4,192,512]{2,1,0:T(8,128)(2,1)} %all-to-all-done.res_ref, bf16[1024,512]{1,0:T(8,128)(2,1)} %w_ref.1, bf16[768,128]{1,0:T(8,128)(2,1)} %copy-done.8, bf16[768,128]{1,0:T(8,128)(2,1)} %copy-done.12, ...), custom_call_target="tpu_custom_call" | custom-call | flops 805306368 | bytes 2621440 | tf_op jit(solution)/shard_map/pallas_call | solution.py:454
  (68 shorter events, 2.0 us)
Async XLA Ops:
  0.0 18.4 %collective-permute-start.6 = (bf16[768,512]{1,0:T(8,128)(2,1)}, bf16[768,512]{1,0:T(8,128)(2,1)}, u32[]{:S(2)}, u32[]{:S(2)}) collective-permute-start(bf16[768,512]{1,0:T(8,128)(2,1)} %own_a.1), channel_id=1, source_target_pairs={{0,9},{4,13},{8,1},{12,5},{17,24},{21,28},{25,16},{29,20},{2,11},{... | collective-permute-start | bytes 2359304 | tf_op jit(solution)/shard_map/ppermute | solution.py:173
  3.4 13.7 %collective-permute-start = (bf16[384,512]{1,0:T(8,128)(2,1)S(1)}, bf16[384,512]{1,0:T(8,128)(2,1)}, u32[]{:S(2)}, u32[]{:S(2)}) collective-permute-start(bf16[384,512]{1,0:T(8,128)(2,1)S(1)} %get-tuple-element.33), channel_id=1, source_target_pairs={{1,16},{5,20},{9,17},{13,21},{16,8},{20,12},{24,9},{28,13},{3,18},... | collective-permute-start | bytes 1179656 | tf_op jit(solution)/shard_map/ppermute | solution.py:173
  4.7 35.4 %collective-permute-start.7 = (bf16[768,512]{1,0:T(8,128)(2,1)}, bf16[768,512]{1,0:T(8,128)(2,1)}, u32[]{:S(2)}, u32[]{:S(2)}) collective-permute-start(bf16[768,512]{1,0:T(8,128)(2,1)} %own_a.1), channel_id=1, source_target_pairs={{0,4},{4,0},{8,12},{12,8},{17,21},{21,17},{25,29},{29,25},{2,6},{6... | collective-permute-start | bytes 2359304 | tf_op jit(solution)/shard_map/ppermute | solution.py:173
  17.1 13.9 %collective-permute-start.1 = (bf16[384,512]{1,0:T(8,128)(2,1)S(1)}, bf16[384,512]{1,0:T(8,128)(2,1)S(1)}, u32[]{:S(2)}, u32[]{:S(2)}) collective-permute-start(bf16[384,512]{1,0:T(8,128)(2,1)S(1)} %get-tuple-element.19), channel_id=1, source_target_pairs={{1,16},{5,20},{9,17},{13,21},{16,8},{20,12},{24,9},{28,13},{3,18},... | collective-permute-start | bytes 1179656 | tf_op jit(solution)/shard_map/ppermute | solution.py:173
  18.4 24.8 %collective-permute-start.8 = (bf16[768,512]{1,0:T(8,128)(2,1)}, bf16[768,512]{1,0:T(8,128)(2,1)}, u32[]{:S(2)}, u32[]{:S(2)}) collective-permute-start(bf16[768,512]{1,0:T(8,128)(2,1)} %collective-permute-done.6.own_b), channel_id=1, source_target_pairs={{1,5},{5,1},{9,13},{13,9},{16,20},{20,16},{24,28},{28,24},{3,7},{7... | collective-permute-start | bytes 2359304 | tf_op jit(solution)/shard_map/ppermute | solution.py:173
  20.0 18.5 %collective-permute-start.9 = (bf16[384,512]{1,0:T(8,128)(2,1)}, bf16[384,512]{1,0:T(8,128)(2,1)}, u32[]{:S(2)}, u32[]{:S(2)}) collective-permute-start(bf16[384,512]{1,0:T(8,128)(2,1)} %collective-permute-done.own_a), channel_id=1, source_target_pairs={{8,0},{9,1},{12,4},{13,5},{16,24},{17,25},{20,28},{21,29},{10,2},{... | collective-permute-start | bytes 1179656 | tf_op jit(solution)/shard_map/ppermute | solution.py:173
  31.0 11.5 %collective-permute-start.2 = (bf16[384,512]{1,0:T(8,128)(2,1)S(1)}, bf16[384,512]{1,0:T(8,128)(2,1)}, u32[]{:S(2)}, u32[]{:S(2)}) collective-permute-start(bf16[384,512]{1,0:T(8,128)(2,1)S(1)} %collective-permute-done.1.own_a), channel_id=1, source_target_pairs={{8,0},{9,1},{12,4},{13,5},{16,24},{17,25},{20,28},{21,29},{10,2},{... | collective-permute-start | bytes 1179656 | tf_op jit(solution)/shard_map/ppermute | solution.py:173
  33.0 10.1 %copy-start = (bf16[768,512]{1,0:T(8,128)(2,1)S(1)}, bf16[768,512]{1,0:T(8,128)(2,1)}, u32[]{:S(2)}) copy-start(bf16[768,512]{1,0:T(8,128)(2,1)} %own_a.1) | copy-start | bytes 2359300
  34.8 14.7 %collective-permute-start.10 = (bf16[384,512]{1,0:T(8,128)(2,1)}, bf16[384,512]{1,0:T(8,128)(2,1)}, u32[]{:S(2)}, u32[]{:S(2)}) collective-permute-start(bf16[384,512]{1,0:T(8,128)(2,1)} %collective-permute-done.own_a), channel_id=1, source_target_pairs={{8,12},{9,13},{12,8},{13,9},{16,20},{17,21},{20,16},{21,17},{10,14... | collective-permute-start | bytes 1179656 | tf_op jit(solution)/shard_map/ppermute | solution.py:173
  38.5 11.5 %collective-permute-start.11 = (bf16[384,512]{1,0:T(8,128)(2,1)}, bf16[384,512]{1,0:T(8,128)(2,1)}, u32[]{:S(2)}, u32[]{:S(2)}) collective-permute-start(bf16[384,512]{1,0:T(8,128)(2,1)} %collective-permute-done.9.own_b), channel_id=1, source_target_pairs={{0,4},{1,5},{4,0},{5,1},{24,28},{25,29},{28,24},{29,25},{2,6},{3,7... | collective-permute-start | bytes 1179656 | tf_op jit(solution)/shard_map/ppermute | solution.py:173
  40.1 9.3 %copy-start.16 = (s32[192]{0:T(256)S(1)}, s32[192]{0:T(256)}, u32[]{:S(2)}) copy-start(s32[192]{0:T(256)} %targets.1) | copy-start | bytes 2308
  40.1 9.3 %copy-start.18 = (s32[3]{0:T(128)S(1)}, s32[3]{0:T(128)}, u32[]{:S(2)}) copy-start(s32[3]{0:T(128)} %param.9) | copy-start | bytes 40
  40.1 15.3 %collective-permute-start.3 = (bf16[384,512]{1,0:T(8,128)(2,1)S(1)}, bf16[384,512]{1,0:T(8,128)(2,1)S(1)}, u32[]{:S(2)}, u32[]{:S(2)}) collective-permute-start(bf16[384,512]{1,0:T(8,128)(2,1)S(1)} %collective-permute-done.1.own_a), channel_id=1, source_target_pairs={{8,12},{9,13},{12,8},{13,9},{16,20},{17,21},{20,16},{21,17},{10,14... | collective-permute-start | bytes 1179656 | tf_op jit(solution)/shard_map/ppermute | solution.py:173
  42.5 12.9 %collective-permute-start.4 = (bf16[384,512]{1,0:T(8,128)(2,1)}, bf16[384,512]{1,0:T(8,128)(2,1)S(1)}, u32[]{:S(2)}, u32[]{:S(2)}) collective-permute-start(bf16[384,512]{1,0:T(8,128)(2,1)} %collective-permute-done.2.own_b), channel_id=1, source_target_pairs={{0,4},{1,5},{4,0},{5,1},{24,28},{25,29},{28,24},{29,25},{2,6},{3,7... | collective-permute-start | bytes 1179656 | tf_op jit(solution)/shard_map/ppermute | solution.py:173
  49.3 9.6 %copy-start.6 = (bf16[768,512]{1,0:T(8,128)(2,1)}, bf16[768,512]{1,0:T(8,128)(2,1)S(1)}, u32[]{:S(2)}) copy-start(bf16[768,512]{1,0:T(8,128)(2,1)S(1)} %get-tuple-element.21.refs_0_) | copy-start | bytes 2359300
  49.3 20.8 %collective-permute-start.12 = (bf16[768,512]{1,0:T(8,128)(2,1)}, bf16[768,512]{1,0:T(8,128)(2,1)}, u32[]{:S(2)}, u32[]{:S(2)}) collective-permute-start(bf16[768,512]{1,0:T(8,128)(2,1)} %get-tuple-element.23), channel_id=1, source_target_pairs={{0,1},{1,0},{4,5},{5,4},{8,9},{9,8},{12,13},{13,12},{16,17},{17,16... | collective-permute-start | bytes 2359304 | tf_op jit(solution)/shard_map/ppermute | solution.py:173
  49.5 20.4 %collective-permute-start.5 = (s32[195]{0:T(256)S(1)}, s32[195]{0:T(256)S(1)}, u32[]{:S(2)}, u32[]{:S(2)}) collective-permute-start(s32[195]{0:T(256)S(1)} %pad_add_fusion), channel_id=1, source_target_pairs={{0,1},{1,0},{4,5},{5,4},{8,9},{9,8},{12,13},{13,12},{16,17},{17,16... | collective-permute-start | bytes 2348 | tf_op jit(solution)/shard_map/ppermute | solution.py:173
  54.2 0.7 copy-start.4
  54.9 15.1 %collective-permute-start.13 = (bf16[384,512]{1,0:T(8,128)(2,1)}, bf16[384,512]{1,0:T(8,128)(2,1)}, u32[]{:S(2)}, u32[]{:S(2)}) collective-permute-start(bf16[384,512]{1,0:T(8,128)(2,1)} %get-tuple-element.24), channel_id=1, source_target_pairs={{0,1},{1,0},{4,5},{5,4},{8,9},{9,8},{12,13},{13,12},{16,17},{17,16... | collective-permute-start | bytes 1179656 | tf_op jit(solution)/shard_map/ppermute | solution.py:173
  58.9 0.8 copy-start.2
  59.7 10.4 %copy-start.17 = (s32[192]{0:T(256)S(1)}, s32[192]{0:T(256)}, u32[]{:S(2)}) copy-start(s32[192]{0:T(256)} %targets.1) | copy-start | bytes 2308
  59.7 10.5 %copy-start.5 = (bf16[384,512]{1,0:T(8,128)(2,1)S(1)}, bf16[384,512]{1,0:T(8,128)(2,1)}, u32[]{:S(2)}) copy-start(bf16[384,512]{1,0:T(8,128)(2,1)} %copy-done.4) | copy-start | bytes 1179652
  59.7 10.5 %copy-start.3 = (bf16[384,512]{1,0:T(8,128)(2,1)S(1)}, bf16[384,512]{1,0:T(8,128)(2,1)}, u32[]{:S(2)}) copy-start(bf16[384,512]{1,0:T(8,128)(2,1)} %copy-done.2) | copy-start | bytes 1179652
  59.7 10.5 %copy-start.7 = (bf16[768,512]{1,0:T(8,128)(2,1)S(1)}, bf16[768,512]{1,0:T(8,128)(2,1)}, u32[]{:S(2)}) copy-start(bf16[768,512]{1,0:T(8,128)(2,1)} %copy-done.6) | copy-start | bytes 2359300
  59.7 10.4 %collective-permute-start.14 = (bf16[384,512]{1,0:T(8,128)(2,1)}, bf16[384,512]{1,0:T(8,128)(2,1)S(1)}, u32[]{:S(2)}, u32[]{:S(2)}) collective-permute-start(bf16[384,512]{1,0:T(8,128)(2,1)} %get-tuple-element.25), channel_id=1, source_target_pairs={{0,1},{1,0},{4,5},{5,4},{8,9},{9,8},{12,13},{13,12},{16,17},{17,16... | collective-permute-start | bytes 1179656 | tf_op jit(solution)/shard_map/ppermute | solution.py:173
  62.4 61.8 %all-to-all-start = ((bf16[4,192,512]{2,1,0:T(8,128)(2,1)}), bf16[4,192,512]{2,1,0:T(8,128)(2,1)}, u32[]{:S(2)}, u32[]{:S(2)}) async-start(bf16[4,192,512]{2,1,0:T(8,128)(2,1)} %shard_map.56), calls=%async_computation | async-start | bytes 1572864 | tf_op jit(solution)/shard_map/all_to_all | solution.py:524
  87.2 1.2 collective-permute-start.15
  88.4 3.9 %collective-permute-start.16 = (f32[2,3072]{1,0:T(2,128)S(1)}, f32[2,3072]{1,0:T(2,128)S(1)}, u32[]{:S(2)}, u32[]{:S(2)}) collective-permute-start(f32[2,3072]{1,0:T(2,128)S(1)} %add.89.refs_0_), channel_id=1, source_target_pairs={{0,4},{1,5},{4,0},{5,1},{8,12},{9,13},{12,8},{13,9},{16,20},{17,21... | collective-permute-start | bytes 73736 | tf_op jit(solution)/shard_map/ppermute | solution.py:173
  89.0 3.9 %collective-permute-start.17 = (f32[2,3072]{1,0:T(2,128)S(1)}, f32[2,3072]{1,0:T(2,128)S(1)}, u32[]{:S(2)}, u32[]{:S(2)}) collective-permute-start(f32[2,3072]{1,0:T(2,128)S(1)} %add.89.refs_0_), channel_id=1, source_target_pairs={{0,8},{1,9},{4,12},{5,13},{8,0},{9,1},{12,4},{13,5},{16,24},{17,25... | collective-permute-start | bytes 73736 | tf_op jit(solution)/shard_map/ppermute | solution.py:173
  89.3 4.8 %collective-permute-start.18 = (f32[2,3072]{1,0:T(2,128)S(1)}, f32[2,3072]{1,0:T(2,128)S(1)}, u32[]{:S(2)}, u32[]{:S(2)}) collective-permute-start(f32[2,3072]{1,0:T(2,128)S(1)} %add.89.refs_0_), channel_id=1, source_target_pairs={{0,12},{1,13},{4,8},{5,9},{8,4},{9,5},{12,0},{13,1},{16,28},{17,29... | collective-permute-start | bytes 73736 | tf_op jit(solution)/shard_map/ppermute | solution.py:173
  94.1 1.4 %copy-start.1 = (f32[3072,128]{1,0:T(8,128)S(1)}, f32[3072,128]{1,0:T(8,128)}, u32[]{:S(2)}) copy-start(f32[3072,128]{1,0:T(8,128)} %get-tuple-element.26.att_ref) | copy-start | bytes 4718596
  97.2 12.1 %collective-permute-start.19 = (bf16[768,128]{1,0:T(8,128)(2,1)S(1)}, bf16[768,128]{1,0:T(8,128)(2,1)S(1)}, u32[]{:S(2)}, u32[]{:S(2)}) collective-permute-start(bf16[768,128]{1,0:T(8,128)(2,1)S(1)} %get-tuple-element.29), channel_id=1, source_target_pairs={{0,0},{1,8},{4,4},{5,12},{8,16},{9,24},{12,20},{13,28},{16,1},{17,... | collective-permute-start | bytes 589832 | tf_op jit(solution)/shard_map/ppermute | solution.py:173
  101.8 17.3 %collective-permute-start.21 = (bf16[768,128]{1,0:T(8,128)(2,1)S(1)}, bf16[768,128]{1,0:T(8,128)(2,1)S(1)}, u32[]{:S(2)}, u32[]{:S(2)}) collective-permute-start(bf16[768,128]{1,0:T(8,128)(2,1)S(1)} %get-tuple-element.30), channel_id=1, source_target_pairs={{0,8},{1,16},{4,12},{5,20},{8,24},{9,0},{12,28},{13,4},{16,9},{17,... | collective-permute-start | bytes 589832 | tf_op jit(solution)/shard_map/ppermute | solution.py:173
  103.7 16.9 %collective-permute-start.23 = (bf16[768,128]{1,0:T(8,128)(2,1)S(1)}, bf16[768,128]{1,0:T(8,128)(2,1)S(1)}, u32[]{:S(2)}, u32[]{:S(2)}) collective-permute-start(bf16[768,128]{1,0:T(8,128)(2,1)S(1)} %get-tuple-element.31), channel_id=1, source_target_pairs={{0,16},{1,24},{4,20},{5,28},{8,0},{9,8},{12,4},{13,12},{16,17},{17... | collective-permute-start | bytes 589832 | tf_op jit(solution)/shard_map/ppermute | solution.py:173
  105.8 15.4 %collective-permute-start.25 = (bf16[768,128]{1,0:T(8,128)(2,1)S(1)}, bf16[768,128]{1,0:T(8,128)(2,1)S(1)}, u32[]{:S(2)}, u32[]{:S(2)}) collective-permute-start(bf16[768,128]{1,0:T(8,128)(2,1)S(1)} %get-tuple-element.32), channel_id=1, source_target_pairs={{0,24},{1,0},{4,28},{5,4},{8,8},{9,16},{12,12},{13,20},{16,25},{17... | collective-permute-start | bytes 589832 | tf_op jit(solution)/shard_map/ppermute | solution.py:173
  109.3 24.4 %copy-start.8 = (bf16[768,128]{1,0:T(8,128)(2,1)}, bf16[768,128]{1,0:T(8,128)(2,1)S(1)}, u32[]{:S(2)}) copy-start(bf16[768,128]{1,0:T(8,128)(2,1)S(1)} %collective-permute-done.19.refs_0_) | copy-start | bytes 589828
  109.3 14.9 %collective-permute-start.20 = (bf16[768,128]{1,0:T(8,128)(2,1)S(1)}, bf16[768,128]{1,0:T(8,128)(2,1)S(1)}, u32[]{:S(2)}, u32[]{:S(2)}) collective-permute-start(bf16[768,128]{1,0:T(8,128)(2,1)S(1)} %collective-permute-done.19.refs_0_), channel_id=1, source_target_pairs={{0,4},{1,5},{4,0},{5,1},{8,12},{9,13},{12,8},{13,9},{16,20},{17,21... | collective-permute-start | bytes 589832 | tf_op jit(solution)/shard_map/ppermute | solution.py:173
  119.1 14.6 %copy-start.9 = (bf16[768,128]{1,0:T(8,128)(2,1)}, bf16[768,128]{1,0:T(8,128)(2,1)S(1)}, u32[]{:S(2)}) copy-start(bf16[768,128]{1,0:T(8,128)(2,1)S(1)} %collective-permute-done.21.refs_2_) | copy-start | bytes 589828
  119.1 7.8 %collective-permute-start.22 = (bf16[768,128]{1,0:T(8,128)(2,1)S(1)}, bf16[768,128]{1,0:T(8,128)(2,1)S(1)}, u32[]{:S(2)}, u32[]{:S(2)}) collective-permute-start(bf16[768,128]{1,0:T(8,128)(2,1)S(1)} %collective-permute-done.21.refs_2_), channel_id=1, source_target_pairs={{0,4},{1,5},{4,0},{5,1},{8,12},{9,13},{12,8},{13,9},{16,20},{17,21... | collective-permute-start | bytes 589832 | tf_op jit(solution)/shard_map/ppermute | solution.py:173
  120.6 13.1 %copy-start.10 = (bf16[768,128]{1,0:T(8,128)(2,1)}, bf16[768,128]{1,0:T(8,128)(2,1)S(1)}, u32[]{:S(2)}) copy-start(bf16[768,128]{1,0:T(8,128)(2,1)S(1)} %collective-permute-done.23.refs_4_) | copy-start | bytes 589828
  120.6 10.6 %collective-permute-start.24 = (bf16[768,128]{1,0:T(8,128)(2,1)S(1)}, bf16[768,128]{1,0:T(8,128)(2,1)S(1)}, u32[]{:S(2)}, u32[]{:S(2)}) collective-permute-start(bf16[768,128]{1,0:T(8,128)(2,1)S(1)} %collective-permute-done.23.refs_4_), channel_id=1, source_target_pairs={{0,4},{1,5},{4,0},{5,1},{8,12},{9,13},{12,8},{13,9},{16,20},{17,21... | collective-permute-start | bytes 589832 | tf_op jit(solution)/shard_map/ppermute | solution.py:173
  121.2 12.5 %copy-start.11 = (bf16[768,128]{1,0:T(8,128)(2,1)}, bf16[768,128]{1,0:T(8,128)(2,1)S(1)}, u32[]{:S(2)}) copy-start(bf16[768,128]{1,0:T(8,128)(2,1)S(1)} %collective-permute-done.25.refs_6_) | copy-start | bytes 589828
  121.2 12.5 %collective-permute-start.26 = (bf16[768,128]{1,0:T(8,128)(2,1)S(1)}, bf16[768,128]{1,0:T(8,128)(2,1)S(1)}, u32[]{:S(2)}, u32[]{:S(2)}) collective-permute-start(bf16[768,128]{1,0:T(8,128)(2,1)S(1)} %collective-permute-done.25.refs_6_), channel_id=1, source_target_pairs={{0,4},{1,5},{4,0},{5,1},{8,12},{9,13},{12,8},{13,9},{16,20},{17,21... | collective-permute-start | bytes 589832 | tf_op jit(solution)/shard_map/ppermute | solution.py:173
  124.2 9.5 %copy-start.12 = (bf16[768,128]{1,0:T(8,128)(2,1)}, bf16[768,128]{1,0:T(8,128)(2,1)S(1)}, u32[]{:S(2)}) copy-start(bf16[768,128]{1,0:T(8,128)(2,1)S(1)} %collective-permute-done.20.refs_1_) | copy-start | bytes 589828
  127.0 6.8 %copy-start.13 = (bf16[768,128]{1,0:T(8,128)(2,1)}, bf16[768,128]{1,0:T(8,128)(2,1)S(1)}, u32[]{:S(2)}) copy-start(bf16[768,128]{1,0:T(8,128)(2,1)S(1)} %collective-permute-done.22.refs_3_) | copy-start | bytes 589828
  131.2 2.6 %copy-start.14 = (bf16[768,128]{1,0:T(8,128)(2,1)}, bf16[768,128]{1,0:T(8,128)(2,1)S(1)}, u32[]{:S(2)}) copy-start(bf16[768,128]{1,0:T(8,128)(2,1)S(1)} %collective-permute-done.24.refs_5_) | copy-start | bytes 589828
  133.7 0.7 copy-start.15

commit v3 on v2

--- a/solution.py
+++ b/solution.py
@@ -1,3 +1,5 @@
+import functools
+
 import jax
 import jax.numpy as jnp
 from jax import lax
@@ -206,31 +208,35 @@
     return (half, zlo, head, 1 - core)
 
 
-def project_kernel(info, own_a, own_b, other_a, other_b, w_ref, mine_ref, sib_ref, own_v, other_v, sems):
-    rows = own_v.shape[0]
-    width = own_v.shape[1]
-    first = info[0] == 0
-
-    @pl.when(first)
-    def _():
-        pltpu.make_async_copy(own_a, own_v, sems.at[0]).start()
-        pltpu.make_async_copy(other_a, other_v, sems.at[1]).start()
-
-    @pl.when(jnp.logical_not(first))
-    def _():
-        pltpu.make_async_copy(own_b, own_v, sems.at[0]).start()
-        pltpu.make_async_copy(other_b, other_v, sems.at[1]).start()
-
-    pltpu.make_async_copy(own_a, own_v, sems.at[0]).wait()
-    pltpu.make_async_copy(other_a, other_v, sems.at[1]).wait()
+def project_kernel(waited, info, lengths, *refs):
+    pairs = refs[: -6 - waited]
+    w_ref, mine_ref, sib_ref, own_v, other_v, sems = refs[-6:]
+    pairs = [(pairs[i], pairs[i + 1]) for i in range(0, len(pairs), 2)]
+    rows, width = own_v.shape
+    step = rows // 2
+
+    def copies(pair, i):
+        at = pl.ds(i * step, step)
+        return (
+            pltpu.make_async_copy(pair[0].at[at, :], own_v.at[at, :], sems.at[2 * i]),
+            pltpu.make_async_copy(pair[1].at[at, :], other_v.at[at, :], sems.at[2 * i + 1]),
+        )
+
+    for n, pair in enumerate(pairs):
+
+        @pl.when(info[0] == n)
+        def _():
+            for i in range(2):
+                for copy in copies(pair, i):
+                    copy.start()
+
     own_rows = pl.multiple_of(info[1] * width, width)
     other_rows = pl.multiple_of(info[2] * width, width)
     low_core = info[3] == 0
-    step = 128
-
-    @pl.loop(0, rows // step)
-    def _(i):
-        at = pl.ds(pl.multiple_of(i * step, step), step)
+    for i in range(2):
+        for copy in copies(pairs[0], i):
+            copy.wait()
+        at = pl.ds(i * step, step)
         a = own_v[at, :].astype(jnp.float32)
         b = other_v[at, :].astype(jnp.float32)
         mean = (jnp.sum(a, axis=1, keepdims=True) + jnp.sum(b, axis=1, keepdims=True)) / (2 * width)
@@ -254,25 +260,26 @@
             sib_ref[at, cols] = jnp.where(low_core, high, low)
 
 
-def project(info, own_a, own_b, other_a, other_b, w, zlo):
-    rows, width = own_a.shape
+def project(info, lengths, pairs, w, after):
+    rows, width = pairs[0].shape
     anywhere = pl.BlockSpec(memory_space=pl.ANY)
+    vmem = pl.BlockSpec(memory_space=pltpu.VMEM)
     out = jax.ShapeDtypeStruct((rows, 512), jnp.bfloat16)
     return pl.pallas_call(
-        project_kernel,
+        functools.partial(project_kernel, len(after)),
         out_shape=(out, out),
-        in_specs=[pl.BlockSpec(memory_space=pltpu.SMEM)] + [anywhere] * 4 + [pl.BlockSpec(memory_space=pltpu.VMEM)],
-        out_specs=(pl.BlockSpec(memory_space=pltpu.VMEM),) * 2,
+        in_specs=[pl.BlockSpec(memory_space=pltpu.SMEM)] * 2 + [anywhere] * (len(pairs) + len(after)) + [vmem],
+        out_specs=(vmem, vmem),
         scratch_shapes=[
             pltpu.VMEM((rows, width), jnp.bfloat16),
             pltpu.VMEM((rows, width), jnp.bfloat16),
-            pltpu.SemaphoreType.DMA((2,)),
+            pltpu.SemaphoreType.DMA((4,)),
         ],
-        compiler_params=pltpu.CompilerParams(vmem_limit_bytes=40 * 1024 * 1024),
+        compiler_params=pltpu.CompilerParams(vmem_limit_bytes=16 * 1024 * 1024),
         cost_estimate=pl.CostEstimate(
             flops=2 * rows * D * 1024, bytes_accessed=rows * D * 4 + w.size * 2, transcendentals=rows * 1024
         ),
-    )(info, own_a, own_b, other_a, other_b, w)
+    )(info, lengths, *pairs, *after, w)
 
 
 TQ = 1536
@@ -288,6 +295,7 @@
     zero = jnp.zeros((RB, 128), jnp.bfloat16)
     for n, piece in enumerate(pieces):
         base = info[n]
+
         @pl.loop(0, piece.shape[0] // RB, unroll=8)
         def _(b):
             frm = pl.ds(pl.multiple_of(b * RB, RB), RB)
@@ -359,9 +367,10 @@
     return pl.pallas_call(
         attend_kernel,
         out_shape=(jax.ShapeDtypeStruct((seq, 128), jnp.float32), jax.ShapeDtypeStruct((seq, 128), jnp.bfloat16), jax.ShapeDtypeStruct((2, seq), jnp.float32)),
-        in_specs=[smem] * 3 + [vmem] * len(pieces), out_specs=(vmem,) * 3,
+        in_specs=[smem] * 3 + [vmem] * len(pieces),
+        out_specs=(vmem,) * 3,
         scratch_shapes=[pltpu.VMEM((seq, 128), jnp.bfloat16)] * 5,
-        compiler_params=pltpu.CompilerParams(vmem_limit_bytes=50 * 1024 * 1024),
+        compiler_params=pltpu.CompilerParams(vmem_limit_bytes=56 * 1024 * 1024),
         cost_estimate=pl.CostEstimate(
             flops=2 * seq * seq * 128, bytes_accessed=seq * 128 * 14, transcendentals=seq * seq
         ),
@@ -399,7 +408,7 @@
         out_shape=(out,) * count,
         in_specs=[pl.BlockSpec(memory_space=pltpu.SMEM)] + [vmem] * (2 + len(stats)),
         out_specs=(vmem,) * count,
-        compiler_params=pltpu.CompilerParams(vmem_limit_bytes=40 * 1024 * 1024),
+        compiler_params=pltpu.CompilerParams(vmem_limit_bytes=14 * 1024 * 1024),
         cost_estimate=pl.CostEstimate(flops=att.size * 8, bytes_accessed=att.size * 8, transcendentals=0),
     )(info, att, u, *stats)
 
@@ -425,41 +434,48 @@
         out_shape=jax.ShapeDtypeStruct((count, events.shape[0] // count, events.shape[1]), events.dtype),
         in_specs=[smem, smem, vmem, pl.BlockSpec(memory_space=pl.ANY)],
         out_specs=vmem,
+        compiler_params=pltpu.CompilerParams(vmem_limit_bytes=8 * 1024 * 1024),
         cost_estimate=pl.CostEstimate(flops=0, bytes_accessed=events.size * 4, transcendentals=0),
     )(info, targets, events, after)
 
 
-def finish_kernel(info, quarter, res_ref, w_ref, *refs):
-    pieces, out_ref = refs[:-1], refs[-1]
-    count, step = res_ref.shape[0], res_ref.shape[1]
-
-    @pl.loop(0, count)
-    def _(i):
-        at = pl.ds(pl.multiple_of(quarter[i] * step, step), step)
-        acc = res_ref[i].astype(jnp.float32)
+def finish_kernel(info, quarter, w_ref, *refs):
+    residual, pieces, (out_ref, acc_ref) = refs[0], refs[1:-2], refs[-2:]
+    count, part = residual.shape[0], residual.shape[1]
+    step = acc_ref.shape[0] // 2
+    for i in range(2):
+        at = pl.ds(i * step, step)
+        acc = None
         for n in range(0, len(pieces), 2):
             two = (n, n + 1)
             left = jnp.concatenate([pieces[m][at, :] for m in two], axis=1)
             right = jnp.concatenate(
                 [w_ref[pl.ds(pl.multiple_of(info[m] * 128, 128), 128), :] for m in two], axis=0
             )
-            acc = acc + jnp.dot(left, right, preferred_element_type=jnp.float32)
-        out_ref[at, :] = acc.astype(out_ref.dtype)
+            term = jnp.dot(left, right, preferred_element_type=jnp.float32)
+            acc = term if acc is None else acc + term
+        acc_ref[at, :] = acc
+
+    for i in range(count):
+        at = pl.ds(pl.multiple_of(quarter[i] * part, part), part)
+        out_ref[at, :] = (acc_ref[at, :] + residual[i].astype(jnp.float32)).astype(out_ref.dtype)
 
 
 def finish(info, quarter, residual, w_out, pieces):
     smem = pl.BlockSpec(memory_space=pltpu.SMEM)
     vmem = pl.BlockSpec(memory_space=pltpu.VMEM)
-    rows = residual.shape[0] * residual.shape[1]
+    shape = (residual.shape[0] * residual.shape[1], residual.shape[2])
     return pl.pallas_call(
         finish_kernel,
-        out_shape=jax.ShapeDtypeStruct((rows, residual.shape[2]), jnp.bfloat16),
+        out_shape=jax.ShapeDtypeStruct(shape, jnp.bfloat16),
         in_specs=[smem] * 2 + [vmem] * (2 + len(pieces)),
         out_specs=vmem,
+        scratch_shapes=[pltpu.VMEM(shape, jnp.float32)],
+        compiler_params=pltpu.CompilerParams(vmem_limit_bytes=14 * 1024 * 1024),
         cost_estimate=pl.CostEstimate(
-            flops=2 * residual.size * D, bytes_accessed=residual.size * 4 + w_out.size * 2, transcendentals=0
+            flops=2 * shape[0] * shape[1] * D, bytes_accessed=8 * 1024 * 1024, transcendentals=0
         ),
-    )(info, quarter, residual, w_out, *pieces)
+    )(info, quarter, w_out, residual, *pieces)
 
 
 def team_body(events, w_proj, w_out, block_target, user_lengths):
@@ -476,10 +492,10 @@
     lengths = jnp.where(foreign == 0, user_lengths, other_ints[block_target.shape[0] :])
     w_mine = lax.dynamic_slice_in_dim(w_proj, zlo * 256, 256, axis=2)
 
-    x_own = move(events, across(lambda half, zlo, head, core: core == half))
-    partner = move(events, to_partner)
     parts = 2
     span = rows // parts
+    partner = move(events, to_partner)
+    x_own = move(events, across(lambda half, zlo, head, core: core == half))
     remote = []
     for i in range(parts):
         chunk = events[i * span : (i + 1) * span]
@@ -488,40 +504,40 @@
         remote.append(move(chunk, to_other_team))
     x_partner = move(partner, across(lambda half, zlo, head, core: core != half))
     relayed = [move(r, inner_to_outer) for r in remote]
+
+    def ints(*values):
+        return jnp.stack([jnp.asarray(v, jnp.int32) for v in values])
+
+    mine1, sib1 = project(
+        ints(foreign, head, 1 - head, core), user_lengths, [events, x_own, partner, x_partner], w_mine, []
+    )
     x_inner = [move(r, across(lambda half, zlo, head, core: (zlo ^ half) == 1)) for r in remote]
     x_outer = [move(r, across(lambda half, zlo, head, core: (zlo ^ half) == 0)) for r in relayed]
-
-    def ints(*values):
-        return jnp.stack([jnp.asarray(v, jnp.int32) for v in values])
-
-    mine1, sib1 = project(
-        ints(foreign, head, 1 - head, core), events, partner, x_own, x_partner, w_mine, zlo
-    )
-    got1 = move(sib1, other_core)
-    mine, got = [mine1], [got1]
+    mine, got = [mine1], [move(sib1, other_core)]
+    send = outgoing(ints(z), targets_here, events, remote[-1], 4)
+    residual = lax.all_to_all(send, ("half", "zlo"), split_axis=0, concat_axis=0, tiled=True)
     for i in range(parts):
         m, s = project(
-            ints(outer, head, 1 - head, core), remote[i], relayed[i], x_inner[i], x_outer[i], w_mine, zlo
+            ints(outer, head, 1 - head, core),
+            user_lengths,
+            [remote[i], x_inner[i], relayed[i], x_outer[i]],
+            w_mine,
+            [send] if i == 0 else [],
         )
         mine.append(m)
         got.append(move(s, other_core))
 
-    near = half + 1
     near = jnp.where(half == 0, 2, 1)
     far = jnp.where(half == 0, 3, 0)
-    slot1 = jnp.where(foreign == 0, z, z ^ 1)
-    slot2 = jnp.where(foreign == 0, near, far)
-    sib_slot1 = jnp.where(foreign == 0, z ^ 1, z)
-    sib_slot2 = jnp.where(foreign == 0, far, near)
+    mine_second = jnp.where(foreign == 0, near, far)
+    other_second = jnp.where(foreign == 0, far, near)
     part_blocks = span // RB
-    starts = [slot1 * blocks]
-    starts += [slot2 * blocks + i * part_blocks for i in range(parts)]
-    starts += [sib_slot1 * blocks]
-    starts += [sib_slot2 * blocks + i * part_blocks for i in range(parts)]
+    starts = [jnp.where(foreign == 0, z, z ^ 1) * blocks]
+    starts += [mine_second * blocks + i * part_blocks for i in range(parts)]
+    starts += [jnp.where(foreign == 0, z ^ 1, z) * blocks]
+    starts += [other_second * blocks + i * part_blocks for i in range(parts)]
     att, u, stat = attend(ints(*starts), targets, lengths, mine + got)
 
-    send = outgoing(ints(z), targets_here, events, mine[-1], 4)
-    residual = lax.all_to_all(send, ("half", "zlo"), split_axis=0, concat_axis=0, tiled=True)
     by_shard = targets_here.reshape(4, blocks)
     quarter = jnp.max(
         jnp.where(by_shard // blocks == z, by_shard % blocks // (blocks // 4), 0), axis=1

time: 139 us -> 138 us (level)
  Pallas kernels: 39.4 us -> 35.8 us
  starting transfers between devices: 48.5 us -> 47 us
    pallas_call x4, Pallas kernels: 18 us -> 14.4 us  [the longest x3 11.8 us: project(): pl.pallas_call(functools.partial(project_kernel, len(after)), out_shape=(...]
    all_to_all x1, starting transfers between devices: 7.58 us -> 5.14 us  [team_body(): lax.all_to_all(send, ('half', 'zlo'), split_axis=0, concat_axis=0, tiled=...]
    unnamed x38 -> x22, local copies, waits for them, and re-layouts: 3.64 us -> 4.92 us
  transfers between devices with their start and end apart: 28 -> 28, of which waited for: 12 -> 12; matrix products, arithmetic and copies ran while one was open for 4% -> 5% of each run, Pallas kernels for 25% -> 24%
where the time goes in v3:
time: 138 us; the launch traced here: 137 us
  starting transfers between devices  47 us (34%)
  waiting for transfers between devices  42.8 us (31%)
  Pallas kernels  35.8 us (26%)
  local copies, waits for them, and re-layouts  8.89 us (6%)
  other arithmetic  2.3 us (2%)
    ppermute x27, waiting for transfers between devices, move(): return lax.ppermute(value, ROUTE, route(rule))  42.8 us
    ppermute x27, starting transfers between devices, move(): return lax.ppermute(value, ROUTE, route(rule))  41.9 us
    pallas_call x1, Pallas kernels, attend(): pl.pallas_call(attend_kernel, out_shape=(jax.ShapeDtypeStruct((seq, 128),...  17.8 us
    pallas_call x3, Pallas kernels, project(): pl.pallas_call(functools.partial(project_kernel, len(after)), out_shape=(...  11.8 us
    all_to_all x1, starting transfers between devices, team_body(): lax.all_to_all(send, ('half', 'zlo'), split_axis=0, concat_axis=0, tiled=...  5.14 us
    unnamed x22, local copies, waits for them, and re-layouts  4.92 us
  transfers between devices with their start and end apart: 28, of which 12 were waited for; matrix products, arithmetic and copies ran while one was open for 5% of the time, Pallas kernels for 24%

profile of v3, /device:TPU:8, one launch (start us, length us, event | category | flops | bytes accessed | tf_op | source)
XLA Modules:
  0.0 137.1 jit_solution(5544692611918816032)
XLA Ops:
  0.0 2.2 %collective-permute-start.4 = (bf16[768,512]{1,0:T(8,128)(2,1)}, bf16[768,512]{1,0:T(8,128)(2,1)}, u32[]{:S(2)}, u32[]{:S(2)}) collective-permute-start(bf16[768,512]{1,0:T(8,128)(2,1)} %refs_0_.1), channel_id=1, source_target_pairs={{0,9},{4,13},{8,1},{12,5},{17,24},{21,28},{25,16},{29,20},{2,11},{... | collective-permute-start | bytes 2359304 | tf_op jit(solution)/shard_map/ppermute | solution.py:175
  2.2 1.2 fusion.4
  3.3 1.3 collective-permute-start
  4.6 3.9 %collective-permute-start.3 = (bf16[768,512]{1,0:T(8,128)(2,1)}, bf16[768,512]{1,0:T(8,128)(2,1)}, u32[]{:S(2)}, u32[]{:S(2)}) collective-permute-start(bf16[768,512]{1,0:T(8,128)(2,1)} %refs_0_.1), channel_id=1, source_target_pairs={{0,4},{4,0},{8,12},{12,8},{17,21},{21,17},{25,29},{29,25},{2,6},{6... | collective-permute-start | bytes 2359304 | tf_op jit(solution)/shard_map/ppermute | solution.py:175
  8.6 8.5 %collective-permute-done.refs_0_ = bf16[384,512]{1,0:T(8,128)(2,1)} collective-permute-done((bf16[384,512]{1,0:T(8,128)(2,1)S(1)}, bf16[384,512]{1,0:T(8,128)(2,1)}, u32[]{:S(2)}, u32[]{:S(2)}) %collective-permute-start) | collective-permute-done | bytes 393248 | tf_op jit(solution)/shard_map/ppermute | solution.py:175
  17.1 1.3 collective-permute-start.1
  18.4 1.6 %collective-permute-start.5 = (bf16[768,512]{1,0:T(8,128)(2,1)}, bf16[768,512]{1,0:T(8,128)(2,1)}, u32[]{:S(2)}, u32[]{:S(2)}) collective-permute-start(bf16[768,512]{1,0:T(8,128)(2,1)} %collective-permute-done.4.refs_2_), channel_id=1, source_target_pairs={{1,5},{5,1},{9,13},{13,9},{16,20},{20,16},{24,28},{28,24},{3,7},{7... | collective-permute-start | bytes 2359304 | tf_op jit(solution)/shard_map/ppermute | solution.py:175
  20.0 2.0 %collective-permute-start.7 = (bf16[384,512]{1,0:T(8,128)(2,1)}, bf16[384,512]{1,0:T(8,128)(2,1)}, u32[]{:S(2)}, u32[]{:S(2)}) collective-permute-start(bf16[384,512]{1,0:T(8,128)(2,1)} %collective-permute-done.refs_0_), channel_id=1, source_target_pairs={{8,0},{9,1},{12,4},{13,5},{16,24},{17,25},{20,28},{21,29},{10,2},{... | collective-permute-start | bytes 1179656 | tf_op jit(solution)/shard_map/ppermute | solution.py:175
  22.0 9.0 %collective-permute-done.1.after_ref.refs_0_ = bf16[384,512]{1,0:T(8,128)(2,1)S(1)} collective-permute-done((bf16[384,512]{1,0:T(8,128)(2,1)S(1)}, bf16[384,512]{1,0:T(8,128)(2,1)S(1)}, u32[]{:S(2)}, u32[]{:S(2)}) %collective-permute-start.1) | collective-permute-done | bytes 393248 | tf_op jit(solution)/shard_map/ppermute | solution.py:175
  31.0 2.0 %collective-permute-start.10 = (bf16[384,512]{1,0:T(8,128)(2,1)S(1)}, bf16[384,512]{1,0:T(8,128)(2,1)}, u32[]{:S(2)}, u32[]{:S(2)}) collective-permute-start(bf16[384,512]{1,0:T(8,128)(2,1)S(1)} %collective-permute-done.1.after_ref.refs_0_), channel_id=1, source_target_pairs={{8,0},{9,1},{12,4},{13,5},{16,24},{17,25},{20,28},{21,29},{10,2},{... | collective-permute-start | bytes 1179656 | tf_op jit(solution)/shard_map/ppermute | solution.py:175
  33.0 1.8 %constant_dynamic-slice_fusion.refs_4_.refs_5_ = bf16[4,1024,256]{2,1,0:T(8,128)(2,1)S(1)} fusion(bf16[4,1024,512]{2,1,0:T(8,128)(2,1)} %param.6, s32[]{:T(128)S(6)} %select_n.72), kind=kLoop, calls=%fused_computation.17 | loop fusion | bytes 4194308 | tf_op jit(solution)/shard_map/dynamic_slice | solution.py:493
  34.8 3.7 %collective-permute-start.6 = (bf16[384,512]{1,0:T(8,128)(2,1)}, bf16[384,512]{1,0:T(8,128)(2,1)}, u32[]{:S(2)}, u32[]{:S(2)}) collective-permute-start(bf16[384,512]{1,0:T(8,128)(2,1)} %collective-permute-done.refs_0_), channel_id=1, source_target_pairs={{8,12},{9,13},{12,8},{13,9},{16,20},{17,21},{20,16},{21,17},{10,14... | collective-permute-start | bytes 1179656 | tf_op jit(solution)/shard_map/ppermute | solution.py:175
  38.5 1.4 %collective-permute-start.8 = (bf16[384,512]{1,0:T(8,128)(2,1)}, bf16[384,512]{1,0:T(8,128)(2,1)}, u32[]{:S(2)}, u32[]{:S(2)}) collective-permute-start(bf16[384,512]{1,0:T(8,128)(2,1)} %collective-permute-done.7.refs_2_), channel_id=1, source_target_pairs={{0,4},{1,5},{4,0},{5,1},{24,28},{25,29},{28,24},{29,25},{2,6},{3,7... | collective-permute-start | bytes 1179656 | tf_op jit(solution)/shard_map/ppermute | solution.py:175
  40.0 0.7 stack.100.info
  40.6 2.3 %collective-permute-start.9 = (bf16[384,512]{1,0:T(8,128)(2,1)S(1)}, bf16[384,512]{1,0:T(8,128)(2,1)}, u32[]{:S(2)}, u32[]{:S(2)}) collective-permute-start(bf16[384,512]{1,0:T(8,128)(2,1)S(1)} %collective-permute-done.1.after_ref.refs_0_), channel_id=1, source_target_pairs={{8,12},{9,13},{12,8},{13,9},{16,20},{17,21},{20,16},{21,17},{10,14... | collective-permute-start | bytes 1179656 | tf_op jit(solution)/shard_map/ppermute | solution.py:175
  43.0 1.4 %collective-permute-start.11 = (bf16[384,512]{1,0:T(8,128)(2,1)}, bf16[384,512]{1,0:T(8,128)(2,1)}, u32[]{:S(2)}, u32[]{:S(2)}) collective-permute-start(bf16[384,512]{1,0:T(8,128)(2,1)} %collective-permute-done.10.refs_2_), channel_id=1, source_target_pairs={{0,4},{1,5},{4,0},{5,1},{24,28},{25,29},{28,24},{29,25},{2,6},{3,7... | collective-permute-start | bytes 1179656 | tf_op jit(solution)/shard_map/ppermute | solution.py:175
  44.4 5.3 %shard_map.56 = (bf16[768,512]{1,0:T(8,128)(2,1)S(1)}, bf16[768,512]{1,0:T(8,128)(2,1)}) custom-call(s32[4]{0:T(128)S(1)} %add_add_fusion.info, s32[3]{0:T(128)S(1)} %copy-done.5, bf16[768,512]{1,0:T(8,128)(2,1)S(1)} %copy-done, bf16[768,512]{1,0:T(8,128)(2,1)} %collective-permute-done.3.refs_1_, bf16[768,512]{1,0:T(8,128)(2,1)} %collective-permute-done.4.refs_2_, ...), custom_call_target="tpu_custom_call" | custom-call | flops 1610612736 | bytes 5242880 | tf_op jit(solution)/shard_map/pallas_call | solution.py:268
  49.8 0.9 copy-done.8
  50.8 1.9 %shard_map.55.refs_4_ = bf16[4,192,512]{2,1,0:T(8,128)(2,1)} custom-call(s32[1]{0:T(128)} %bitcast.8.info, s32[192]{0:T(256)S(1)} %copy-done.4, bf16[768,512]{1,0:T(8,128)(2,1)S(1)} %copy-done, bf16[384,512]{1,0:T(8,128)(2,1)S(1)} %collective-permute-done.1.after_ref.refs_0_), custom_call_target="tpu_custom_call" | custom-call | bytes 1572864 | tf_op jit(solution)/shard_map/pallas_call | solution.py:432
  52.7 5.1 %all-to-all-start = ((bf16[4,192,512]{2,1,0:T(8,128)(2,1)}), bf16[4,192,512]{2,1,0:T(8,128)(2,1)S(1)}, u32[]{:S(2)}, u32[]{:S(2)}) async-start(bf16[4,192,512]{2,1,0:T(8,128)(2,1)} %shard_map.55.refs_4_), calls=%async_computation | async-start | bytes 1572864 | tf_op jit(solution)/shard_map/all_to_all | solution.py:518
  58.1 3.1 %shard_map.57 = (bf16[384,512]{1,0:T(8,128)(2,1)S(1)}, bf16[384,512]{1,0:T(8,128)(2,1)S(1)}) custom-call(s32[4]{0:T(128)S(1)} %add_add_fusion.1.info, s32[3]{0:T(128)S(1)} %copy-done.5, bf16[384,512]{1,0:T(8,128)(2,1)} %collective-permute-done.refs_0_, bf16[384,512]{1,0:T(8,128)(2,1)} %collective-permute-done.6.refs_1_, ...), custom_call_target="tpu_custom_call" | custom-call | flops 805306368 | bytes 3670016 | tf_op jit(solution)/shard_map/pallas_call | solution.py:268
  61.6 3.3 %shard_map.58 = (bf16[384,512]{1,0:T(8,128)(2,1)S(1)}, bf16[384,512]{1,0:T(8,128)(2,1)S(1)}) custom-call(s32[4]{0:T(128)S(1)} %add_add_fusion.1.info, s32[3]{0:T(128)S(1)} %copy-done.5, bf16[384,512]{1,0:T(8,128)(2,1)S(1)} %collective-permute-done.1.after_ref.refs_0_, bf16[384,512]{1,0:T(8,128)(2,1)} %collective-permute-done.9.refs_1_, ...), custom_call_target="tpu_custom_call" | custom-call | flops 805306368 | bytes 3670016 | tf_op jit(solution)/shard_map/pallas_call | solution.py:268
  65.0 0.7 copy-done.7
  65.9 0.6 broadcast_select_fusion.lengths
  66.5 0.6 slice_select_fusion
  68.2 17.8 %shard_map.59 = (f32[3072,128]{1,0:T(8,128)}, bf16[3072,128]{1,0:T(8,128)(2,1)}, f32[2,3072]{1,0:T(2,128)}) custom-call(s32[6]{0:T(128)} %stack.100.info, s32[192]{0:T(256)} %get-tuple-element.35.targets, s32[3]{0:T(128)} %broadcast_select_fusion.lengths, bf16[768,512]{1,0:T(8,128)(2,1)} %copy-done.8, bf16[384,512]{1,0:T(8,128)(2,1)} %copy-done.6, ...), custom_call_target="tpu_custom_call" | custom-call | flops 2415919104 | bytes 5505024 | tf_op jit(solution)/shard_map/pallas_call | solution.py:367
  86.2 1.2 collective-permute-done.15
  87.4 0.8 add.89.refs_0_
  88.1 0.6 collective-permute-start.16
  89.0 2.7 %collective-permute-start.18 = (f32[2,3072]{1,0:T(2,128)S(1)}, f32[2,3072]{1,0:T(2,128)S(1)}, u32[]{:S(2)}, u32[]{:S(2)}) collective-permute-start(f32[2,3072]{1,0:T(2,128)S(1)} %add.89.refs_0_), channel_id=1, source_target_pairs={{0,12},{1,13},{4,8},{5,9},{8,4},{9,5},{12,0},{13,1},{16,28},{17,29... | collective-permute-start | bytes 73736 | tf_op jit(solution)/shard_map/ppermute | solution.py:175
  92.0 0.7 collective-permute-done.17.refs_2_
  92.8 1.0 collective-permute-done.18.refs_3_
  93.8 1.4 %copy-done.1 = f32[3072,128]{1,0:T(8,128)S(1)} copy-done((f32[3072,128]{1,0:T(8,128)S(1)}, f32[3072,128]{1,0:T(8,128)}, u32[]{:S(2)}) %copy-start.1) | copy-done | bytes 1572888
  95.2 1.1 copy-done.3
  96.3 1.7 %shard_map.60 = (bf16[768,128]{1,0:T(8,128)(2,1)S(1)}, bf16[768,128]{1,0:T(8,128)(2,1)S(1)}, bf16[768,128]{1,0:T(8,128)(2,1)S(1)}, bf16[768,128]{1,0:T(8,128)(2,1)S(1)}) custom-call(s32[1]{0:T(128)} %bitcast.9.info, f32[3072,128]{1,0:T(8,128)S(1)} %copy-done.1, bf16[3072,128]{1,0:T(8,128)(2,1)S(1)} %copy-done.3, f32[2,3072]{1,0:T(2,128)S(1)} %add.89.refs_0_, ...), custom_call_target="tpu_custom_call" | custom-call | flops 3145728 | bytes 3145728 | tf_op jit(solution)/shard_map/pallas_call | solution.py:406
  98.0 4.5 %collective-permute-start.19 = (bf16[768,128]{1,0:T(8,128)(2,1)S(1)}, bf16[768,128]{1,0:T(8,128)(2,1)S(1)}, u32[]{:S(2)}, u32[]{:S(2)}) collective-permute-start(bf16[768,128]{1,0:T(8,128)(2,1)S(1)} %get-tuple-element.29), channel_id=1, source_target_pairs={{0,0},{1,8},{4,4},{5,12},{8,16},{9,24},{12,20},{13,28},{16,1},{17,... | collective-permute-start | bytes 589832 | tf_op jit(solution)/shard_map/ppermute | solution.py:175
  102.6 1.9 %collective-permute-start.21 = (bf16[768,128]{1,0:T(8,128)(2,1)S(1)}, bf16[768,128]{1,0:T(8,128)(2,1)S(1)}, u32[]{:S(2)}, u32[]{:S(2)}) collective-permute-start(bf16[768,128]{1,0:T(8,128)(2,1)S(1)} %get-tuple-element.30), channel_id=1, source_target_pairs={{0,8},{1,16},{4,12},{5,20},{8,24},{9,0},{12,28},{13,4},{16,9},{17,... | collective-permute-start | bytes 589832 | tf_op jit(solution)/shard_map/ppermute | solution.py:175
  104.5 2.1 %collective-permute-start.23 = (bf16[768,128]{1,0:T(8,128)(2,1)S(1)}, bf16[768,128]{1,0:T(8,128)(2,1)S(1)}, u32[]{:S(2)}, u32[]{:S(2)}) collective-permute-start(bf16[768,128]{1,0:T(8,128)(2,1)S(1)} %get-tuple-element.31), channel_id=1, source_target_pairs={{0,16},{1,24},{4,20},{5,28},{8,0},{9,8},{12,4},{13,12},{16,17},{17... | collective-permute-start | bytes 589832 | tf_op jit(solution)/shard_map/ppermute | solution.py:175
  106.6 0.7 collective-permute-start.25
  107.3 2.7 %collective-permute-done.19.refs_1_ = bf16[768,128]{1,0:T(8,128)(2,1)S(1)} collective-permute-done((bf16[768,128]{1,0:T(8,128)(2,1)S(1)}, bf16[768,128]{1,0:T(8,128)(2,1)S(1)}, u32[]{:S(2)}, u32[]{:S(2)}) %collective-permute-start.19) | collective-permute-done | bytes 196640 | tf_op jit(solution)/shard_map/ppermute | solution.py:175
  110.0 1.5 %collective-permute-start.20 = (bf16[768,128]{1,0:T(8,128)(2,1)S(1)}, bf16[768,128]{1,0:T(8,128)(2,1)S(1)}, u32[]{:S(2)}, u32[]{:S(2)}) collective-permute-start(bf16[768,128]{1,0:T(8,128)(2,1)S(1)} %collective-permute-done.19.refs_1_), channel_id=1, source_target_pairs={{0,4},{1,5},{4,0},{5,1},{8,12},{9,13},{12,8},{13,9},{16,20},{17,21... | collective-permute-start | bytes 589832 | tf_op jit(solution)/shard_map/ppermute | solution.py:175
  111.5 8.4 %collective-permute-done.21.refs_3_ = bf16[768,128]{1,0:T(8,128)(2,1)S(1)} collective-permute-done((bf16[768,128]{1,0:T(8,128)(2,1)S(1)}, bf16[768,128]{1,0:T(8,128)(2,1)S(1)}, u32[]{:S(2)}, u32[]{:S(2)}) %collective-permute-start.21) | collective-permute-done | bytes 196640 | tf_op jit(solution)/shard_map/ppermute | solution.py:175
  119.9 1.5 %collective-permute-start.22 = (bf16[768,128]{1,0:T(8,128)(2,1)S(1)}, bf16[768,128]{1,0:T(8,128)(2,1)S(1)}, u32[]{:S(2)}, u32[]{:S(2)}) collective-permute-start(bf16[768,128]{1,0:T(8,128)(2,1)S(1)} %collective-permute-done.21.refs_3_), channel_id=1, source_target_pairs={{0,4},{1,5},{4,0},{5,1},{8,12},{9,13},{12,8},{13,9},{16,20},{17,21... | collective-permute-start | bytes 589832 | tf_op jit(solution)/shard_map/ppermute | solution.py:175
  121.9 1.5 %collective-permute-start.26 = (bf16[768,128]{1,0:T(8,128)(2,1)S(1)}, bf16[768,128]{1,0:T(8,128)(2,1)S(1)}, u32[]{:S(2)}, u32[]{:S(2)}) collective-permute-start(bf16[768,128]{1,0:T(8,128)(2,1)S(1)} %collective-permute-done.25.refs_7_), channel_id=1, source_target_pairs={{0,4},{1,5},{4,0},{5,1},{8,12},{9,13},{12,8},{13,9},{16,20},{17,21... | collective-permute-start | bytes 589832 | tf_op jit(solution)/shard_map/ppermute | solution.py:175
  123.9 3.8 %collective-permute-done.22.refs_4_ = bf16[768,128]{1,0:T(8,128)(2,1)S(1)} collective-permute-done((bf16[768,128]{1,0:T(8,128)(2,1)S(1)}, bf16[768,128]{1,0:T(8,128)(2,1)S(1)}, u32[]{:S(2)}, u32[]{:S(2)}) %collective-permute-start.22) | collective-permute-done | bytes 196640 | tf_op jit(solution)/shard_map/ppermute | solution.py:175
  127.7 4.2 %collective-permute-done.24.refs_6_ = bf16[768,128]{1,0:T(8,128)(2,1)S(1)} collective-permute-done((bf16[768,128]{1,0:T(8,128)(2,1)S(1)}, bf16[768,128]{1,0:T(8,128)(2,1)S(1)}, u32[]{:S(2)}, u32[]{:S(2)}) %collective-permute-start.24) | collective-permute-done | bytes 196640 | tf_op jit(solution)/shard_map/ppermute | solution.py:175
  132.0 2.6 %collective-permute-done.26.refs_8_ = bf16[768,128]{1,0:T(8,128)(2,1)S(1)} collective-permute-done((bf16[768,128]{1,0:T(8,128)(2,1)S(1)}, bf16[768,128]{1,0:T(8,128)(2,1)S(1)}, u32[]{:S(2)}, u32[]{:S(2)}) %collective-permute-start.26) | collective-permute-done | bytes 196640 | tf_op jit(solution)/shard_map/ppermute | solution.py:175
  134.5 2.6 %shard_map.61 = bf16[768,512]{1,0:T(8,128)(2,1)} custom-call(s32[8]{0:T(128)S(1)} %stack.91.info, s32[4]{0:T(128)S(1)} %fusion.2.quarter, bf16[1024,512]{1,0:T(8,128)(2,1)S(1)} %copy-done.2, bf16[4,192,512]{2,1,0:T(8,128)(2,1)S(1)} %all-to-all-done.refs_0_, bf16[768,128]{1,0:T(8,128)(2,1)S(1)} %collective-permute-done.19.refs_1_, ...), custom_call_target="tpu_custom_call" | custom-call | flops 805306368 | bytes 8388608 | tf_op jit(solution)/shard_map/pallas_call | solution.py:468
  (52 shorter events, 4.0 us)
Async XLA Ops:
  0.0 18.4 %collective-permute-start.4 = (bf16[768,512]{1,0:T(8,128)(2,1)}, bf16[768,512]{1,0:T(8,128)(2,1)}, u32[]{:S(2)}, u32[]{:S(2)}) collective-permute-start(bf16[768,512]{1,0:T(8,128)(2,1)} %refs_0_.1), channel_id=1, source_target_pairs={{0,9},{4,13},{8,1},{12,5},{17,24},{21,28},{25,16},{29,20},{2,11},{... | collective-permute-start | bytes 2359304 | tf_op jit(solution)/shard_map/ppermute | solution.py:175
  3.3 13.7 %collective-permute-start = (bf16[384,512]{1,0:T(8,128)(2,1)S(1)}, bf16[384,512]{1,0:T(8,128)(2,1)}, u32[]{:S(2)}, u32[]{:S(2)}) collective-permute-start(bf16[384,512]{1,0:T(8,128)(2,1)S(1)} %get-tuple-element.33), channel_id=1, source_target_pairs={{1,16},{5,20},{9,17},{13,21},{16,8},{20,12},{24,9},{28,13},{3,18},... | collective-permute-start | bytes 1179656 | tf_op jit(solution)/shard_map/ppermute | solution.py:175
  4.6 36.0 %collective-permute-start.3 = (bf16[768,512]{1,0:T(8,128)(2,1)}, bf16[768,512]{1,0:T(8,128)(2,1)}, u32[]{:S(2)}, u32[]{:S(2)}) collective-permute-start(bf16[768,512]{1,0:T(8,128)(2,1)} %refs_0_.1), channel_id=1, source_target_pairs={{0,4},{4,0},{8,12},{12,8},{17,21},{21,17},{25,29},{29,25},{2,6},{6... | collective-permute-start | bytes 2359304 | tf_op jit(solution)/shard_map/ppermute | solution.py:175
  17.1 13.9 %collective-permute-start.1 = (bf16[384,512]{1,0:T(8,128)(2,1)S(1)}, bf16[384,512]{1,0:T(8,128)(2,1)S(1)}, u32[]{:S(2)}, u32[]{:S(2)}) collective-permute-start(bf16[384,512]{1,0:T(8,128)(2,1)S(1)} %get-tuple-element.19), channel_id=1, source_target_pairs={{1,16},{5,20},{9,17},{13,21},{16,8},{20,12},{24,9},{28,13},{3,18},... | collective-permute-start | bytes 1179656 | tf_op jit(solution)/shard_map/ppermute | solution.py:175
  18.4 26.0 %collective-permute-start.5 = (bf16[768,512]{1,0:T(8,128)(2,1)}, bf16[768,512]{1,0:T(8,128)(2,1)}, u32[]{:S(2)}, u32[]{:S(2)}) collective-permute-start(bf16[768,512]{1,0:T(8,128)(2,1)} %collective-permute-done.4.refs_2_), channel_id=1, source_target_pairs={{1,5},{5,1},{9,13},{13,9},{16,20},{20,16},{24,28},{28,24},{3,7},{7... | collective-permute-start | bytes 2359304 | tf_op jit(solution)/shard_map/ppermute | solution.py:175
  20.0 18.5 %collective-permute-start.7 = (bf16[384,512]{1,0:T(8,128)(2,1)}, bf16[384,512]{1,0:T(8,128)(2,1)}, u32[]{:S(2)}, u32[]{:S(2)}) collective-permute-start(bf16[384,512]{1,0:T(8,128)(2,1)} %collective-permute-done.refs_0_), channel_id=1, source_target_pairs={{8,0},{9,1},{12,4},{13,5},{16,24},{17,25},{20,28},{21,29},{10,2},{... | collective-permute-start | bytes 1179656 | tf_op jit(solution)/shard_map/ppermute | solution.py:175
  31.0 12.0 %collective-permute-start.10 = (bf16[384,512]{1,0:T(8,128)(2,1)S(1)}, bf16[384,512]{1,0:T(8,128)(2,1)}, u32[]{:S(2)}, u32[]{:S(2)}) collective-permute-start(bf16[384,512]{1,0:T(8,128)(2,1)S(1)} %collective-permute-done.1.after_ref.refs_0_), channel_id=1, source_target_pairs={{8,0},{9,1},{12,4},{13,5},{16,24},{17,25},{20,28},{21,29},{10,2},{... | collective-permute-start | bytes 1179656 | tf_op jit(solution)/shard_map/ppermute | solution.py:175
  33.0 11.4 %copy-start = (bf16[768,512]{1,0:T(8,128)(2,1)S(1)}, bf16[768,512]{1,0:T(8,128)(2,1)}, u32[]{:S(2)}) copy-start(bf16[768,512]{1,0:T(8,128)(2,1)} %refs_0_.1) | copy-start | bytes 2359300
  33.0 11.4 %copy-start.5 = (s32[3]{0:T(128)S(1)}, s32[3]{0:T(128)}, u32[]{:S(2)}) copy-start(s32[3]{0:T(128)} %lengths.5) | copy-start | bytes 40
  34.8 23.1 %collective-permute-start.6 = (bf16[384,512]{1,0:T(8,128)(2,1)}, bf16[384,512]{1,0:T(8,128)(2,1)}, u32[]{:S(2)}, u32[]{:S(2)}) collective-permute-start(bf16[384,512]{1,0:T(8,128)(2,1)} %collective-permute-done.refs_0_), channel_id=1, source_target_pairs={{8,12},{9,13},{12,8},{13,9},{16,20},{17,21},{20,16},{21,17},{10,14... | collective-permute-start | bytes 1179656 | tf_op jit(solution)/shard_map/ppermute | solution.py:175
  38.5 19.6 %collective-permute-start.8 = (bf16[384,512]{1,0:T(8,128)(2,1)}, bf16[384,512]{1,0:T(8,128)(2,1)}, u32[]{:S(2)}, u32[]{:S(2)}) collective-permute-start(bf16[384,512]{1,0:T(8,128)(2,1)} %collective-permute-done.7.refs_2_), channel_id=1, source_target_pairs={{0,4},{1,5},{4,0},{5,1},{24,28},{25,29},{28,24},{29,25},{2,6},{3,7... | collective-permute-start | bytes 1179656 | tf_op jit(solution)/shard_map/ppermute | solution.py:175
  40.6 10.1 %copy-start.4 = (s32[192]{0:T(256)S(1)}, s32[192]{0:T(256)}, u32[]{:S(2)}) copy-start(s32[192]{0:T(256)} %targets.1) | copy-start | bytes 2308
  40.6 21.0 %collective-permute-start.9 = (bf16[384,512]{1,0:T(8,128)(2,1)S(1)}, bf16[384,512]{1,0:T(8,128)(2,1)}, u32[]{:S(2)}, u32[]{:S(2)}) collective-permute-start(bf16[384,512]{1,0:T(8,128)(2,1)S(1)} %collective-permute-done.1.after_ref.refs_0_), channel_id=1, source_target_pairs={{8,12},{9,13},{12,8},{13,9},{16,20},{17,21},{20,16},{21,17},{10,14... | collective-permute-start | bytes 1179656 | tf_op jit(solution)/shard_map/ppermute | solution.py:175
  43.0 18.6 %collective-permute-start.11 = (bf16[384,512]{1,0:T(8,128)(2,1)}, bf16[384,512]{1,0:T(8,128)(2,1)}, u32[]{:S(2)}, u32[]{:S(2)}) collective-permute-start(bf16[384,512]{1,0:T(8,128)(2,1)} %collective-permute-done.10.refs_2_), channel_id=1, source_target_pairs={{0,4},{1,5},{4,0},{5,1},{24,28},{25,29},{28,24},{29,25},{2,6},{3,7... | collective-permute-start | bytes 1179656 | tf_op jit(solution)/shard_map/ppermute | solution.py:175
  49.8 0.9 copy-start.8
  50.6 16.8 %collective-permute-start.12 = (bf16[768,512]{1,0:T(8,128)(2,1)}, bf16[768,512]{1,0:T(8,128)(2,1)}, u32[]{:S(2)}, u32[]{:S(2)}) collective-permute-start(bf16[768,512]{1,0:T(8,128)(2,1)} %get-tuple-element.23), channel_id=1, source_target_pairs={{0,1},{1,0},{4,5},{5,4},{8,9},{9,8},{12,13},{13,12},{16,17},{17,16... | collective-permute-start | bytes 2359304 | tf_op jit(solution)/shard_map/ppermute | solution.py:175
  52.7 71.2 %all-to-all-start = ((bf16[4,192,512]{2,1,0:T(8,128)(2,1)}), bf16[4,192,512]{2,1,0:T(8,128)(2,1)S(1)}, u32[]{:S(2)}, u32[]{:S(2)}) async-start(bf16[4,192,512]{2,1,0:T(8,128)(2,1)} %shard_map.55.refs_4_), calls=%async_computation | async-start | bytes 1572864 | tf_op jit(solution)/shard_map/all_to_all | solution.py:518
  57.9 8.0 %collective-permute-start.2 = (s32[195]{0:T(256)S(1)}, s32[195]{0:T(256)S(1)}, u32[]{:S(2)}, u32[]{:S(2)}) collective-permute-start(s32[195]{0:T(256)S(1)} %pad_add_fusion), channel_id=1, source_target_pairs={{0,1},{1,0},{4,5},{5,4},{8,9},{9,8},{12,13},{13,12},{16,17},{17,16... | collective-permute-start | bytes 2348 | tf_op jit(solution)/shard_map/ppermute | solution.py:175
  61.3 6.2 %copy-start.6 = (bf16[384,512]{1,0:T(8,128)(2,1)}, bf16[384,512]{1,0:T(8,128)(2,1)S(1)}, u32[]{:S(2)}) copy-start(bf16[384,512]{1,0:T(8,128)(2,1)S(1)} %get-tuple-element.21.refs_1_) | copy-start | bytes 1179652
  61.3 5.8 %collective-permute-start.13 = (bf16[384,512]{1,0:T(8,128)(2,1)S(1)}, bf16[384,512]{1,0:T(8,128)(2,1)S(1)}, u32[]{:S(2)}, u32[]{:S(2)}) collective-permute-start(bf16[384,512]{1,0:T(8,128)(2,1)S(1)} %get-tuple-element.24), channel_id=1, source_target_pairs={{0,1},{1,0},{4,5},{5,4},{8,9},{9,8},{12,13},{13,12},{16,17},{17,16... | collective-permute-start | bytes 1179656 | tf_op jit(solution)/shard_map/ppermute | solution.py:175
  64.9 0.7 copy-start.7
  65.7 1.7 %collective-permute-start.14 = (bf16[384,512]{1,0:T(8,128)(2,1)S(1)}, bf16[384,512]{1,0:T(8,128)(2,1)S(1)}, u32[]{:S(2)}, u32[]{:S(2)}) collective-permute-start(bf16[384,512]{1,0:T(8,128)(2,1)S(1)} %get-tuple-element.25), channel_id=1, source_target_pairs={{0,1},{1,0},{4,5},{5,4},{8,9},{9,8},{12,13},{13,12},{16,17},{17,16... | collective-permute-start | bytes 1179656 | tf_op jit(solution)/shard_map/ppermute | solution.py:175
  67.1 0.7 copy-start.9
  67.4 0.8 copy-start.10
  68.2 66.4 %copy-start.2 = (bf16[1024,512]{1,0:T(8,128)(2,1)S(1)}, bf16[1024,512]{1,0:T(8,128)(2,1)}, u32[]{:S(2)}) copy-start(bf16[1024,512]{1,0:T(8,128)(2,1)} %w_ref.1) | copy-start | bytes 3145732
  86.0 1.4 %collective-permute-start.15 = (f32[2,3072]{1,0:T(2,128)}, f32[2,3072]{1,0:T(2,128)S(1)}, u32[]{:S(2)}, u32[]{:S(2)}) collective-permute-start(f32[2,3072]{1,0:T(2,128)} %get-tuple-element.28), channel_id=1, source_target_pairs={{0,1},{1,0},{4,5},{5,4},{8,9},{9,8},{12,13},{13,12},{16,17},{17,16... | collective-permute-start | bytes 73736 | tf_op jit(solution)/shard_map/ppermute | solution.py:175
  88.1 3.9 %collective-permute-start.16 = (f32[2,3072]{1,0:T(2,128)S(1)}, f32[2,3072]{1,0:T(2,128)S(1)}, u32[]{:S(2)}, u32[]{:S(2)}) collective-permute-start(f32[2,3072]{1,0:T(2,128)S(1)} %add.89.refs_0_), channel_id=1, source_target_pairs={{0,4},{1,5},{4,0},{5,1},{8,12},{9,13},{12,8},{13,9},{16,20},{17,21... | collective-permute-start | bytes 73736 | tf_op jit(solution)/shard_map/ppermute | solution.py:175
  88.7 4.0 %collective-permute-start.17 = (f32[2,3072]{1,0:T(2,128)S(1)}, f32[2,3072]{1,0:T(2,128)S(1)}, u32[]{:S(2)}, u32[]{:S(2)}) collective-permute-start(f32[2,3072]{1,0:T(2,128)S(1)} %add.89.refs_0_), channel_id=1, source_target_pairs={{0,8},{1,9},{4,12},{5,13},{8,0},{9,1},{12,4},{13,5},{16,24},{17,25... | collective-permute-start | bytes 73736 | tf_op jit(solution)/shard_map/ppermute | solution.py:175
  89.0 4.7 %collective-permute-start.18 = (f32[2,3072]{1,0:T(2,128)S(1)}, f32[2,3072]{1,0:T(2,128)S(1)}, u32[]{:S(2)}, u32[]{:S(2)}) collective-permute-start(f32[2,3072]{1,0:T(2,128)S(1)} %add.89.refs_0_), channel_id=1, source_target_pairs={{0,12},{1,13},{4,8},{5,9},{8,4},{9,5},{12,0},{13,1},{16,28},{17,29... | collective-permute-start | bytes 73736 | tf_op jit(solution)/shard_map/ppermute | solution.py:175
  93.8 1.4 %copy-start.1 = (f32[3072,128]{1,0:T(8,128)S(1)}, f32[3072,128]{1,0:T(8,128)}, u32[]{:S(2)}) copy-start(f32[3072,128]{1,0:T(8,128)} %get-tuple-element.26.att_ref) | copy-start | bytes 4718596
  95.2 1.1 copy-start.3
  98.0 12.0 %collective-permute-start.19 = (bf16[768,128]{1,0:T(8,128)(2,1)S(1)}, bf16[768,128]{1,0:T(8,128)(2,1)S(1)}, u32[]{:S(2)}, u32[]{:S(2)}) collective-permute-start(bf16[768,128]{1,0:T(8,128)(2,1)S(1)} %get-tuple-element.29), channel_id=1, source_target_pairs={{0,0},{1,8},{4,4},{5,12},{8,16},{9,24},{12,20},{13,28},{16,1},{17,... | collective-permute-start | bytes 589832 | tf_op jit(solution)/shard_map/ppermute | solution.py:175
  102.6 17.3 %collective-permute-start.21 = (bf16[768,128]{1,0:T(8,128)(2,1)S(1)}, bf16[768,128]{1,0:T(8,128)(2,1)S(1)}, u32[]{:S(2)}, u32[]{:S(2)}) collective-permute-start(bf16[768,128]{1,0:T(8,128)(2,1)S(1)} %get-tuple-element.30), channel_id=1, source_target_pairs={{0,8},{1,16},{4,12},{5,20},{8,24},{9,0},{12,28},{13,4},{16,9},{17,... | collective-permute-start | bytes 589832 | tf_op jit(solution)/shard_map/ppermute | solution.py:175
  104.5 16.9 %collective-permute-start.23 = (bf16[768,128]{1,0:T(8,128)(2,1)S(1)}, bf16[768,128]{1,0:T(8,128)(2,1)S(1)}, u32[]{:S(2)}, u32[]{:S(2)}) collective-permute-start(bf16[768,128]{1,0:T(8,128)(2,1)S(1)} %get-tuple-element.31), channel_id=1, source_target_pairs={{0,16},{1,24},{4,20},{5,28},{8,0},{9,8},{12,4},{13,12},{16,17},{17... | collective-permute-start | bytes 589832 | tf_op jit(solution)/shard_map/ppermute | solution.py:175
  106.6 15.3 %collective-permute-start.25 = (bf16[768,128]{1,0:T(8,128)(2,1)S(1)}, bf16[768,128]{1,0:T(8,128)(2,1)S(1)}, u32[]{:S(2)}, u32[]{:S(2)}) collective-permute-start(bf16[768,128]{1,0:T(8,128)(2,1)S(1)} %get-tuple-element.32), channel_id=1, source_target_pairs={{0,24},{1,0},{4,28},{5,4},{8,8},{9,16},{12,12},{13,20},{16,25},{17... | collective-permute-start | bytes 589832 | tf_op jit(solution)/shard_map/ppermute | solution.py:175
  110.0 13.9 %collective-permute-start.20 = (bf16[768,128]{1,0:T(8,128)(2,1)S(1)}, bf16[768,128]{1,0:T(8,128)(2,1)S(1)}, u32[]{:S(2)}, u32[]{:S(2)}) collective-permute-start(bf16[768,128]{1,0:T(8,128)(2,1)S(1)} %collective-permute-done.19.refs_1_), channel_id=1, source_target_pairs={{0,4},{1,5},{4,0},{5,1},{8,12},{9,13},{12,8},{13,9},{16,20},{17,21... | collective-permute-start | bytes 589832 | tf_op jit(solution)/shard_map/ppermute | solution.py:175
  119.9 7.8 %collective-permute-start.22 = (bf16[768,128]{1,0:T(8,128)(2,1)S(1)}, bf16[768,128]{1,0:T(8,128)(2,1)S(1)}, u32[]{:S(2)}, u32[]{:S(2)}) collective-permute-start(bf16[768,128]{1,0:T(8,128)(2,1)S(1)} %collective-permute-done.21.refs_3_), channel_id=1, source_target_pairs={{0,4},{1,5},{4,0},{5,1},{8,12},{9,13},{12,8},{13,9},{16,20},{17,21... | collective-permute-start | bytes 589832 | tf_op jit(solution)/shard_map/ppermute | solution.py:175
  121.4 10.6 %collective-permute-start.24 = (bf16[768,128]{1,0:T(8,128)(2,1)S(1)}, bf16[768,128]{1,0:T(8,128)(2,1)S(1)}, u32[]{:S(2)}, u32[]{:S(2)}) collective-permute-start(bf16[768,128]{1,0:T(8,128)(2,1)S(1)} %collective-permute-done.23.refs_5_), channel_id=1, source_target_pairs={{0,4},{1,5},{4,0},{5,1},{8,12},{9,13},{12,8},{13,9},{16,20},{17,21... | collective-permute-start | bytes 589832 | tf_op jit(solution)/shard_map/ppermute | solution.py:175
  121.9 12.6 %collective-permute-start.26 = (bf16[768,128]{1,0:T(8,128)(2,1)S(1)}, bf16[768,128]{1,0:T(8,128)(2,1)S(1)}, u32[]{:S(2)}, u32[]{:S(2)}) collective-permute-start(bf16[768,128]{1,0:T(8,128)(2,1)S(1)} %collective-permute-done.25.refs_7_), channel_id=1, source_target_pairs={{0,4},{1,5},{4,0},{5,1},{8,12},{9,13},{12,8},{13,9},{16,20},{17,21... | collective-permute-start | bytes 589832 | tf_op jit(solution)/shard_map/ppermute | solution.py:175

commit v4 on v3

--- a/solution.py
+++ b/solution.py
@@ -254,6 +254,8 @@
             )
             t = 0.5 * z
             act = (t + t * jnp.tanh(t)).astype(jnp.bfloat16)
+            if j == 2:
+                act = act * 0.5
             low, high = act[:, :128], act[:, 128:]
             cols = pl.ds(j * 128, 128)
             mine_ref[at, cols] = jnp.where(low_core, low, high)
@@ -288,30 +290,29 @@
 DSUB = 256
 
 
-def attend_kernel(info, targets, lengths, *refs):
-    pieces, (att_ref, u_ref, stat_ref, q_s, v0, v1, k0, k1) = refs[:-8], refs[-8:]
+def attend_kernel(info, here_targets, here_lengths, there, *refs):
+    pieces, (att_ref, u_ref, stat_ref, held) = refs[:-4], refs[-4:]
+    own = info[len(pieces)] == 0
+    blocks = here_targets.shape[0]
     seq = att_ref.shape[0]
-    low = lax.broadcasted_iota(jnp.int32, (RB, 128), 1) < DH
-    zero = jnp.zeros((RB, 128), jnp.bfloat16)
+    low = lax.broadcasted_iota(jnp.int32, (SUB, 128), 1) < DH
+    zero = jnp.zeros((SUB, 128), jnp.bfloat16)
     for n, piece in enumerate(pieces):
         base = info[n]
 
         @pl.loop(0, piece.shape[0] // RB, unroll=8)
         def _(b):
             frm = pl.ds(pl.multiple_of(b * RB, RB), RB)
-            to = pl.ds(pl.multiple_of(targets[base + b] * RB, RB), RB)
+            to = pl.ds(
+                pl.multiple_of(jnp.where(own, here_targets[base + b], there[base + b]) * RB, RB), RB
+            )
             u_ref[to, :] = piece[frm, 0:128]
-            v = piece[frm, 128:256]
-            v0[to, :] = jnp.where(low, v, zero)
-            v1[to, :] = jnp.where(low, zero, v)
-            q_s[to, :] = piece[frm, 256:384] * 0.5
-            k = piece[frm, 384:512]
-            k0[to, :] = jnp.where(low, k, zero)
-            k1[to, :] = jnp.where(low, zero, k)
+            held[to, :] = piece[frm, 128:512]
+
     ends = []
     total = jnp.int32(0)
-    for i in range(lengths.shape[0]):
-        total = total + lengths[i]
+    for i in range(here_lengths.shape[0]):
+        total = total + jnp.where(own, here_lengths[i], there[blocks + i])
         ends.append(total)
     def start_of(p):
         best = p * 0
@@ -320,7 +321,7 @@
         return best
     def term(q0, rows, k0_at, keys, first, causal):
         at = pl.ds(pl.multiple_of(q0, 256), rows)
-        q = q_s[at, :]
+        q = held[at, 128:256]
         total = None
         for s in range(keys // SUB):
             ks = pl.ds(pl.multiple_of(k0_at + s * SUB, SUB), SUB)
@@ -329,12 +330,14 @@
                 ok = kp >= first
                 if causal:
                     ok = ok & (kp <= q0 + lax.broadcasted_iota(jnp.int32, (rows, 1), 0))
-            for kk, vv in ((k0, v0), (k1, v1)):
-                t = lax.dot_general(q, kk[ks, :], (((1,), (1,)), ((), ())), preferred_element_type=jnp.float32)
+            v, k = held[ks, 0:128], held[ks, 256:384]
+            for upper in (False, True):
+                kk, vv = (jnp.where(low, zero, m) if upper else jnp.where(low, m, zero) for m in (k, v))
+                t = lax.dot_general(q, kk, (((1,), (1,)), ((), ())), preferred_element_type=jnp.float32)
                 w = t + t * jnp.tanh(t)
                 if first is not None:
                     w = jnp.where(ok, w, 0.0)
-                d = jnp.dot(w.astype(jnp.bfloat16), vv[ks, :], preferred_element_type=jnp.float32)
+                d = jnp.dot(w.astype(jnp.bfloat16), vv, preferred_element_type=jnp.float32)
                 total = d if total is None else total + d
         att_ref[at, :] += total
     @pl.loop(0, seq // TQ)
@@ -360,21 +363,21 @@
             flip = att_ref[part, :].T
             stat_ref[0:1, part] = jnp.sum(flip, axis=0, keepdims=True)
             stat_ref[1:2, part] = jnp.sum(flip * flip, axis=0, keepdims=True)
-def attend(info, targets, lengths, pieces):
+def attend(info, targets, lengths, there, pieces):
     seq = sum(p.shape[0] for p in pieces)
     smem = pl.BlockSpec(memory_space=pltpu.SMEM)
     vmem = pl.BlockSpec(memory_space=pltpu.VMEM)
     return pl.pallas_call(
         attend_kernel,
         out_shape=(jax.ShapeDtypeStruct((seq, 128), jnp.float32), jax.ShapeDtypeStruct((seq, 128), jnp.bfloat16), jax.ShapeDtypeStruct((2, seq), jnp.float32)),
-        in_specs=[smem] * 3 + [vmem] * len(pieces),
+        in_specs=[smem] * 4 + [vmem] * len(pieces),
         out_specs=(vmem,) * 3,
-        scratch_shapes=[pltpu.VMEM((seq, 128), jnp.bfloat16)] * 5,
+        scratch_shapes=[pltpu.VMEM((seq, 384), jnp.bfloat16)],
         compiler_params=pltpu.CompilerParams(vmem_limit_bytes=56 * 1024 * 1024),
         cost_estimate=pl.CostEstimate(
             flops=2 * seq * seq * 128, bytes_accessed=seq * 128 * 14, transcendentals=seq * seq
         ),
-    )(info, targets, lengths, *pieces)
+    )(info, targets, lengths, there, *pieces)
 
 
 def gate_kernel(info, att_ref, u_ref, *refs):
@@ -488,8 +491,6 @@
     blocks = rows // RB
     targets_here = block_target
     other_ints = move(jnp.concatenate([block_target, user_lengths]), other_core)
-    targets = jnp.where(foreign == 0, block_target, other_ints[: block_target.shape[0]])
-    lengths = jnp.where(foreign == 0, user_lengths, other_ints[block_target.shape[0] :])
     w_mine = lax.dynamic_slice_in_dim(w_proj, zlo * 256, 256, axis=2)
 
     parts = 2
@@ -536,7 +537,7 @@
     starts += [mine_second * blocks + i * part_blocks for i in range(parts)]
     starts += [jnp.where(foreign == 0, z ^ 1, z) * blocks]
     starts += [other_second * blocks + i * part_blocks for i in range(parts)]
-    att, u, stat = attend(ints(*starts), targets, lengths, mine + got)
+    att, u, stat = attend(ints(*starts, foreign), block_target, user_lengths, other_ints, mine + got)
 
     by_shard = targets_here.reshape(4, blocks)
     quarter = jnp.max(

time: 138 us -> 137 us (level)
    unnamed x22 -> x24, local copies, waits for them, and re-layouts: 4.92 us -> 4.95 us
  transfers between devices with their start and end apart: 28 -> 28, of which waited for: 12 -> 12; matrix products, arithmetic and copies ran while one was open for 5% -> 4% of each run, Pallas kernels for 24% -> 24%
where the time goes in v4:
time: 137 us
  starting transfers between devices  47.4 us (35%)
  waiting for transfers between devices  43 us (31%)
  Pallas kernels  35.8 us (26%)
  local copies, waits for them, and re-layouts  8.88 us (6%)
    ppermute x27, waiting for transfers between devices, move(): return lax.ppermute(value, ROUTE, route(rule))  43 us
    ppermute x27, starting transfers between devices, move(): return lax.ppermute(value, ROUTE, route(rule))  41.7 us
    pallas_call x1, Pallas kernels, attend(): pl.pallas_call(attend_kernel, out_shape=(jax.ShapeDtypeStruct((seq, 128),...  17.7 us
    pallas_call x3, Pallas kernels, project(): pl.pallas_call(functools.partial(project_kernel, len(after)), out_shape=(...  11.9 us
    all_to_all x1, starting transfers between devices, team_body(): lax.all_to_all(send, ('half', 'zlo'), split_axis=0, concat_axis=0, tiled=...  5.75 us
    unnamed x24, local copies, waits for them, and re-layouts  4.95 us
  transfers between devices with their start and end apart: 28, of which 12 were waited for; matrix products, arithmetic and copies ran while one was open for 4% of the time, Pallas kernels for 24%

profile of v4, /device:TPU:8, one launch (start us, length us, event | category | flops | bytes accessed | tf_op | source)
XLA Modules:
  0.0 136.5 jit_solution(6496570972183967103)
XLA Ops:
  0.0 2.2 %collective-permute-start.4 = (bf16[768,512]{1,0:T(8,128)(2,1)}, bf16[768,512]{1,0:T(8,128)(2,1)}, u32[]{:S(2)}, u32[]{:S(2)}) collective-permute-start(bf16[768,512]{1,0:T(8,128)(2,1)} %refs_0_.1), channel_id=1, source_target_pairs={{0,9},{4,13},{8,1},{12,5},{17,24},{21,28},{25,16},{29,20},{2,11},{... | collective-permute-start | bytes 2359304 | tf_op jit(solution)/shard_map/ppermute | solution.py:175
  2.2 1.2 fusion.4
  3.3 1.3 collective-permute-start
  4.6 3.9 %collective-permute-start.3 = (bf16[768,512]{1,0:T(8,128)(2,1)}, bf16[768,512]{1,0:T(8,128)(2,1)}, u32[]{:S(2)}, u32[]{:S(2)}) collective-permute-start(bf16[768,512]{1,0:T(8,128)(2,1)} %refs_0_.1), channel_id=1, source_target_pairs={{0,4},{4,0},{8,12},{12,8},{17,21},{21,17},{25,29},{29,25},{2,6},{6... | collective-permute-start | bytes 2359304 | tf_op jit(solution)/shard_map/ppermute | solution.py:175
  8.6 8.5 %collective-permute-done.refs_0_ = bf16[384,512]{1,0:T(8,128)(2,1)} collective-permute-done((bf16[384,512]{1,0:T(8,128)(2,1)S(1)}, bf16[384,512]{1,0:T(8,128)(2,1)}, u32[]{:S(2)}, u32[]{:S(2)}) %collective-permute-start) | collective-permute-done | bytes 393248 | tf_op jit(solution)/shard_map/ppermute | solution.py:175
  17.1 1.3 collective-permute-start.1
  18.4 1.6 %collective-permute-start.5 = (bf16[768,512]{1,0:T(8,128)(2,1)}, bf16[768,512]{1,0:T(8,128)(2,1)}, u32[]{:S(2)}, u32[]{:S(2)}) collective-permute-start(bf16[768,512]{1,0:T(8,128)(2,1)} %collective-permute-done.4.refs_2_), channel_id=1, source_target_pairs={{1,5},{5,1},{9,13},{13,9},{16,20},{20,16},{24,28},{28,24},{3,7},{7... | collective-permute-start | bytes 2359304 | tf_op jit(solution)/shard_map/ppermute | solution.py:175
  20.0 2.0 %collective-permute-start.7 = (bf16[384,512]{1,0:T(8,128)(2,1)}, bf16[384,512]{1,0:T(8,128)(2,1)}, u32[]{:S(2)}, u32[]{:S(2)}) collective-permute-start(bf16[384,512]{1,0:T(8,128)(2,1)} %collective-permute-done.refs_0_), channel_id=1, source_target_pairs={{8,0},{9,1},{12,4},{13,5},{16,24},{17,25},{20,28},{21,29},{10,2},{... | collective-permute-start | bytes 1179656 | tf_op jit(solution)/shard_map/ppermute | solution.py:175
  22.0 9.0 %collective-permute-done.1.after_ref.refs_0_ = bf16[384,512]{1,0:T(8,128)(2,1)S(1)} collective-permute-done((bf16[384,512]{1,0:T(8,128)(2,1)S(1)}, bf16[384,512]{1,0:T(8,128)(2,1)S(1)}, u32[]{:S(2)}, u32[]{:S(2)}) %collective-permute-start.1) | collective-permute-done | bytes 393248 | tf_op jit(solution)/shard_map/ppermute | solution.py:175
  31.0 2.0 %collective-permute-start.10 = (bf16[384,512]{1,0:T(8,128)(2,1)S(1)}, bf16[384,512]{1,0:T(8,128)(2,1)}, u32[]{:S(2)}, u32[]{:S(2)}) collective-permute-start(bf16[384,512]{1,0:T(8,128)(2,1)S(1)} %collective-permute-done.1.after_ref.refs_0_), channel_id=1, source_target_pairs={{8,0},{9,1},{12,4},{13,5},{16,24},{17,25},{20,28},{21,29},{10,2},{... | collective-permute-start | bytes 1179656 | tf_op jit(solution)/shard_map/ppermute | solution.py:175
  33.1 1.8 %constant_dynamic-slice_fusion.refs_4_.refs_5_ = bf16[4,1024,256]{2,1,0:T(8,128)(2,1)S(1)} fusion(bf16[4,1024,512]{2,1,0:T(8,128)(2,1)} %param.6, s32[]{:T(128)S(6)} %select_n.52), kind=kLoop, calls=%fused_computation.15 | loop fusion | bytes 4194308 | tf_op jit(solution)/shard_map/dynamic_slice | solution.py:494
  34.9 3.7 %collective-permute-start.6 = (bf16[384,512]{1,0:T(8,128)(2,1)}, bf16[384,512]{1,0:T(8,128)(2,1)}, u32[]{:S(2)}, u32[]{:S(2)}) collective-permute-start(bf16[384,512]{1,0:T(8,128)(2,1)} %collective-permute-done.refs_0_), channel_id=1, source_target_pairs={{8,12},{9,13},{12,8},{13,9},{16,20},{17,21},{20,16},{21,17},{10,14... | collective-permute-start | bytes 1179656 | tf_op jit(solution)/shard_map/ppermute | solution.py:175
  38.6 1.4 %collective-permute-start.8 = (bf16[384,512]{1,0:T(8,128)(2,1)}, bf16[384,512]{1,0:T(8,128)(2,1)}, u32[]{:S(2)}, u32[]{:S(2)}) collective-permute-start(bf16[384,512]{1,0:T(8,128)(2,1)} %collective-permute-done.7.refs_2_), channel_id=1, source_target_pairs={{0,4},{1,5},{4,0},{5,1},{24,28},{25,29},{28,24},{29,25},{2,6},{3,7... | collective-permute-start | bytes 1179656 | tf_op jit(solution)/shard_map/ppermute | solution.py:175
  40.0 2.2 %collective-permute-start.9 = (bf16[384,512]{1,0:T(8,128)(2,1)S(1)}, bf16[384,512]{1,0:T(8,128)(2,1)}, u32[]{:S(2)}, u32[]{:S(2)}) collective-permute-start(bf16[384,512]{1,0:T(8,128)(2,1)S(1)} %collective-permute-done.1.after_ref.refs_0_), channel_id=1, source_target_pairs={{8,12},{9,13},{12,8},{13,9},{16,20},{17,21},{20,16},{21,17},{10,14... | collective-permute-start | bytes 1179656 | tf_op jit(solution)/shard_map/ppermute | solution.py:175
  42.2 1.4 %collective-permute-start.11 = (bf16[384,512]{1,0:T(8,128)(2,1)}, bf16[384,512]{1,0:T(8,128)(2,1)}, u32[]{:S(2)}, u32[]{:S(2)}) collective-permute-start(bf16[384,512]{1,0:T(8,128)(2,1)} %collective-permute-done.10.refs_2_), channel_id=1, source_target_pairs={{0,4},{1,5},{4,0},{5,1},{24,28},{25,29},{28,24},{29,25},{2,6},{3,7... | collective-permute-start | bytes 1179656 | tf_op jit(solution)/shard_map/ppermute | solution.py:175
  43.7 5.4 %shard_map.56 = (bf16[768,512]{1,0:T(8,128)(2,1)S(1)}, bf16[768,512]{1,0:T(8,128)(2,1)}) custom-call(s32[4]{0:T(128)S(1)} %add_add_fusion.info, s32[3]{0:T(128)S(1)} %copy-done.6, bf16[768,512]{1,0:T(8,128)(2,1)S(1)} %copy-done, bf16[768,512]{1,0:T(8,128)(2,1)} %collective-permute-done.3.refs_1_, bf16[768,512]{1,0:T(8,128)(2,1)} %collective-permute-done.4.refs_2_, ...), custom_call_target="tpu_custom_call" | custom-call | flops 1610612736 | bytes 5242880 | tf_op jit(solution)/shard_map/pallas_call | solution.py:270
  49.0 0.9 copy-done.9
  50.0 1.9 %shard_map.55.refs_4_ = bf16[4,192,512]{2,1,0:T(8,128)(2,1)} custom-call(s32[1]{0:T(128)} %bitcast.8.info, s32[192]{0:T(256)S(1)} %copy-done.4, bf16[768,512]{1,0:T(8,128)(2,1)S(1)} %copy-done, bf16[384,512]{1,0:T(8,128)(2,1)S(1)} %collective-permute-done.1.after_ref.refs_0_), custom_call_target="tpu_custom_call" | custom-call | bytes 1572864 | tf_op jit(solution)/shard_map/pallas_call | solution.py:435
  51.9 3.2 %shard_map.57 = (bf16[384,512]{1,0:T(8,128)(2,1)S(1)}, bf16[384,512]{1,0:T(8,128)(2,1)S(1)}) custom-call(s32[4]{0:T(128)S(1)} %add_add_fusion.1.info, s32[3]{0:T(128)S(1)} %copy-done.6, bf16[384,512]{1,0:T(8,128)(2,1)} %collective-permute-done.refs_0_, bf16[384,512]{1,0:T(8,128)(2,1)} %collective-permute-done.6.refs_1_, ...), custom_call_target="tpu_custom_call" | custom-call | flops 805306368 | bytes 3670016 | tf_op jit(solution)/shard_map/pallas_call | solution.py:270
  55.1 0.6 collective-permute-start.13
  55.7 3.3 %shard_map.58 = (bf16[384,512]{1,0:T(8,128)(2,1)S(1)}, bf16[384,512]{1,0:T(8,128)(2,1)S(1)}) custom-call(s32[4]{0:T(128)S(1)} %add_add_fusion.1.info, s32[3]{0:T(128)S(1)} %copy-done.6, bf16[384,512]{1,0:T(8,128)(2,1)S(1)} %collective-permute-done.1.after_ref.refs_0_, bf16[384,512]{1,0:T(8,128)(2,1)} %collective-permute-done.9.refs_1_, ...), custom_call_target="tpu_custom_call" | custom-call | flops 805306368 | bytes 3670016 | tf_op jit(solution)/shard_map/pallas_call | solution.py:270
  59.1 0.8 copy-done.8
  59.9 5.8 %all-to-all-start = ((bf16[4,192,512]{2,1,0:T(8,128)(2,1)}), bf16[4,192,512]{2,1,0:T(8,128)(2,1)S(1)}, u32[]{:S(2)}, u32[]{:S(2)}) async-start(bf16[4,192,512]{2,1,0:T(8,128)(2,1)} %shard_map.55.refs_4_), calls=%async_computation | async-start | bytes 1572864 | tf_op jit(solution)/shard_map/all_to_all | solution.py:519
  65.9 0.6 stack.102.info
  67.6 17.7 %shard_map.59 = (f32[3072,128]{1,0:T(8,128)}, bf16[3072,128]{1,0:T(8,128)(2,1)}, f32[2,3072]{1,0:T(2,128)}) custom-call(s32[7]{0:T(128)} %stack.102.info, s32[192]{0:T(256)} %here_targets.1, s32[3]{0:T(128)} %here_lengths.1, s32[195]{0:T(256)} %copy-done.11, bf16[768,512]{1,0:T(8,128)(2,1)} %copy-done.9, bf16[384,512]{1,0:T(8,128)(2,1)} %copy-done.7, ...), custom_call_target="tpu_custom_call" | custom-call | flops 2415919104 | bytes 5505024 | tf_op jit(solution)/shard_map/pallas_call | solution.py:370
  85.5 1.2 collective-permute-done.15
  86.7 0.8 add.89.refs_0_
  87.5 0.6 collective-permute-start.16
  88.5 2.6 %collective-permute-start.18 = (f32[2,3072]{1,0:T(2,128)S(1)}, f32[2,3072]{1,0:T(2,128)S(1)}, u32[]{:S(2)}, u32[]{:S(2)}) collective-permute-start(f32[2,3072]{1,0:T(2,128)S(1)} %add.89.refs_0_), channel_id=1, source_target_pairs={{0,12},{1,13},{4,8},{5,9},{8,4},{9,5},{12,0},{13,1},{16,28},{17,29... | collective-permute-start | bytes 73736 | tf_op jit(solution)/shard_map/ppermute | solution.py:175
  91.4 0.7 collective-permute-done.17.refs_2_
  92.1 1.1 collective-permute-done.18.refs_3_
  93.2 1.4 %copy-done.1 = f32[3072,128]{1,0:T(8,128)S(1)} copy-done((f32[3072,128]{1,0:T(8,128)S(1)}, f32[3072,128]{1,0:T(8,128)}, u32[]{:S(2)}) %copy-start.1) | copy-done | bytes 1572888
  94.6 1.1 copy-done.3
  95.7 1.7 %shard_map.60 = (bf16[768,128]{1,0:T(8,128)(2,1)S(1)}, bf16[768,128]{1,0:T(8,128)(2,1)S(1)}, bf16[768,128]{1,0:T(8,128)(2,1)S(1)}, bf16[768,128]{1,0:T(8,128)(2,1)S(1)}) custom-call(s32[1]{0:T(128)} %bitcast.9.info, f32[3072,128]{1,0:T(8,128)S(1)} %copy-done.1, bf16[3072,128]{1,0:T(8,128)(2,1)S(1)} %copy-done.3, f32[2,3072]{1,0:T(2,128)S(1)} %add.89.refs_0_, ...), custom_call_target="tpu_custom_call" | custom-call | flops 3145728 | bytes 3145728 | tf_op jit(solution)/shard_map/pallas_call | solution.py:409
  97.5 4.5 %collective-permute-start.19 = (bf16[768,128]{1,0:T(8,128)(2,1)S(1)}, bf16[768,128]{1,0:T(8,128)(2,1)S(1)}, u32[]{:S(2)}, u32[]{:S(2)}) collective-permute-start(bf16[768,128]{1,0:T(8,128)(2,1)S(1)} %get-tuple-element.29), channel_id=1, source_target_pairs={{0,0},{1,8},{4,4},{5,12},{8,16},{9,24},{12,20},{13,28},{16,1},{17,... | collective-permute-start | bytes 589832 | tf_op jit(solution)/shard_map/ppermute | solution.py:175
  101.9 1.9 %collective-permute-start.21 = (bf16[768,128]{1,0:T(8,128)(2,1)S(1)}, bf16[768,128]{1,0:T(8,128)(2,1)S(1)}, u32[]{:S(2)}, u32[]{:S(2)}) collective-permute-start(bf16[768,128]{1,0:T(8,128)(2,1)S(1)} %get-tuple-element.30), channel_id=1, source_target_pairs={{0,8},{1,16},{4,12},{5,20},{8,24},{9,0},{12,28},{13,4},{16,9},{17,... | collective-permute-start | bytes 589832 | tf_op jit(solution)/shard_map/ppermute | solution.py:175
  103.9 2.1 %collective-permute-start.23 = (bf16[768,128]{1,0:T(8,128)(2,1)S(1)}, bf16[768,128]{1,0:T(8,128)(2,1)S(1)}, u32[]{:S(2)}, u32[]{:S(2)}) collective-permute-start(bf16[768,128]{1,0:T(8,128)(2,1)S(1)} %get-tuple-element.31), channel_id=1, source_target_pairs={{0,16},{1,24},{4,20},{5,28},{8,0},{9,8},{12,4},{13,12},{16,17},{17... | collective-permute-start | bytes 589832 | tf_op jit(solution)/shard_map/ppermute | solution.py:175
  105.9 0.7 collective-permute-start.25
  106.6 2.8 %collective-permute-done.19.refs_1_ = bf16[768,128]{1,0:T(8,128)(2,1)S(1)} collective-permute-done((bf16[768,128]{1,0:T(8,128)(2,1)S(1)}, bf16[768,128]{1,0:T(8,128)(2,1)S(1)}, u32[]{:S(2)}, u32[]{:S(2)}) %collective-permute-start.19) | collective-permute-done | bytes 196640 | tf_op jit(solution)/shard_map/ppermute | solution.py:175
  109.4 1.5 %collective-permute-start.20 = (bf16[768,128]{1,0:T(8,128)(2,1)S(1)}, bf16[768,128]{1,0:T(8,128)(2,1)S(1)}, u32[]{:S(2)}, u32[]{:S(2)}) collective-permute-start(bf16[768,128]{1,0:T(8,128)(2,1)S(1)} %collective-permute-done.19.refs_1_), channel_id=1, source_target_pairs={{0,4},{1,5},{4,0},{5,1},{8,12},{9,13},{12,8},{13,9},{16,20},{17,21... | collective-permute-start | bytes 589832 | tf_op jit(solution)/shard_map/ppermute | solution.py:175
  110.9 8.4 %collective-permute-done.21.refs_3_ = bf16[768,128]{1,0:T(8,128)(2,1)S(1)} collective-permute-done((bf16[768,128]{1,0:T(8,128)(2,1)S(1)}, bf16[768,128]{1,0:T(8,128)(2,1)S(1)}, u32[]{:S(2)}, u32[]{:S(2)}) %collective-permute-start.21) | collective-permute-done | bytes 196640 | tf_op jit(solution)/shard_map/ppermute | solution.py:175
  119.3 1.5 %collective-permute-start.22 = (bf16[768,128]{1,0:T(8,128)(2,1)S(1)}, bf16[768,128]{1,0:T(8,128)(2,1)S(1)}, u32[]{:S(2)}, u32[]{:S(2)}) collective-permute-start(bf16[768,128]{1,0:T(8,128)(2,1)S(1)} %collective-permute-done.21.refs_3_), channel_id=1, source_target_pairs={{0,4},{1,5},{4,0},{5,1},{8,12},{9,13},{12,8},{13,9},{16,20},{17,21... | collective-permute-start | bytes 589832 | tf_op jit(solution)/shard_map/ppermute | solution.py:175
  120.8 0.5 collective-permute-start.24
  121.3 1.5 %collective-permute-start.26 = (bf16[768,128]{1,0:T(8,128)(2,1)S(1)}, bf16[768,128]{1,0:T(8,128)(2,1)S(1)}, u32[]{:S(2)}, u32[]{:S(2)}) collective-permute-start(bf16[768,128]{1,0:T(8,128)(2,1)S(1)} %collective-permute-done.25.refs_7_), channel_id=1, source_target_pairs={{0,4},{1,5},{4,0},{5,1},{8,12},{9,13},{12,8},{13,9},{16,20},{17,21... | collective-permute-start | bytes 589832 | tf_op jit(solution)/shard_map/ppermute | solution.py:175
  123.3 3.8 %collective-permute-done.22.refs_4_ = bf16[768,128]{1,0:T(8,128)(2,1)S(1)} collective-permute-done((bf16[768,128]{1,0:T(8,128)(2,1)S(1)}, bf16[768,128]{1,0:T(8,128)(2,1)S(1)}, u32[]{:S(2)}, u32[]{:S(2)}) %collective-permute-start.22) | collective-permute-done | bytes 196640 | tf_op jit(solution)/shard_map/ppermute | solution.py:175
  127.1 4.2 %collective-permute-done.24.refs_6_ = bf16[768,128]{1,0:T(8,128)(2,1)S(1)} collective-permute-done((bf16[768,128]{1,0:T(8,128)(2,1)S(1)}, bf16[768,128]{1,0:T(8,128)(2,1)S(1)}, u32[]{:S(2)}, u32[]{:S(2)}) %collective-permute-start.24) | collective-permute-done | bytes 196640 | tf_op jit(solution)/shard_map/ppermute | solution.py:175
  131.3 2.6 %collective-permute-done.26.refs_8_ = bf16[768,128]{1,0:T(8,128)(2,1)S(1)} collective-permute-done((bf16[768,128]{1,0:T(8,128)(2,1)S(1)}, bf16[768,128]{1,0:T(8,128)(2,1)S(1)}, u32[]{:S(2)}, u32[]{:S(2)}) %collective-permute-start.26) | collective-permute-done | bytes 196640 | tf_op jit(solution)/shard_map/ppermute | solution.py:175
  133.9 2.6 %shard_map.61 = bf16[768,512]{1,0:T(8,128)(2,1)} custom-call(s32[8]{0:T(128)S(1)} %stack.92.info, s32[4]{0:T(128)S(1)} %fusion.2.quarter, bf16[1024,512]{1,0:T(8,128)(2,1)S(1)} %copy-done.2, bf16[4,192,512]{2,1,0:T(8,128)(2,1)S(1)} %all-to-all-done.refs_0_, bf16[768,128]{1,0:T(8,128)(2,1)S(1)} %collective-permute-done.19.refs_1_, ...), custom_call_target="tpu_custom_call" | custom-call | flops 805306368 | bytes 8388608 | tf_op jit(solution)/shard_map/pallas_call | solution.py:471
  (53 shorter events, 3.0 us)
Async XLA Ops:
  0.0 18.4 %collective-permute-start.4 = (bf16[768,512]{1,0:T(8,128)(2,1)}, bf16[768,512]{1,0:T(8,128)(2,1)}, u32[]{:S(2)}, u32[]{:S(2)}) collective-permute-start(bf16[768,512]{1,0:T(8,128)(2,1)} %refs_0_.1), channel_id=1, source_target_pairs={{0,9},{4,13},{8,1},{12,5},{17,24},{21,28},{25,16},{29,20},{2,11},{... | collective-permute-start | bytes 2359304 | tf_op jit(solution)/shard_map/ppermute | solution.py:175
  3.3 13.8 %collective-permute-start = (bf16[384,512]{1,0:T(8,128)(2,1)S(1)}, bf16[384,512]{1,0:T(8,128)(2,1)}, u32[]{:S(2)}, u32[]{:S(2)}) collective-permute-start(bf16[384,512]{1,0:T(8,128)(2,1)S(1)} %get-tuple-element.33), channel_id=1, source_target_pairs={{1,16},{5,20},{9,17},{13,21},{16,8},{20,12},{24,9},{28,13},{3,18},... | collective-permute-start | bytes 1179656 | tf_op jit(solution)/shard_map/ppermute | solution.py:175
  4.6 35.4 %collective-permute-start.3 = (bf16[768,512]{1,0:T(8,128)(2,1)}, bf16[768,512]{1,0:T(8,128)(2,1)}, u32[]{:S(2)}, u32[]{:S(2)}) collective-permute-start(bf16[768,512]{1,0:T(8,128)(2,1)} %refs_0_.1), channel_id=1, source_target_pairs={{0,4},{4,0},{8,12},{12,8},{17,21},{21,17},{25,29},{29,25},{2,6},{6... | collective-permute-start | bytes 2359304 | tf_op jit(solution)/shard_map/ppermute | solution.py:175
  17.1 13.9 %collective-permute-start.1 = (bf16[384,512]{1,0:T(8,128)(2,1)S(1)}, bf16[384,512]{1,0:T(8,128)(2,1)S(1)}, u32[]{:S(2)}, u32[]{:S(2)}) collective-permute-start(bf16[384,512]{1,0:T(8,128)(2,1)S(1)} %get-tuple-element.19), channel_id=1, source_target_pairs={{1,16},{5,20},{9,17},{13,21},{16,8},{20,12},{24,9},{28,13},{3,18},... | collective-permute-start | bytes 1179656 | tf_op jit(solution)/shard_map/ppermute | solution.py:175
  18.4 25.3 %collective-permute-start.5 = (bf16[768,512]{1,0:T(8,128)(2,1)}, bf16[768,512]{1,0:T(8,128)(2,1)}, u32[]{:S(2)}, u32[]{:S(2)}) collective-permute-start(bf16[768,512]{1,0:T(8,128)(2,1)} %collective-permute-done.4.refs_2_), channel_id=1, source_target_pairs={{1,5},{5,1},{9,13},{13,9},{16,20},{20,16},{24,28},{28,24},{3,7},{7... | collective-permute-start | bytes 2359304 | tf_op jit(solution)/shard_map/ppermute | solution.py:175
  20.0 18.6 %collective-permute-start.7 = (bf16[384,512]{1,0:T(8,128)(2,1)}, bf16[384,512]{1,0:T(8,128)(2,1)}, u32[]{:S(2)}, u32[]{:S(2)}) collective-permute-start(bf16[384,512]{1,0:T(8,128)(2,1)} %collective-permute-done.refs_0_), channel_id=1, source_target_pairs={{8,0},{9,1},{12,4},{13,5},{16,24},{17,25},{20,28},{21,29},{10,2},{... | collective-permute-start | bytes 1179656 | tf_op jit(solution)/shard_map/ppermute | solution.py:175
  31.0 11.2 %collective-permute-start.10 = (bf16[384,512]{1,0:T(8,128)(2,1)S(1)}, bf16[384,512]{1,0:T(8,128)(2,1)}, u32[]{:S(2)}, u32[]{:S(2)}) collective-permute-start(bf16[384,512]{1,0:T(8,128)(2,1)S(1)} %collective-permute-done.1.after_ref.refs_0_), channel_id=1, source_target_pairs={{8,0},{9,1},{12,4},{13,5},{16,24},{17,25},{20,28},{21,29},{10,2},{... | collective-permute-start | bytes 1179656 | tf_op jit(solution)/shard_map/ppermute | solution.py:175
  33.1 10.6 %copy-start = (bf16[768,512]{1,0:T(8,128)(2,1)S(1)}, bf16[768,512]{1,0:T(8,128)(2,1)}, u32[]{:S(2)}) copy-start(bf16[768,512]{1,0:T(8,128)(2,1)} %refs_0_.1) | copy-start | bytes 2359300
  33.1 10.6 %copy-start.6 = (s32[3]{0:T(128)S(1)}, s32[3]{0:T(128)}, u32[]{:S(2)}) copy-start(s32[3]{0:T(128)} %here_lengths.1) | copy-start | bytes 40
  34.9 15.1 %copy-start.4 = (s32[192]{0:T(256)S(1)}, s32[192]{0:T(256)}, u32[]{:S(2)}) copy-start(s32[192]{0:T(256)} %here_targets.1) | copy-start | bytes 2308
  34.9 17.0 %collective-permute-start.6 = (bf16[384,512]{1,0:T(8,128)(2,1)}, bf16[384,512]{1,0:T(8,128)(2,1)}, u32[]{:S(2)}, u32[]{:S(2)}) collective-permute-start(bf16[384,512]{1,0:T(8,128)(2,1)} %collective-permute-done.refs_0_), channel_id=1, source_target_pairs={{8,12},{9,13},{12,8},{13,9},{16,20},{17,21},{20,16},{21,17},{10,14... | collective-permute-start | bytes 1179656 | tf_op jit(solution)/shard_map/ppermute | solution.py:175
  38.6 13.4 %collective-permute-start.8 = (bf16[384,512]{1,0:T(8,128)(2,1)}, bf16[384,512]{1,0:T(8,128)(2,1)}, u32[]{:S(2)}, u32[]{:S(2)}) collective-permute-start(bf16[384,512]{1,0:T(8,128)(2,1)} %collective-permute-done.7.refs_2_), channel_id=1, source_target_pairs={{0,4},{1,5},{4,0},{5,1},{24,28},{25,29},{28,24},{29,25},{2,6},{3,7... | collective-permute-start | bytes 1179656 | tf_op jit(solution)/shard_map/ppermute | solution.py:175
  40.0 15.7 %collective-permute-start.9 = (bf16[384,512]{1,0:T(8,128)(2,1)S(1)}, bf16[384,512]{1,0:T(8,128)(2,1)}, u32[]{:S(2)}, u32[]{:S(2)}) collective-permute-start(bf16[384,512]{1,0:T(8,128)(2,1)S(1)} %collective-permute-done.1.after_ref.refs_0_), channel_id=1, source_target_pairs={{8,12},{9,13},{12,8},{13,9},{16,20},{17,21},{20,16},{21,17},{10,14... | collective-permute-start | bytes 1179656 | tf_op jit(solution)/shard_map/ppermute | solution.py:175
  42.2 13.5 %collective-permute-start.11 = (bf16[384,512]{1,0:T(8,128)(2,1)}, bf16[384,512]{1,0:T(8,128)(2,1)}, u32[]{:S(2)}, u32[]{:S(2)}) collective-permute-start(bf16[384,512]{1,0:T(8,128)(2,1)} %collective-permute-done.10.refs_2_), channel_id=1, source_target_pairs={{0,4},{1,5},{4,0},{5,1},{24,28},{25,29},{28,24},{29,25},{2,6},{3,7... | collective-permute-start | bytes 1179656 | tf_op jit(solution)/shard_map/ppermute | solution.py:175
  49.0 0.9 copy-start.9
  49.9 16.9 %collective-permute-start.12 = (bf16[768,512]{1,0:T(8,128)(2,1)}, bf16[768,512]{1,0:T(8,128)(2,1)}, u32[]{:S(2)}, u32[]{:S(2)}) collective-permute-start(bf16[768,512]{1,0:T(8,128)(2,1)} %get-tuple-element.23), channel_id=1, source_target_pairs={{0,1},{1,0},{4,5},{5,4},{8,9},{9,8},{12,13},{13,12},{16,17},{17,16... | collective-permute-start | bytes 2359304 | tf_op jit(solution)/shard_map/ppermute | solution.py:175
  55.1 3.9 %copy-start.7 = (bf16[384,512]{1,0:T(8,128)(2,1)}, bf16[384,512]{1,0:T(8,128)(2,1)S(1)}, u32[]{:S(2)}) copy-start(bf16[384,512]{1,0:T(8,128)(2,1)S(1)} %get-tuple-element.21.refs_1_) | copy-start | bytes 1179652
  55.1 11.7 %collective-permute-start.13 = (bf16[384,512]{1,0:T(8,128)(2,1)S(1)}, bf16[384,512]{1,0:T(8,128)(2,1)}, u32[]{:S(2)}, u32[]{:S(2)}) collective-permute-start(bf16[384,512]{1,0:T(8,128)(2,1)S(1)} %get-tuple-element.24), channel_id=1, source_target_pairs={{0,1},{1,0},{4,5},{5,4},{8,9},{9,8},{12,13},{13,12},{16,17},{17,16... | collective-permute-start | bytes 1179656 | tf_op jit(solution)/shard_map/ppermute | solution.py:175
  59.1 0.8 copy-start.8
  59.8 7.0 %collective-permute-start.14 = (bf16[384,512]{1,0:T(8,128)(2,1)S(1)}, bf16[384,512]{1,0:T(8,128)(2,1)S(1)}, u32[]{:S(2)}, u32[]{:S(2)}) collective-permute-start(bf16[384,512]{1,0:T(8,128)(2,1)S(1)} %get-tuple-element.25), channel_id=1, source_target_pairs={{0,1},{1,0},{4,5},{5,4},{8,9},{9,8},{12,13},{13,12},{16,17},{17,16... | collective-permute-start | bytes 1179656 | tf_op jit(solution)/shard_map/ppermute | solution.py:175
  59.9 63.4 %all-to-all-start = ((bf16[4,192,512]{2,1,0:T(8,128)(2,1)}), bf16[4,192,512]{2,1,0:T(8,128)(2,1)S(1)}, u32[]{:S(2)}, u32[]{:S(2)}) async-start(bf16[4,192,512]{2,1,0:T(8,128)(2,1)} %shard_map.55.refs_4_), calls=%async_computation | async-start | bytes 1572864 | tf_op jit(solution)/shard_map/all_to_all | solution.py:519
  65.7 1.1 collective-permute-start.2
  66.8 0.5 copy-start.11
  66.8 0.8 copy-start.10
  67.6 66.3 %copy-start.2 = (bf16[1024,512]{1,0:T(8,128)(2,1)S(1)}, bf16[1024,512]{1,0:T(8,128)(2,1)}, u32[]{:S(2)}) copy-start(bf16[1024,512]{1,0:T(8,128)(2,1)} %w_ref.1) | copy-start | bytes 3145732
  85.3 21.3 %copy-start.5 = (s32[192]{0:T(256)S(1)}, s32[192]{0:T(256)}, u32[]{:S(2)}) copy-start(s32[192]{0:T(256)} %here_targets.1) | copy-start | bytes 2308
  85.3 1.4 %collective-permute-start.15 = (f32[2,3072]{1,0:T(2,128)}, f32[2,3072]{1,0:T(2,128)S(1)}, u32[]{:S(2)}, u32[]{:S(2)}) collective-permute-start(f32[2,3072]{1,0:T(2,128)} %get-tuple-element.28), channel_id=1, source_target_pairs={{0,1},{1,0},{4,5},{5,4},{8,9},{9,8},{12,13},{13,12},{16,17},{17,16... | collective-permute-start | bytes 73736 | tf_op jit(solution)/shard_map/ppermute | solution.py:175
  87.5 3.9 %collective-permute-start.16 = (f32[2,3072]{1,0:T(2,128)S(1)}, f32[2,3072]{1,0:T(2,128)S(1)}, u32[]{:S(2)}, u32[]{:S(2)}) collective-permute-start(f32[2,3072]{1,0:T(2,128)S(1)} %add.89.refs_0_), channel_id=1, source_target_pairs={{0,4},{1,5},{4,0},{5,1},{8,12},{9,13},{12,8},{13,9},{16,20},{17,21... | collective-permute-start | bytes 73736 | tf_op jit(solution)/shard_map/ppermute | solution.py:175
  88.1 4.0 %collective-permute-start.17 = (f32[2,3072]{1,0:T(2,128)S(1)}, f32[2,3072]{1,0:T(2,128)S(1)}, u32[]{:S(2)}, u32[]{:S(2)}) collective-permute-start(f32[2,3072]{1,0:T(2,128)S(1)} %add.89.refs_0_), channel_id=1, source_target_pairs={{0,8},{1,9},{4,12},{5,13},{8,0},{9,1},{12,4},{13,5},{16,24},{17,25... | collective-permute-start | bytes 73736 | tf_op jit(solution)/shard_map/ppermute | solution.py:175
  88.5 4.7 %collective-permute-start.18 = (f32[2,3072]{1,0:T(2,128)S(1)}, f32[2,3072]{1,0:T(2,128)S(1)}, u32[]{:S(2)}, u32[]{:S(2)}) collective-permute-start(f32[2,3072]{1,0:T(2,128)S(1)} %add.89.refs_0_), channel_id=1, source_target_pairs={{0,12},{1,13},{4,8},{5,9},{8,4},{9,5},{12,0},{13,1},{16,28},{17,29... | collective-permute-start | bytes 73736 | tf_op jit(solution)/shard_map/ppermute | solution.py:175
  93.2 1.4 %copy-start.1 = (f32[3072,128]{1,0:T(8,128)S(1)}, f32[3072,128]{1,0:T(8,128)}, u32[]{:S(2)}) copy-start(f32[3072,128]{1,0:T(8,128)} %get-tuple-element.26.att_ref) | copy-start | bytes 4718596
  94.6 1.1 copy-start.3
  97.5 12.0 %collective-permute-start.19 = (bf16[768,128]{1,0:T(8,128)(2,1)S(1)}, bf16[768,128]{1,0:T(8,128)(2,1)S(1)}, u32[]{:S(2)}, u32[]{:S(2)}) collective-permute-start(bf16[768,128]{1,0:T(8,128)(2,1)S(1)} %get-tuple-element.29), channel_id=1, source_target_pairs={{0,0},{1,8},{4,4},{5,12},{8,16},{9,24},{12,20},{13,28},{16,1},{17,... | collective-permute-start | bytes 589832 | tf_op jit(solution)/shard_map/ppermute | solution.py:175
  101.9 17.3 %collective-permute-start.21 = (bf16[768,128]{1,0:T(8,128)(2,1)S(1)}, bf16[768,128]{1,0:T(8,128)(2,1)S(1)}, u32[]{:S(2)}, u32[]{:S(2)}) collective-permute-start(bf16[768,128]{1,0:T(8,128)(2,1)S(1)} %get-tuple-element.30), channel_id=1, source_target_pairs={{0,8},{1,16},{4,12},{5,20},{8,24},{9,0},{12,28},{13,4},{16,9},{17,... | collective-permute-start | bytes 589832 | tf_op jit(solution)/shard_map/ppermute | solution.py:175
  103.9 16.9 %collective-permute-start.23 = (bf16[768,128]{1,0:T(8,128)(2,1)S(1)}, bf16[768,128]{1,0:T(8,128)(2,1)S(1)}, u32[]{:S(2)}, u32[]{:S(2)}) collective-permute-start(bf16[768,128]{1,0:T(8,128)(2,1)S(1)} %get-tuple-element.31), channel_id=1, source_target_pairs={{0,16},{1,24},{4,20},{5,28},{8,0},{9,8},{12,4},{13,12},{16,17},{17... | collective-permute-start | bytes 589832 | tf_op jit(solution)/shard_map/ppermute | solution.py:175
  105.9 15.4 %collective-permute-start.25 = (bf16[768,128]{1,0:T(8,128)(2,1)S(1)}, bf16[768,128]{1,0:T(8,128)(2,1)S(1)}, u32[]{:S(2)}, u32[]{:S(2)}) collective-permute-start(bf16[768,128]{1,0:T(8,128)(2,1)S(1)} %get-tuple-element.32), channel_id=1, source_target_pairs={{0,24},{1,0},{4,28},{5,4},{8,8},{9,16},{12,12},{13,20},{16,25},{17... | collective-permute-start | bytes 589832 | tf_op jit(solution)/shard_map/ppermute | solution.py:175
  109.4 13.8 %collective-permute-start.20 = (bf16[768,128]{1,0:T(8,128)(2,1)S(1)}, bf16[768,128]{1,0:T(8,128)(2,1)S(1)}, u32[]{:S(2)}, u32[]{:S(2)}) collective-permute-start(bf16[768,128]{1,0:T(8,128)(2,1)S(1)} %collective-permute-done.19.refs_1_), channel_id=1, source_target_pairs={{0,4},{1,5},{4,0},{5,1},{8,12},{9,13},{12,8},{13,9},{16,20},{17,21... | collective-permute-start | bytes 589832 | tf_op jit(solution)/shard_map/ppermute | solution.py:175
  119.3 7.8 %collective-permute-start.22 = (bf16[768,128]{1,0:T(8,128)(2,1)S(1)}, bf16[768,128]{1,0:T(8,128)(2,1)S(1)}, u32[]{:S(2)}, u32[]{:S(2)}) collective-permute-start(bf16[768,128]{1,0:T(8,128)(2,1)S(1)} %collective-permute-done.21.refs_3_), channel_id=1, source_target_pairs={{0,4},{1,5},{4,0},{5,1},{8,12},{9,13},{12,8},{13,9},{16,20},{17,21... | collective-permute-start | bytes 589832 | tf_op jit(solution)/shard_map/ppermute | solution.py:175
  120.8 10.6 %collective-permute-start.24 = (bf16[768,128]{1,0:T(8,128)(2,1)S(1)}, bf16[768,128]{1,0:T(8,128)(2,1)S(1)}, u32[]{:S(2)}, u32[]{:S(2)}) collective-permute-start(bf16[768,128]{1,0:T(8,128)(2,1)S(1)} %collective-permute-done.23.refs_5_), channel_id=1, source_target_pairs={{0,4},{1,5},{4,0},{5,1},{8,12},{9,13},{12,8},{13,9},{16,20},{17,21... | collective-permute-start | bytes 589832 | tf_op jit(solution)/shard_map/ppermute | solution.py:175
  121.3 12.6 %collective-permute-start.26 = (bf16[768,128]{1,0:T(8,128)(2,1)S(1)}, bf16[768,128]{1,0:T(8,128)(2,1)S(1)}, u32[]{:S(2)}, u32[]{:S(2)}) collective-permute-start(bf16[768,128]{1,0:T(8,128)(2,1)S(1)} %collective-permute-done.25.refs_7_), channel_id=1, source_target_pairs={{0,4},{1,5},{4,0},{5,1},{8,12},{9,13},{12,8},{13,9},{16,20},{17,21... | collective-permute-start | bytes 589832 | tf_op jit(solution)/shard_map/ppermute | solution.py:175

commit v5 on v4

--- a/solution.py
+++ b/solution.py
@@ -291,7 +291,7 @@
 
 
 def attend_kernel(info, here_targets, here_lengths, there, *refs):
-    pieces, (att_ref, u_ref, stat_ref, held) = refs[:-4], refs[-4:]
+    pieces, (out_ref, u_ref, stat_ref, held, att_ref) = refs[:-5], refs[-5:]
     own = info[len(pieces)] == 0
     blocks = here_targets.shape[0]
     seq = att_ref.shape[0]
@@ -360,7 +360,9 @@
             term(q0 + s * DSUB, TQ - s * DSUB, q0 + s * DSUB, DSUB, first[s * DSUB :], True)
         for s in range(TQ // 256):
             part = pl.ds(pl.multiple_of(q0 + s * 256, 256), 256)
-            flip = att_ref[part, :].T
+            sums = att_ref[part, :]
+            out_ref[part, :] = sums.astype(jnp.bfloat16)
+            flip = sums.T
             stat_ref[0:1, part] = jnp.sum(flip, axis=0, keepdims=True)
             stat_ref[1:2, part] = jnp.sum(flip * flip, axis=0, keepdims=True)
 def attend(info, targets, lengths, there, pieces):
@@ -369,15 +371,28 @@
     vmem = pl.BlockSpec(memory_space=pltpu.VMEM)
     return pl.pallas_call(
         attend_kernel,
-        out_shape=(jax.ShapeDtypeStruct((seq, 128), jnp.float32), jax.ShapeDtypeStruct((seq, 128), jnp.bfloat16), jax.ShapeDtypeStruct((2, seq), jnp.float32)),
+        out_shape=(jax.ShapeDtypeStruct((seq, 128), jnp.bfloat16), jax.ShapeDtypeStruct((seq, 128), jnp.bfloat16), jax.ShapeDtypeStruct((2, seq), jnp.float32)),
         in_specs=[smem] * 4 + [vmem] * len(pieces),
         out_specs=(vmem,) * 3,
-        scratch_shapes=[pltpu.VMEM((seq, 384), jnp.bfloat16)],
+        scratch_shapes=[pltpu.VMEM((seq, 384), jnp.bfloat16), pltpu.VMEM((seq, 128), jnp.float32)],
         compiler_params=pltpu.CompilerParams(vmem_limit_bytes=56 * 1024 * 1024),
         cost_estimate=pl.CostEstimate(
             flops=2 * seq * seq * 128, bytes_accessed=seq * 128 * 14, transcendentals=seq * seq
         ),
     )(info, targets, lengths, there, *pieces)
+
+
+def add_kernel(a_ref, b_ref, out_ref):
+    out_ref[...] = a_ref[...] + b_ref[...]
+
+
+def add(a, b):
+    return pl.pallas_call(
+        add_kernel,
+        out_shape=jax.ShapeDtypeStruct(a.shape, a.dtype),
+        compiler_params=pltpu.CompilerParams(vmem_limit_bytes=1024 * 1024),
+        cost_estimate=pl.CostEstimate(flops=a.size, bytes_accessed=a.size * 12, transcendentals=0),
+    )(a, b)
 
 
 def gate_kernel(info, att_ref, u_ref, *refs):
@@ -398,7 +413,7 @@
             scale = lax.rsqrt(square - mean * mean + eps_norm)
             mean = jnp.broadcast_to(mean, (128, step)).T
             scale = jnp.broadcast_to(scale, (128, step)).T
-            gated = ((att_ref[at, :] - mean) * scale) * u_ref[at, :].astype(jnp.float32)
+            gated = ((att_ref[at, :].astype(jnp.float32) - mean) * scale) * u_ref[at, :].astype(jnp.float32)
             out[pl.ds(pl.multiple_of(i * step, step), step), :] = gated.astype(jnp.bfloat16)
 
 
@@ -503,6 +518,8 @@
         if remote:
             chunk, _ = lax.optimization_barrier((chunk, remote[-1]))
         remote.append(move(chunk, to_other_team))
+    send = outgoing(jnp.stack([z]), targets_here, events, events, 4)
+    partner, send = lax.optimization_barrier((partner, send))
     x_partner = move(partner, across(lambda half, zlo, head, core: core != half))
     relayed = [move(r, inner_to_outer) for r in remote]
 
@@ -515,7 +532,6 @@
     x_inner = [move(r, across(lambda half, zlo, head, core: (zlo ^ half) == 1)) for r in remote]
     x_outer = [move(r, across(lambda half, zlo, head, core: (zlo ^ half) == 0)) for r in relayed]
     mine, got = [mine1], [move(sib1, other_core)]
-    send = outgoing(ints(z), targets_here, events, remote[-1], 4)
     residual = lax.all_to_all(send, ("half", "zlo"), split_axis=0, concat_axis=0, tiled=True)
     for i in range(parts):
         m, s = project(
@@ -544,7 +560,7 @@
         jnp.where(by_shard // blocks == z, by_shard % blocks // (blocks // 4), 0), axis=1
     )
 
-    stat = stat + move(stat, other_core)
+    stat = add(stat, move(stat, other_core))
     stats = [stat]
     for dz, dx in ((0, 1), (1, 0), (1, 1)):
         stats.append(

time: 137 us -> 136 us (level)
  local copies, waits for them, and re-layouts: 8.88 us -> 11.2 us
  waiting for transfers between devices: 43 us -> 41.1 us
  starting transfers between devices: 47.4 us -> 46 us
    unnamed x24 -> x32, local copies, waits for them, and re-layouts: 4.95 us -> 7.36 us
    ppermute x27, waiting for transfers between devices: 43 us -> 41.1 us  [move(): return lax.ppermute(value, ROUTE, route(rule))]
  transfers between devices with their start and end apart: 28 -> 28, of which waited for: 12 -> 13; matrix products, arithmetic and copies ran while one was open for 4% -> 3% of each run, Pallas kernels for 24% -> 25%
where the time goes in v5:
time: 136 us; the launch traced here: 135 us
  starting transfers between devices  46 us (34%)
  waiting for transfers between devices  41.1 us (30%)
  Pallas kernels  35.8 us (26%)
  local copies, waits for them, and re-layouts  11.2 us (8%)
    ppermute x27, starting transfers between devices, move(): return lax.ppermute(value, ROUTE, route(rule))  41.3 us
    ppermute x27, waiting for transfers between devices, move(): return lax.ppermute(value, ROUTE, route(rule))  41.1 us
    pallas_call x1, Pallas kernels, attend(): pl.pallas_call(attend_kernel, out_shape=(jax.ShapeDtypeStruct((seq, 128),...  17.7 us
    pallas_call x3, Pallas kernels, project(): pl.pallas_call(functools.partial(project_kernel, len(after)), out_shape=(...  11.9 us
    unnamed x32, local copies, waits for them, and re-layouts  7.36 us
    all_to_all x1, starting transfers between devices, team_body(): lax.all_to_all(send, ('half', 'zlo'), split_axis=0, concat_axis=0, tiled=...  4.74 us
  transfers between devices with their start and end apart: 28, of which 13 were waited for; matrix products, arithmetic and copies ran while one was open for 3% of the time, Pallas kernels for 25%

profile of v5, /device:TPU:8, one launch (start us, length us, event | category | flops | bytes accessed | tf_op | source)
XLA Modules:
  0.0 134.8 jit_solution(18434995967110808185)
XLA Ops:
  0.0 2.3 %collective-permute-start = (bf16[768,512]{1,0:T(8,128)(2,1)}, bf16[768,512]{1,0:T(8,128)(2,1)}, u32[]{:S(2)}, u32[]{:S(2)}) collective-permute-start(bf16[768,512]{1,0:T(8,128)(2,1)} %refs_0_.1), channel_id=1, source_target_pairs={{0,9},{4,13},{8,1},{12,5},{17,24},{21,28},{25,16},{29,20},{2,11},{... | collective-permute-start | bytes 2359304 | tf_op jit(solution)/shard_map/ppermute | solution.py:175
  2.3 1.2 fusion.4
  3.5 1.3 collective-permute-start.4
  4.8 3.9 %collective-permute-start.2 = (bf16[768,512]{1,0:T(8,128)(2,1)}, bf16[768,512]{1,0:T(8,128)(2,1)}, u32[]{:S(2)}, u32[]{:S(2)}) collective-permute-start(bf16[768,512]{1,0:T(8,128)(2,1)} %refs_0_.1), channel_id=1, source_target_pairs={{0,4},{4,0},{8,12},{12,8},{17,21},{21,17},{25,29},{29,25},{2,6},{6... | collective-permute-start | bytes 2359304 | tf_op jit(solution)/shard_map/ppermute | solution.py:175
  8.7 1.1 copy-done
  10.5 1.9 %shard_map.55.refs_4_ = bf16[4,192,512]{2,1,0:T(8,128)(2,1)} custom-call(s32[1]{0:T(128)} %bitcast.8.info, s32[192]{0:T(256)S(1)} %copy-done.6, bf16[768,512]{1,0:T(8,128)(2,1)S(1)} %copy-done, bf16[768,512]{1,0:T(8,128)(2,1)S(1)} %copy-done), custom_call_target="tpu_custom_call" | custom-call | bytes 1572864 | tf_op jit(solution)/shard_map/pallas_call | solution.py:450
  12.5 4.7 %collective-permute-done.4.refs_0_ = bf16[384,512]{1,0:T(8,128)(2,1)S(1)} collective-permute-done((bf16[384,512]{1,0:T(8,128)(2,1)S(1)}, bf16[384,512]{1,0:T(8,128)(2,1)S(1)}, u32[]{:S(2)}, u32[]{:S(2)}) %collective-permute-start.4) | collective-permute-done | bytes 393248 | tf_op jit(solution)/shard_map/ppermute | solution.py:175
  17.1 1.3 collective-permute-start.8
  18.4 1.5 %collective-permute-start.3 = (bf16[768,512]{1,0:T(8,128)(2,1)}, bf16[768,512]{1,0:T(8,128)(2,1)}, u32[]{:S(2)}, u32[]{:S(2)}) collective-permute-start(bf16[768,512]{1,0:T(8,128)(2,1)} %collective-permute-done.refs_2_), channel_id=1, source_target_pairs={{1,5},{5,1},{9,13},{13,9},{16,20},{20,16},{24,28},{28,24},{3,7},{7... | collective-permute-start | bytes 2359304 | tf_op jit(solution)/shard_map/ppermute | solution.py:175
  20.0 2.0 %collective-permute-start.6 = (bf16[384,512]{1,0:T(8,128)(2,1)S(1)}, bf16[384,512]{1,0:T(8,128)(2,1)}, u32[]{:S(2)}, u32[]{:S(2)}) collective-permute-start(bf16[384,512]{1,0:T(8,128)(2,1)S(1)} %collective-permute-done.4.refs_0_), channel_id=1, source_target_pairs={{8,0},{9,1},{12,4},{13,5},{16,24},{17,25},{20,28},{21,29},{10,2},{... | collective-permute-start | bytes 1179656 | tf_op jit(solution)/shard_map/ppermute | solution.py:175
  22.0 9.1 %collective-permute-done.8.refs_0_ = bf16[384,512]{1,0:T(8,128)(2,1)} collective-permute-done((bf16[384,512]{1,0:T(8,128)(2,1)S(1)}, bf16[384,512]{1,0:T(8,128)(2,1)}, u32[]{:S(2)}, u32[]{:S(2)}) %collective-permute-start.8) | collective-permute-done | bytes 393248 | tf_op jit(solution)/shard_map/ppermute | solution.py:175
  31.1 2.0 %collective-permute-start.10 = (bf16[384,512]{1,0:T(8,128)(2,1)}, bf16[384,512]{1,0:T(8,128)(2,1)}, u32[]{:S(2)}, u32[]{:S(2)}) collective-permute-start(bf16[384,512]{1,0:T(8,128)(2,1)} %collective-permute-done.8.refs_0_), channel_id=1, source_target_pairs={{8,0},{9,1},{12,4},{13,5},{16,24},{17,25},{20,28},{21,29},{10,2},{... | collective-permute-start | bytes 1179656 | tf_op jit(solution)/shard_map/ppermute | solution.py:175
  33.1 1.7 %constant_dynamic-slice_fusion.refs_4_.refs_5_ = bf16[4,1024,256]{2,1,0:T(8,128)(2,1)S(1)} fusion(bf16[4,1024,512]{2,1,0:T(8,128)(2,1)} %param.6, s32[]{:T(128)S(6)} %select_n.52), kind=kLoop, calls=%fused_computation.15 | loop fusion | bytes 4194308 | tf_op jit(solution)/shard_map/dynamic_slice | solution.py:509
  34.9 3.7 %collective-permute-start.5 = (bf16[384,512]{1,0:T(8,128)(2,1)S(1)}, bf16[384,512]{1,0:T(8,128)(2,1)}, u32[]{:S(2)}, u32[]{:S(2)}) collective-permute-start(bf16[384,512]{1,0:T(8,128)(2,1)S(1)} %collective-permute-done.4.refs_0_), channel_id=1, source_target_pairs={{8,12},{9,13},{12,8},{13,9},{16,20},{17,21},{20,16},{21,17},{10,14... | collective-permute-start | bytes 1179656 | tf_op jit(solution)/shard_map/ppermute | solution.py:175
  38.5 1.4 %collective-permute-start.7 = (bf16[384,512]{1,0:T(8,128)(2,1)}, bf16[384,512]{1,0:T(8,128)(2,1)}, u32[]{:S(2)}, u32[]{:S(2)}) collective-permute-start(bf16[384,512]{1,0:T(8,128)(2,1)} %collective-permute-done.6.refs_2_), channel_id=1, source_target_pairs={{0,4},{1,5},{4,0},{5,1},{24,28},{25,29},{28,24},{29,25},{2,6},{3,7... | collective-permute-start | bytes 1179656 | tf_op jit(solution)/shard_map/ppermute | solution.py:175
  40.1 2.2 %collective-permute-start.9 = (bf16[384,512]{1,0:T(8,128)(2,1)}, bf16[384,512]{1,0:T(8,128)(2,1)}, u32[]{:S(2)}, u32[]{:S(2)}) collective-permute-start(bf16[384,512]{1,0:T(8,128)(2,1)} %collective-permute-done.8.refs_0_), channel_id=1, source_target_pairs={{8,12},{9,13},{12,8},{13,9},{16,20},{17,21},{20,16},{21,17},{10,14... | collective-permute-start | bytes 1179656 | tf_op jit(solution)/shard_map/ppermute | solution.py:175
  42.3 1.5 %collective-permute-start.11 = (bf16[384,512]{1,0:T(8,128)(2,1)}, bf16[384,512]{1,0:T(8,128)(2,1)}, u32[]{:S(2)}, u32[]{:S(2)}) collective-permute-start(bf16[384,512]{1,0:T(8,128)(2,1)} %collective-permute-done.10.refs_2_), channel_id=1, source_target_pairs={{0,4},{1,5},{4,0},{5,1},{24,28},{25,29},{28,24},{29,25},{2,6},{3,7... | collective-permute-start | bytes 1179656 | tf_op jit(solution)/shard_map/ppermute | solution.py:175
  43.7 5.4 %shard_map.56 = (bf16[768,512]{1,0:T(8,128)(2,1)S(1)}, bf16[768,512]{1,0:T(8,128)(2,1)}) custom-call(s32[4]{0:T(128)S(1)} %add_add_fusion.info, s32[3]{0:T(128)S(1)} %copy-done.9, bf16[768,512]{1,0:T(8,128)(2,1)S(1)} %copy-done.1, bf16[768,512]{1,0:T(8,128)(2,1)} %collective-permute-done.2.refs_1_, bf16[768,512]{1,0:T(8,128)(2,1)} %collective-permute-done.refs_2_, ...), custom_call_target="tpu_custom_call" | custom-call | flops 1610612736 | bytes 5242880 | tf_op jit(solution)/shard_map/pallas_call | solution.py:270
  49.1 0.9 copy-done.12
  50.1 3.3 %shard_map.57 = (bf16[384,512]{1,0:T(8,128)(2,1)S(1)}, bf16[384,512]{1,0:T(8,128)(2,1)S(1)}) custom-call(s32[4]{0:T(128)S(1)} %add_add_fusion.1.info, s32[3]{0:T(128)S(1)} %copy-done.9, bf16[384,512]{1,0:T(8,128)(2,1)S(1)} %collective-permute-done.4.refs_0_, bf16[384,512]{1,0:T(8,128)(2,1)} %collective-permute-done.5.refs_1_, ...), custom_call_target="tpu_custom_call" | custom-call | flops 805306368 | bytes 3670016 | tf_op jit(solution)/shard_map/pallas_call | solution.py:270
  54.0 1.3 collective-permute-done.9.refs_1_
  55.3 3.2 %shard_map.58 = (bf16[384,512]{1,0:T(8,128)(2,1)S(1)}, bf16[384,512]{1,0:T(8,128)(2,1)S(1)}) custom-call(s32[4]{0:T(128)S(1)} %add_add_fusion.1.info, s32[3]{0:T(128)S(1)} %copy-done.9, bf16[384,512]{1,0:T(8,128)(2,1)} %collective-permute-done.8.refs_0_, bf16[384,512]{1,0:T(8,128)(2,1)} %collective-permute-done.9.refs_1_, ...), custom_call_target="tpu_custom_call" | custom-call | flops 805306368 | bytes 3670016 | tf_op jit(solution)/shard_map/pallas_call | solution.py:270
  58.5 0.7 copy-done.11
  59.3 4.7 %all-to-all-start = ((bf16[4,192,512]{2,1,0:T(8,128)(2,1)}), bf16[4,192,512]{2,1,0:T(8,128)(2,1)S(1)}, u32[]{:S(2)}, u32[]{:S(2)}) async-start(bf16[4,192,512]{2,1,0:T(8,128)(2,1)} %shard_map.55.refs_4_), calls=%async_computation | async-start | bytes 1572864 | tf_op jit(solution)/shard_map/all_to_all | solution.py:535
  65.3 0.8 copy-done.14
  66.2 17.7 %shard_map.59 = (bf16[3072,128]{1,0:T(8,128)(2,1)}, bf16[3072,128]{1,0:T(8,128)(2,1)}, f32[2,3072]{1,0:T(2,128)}) custom-call(s32[7]{0:T(128)} %stack.102.info, s32[192]{0:T(256)} %here_targets.1, s32[3]{0:T(128)} %here_lengths.1, s32[195]{0:T(256)} %copy-done.15, bf16[768,512]{1,0:T(8,128)(2,1)} %copy-done.12, bf16[384,512]{1,0:T(8,128)(2,1)} %copy-done.10, ...), custom_call_target="tpu_custom_call" | custom-call | flops 2415919104 | bytes 5505024 | tf_op jit(solution)/shard_map/pallas_call | solution.py:372
  84.1 1.2 collective-permute-done.15.b_ref
  85.3 0.7 copy-done.5
  86.0 0.9 collective-permute-start.16
  87.0 2.5 %collective-permute-start.18 = (f32[2,3072]{1,0:T(2,128)S(1)}, f32[2,3072]{1,0:T(2,128)S(1)}, u32[]{:S(2)}, u32[]{:S(2)}) collective-permute-start(f32[2,3072]{1,0:T(2,128)S(1)} %shard_map.60.refs_0_), channel_id=1, source_target_pairs={{0,12},{1,13},{4,8},{5,9},{8,4},{9,5},{12,0},{13,1},{16,28},{17,29... | collective-permute-start | bytes 73736 | tf_op jit(solution)/shard_map/ppermute | solution.py:175
  89.8 0.9 collective-permute-done.17.refs_2_
  90.8 0.9 collective-permute-done.18.refs_3_
  91.7 1.1 copy-done.3
  92.8 1.1 copy-done.4
  94.0 1.7 %shard_map.61 = (bf16[768,128]{1,0:T(8,128)(2,1)S(1)}, bf16[768,128]{1,0:T(8,128)(2,1)S(1)}, bf16[768,128]{1,0:T(8,128)(2,1)S(1)}, bf16[768,128]{1,0:T(8,128)(2,1)S(1)}) custom-call(s32[1]{0:T(128)} %bitcast.9.info, bf16[3072,128]{1,0:T(8,128)(2,1)S(1)} %copy-done.3, bf16[3072,128]{1,0:T(8,128)(2,1)S(1)} %copy-done.4, f32[2,3072]{1,0:T(2,128)S(1)} %shard_map.60.refs_0_, ...), custom_call_target="tpu_custom_call" | custom-call | flops 3145728 | bytes 3145728 | tf_op jit(solution)/shard_map/pallas_call | solution.py:424
  95.7 4.8 %collective-permute-start.19 = (bf16[768,128]{1,0:T(8,128)(2,1)S(1)}, bf16[768,128]{1,0:T(8,128)(2,1)S(1)}, u32[]{:S(2)}, u32[]{:S(2)}) collective-permute-start(bf16[768,128]{1,0:T(8,128)(2,1)S(1)} %get-tuple-element.33), channel_id=1, source_target_pairs={{0,0},{1,8},{4,4},{5,12},{8,16},{9,24},{12,20},{13,28},{16,1},{17,... | collective-permute-start | bytes 589832 | tf_op jit(solution)/shard_map/ppermute | solution.py:175
  100.5 1.9 %collective-permute-start.21 = (bf16[768,128]{1,0:T(8,128)(2,1)S(1)}, bf16[768,128]{1,0:T(8,128)(2,1)S(1)}, u32[]{:S(2)}, u32[]{:S(2)}) collective-permute-start(bf16[768,128]{1,0:T(8,128)(2,1)S(1)} %get-tuple-element.34), channel_id=1, source_target_pairs={{0,8},{1,16},{4,12},{5,20},{8,24},{9,0},{12,28},{13,4},{16,9},{17,... | collective-permute-start | bytes 589832 | tf_op jit(solution)/shard_map/ppermute | solution.py:175
  102.5 2.1 %collective-permute-start.23 = (bf16[768,128]{1,0:T(8,128)(2,1)S(1)}, bf16[768,128]{1,0:T(8,128)(2,1)S(1)}, u32[]{:S(2)}, u32[]{:S(2)}) collective-permute-start(bf16[768,128]{1,0:T(8,128)(2,1)S(1)} %get-tuple-element.35), channel_id=1, source_target_pairs={{0,16},{1,24},{4,20},{5,28},{8,0},{9,8},{12,4},{13,12},{16,17},{17... | collective-permute-start | bytes 589832 | tf_op jit(solution)/shard_map/ppermute | solution.py:175
  105.2 2.8 %collective-permute-done.19.refs_1_ = bf16[768,128]{1,0:T(8,128)(2,1)S(1)} collective-permute-done((bf16[768,128]{1,0:T(8,128)(2,1)S(1)}, bf16[768,128]{1,0:T(8,128)(2,1)S(1)}, u32[]{:S(2)}, u32[]{:S(2)}) %collective-permute-start.19) | collective-permute-done | bytes 196640 | tf_op jit(solution)/shard_map/ppermute | solution.py:175
  108.0 1.1 collective-permute-start.20
  109.1 8.8 %collective-permute-done.21.refs_3_ = bf16[768,128]{1,0:T(8,128)(2,1)S(1)} collective-permute-done((bf16[768,128]{1,0:T(8,128)(2,1)S(1)}, bf16[768,128]{1,0:T(8,128)(2,1)S(1)}, u32[]{:S(2)}, u32[]{:S(2)}) %collective-permute-start.21) | collective-permute-done | bytes 196640 | tf_op jit(solution)/shard_map/ppermute | solution.py:175
  117.9 1.1 collective-permute-start.22
  119.0 0.9 collective-permute-start.24
  119.9 1.1 collective-permute-start.26
  121.5 4.2 %collective-permute-done.22.refs_4_ = bf16[768,128]{1,0:T(8,128)(2,1)S(1)} collective-permute-done((bf16[768,128]{1,0:T(8,128)(2,1)S(1)}, bf16[768,128]{1,0:T(8,128)(2,1)S(1)}, u32[]{:S(2)}, u32[]{:S(2)}) %collective-permute-start.22) | collective-permute-done | bytes 196640 | tf_op jit(solution)/shard_map/ppermute | solution.py:175
  125.7 4.2 %collective-permute-done.24.refs_6_ = bf16[768,128]{1,0:T(8,128)(2,1)S(1)} collective-permute-done((bf16[768,128]{1,0:T(8,128)(2,1)S(1)}, bf16[768,128]{1,0:T(8,128)(2,1)S(1)}, u32[]{:S(2)}, u32[]{:S(2)}) %collective-permute-start.24) | collective-permute-done | bytes 196640 | tf_op jit(solution)/shard_map/ppermute | solution.py:175
  129.9 2.2 %collective-permute-done.26.refs_8_ = bf16[768,128]{1,0:T(8,128)(2,1)S(1)} collective-permute-done((bf16[768,128]{1,0:T(8,128)(2,1)S(1)}, bf16[768,128]{1,0:T(8,128)(2,1)S(1)}, u32[]{:S(2)}, u32[]{:S(2)}) %collective-permute-start.26) | collective-permute-done | bytes 196640 | tf_op jit(solution)/shard_map/ppermute | solution.py:175
  132.2 2.6 %shard_map.62 = bf16[768,512]{1,0:T(8,128)(2,1)} custom-call(s32[8]{0:T(128)S(1)} %stack.92.info, s32[4]{0:T(128)S(1)} %fusion.2.quarter, bf16[1024,512]{1,0:T(8,128)(2,1)S(1)} %copy-done.2, bf16[4,192,512]{2,1,0:T(8,128)(2,1)S(1)} %all-to-all-done.refs_0_, bf16[768,128]{1,0:T(8,128)(2,1)S(1)} %collective-permute-done.19.refs_1_, ...), custom_call_target="tpu_custom_call" | custom-call | flops 805306368 | bytes 8388608 | tf_op jit(solution)/shard_map/pallas_call | solution.py:486
  (61 shorter events, 4.5 us)
Async XLA Ops:
  0.0 43.7 %copy-start.1 = (bf16[768,512]{1,0:T(8,128)(2,1)S(1)}, bf16[768,512]{1,0:T(8,128)(2,1)}, u32[]{:S(2)}) copy-start(bf16[768,512]{1,0:T(8,128)(2,1)} %refs_0_.1) | copy-start | bytes 2359300
  0.0 43.7 %copy-start.9 = (s32[3]{0:T(128)S(1)}, s32[3]{0:T(128)}, u32[]{:S(2)}) copy-start(s32[3]{0:T(128)} %here_lengths.1) | copy-start | bytes 40
  0.0 18.4 %collective-permute-start = (bf16[768,512]{1,0:T(8,128)(2,1)}, bf16[768,512]{1,0:T(8,128)(2,1)}, u32[]{:S(2)}, u32[]{:S(2)}) collective-permute-start(bf16[768,512]{1,0:T(8,128)(2,1)} %refs_0_.1), channel_id=1, source_target_pairs={{0,9},{4,13},{8,1},{12,5},{17,24},{21,28},{25,16},{29,20},{2,11},{... | collective-permute-start | bytes 2359304 | tf_op jit(solution)/shard_map/ppermute | solution.py:175
  3.5 13.6 %collective-permute-start.4 = (bf16[384,512]{1,0:T(8,128)(2,1)S(1)}, bf16[384,512]{1,0:T(8,128)(2,1)S(1)}, u32[]{:S(2)}, u32[]{:S(2)}) collective-permute-start(bf16[384,512]{1,0:T(8,128)(2,1)S(1)} %get-tuple-element.38), channel_id=1, source_target_pairs={{1,16},{5,20},{9,17},{13,21},{16,8},{20,12},{24,9},{28,13},{3,18},... | collective-permute-start | bytes 1179656 | tf_op jit(solution)/shard_map/ppermute | solution.py:175
  4.8 35.3 %collective-permute-start.2 = (bf16[768,512]{1,0:T(8,128)(2,1)}, bf16[768,512]{1,0:T(8,128)(2,1)}, u32[]{:S(2)}, u32[]{:S(2)}) collective-permute-start(bf16[768,512]{1,0:T(8,128)(2,1)} %refs_0_.1), channel_id=1, source_target_pairs={{0,4},{4,0},{8,12},{12,8},{17,21},{21,17},{25,29},{29,25},{2,6},{6... | collective-permute-start | bytes 2359304 | tf_op jit(solution)/shard_map/ppermute | solution.py:175
  8.7 1.1 copy-start
  9.8 0.7 copy-start.6
  17.1 14.0 %collective-permute-start.8 = (bf16[384,512]{1,0:T(8,128)(2,1)S(1)}, bf16[384,512]{1,0:T(8,128)(2,1)}, u32[]{:S(2)}, u32[]{:S(2)}) collective-permute-start(bf16[384,512]{1,0:T(8,128)(2,1)S(1)} %get-tuple-element.25), channel_id=1, source_target_pairs={{1,16},{5,20},{9,17},{13,21},{16,8},{20,12},{24,9},{28,13},{3,18},... | collective-permute-start | bytes 1179656 | tf_op jit(solution)/shard_map/ppermute | solution.py:175
  18.4 25.3 %collective-permute-start.3 = (bf16[768,512]{1,0:T(8,128)(2,1)}, bf16[768,512]{1,0:T(8,128)(2,1)}, u32[]{:S(2)}, u32[]{:S(2)}) collective-permute-start(bf16[768,512]{1,0:T(8,128)(2,1)} %collective-permute-done.refs_2_), channel_id=1, source_target_pairs={{1,5},{5,1},{9,13},{13,9},{16,20},{20,16},{24,28},{28,24},{3,7},{7... | collective-permute-start | bytes 2359304 | tf_op jit(solution)/shard_map/ppermute | solution.py:175
  20.0 18.6 %collective-permute-start.6 = (bf16[384,512]{1,0:T(8,128)(2,1)S(1)}, bf16[384,512]{1,0:T(8,128)(2,1)}, u32[]{:S(2)}, u32[]{:S(2)}) collective-permute-start(bf16[384,512]{1,0:T(8,128)(2,1)S(1)} %collective-permute-done.4.refs_0_), channel_id=1, source_target_pairs={{8,0},{9,1},{12,4},{13,5},{16,24},{17,25},{20,28},{21,29},{10,2},{... | collective-permute-start | bytes 1179656 | tf_op jit(solution)/shard_map/ppermute | solution.py:175
  31.1 11.1 %collective-permute-start.10 = (bf16[384,512]{1,0:T(8,128)(2,1)}, bf16[384,512]{1,0:T(8,128)(2,1)}, u32[]{:S(2)}, u32[]{:S(2)}) collective-permute-start(bf16[384,512]{1,0:T(8,128)(2,1)} %collective-permute-done.8.refs_0_), channel_id=1, source_target_pairs={{8,0},{9,1},{12,4},{13,5},{16,24},{17,25},{20,28},{21,29},{10,2},{... | collective-permute-start | bytes 1179656 | tf_op jit(solution)/shard_map/ppermute | solution.py:175
  34.9 15.2 %collective-permute-start.5 = (bf16[384,512]{1,0:T(8,128)(2,1)S(1)}, bf16[384,512]{1,0:T(8,128)(2,1)}, u32[]{:S(2)}, u32[]{:S(2)}) collective-permute-start(bf16[384,512]{1,0:T(8,128)(2,1)S(1)} %collective-permute-done.4.refs_0_), channel_id=1, source_target_pairs={{8,12},{9,13},{12,8},{13,9},{16,20},{17,21},{20,16},{21,17},{10,14... | collective-permute-start | bytes 1179656 | tf_op jit(solution)/shard_map/ppermute | solution.py:175
  38.5 11.5 %collective-permute-start.7 = (bf16[384,512]{1,0:T(8,128)(2,1)}, bf16[384,512]{1,0:T(8,128)(2,1)}, u32[]{:S(2)}, u32[]{:S(2)}) collective-permute-start(bf16[384,512]{1,0:T(8,128)(2,1)} %collective-permute-done.6.refs_2_), channel_id=1, source_target_pairs={{0,4},{1,5},{4,0},{5,1},{24,28},{25,29},{28,24},{29,25},{2,6},{3,7... | collective-permute-start | bytes 1179656 | tf_op jit(solution)/shard_map/ppermute | solution.py:175
  40.1 15.3 %collective-permute-start.9 = (bf16[384,512]{1,0:T(8,128)(2,1)}, bf16[384,512]{1,0:T(8,128)(2,1)}, u32[]{:S(2)}, u32[]{:S(2)}) collective-permute-start(bf16[384,512]{1,0:T(8,128)(2,1)} %collective-permute-done.8.refs_0_), channel_id=1, source_target_pairs={{8,12},{9,13},{12,8},{13,9},{16,20},{17,21},{20,16},{21,17},{10,14... | collective-permute-start | bytes 1179656 | tf_op jit(solution)/shard_map/ppermute | solution.py:175
  42.3 13.1 %collective-permute-start.11 = (bf16[384,512]{1,0:T(8,128)(2,1)}, bf16[384,512]{1,0:T(8,128)(2,1)}, u32[]{:S(2)}, u32[]{:S(2)}) collective-permute-start(bf16[384,512]{1,0:T(8,128)(2,1)} %collective-permute-done.10.refs_2_), channel_id=1, source_target_pairs={{0,4},{1,5},{4,0},{5,1},{24,28},{25,29},{28,24},{29,25},{2,6},{3,7... | collective-permute-start | bytes 1179656 | tf_op jit(solution)/shard_map/ppermute | solution.py:175
  49.1 0.9 copy-start.12
  50.0 15.3 %collective-permute-start.12 = (bf16[768,512]{1,0:T(8,128)(2,1)}, bf16[768,512]{1,0:T(8,128)(2,1)}, u32[]{:S(2)}, u32[]{:S(2)}) collective-permute-start(bf16[768,512]{1,0:T(8,128)(2,1)} %get-tuple-element.27), channel_id=1, source_target_pairs={{0,1},{1,0},{4,5},{5,4},{8,9},{9,8},{12,13},{13,12},{16,17},{17,16... | collective-permute-start | bytes 2359304 | tf_op jit(solution)/shard_map/ppermute | solution.py:175
  50.1 14.0 %copy-start.7 = (s32[192]{0:T(256)S(1)}, s32[192]{0:T(256)}, u32[]{:S(2)}) copy-start(s32[192]{0:T(256)} %here_targets.1) | copy-start | bytes 2308
  53.4 5.1 %copy-start.10 = (bf16[384,512]{1,0:T(8,128)(2,1)}, bf16[384,512]{1,0:T(8,128)(2,1)S(1)}, u32[]{:S(2)}) copy-start(bf16[384,512]{1,0:T(8,128)(2,1)S(1)} %get-tuple-element.24.refs_1_) | copy-start | bytes 1179652
  53.4 11.8 %collective-permute-start.13 = (bf16[384,512]{1,0:T(8,128)(2,1)S(1)}, bf16[384,512]{1,0:T(8,128)(2,1)S(1)}, u32[]{:S(2)}, u32[]{:S(2)}) collective-permute-start(bf16[384,512]{1,0:T(8,128)(2,1)S(1)} %get-tuple-element.28), channel_id=1, source_target_pairs={{0,1},{1,0},{4,5},{5,4},{8,9},{9,8},{12,13},{13,12},{16,17},{17,16... | collective-permute-start | bytes 1179656 | tf_op jit(solution)/shard_map/ppermute | solution.py:175
  58.5 0.8 copy-start.11
  59.3 6.0 %collective-permute-start.14 = (bf16[384,512]{1,0:T(8,128)(2,1)S(1)}, bf16[384,512]{1,0:T(8,128)(2,1)S(1)}, u32[]{:S(2)}, u32[]{:S(2)}) collective-permute-start(bf16[384,512]{1,0:T(8,128)(2,1)S(1)} %get-tuple-element.29), channel_id=1, source_target_pairs={{0,1},{1,0},{4,5},{5,4},{8,9},{9,8},{12,13},{13,12},{16,17},{17,16... | collective-permute-start | bytes 1179656 | tf_op jit(solution)/shard_map/ppermute | solution.py:175
  59.3 62.2 %all-to-all-start = ((bf16[4,192,512]{2,1,0:T(8,128)(2,1)}), bf16[4,192,512]{2,1,0:T(8,128)(2,1)S(1)}, u32[]{:S(2)}, u32[]{:S(2)}) async-start(bf16[4,192,512]{2,1,0:T(8,128)(2,1)} %shard_map.55.refs_4_), calls=%async_computation | async-start | bytes 1572864 | tf_op jit(solution)/shard_map/all_to_all | solution.py:535
  64.1 1.1 collective-permute-start.1
  65.2 0.8 copy-start.15
  65.3 0.9 copy-start.13
  65.3 0.8 copy-start.14
  66.2 39.0 %copy-start.8 = (s32[192]{0:T(256)S(1)}, s32[192]{0:T(256)}, u32[]{:S(2)}) copy-start(s32[192]{0:T(256)} %here_targets.1) | copy-start | bytes 2308
  66.2 66.0 %copy-start.2 = (bf16[1024,512]{1,0:T(8,128)(2,1)S(1)}, bf16[1024,512]{1,0:T(8,128)(2,1)}, u32[]{:S(2)}) copy-start(bf16[1024,512]{1,0:T(8,128)(2,1)} %w_ref.1) | copy-start | bytes 3145732
  83.9 1.4 %collective-permute-start.15 = (f32[2,3072]{1,0:T(2,128)}, f32[2,3072]{1,0:T(2,128)S(1)}, u32[]{:S(2)}, u32[]{:S(2)}) collective-permute-start(f32[2,3072]{1,0:T(2,128)} %get-tuple-element.32.a_ref), channel_id=1, source_target_pairs={{0,1},{1,0},{4,5},{5,4},{8,9},{9,8},{12,13},{13,12},{16,17},{17,16... | collective-permute-start | bytes 73736 | tf_op jit(solution)/shard_map/ppermute | solution.py:175
  85.3 0.7 copy-start.5
  86.0 3.8 %collective-permute-start.16 = (f32[2,3072]{1,0:T(2,128)S(1)}, f32[2,3072]{1,0:T(2,128)S(1)}, u32[]{:S(2)}, u32[]{:S(2)}) collective-permute-start(f32[2,3072]{1,0:T(2,128)S(1)} %shard_map.60.refs_0_), channel_id=1, source_target_pairs={{0,4},{1,5},{4,0},{5,1},{8,12},{9,13},{12,8},{13,9},{16,20},{17,21... | collective-permute-start | bytes 73736 | tf_op jit(solution)/shard_map/ppermute | solution.py:175
  87.0 3.8 %collective-permute-start.17 = (f32[2,3072]{1,0:T(2,128)S(1)}, f32[2,3072]{1,0:T(2,128)S(1)}, u32[]{:S(2)}, u32[]{:S(2)}) collective-permute-start(f32[2,3072]{1,0:T(2,128)S(1)} %shard_map.60.refs_0_), channel_id=1, source_target_pairs={{0,8},{1,9},{4,12},{5,13},{8,0},{9,1},{12,4},{13,5},{16,24},{17,25... | collective-permute-start | bytes 73736 | tf_op jit(solution)/shard_map/ppermute | solution.py:175
  87.0 4.7 %collective-permute-start.18 = (f32[2,3072]{1,0:T(2,128)S(1)}, f32[2,3072]{1,0:T(2,128)S(1)}, u32[]{:S(2)}, u32[]{:S(2)}) collective-permute-start(f32[2,3072]{1,0:T(2,128)S(1)} %shard_map.60.refs_0_), channel_id=1, source_target_pairs={{0,12},{1,13},{4,8},{5,9},{8,4},{9,5},{12,0},{13,1},{16,28},{17,29... | collective-permute-start | bytes 73736 | tf_op jit(solution)/shard_map/ppermute | solution.py:175
  91.7 1.1 copy-start.3
  92.8 1.1 copy-start.4
  95.7 12.3 %collective-permute-start.19 = (bf16[768,128]{1,0:T(8,128)(2,1)S(1)}, bf16[768,128]{1,0:T(8,128)(2,1)S(1)}, u32[]{:S(2)}, u32[]{:S(2)}) collective-permute-start(bf16[768,128]{1,0:T(8,128)(2,1)S(1)} %get-tuple-element.33), channel_id=1, source_target_pairs={{0,0},{1,8},{4,4},{5,12},{8,16},{9,24},{12,20},{13,28},{16,1},{17,... | collective-permute-start | bytes 589832 | tf_op jit(solution)/shard_map/ppermute | solution.py:175
  100.5 17.3 %collective-permute-start.21 = (bf16[768,128]{1,0:T(8,128)(2,1)S(1)}, bf16[768,128]{1,0:T(8,128)(2,1)S(1)}, u32[]{:S(2)}, u32[]{:S(2)}) collective-permute-start(bf16[768,128]{1,0:T(8,128)(2,1)S(1)} %get-tuple-element.34), channel_id=1, source_target_pairs={{0,8},{1,16},{4,12},{5,20},{8,24},{9,0},{12,28},{13,4},{16,9},{17,... | collective-permute-start | bytes 589832 | tf_op jit(solution)/shard_map/ppermute | solution.py:175
  102.5 16.5 %collective-permute-start.23 = (bf16[768,128]{1,0:T(8,128)(2,1)S(1)}, bf16[768,128]{1,0:T(8,128)(2,1)S(1)}, u32[]{:S(2)}, u32[]{:S(2)}) collective-permute-start(bf16[768,128]{1,0:T(8,128)(2,1)S(1)} %get-tuple-element.35), channel_id=1, source_target_pairs={{0,16},{1,24},{4,20},{5,28},{8,0},{9,8},{12,4},{13,12},{16,17},{17... | collective-permute-start | bytes 589832 | tf_op jit(solution)/shard_map/ppermute | solution.py:175
  104.5 15.4 %collective-permute-start.25 = (bf16[768,128]{1,0:T(8,128)(2,1)S(1)}, bf16[768,128]{1,0:T(8,128)(2,1)S(1)}, u32[]{:S(2)}, u32[]{:S(2)}) collective-permute-start(bf16[768,128]{1,0:T(8,128)(2,1)S(1)} %get-tuple-element.36), channel_id=1, source_target_pairs={{0,24},{1,0},{4,28},{5,4},{8,8},{9,16},{12,12},{13,20},{16,25},{17... | collective-permute-start | bytes 589832 | tf_op jit(solution)/shard_map/ppermute | solution.py:175
  108.0 13.4 %collective-permute-start.20 = (bf16[768,128]{1,0:T(8,128)(2,1)S(1)}, bf16[768,128]{1,0:T(8,128)(2,1)S(1)}, u32[]{:S(2)}, u32[]{:S(2)}) collective-permute-start(bf16[768,128]{1,0:T(8,128)(2,1)S(1)} %collective-permute-done.19.refs_1_), channel_id=1, source_target_pairs={{0,4},{1,5},{4,0},{5,1},{8,12},{9,13},{12,8},{13,9},{16,20},{17,21... | collective-permute-start | bytes 589832 | tf_op jit(solution)/shard_map/ppermute | solution.py:175
  117.9 7.8 %collective-permute-start.22 = (bf16[768,128]{1,0:T(8,128)(2,1)S(1)}, bf16[768,128]{1,0:T(8,128)(2,1)S(1)}, u32[]{:S(2)}, u32[]{:S(2)}) collective-permute-start(bf16[768,128]{1,0:T(8,128)(2,1)S(1)} %collective-permute-done.21.refs_3_), channel_id=1, source_target_pairs={{0,4},{1,5},{4,0},{5,1},{8,12},{9,13},{12,8},{13,9},{16,20},{17,21... | collective-permute-start | bytes 589832 | tf_op jit(solution)/shard_map/ppermute | solution.py:175
  119.0 11.0 %collective-permute-start.24 = (bf16[768,128]{1,0:T(8,128)(2,1)S(1)}, bf16[768,128]{1,0:T(8,128)(2,1)S(1)}, u32[]{:S(2)}, u32[]{:S(2)}) collective-permute-start(bf16[768,128]{1,0:T(8,128)(2,1)S(1)} %collective-permute-done.23.refs_5_), channel_id=1, source_target_pairs={{0,4},{1,5},{4,0},{5,1},{8,12},{9,13},{12,8},{13,9},{16,20},{17,21... | collective-permute-start | bytes 589832 | tf_op jit(solution)/shard_map/ppermute | solution.py:175
  119.9 12.3 %collective-permute-start.26 = (bf16[768,128]{1,0:T(8,128)(2,1)S(1)}, bf16[768,128]{1,0:T(8,128)(2,1)S(1)}, u32[]{:S(2)}, u32[]{:S(2)}) collective-permute-start(bf16[768,128]{1,0:T(8,128)(2,1)S(1)} %collective-permute-done.25.refs_7_), channel_id=1, source_target_pairs={{0,4},{1,5},{4,0},{5,1},{8,12},{9,13},{12,8},{13,9},{16,20},{17,21... | collective-permute-start | bytes 589832 | tf_op jit(solution)/shard_map/ppermute | solution.py:175

commit v6 on v5

--- a/solution.py
+++ b/solution.py
@@ -291,7 +291,7 @@
 
 
 def attend_kernel(info, here_targets, here_lengths, there, *refs):
-    pieces, (out_ref, u_ref, stat_ref, held, att_ref) = refs[:-5], refs[-5:]
+    pieces, (att_ref, u_ref, stat_ref, held) = refs[:-4], refs[-4:]
     own = info[len(pieces)] == 0
     blocks = here_targets.shape[0]
     seq = att_ref.shape[0]
@@ -360,9 +360,7 @@
             term(q0 + s * DSUB, TQ - s * DSUB, q0 + s * DSUB, DSUB, first[s * DSUB :], True)
         for s in range(TQ // 256):
             part = pl.ds(pl.multiple_of(q0 + s * 256, 256), 256)
-            sums = att_ref[part, :]
-            out_ref[part, :] = sums.astype(jnp.bfloat16)
-            flip = sums.T
+            flip = att_ref[part, :].T
             stat_ref[0:1, part] = jnp.sum(flip, axis=0, keepdims=True)
             stat_ref[1:2, part] = jnp.sum(flip * flip, axis=0, keepdims=True)
 def attend(info, targets, lengths, there, pieces):
@@ -371,10 +369,10 @@
     vmem = pl.BlockSpec(memory_space=pltpu.VMEM)
     return pl.pallas_call(
         attend_kernel,
-        out_shape=(jax.ShapeDtypeStruct((seq, 128), jnp.bfloat16), jax.ShapeDtypeStruct((seq, 128), jnp.bfloat16), jax.ShapeDtypeStruct((2, seq), jnp.float32)),
+        out_shape=(jax.ShapeDtypeStruct((seq, 128), jnp.float32), jax.ShapeDtypeStruct((seq, 128), jnp.bfloat16), jax.ShapeDtypeStruct((2, seq), jnp.float32)),
         in_specs=[smem] * 4 + [vmem] * len(pieces),
         out_specs=(vmem,) * 3,
-        scratch_shapes=[pltpu.VMEM((seq, 384), jnp.bfloat16), pltpu.VMEM((seq, 128), jnp.float32)],
+        scratch_shapes=[pltpu.VMEM((seq, 384), jnp.bfloat16)],
         compiler_params=pltpu.CompilerParams(vmem_limit_bytes=56 * 1024 * 1024),
         cost_estimate=pl.CostEstimate(
             flops=2 * seq * seq * 128, bytes_accessed=seq * 128 * 14, transcendentals=seq * seq
@@ -413,7 +411,7 @@
             scale = lax.rsqrt(square - mean * mean + eps_norm)
             mean = jnp.broadcast_to(mean, (128, step)).T
             scale = jnp.broadcast_to(scale, (128, step)).T
-            gated = ((att_ref[at, :].astype(jnp.float32) - mean) * scale) * u_ref[at, :].astype(jnp.float32)
+            gated = ((att_ref[at, :] - mean) * scale) * u_ref[at, :].astype(jnp.float32)
             out[pl.ds(pl.multiple_of(i * step, step), step), :] = gated.astype(jnp.bfloat16)
 
 

time: 136 us -> 136 us (level)
    unnamed x32 -> x30, local copies, waits for them, and re-layouts: 7.36 us -> 6.53 us
where the time goes in v6:
time: 136 us; the launch traced here: 135 us
  starting transfers between devices  46 us (34%)
  waiting for transfers between devices  42.2 us (31%)
  Pallas kernels  35.9 us (26%)
  local copies, waits for them, and re-layouts  10.4 us (8%)
    ppermute x27, waiting for transfers between devices, move(): return lax.ppermute(value, ROUTE, route(rule))  42.2 us
    ppermute x27, starting transfers between devices, move(): return lax.ppermute(value, ROUTE, route(rule))  41.3 us
    pallas_call x1, Pallas kernels, attend(): pl.pallas_call(attend_kernel, out_shape=(jax.ShapeDtypeStruct((seq, 128),...  17.7 us
    pallas_call x3, Pallas kernels, project(): pl.pallas_call(functools.partial(project_kernel, len(after)), out_shape=(...  11.9 us
    unnamed x30, local copies, waits for them, and re-layouts  6.53 us
    all_to_all x1, starting transfers between devices, team_body(): lax.all_to_all(send, ('half', 'zlo'), split_axis=0, concat_axis=0, tiled=...  4.73 us
  transfers between devices with their start and end apart: 28, of which 13 were waited for; matrix products, arithmetic and copies ran while one was open for 3% of the time, Pallas kernels for 25%

profile of v6, /device:TPU:8, one launch (start us, length us, event | category | flops | bytes accessed | tf_op | source)
XLA Modules:
  0.0 135.1 jit_solution(11224642786422518874)
XLA Ops:
  0.0 2.3 %collective-permute-start = (bf16[768,512]{1,0:T(8,128)(2,1)}, bf16[768,512]{1,0:T(8,128)(2,1)}, u32[]{:S(2)}, u32[]{:S(2)}) collective-permute-start(bf16[768,512]{1,0:T(8,128)(2,1)} %refs_0_.1), channel_id=1, source_target_pairs={{0,9},{4,13},{8,1},{12,5},{17,24},{21,28},{25,16},{29,20},{2,11},{... | collective-permute-start | bytes 2359304 | tf_op jit(solution)/shard_map/ppermute | solution.py:175
  2.3 1.2 fusion.4
  3.5 1.3 collective-permute-start.4
  4.8 3.9 %collective-permute-start.2 = (bf16[768,512]{1,0:T(8,128)(2,1)}, bf16[768,512]{1,0:T(8,128)(2,1)}, u32[]{:S(2)}, u32[]{:S(2)}) collective-permute-start(bf16[768,512]{1,0:T(8,128)(2,1)} %refs_0_.1), channel_id=1, source_target_pairs={{0,4},{4,0},{8,12},{12,8},{17,21},{21,17},{25,29},{29,25},{2,6},{6... | collective-permute-start | bytes 2359304 | tf_op jit(solution)/shard_map/ppermute | solution.py:175
  8.7 0.7 copy-done.5
  9.4 1.9 %shard_map.55.refs_4_ = bf16[4,192,512]{2,1,0:T(8,128)(2,1)} custom-call(s32[1]{0:T(128)} %bitcast.8.info, s32[192]{0:T(256)S(1)} %copy-done.5, bf16[768,512]{1,0:T(8,128)(2,1)S(1)} %copy-done, bf16[768,512]{1,0:T(8,128)(2,1)S(1)} %copy-done), custom_call_target="tpu_custom_call" | custom-call | bytes 1572864 | tf_op jit(solution)/shard_map/pallas_call | solution.py:448
  11.3 5.8 %collective-permute-done.4.refs_0_ = bf16[384,512]{1,0:T(8,128)(2,1)S(1)} collective-permute-done((bf16[384,512]{1,0:T(8,128)(2,1)S(1)}, bf16[384,512]{1,0:T(8,128)(2,1)S(1)}, u32[]{:S(2)}, u32[]{:S(2)}) %collective-permute-start.4) | collective-permute-done | bytes 393248 | tf_op jit(solution)/shard_map/ppermute | solution.py:175
  17.1 1.3 collective-permute-start.8
  18.4 1.6 %collective-permute-start.3 = (bf16[768,512]{1,0:T(8,128)(2,1)}, bf16[768,512]{1,0:T(8,128)(2,1)}, u32[]{:S(2)}, u32[]{:S(2)}) collective-permute-start(bf16[768,512]{1,0:T(8,128)(2,1)} %collective-permute-done.refs_2_), channel_id=1, source_target_pairs={{1,5},{5,1},{9,13},{13,9},{16,20},{20,16},{24,28},{28,24},{3,7},{7... | collective-permute-start | bytes 2359304 | tf_op jit(solution)/shard_map/ppermute | solution.py:175
  20.0 2.0 %collective-permute-start.6 = (bf16[384,512]{1,0:T(8,128)(2,1)S(1)}, bf16[384,512]{1,0:T(8,128)(2,1)}, u32[]{:S(2)}, u32[]{:S(2)}) collective-permute-start(bf16[384,512]{1,0:T(8,128)(2,1)S(1)} %collective-permute-done.4.refs_0_), channel_id=1, source_target_pairs={{8,0},{9,1},{12,4},{13,5},{16,24},{17,25},{20,28},{21,29},{10,2},{... | collective-permute-start | bytes 1179656 | tf_op jit(solution)/shard_map/ppermute | solution.py:175
  22.0 9.1 %collective-permute-done.8.refs_0_ = bf16[384,512]{1,0:T(8,128)(2,1)} collective-permute-done((bf16[384,512]{1,0:T(8,128)(2,1)S(1)}, bf16[384,512]{1,0:T(8,128)(2,1)}, u32[]{:S(2)}, u32[]{:S(2)}) %collective-permute-start.8) | collective-permute-done | bytes 393248 | tf_op jit(solution)/shard_map/ppermute | solution.py:175
  31.1 2.0 %collective-permute-start.10 = (bf16[384,512]{1,0:T(8,128)(2,1)}, bf16[384,512]{1,0:T(8,128)(2,1)}, u32[]{:S(2)}, u32[]{:S(2)}) collective-permute-start(bf16[384,512]{1,0:T(8,128)(2,1)} %collective-permute-done.8.refs_0_), channel_id=1, source_target_pairs={{8,0},{9,1},{12,4},{13,5},{16,24},{17,25},{20,28},{21,29},{10,2},{... | collective-permute-start | bytes 1179656 | tf_op jit(solution)/shard_map/ppermute | solution.py:175
  33.1 1.7 %constant_dynamic-slice_fusion.refs_4_.refs_5_ = bf16[4,1024,256]{2,1,0:T(8,128)(2,1)S(1)} fusion(bf16[4,1024,512]{2,1,0:T(8,128)(2,1)} %param.6, s32[]{:T(128)S(6)} %select_n.52), kind=kLoop, calls=%fused_computation.15 | loop fusion | bytes 4194308 | tf_op jit(solution)/shard_map/dynamic_slice | solution.py:507
  34.9 3.7 %collective-permute-start.5 = (bf16[384,512]{1,0:T(8,128)(2,1)S(1)}, bf16[384,512]{1,0:T(8,128)(2,1)}, u32[]{:S(2)}, u32[]{:S(2)}) collective-permute-start(bf16[384,512]{1,0:T(8,128)(2,1)S(1)} %collective-permute-done.4.refs_0_), channel_id=1, source_target_pairs={{8,12},{9,13},{12,8},{13,9},{16,20},{17,21},{20,16},{21,17},{10,14... | collective-permute-start | bytes 1179656 | tf_op jit(solution)/shard_map/ppermute | solution.py:175
  38.6 1.4 %collective-permute-start.7 = (bf16[384,512]{1,0:T(8,128)(2,1)}, bf16[384,512]{1,0:T(8,128)(2,1)}, u32[]{:S(2)}, u32[]{:S(2)}) collective-permute-start(bf16[384,512]{1,0:T(8,128)(2,1)} %collective-permute-done.6.refs_2_), channel_id=1, source_target_pairs={{0,4},{1,5},{4,0},{5,1},{24,28},{25,29},{28,24},{29,25},{2,6},{3,7... | collective-permute-start | bytes 1179656 | tf_op jit(solution)/shard_map/ppermute | solution.py:175
  40.1 2.2 %collective-permute-start.9 = (bf16[384,512]{1,0:T(8,128)(2,1)}, bf16[384,512]{1,0:T(8,128)(2,1)}, u32[]{:S(2)}, u32[]{:S(2)}) collective-permute-start(bf16[384,512]{1,0:T(8,128)(2,1)} %collective-permute-done.8.refs_0_), channel_id=1, source_target_pairs={{8,12},{9,13},{12,8},{13,9},{16,20},{17,21},{20,16},{21,17},{10,14... | collective-permute-start | bytes 1179656 | tf_op jit(solution)/shard_map/ppermute | solution.py:175
  42.3 1.5 %collective-permute-start.11 = (bf16[384,512]{1,0:T(8,128)(2,1)}, bf16[384,512]{1,0:T(8,128)(2,1)}, u32[]{:S(2)}, u32[]{:S(2)}) collective-permute-start(bf16[384,512]{1,0:T(8,128)(2,1)} %collective-permute-done.10.refs_2_), channel_id=1, source_target_pairs={{0,4},{1,5},{4,0},{5,1},{24,28},{25,29},{28,24},{29,25},{2,6},{3,7... | collective-permute-start | bytes 1179656 | tf_op jit(solution)/shard_map/ppermute | solution.py:175
  43.7 5.4 %shard_map.56 = (bf16[768,512]{1,0:T(8,128)(2,1)S(1)}, bf16[768,512]{1,0:T(8,128)(2,1)}) custom-call(s32[4]{0:T(128)S(1)} %add_add_fusion.info, s32[3]{0:T(128)S(1)} %copy-done.8, bf16[768,512]{1,0:T(8,128)(2,1)S(1)} %copy-done, bf16[768,512]{1,0:T(8,128)(2,1)} %collective-permute-done.2.refs_1_, bf16[768,512]{1,0:T(8,128)(2,1)} %collective-permute-done.refs_2_, ...), custom_call_target="tpu_custom_call" | custom-call | flops 1610612736 | bytes 5242880 | tf_op jit(solution)/shard_map/pallas_call | solution.py:270
  49.1 0.9 copy-done.11
  50.1 3.3 %shard_map.57 = (bf16[384,512]{1,0:T(8,128)(2,1)S(1)}, bf16[384,512]{1,0:T(8,128)(2,1)S(1)}) custom-call(s32[4]{0:T(128)S(1)} %add_add_fusion.1.info, s32[3]{0:T(128)S(1)} %copy-done.8, bf16[384,512]{1,0:T(8,128)(2,1)S(1)} %collective-permute-done.4.refs_0_, bf16[384,512]{1,0:T(8,128)(2,1)} %collective-permute-done.5.refs_1_, ...), custom_call_target="tpu_custom_call" | custom-call | flops 805306368 | bytes 3670016 | tf_op jit(solution)/shard_map/pallas_call | solution.py:270
  54.0 1.3 collective-permute-done.9.refs_1_
  55.3 3.2 %shard_map.58 = (bf16[384,512]{1,0:T(8,128)(2,1)S(1)}, bf16[384,512]{1,0:T(8,128)(2,1)S(1)}) custom-call(s32[4]{0:T(128)S(1)} %add_add_fusion.1.info, s32[3]{0:T(128)S(1)} %copy-done.8, bf16[384,512]{1,0:T(8,128)(2,1)} %collective-permute-done.8.refs_0_, bf16[384,512]{1,0:T(8,128)(2,1)} %collective-permute-done.9.refs_1_, ...), custom_call_target="tpu_custom_call" | custom-call | flops 805306368 | bytes 3670016 | tf_op jit(solution)/shard_map/pallas_call | solution.py:270
  58.5 0.8 copy-done.10
  59.3 4.7 %all-to-all-start = ((bf16[4,192,512]{2,1,0:T(8,128)(2,1)}), bf16[4,192,512]{2,1,0:T(8,128)(2,1)S(1)}, u32[]{:S(2)}, u32[]{:S(2)}) async-start(bf16[4,192,512]{2,1,0:T(8,128)(2,1)} %shard_map.55.refs_4_), calls=%async_computation | async-start | bytes 1572864 | tf_op jit(solution)/shard_map/all_to_all | solution.py:533
  65.3 0.8 copy-done.13
  66.2 17.7 %shard_map.59 = (f32[3072,128]{1,0:T(8,128)}, bf16[3072,128]{1,0:T(8,128)(2,1)}, f32[2,3072]{1,0:T(2,128)}) custom-call(s32[7]{0:T(128)} %stack.102.info, s32[192]{0:T(256)} %here_targets.1, s32[3]{0:T(128)} %here_lengths.1, s32[195]{0:T(256)} %copy-done.14, bf16[768,512]{1,0:T(8,128)(2,1)} %copy-done.11, bf16[384,512]{1,0:T(8,128)(2,1)} %copy-done.9, ...), custom_call_target="tpu_custom_call" | custom-call | flops 2415919104 | bytes 5505024 | tf_op jit(solution)/shard_map/pallas_call | solution.py:370
  84.1 1.2 collective-permute-done.15.b_ref
  85.3 0.7 copy-done.4
  86.1 1.0 collective-permute-start.16
  87.0 2.5 %collective-permute-start.18 = (f32[2,3072]{1,0:T(2,128)S(1)}, f32[2,3072]{1,0:T(2,128)S(1)}, u32[]{:S(2)}, u32[]{:S(2)}) collective-permute-start(f32[2,3072]{1,0:T(2,128)S(1)} %shard_map.60.refs_0_), channel_id=1, source_target_pairs={{0,12},{1,13},{4,8},{5,9},{8,4},{9,5},{12,0},{13,1},{16,28},{17,29... | collective-permute-start | bytes 73736 | tf_op jit(solution)/shard_map/ppermute | solution.py:175
  89.9 1.0 collective-permute-done.17.refs_2_
  90.9 0.9 collective-permute-done.18.refs_3_
  91.8 1.4 %copy-done.1 = f32[3072,128]{1,0:T(8,128)S(1)} copy-done((f32[3072,128]{1,0:T(8,128)S(1)}, f32[3072,128]{1,0:T(8,128)}, u32[]{:S(2)}) %copy-start.1) | copy-done | bytes 1572888
  93.2 1.1 copy-done.3
  94.3 1.7 %shard_map.61 = (bf16[768,128]{1,0:T(8,128)(2,1)S(1)}, bf16[768,128]{1,0:T(8,128)(2,1)S(1)}, bf16[768,128]{1,0:T(8,128)(2,1)S(1)}, bf16[768,128]{1,0:T(8,128)(2,1)S(1)}) custom-call(s32[1]{0:T(128)} %bitcast.9.info, f32[3072,128]{1,0:T(8,128)S(1)} %copy-done.1, bf16[3072,128]{1,0:T(8,128)(2,1)S(1)} %copy-done.3, f32[2,3072]{1,0:T(2,128)S(1)} %shard_map.60.refs_0_, ...), custom_call_target="tpu_custom_call" | custom-call | flops 3145728 | bytes 3145728 | tf_op jit(solution)/shard_map/pallas_call | solution.py:422
  96.0 4.8 %collective-permute-start.19 = (bf16[768,128]{1,0:T(8,128)(2,1)S(1)}, bf16[768,128]{1,0:T(8,128)(2,1)S(1)}, u32[]{:S(2)}, u32[]{:S(2)}) collective-permute-start(bf16[768,128]{1,0:T(8,128)(2,1)S(1)} %get-tuple-element.33), channel_id=1, source_target_pairs={{0,0},{1,8},{4,4},{5,12},{8,16},{9,24},{12,20},{13,28},{16,1},{17,... | collective-permute-start | bytes 589832 | tf_op jit(solution)/shard_map/ppermute | solution.py:175
  100.9 1.9 %collective-permute-start.21 = (bf16[768,128]{1,0:T(8,128)(2,1)S(1)}, bf16[768,128]{1,0:T(8,128)(2,1)S(1)}, u32[]{:S(2)}, u32[]{:S(2)}) collective-permute-start(bf16[768,128]{1,0:T(8,128)(2,1)S(1)} %get-tuple-element.34), channel_id=1, source_target_pairs={{0,8},{1,16},{4,12},{5,20},{8,24},{9,0},{12,28},{13,4},{16,9},{17,... | collective-permute-start | bytes 589832 | tf_op jit(solution)/shard_map/ppermute | solution.py:175
  102.8 2.1 %collective-permute-start.23 = (bf16[768,128]{1,0:T(8,128)(2,1)S(1)}, bf16[768,128]{1,0:T(8,128)(2,1)S(1)}, u32[]{:S(2)}, u32[]{:S(2)}) collective-permute-start(bf16[768,128]{1,0:T(8,128)(2,1)S(1)} %get-tuple-element.35), channel_id=1, source_target_pairs={{0,16},{1,24},{4,20},{5,28},{8,0},{9,8},{12,4},{13,12},{16,17},{17... | collective-permute-start | bytes 589832 | tf_op jit(solution)/shard_map/ppermute | solution.py:175
  105.6 2.8 %collective-permute-done.19.refs_1_ = bf16[768,128]{1,0:T(8,128)(2,1)S(1)} collective-permute-done((bf16[768,128]{1,0:T(8,128)(2,1)S(1)}, bf16[768,128]{1,0:T(8,128)(2,1)S(1)}, u32[]{:S(2)}, u32[]{:S(2)}) %collective-permute-start.19) | collective-permute-done | bytes 196640 | tf_op jit(solution)/shard_map/ppermute | solution.py:175
  108.4 1.1 collective-permute-start.20
  109.4 8.8 %collective-permute-done.21.refs_3_ = bf16[768,128]{1,0:T(8,128)(2,1)S(1)} collective-permute-done((bf16[768,128]{1,0:T(8,128)(2,1)S(1)}, bf16[768,128]{1,0:T(8,128)(2,1)S(1)}, u32[]{:S(2)}, u32[]{:S(2)}) %collective-permute-start.21) | collective-permute-done | bytes 196640 | tf_op jit(solution)/shard_map/ppermute | solution.py:175
  118.2 1.1 collective-permute-start.22
  119.3 1.0 collective-permute-start.24
  120.3 1.1 collective-permute-start.26
  121.8 4.2 %collective-permute-done.22.refs_4_ = bf16[768,128]{1,0:T(8,128)(2,1)S(1)} collective-permute-done((bf16[768,128]{1,0:T(8,128)(2,1)S(1)}, bf16[768,128]{1,0:T(8,128)(2,1)S(1)}, u32[]{:S(2)}, u32[]{:S(2)}) %collective-permute-start.22) | collective-permute-done | bytes 196640 | tf_op jit(solution)/shard_map/ppermute | solution.py:175
  126.1 4.2 %collective-permute-done.24.refs_6_ = bf16[768,128]{1,0:T(8,128)(2,1)S(1)} collective-permute-done((bf16[768,128]{1,0:T(8,128)(2,1)S(1)}, bf16[768,128]{1,0:T(8,128)(2,1)S(1)}, u32[]{:S(2)}, u32[]{:S(2)}) %collective-permute-start.24) | collective-permute-done | bytes 196640 | tf_op jit(solution)/shard_map/ppermute | solution.py:175
  130.3 2.2 %collective-permute-done.26.refs_8_ = bf16[768,128]{1,0:T(8,128)(2,1)S(1)} collective-permute-done((bf16[768,128]{1,0:T(8,128)(2,1)S(1)}, bf16[768,128]{1,0:T(8,128)(2,1)S(1)}, u32[]{:S(2)}, u32[]{:S(2)}) %collective-permute-start.26) | collective-permute-done | bytes 196640 | tf_op jit(solution)/shard_map/ppermute | solution.py:175
  132.5 2.6 %shard_map.62 = bf16[768,512]{1,0:T(8,128)(2,1)} custom-call(s32[8]{0:T(128)S(1)} %stack.92.info, s32[4]{0:T(128)S(1)} %fusion.2.quarter, bf16[1024,512]{1,0:T(8,128)(2,1)S(1)} %copy-done.2, bf16[4,192,512]{2,1,0:T(8,128)(2,1)S(1)} %all-to-all-done.refs_0_, bf16[768,128]{1,0:T(8,128)(2,1)S(1)} %collective-permute-done.19.refs_1_, ...), custom_call_target="tpu_custom_call" | custom-call | flops 805306368 | bytes 8388608 | tf_op jit(solution)/shard_map/pallas_call | solution.py:484
  (59 shorter events, 3.8 us)
Async XLA Ops:
  0.0 8.7 %copy-start = (bf16[768,512]{1,0:T(8,128)(2,1)S(1)}, bf16[768,512]{1,0:T(8,128)(2,1)}, u32[]{:S(2)}) copy-start(bf16[768,512]{1,0:T(8,128)(2,1)} %refs_0_.1) | copy-start | bytes 2359300
  0.0 18.4 %collective-permute-start = (bf16[768,512]{1,0:T(8,128)(2,1)}, bf16[768,512]{1,0:T(8,128)(2,1)}, u32[]{:S(2)}, u32[]{:S(2)}) collective-permute-start(bf16[768,512]{1,0:T(8,128)(2,1)} %refs_0_.1), channel_id=1, source_target_pairs={{0,9},{4,13},{8,1},{12,5},{17,24},{21,28},{25,16},{29,20},{2,11},{... | collective-permute-start | bytes 2359304 | tf_op jit(solution)/shard_map/ppermute | solution.py:175
  3.5 13.6 %collective-permute-start.4 = (bf16[384,512]{1,0:T(8,128)(2,1)S(1)}, bf16[384,512]{1,0:T(8,128)(2,1)S(1)}, u32[]{:S(2)}, u32[]{:S(2)}) collective-permute-start(bf16[384,512]{1,0:T(8,128)(2,1)S(1)} %get-tuple-element.38), channel_id=1, source_target_pairs={{1,16},{5,20},{9,17},{13,21},{16,8},{20,12},{24,9},{28,13},{3,18},... | collective-permute-start | bytes 1179656 | tf_op jit(solution)/shard_map/ppermute | solution.py:175
  4.8 35.3 %collective-permute-start.2 = (bf16[768,512]{1,0:T(8,128)(2,1)}, bf16[768,512]{1,0:T(8,128)(2,1)}, u32[]{:S(2)}, u32[]{:S(2)}) collective-permute-start(bf16[768,512]{1,0:T(8,128)(2,1)} %refs_0_.1), channel_id=1, source_target_pairs={{0,4},{4,0},{8,12},{12,8},{17,21},{21,17},{25,29},{29,25},{2,6},{6... | collective-permute-start | bytes 2359304 | tf_op jit(solution)/shard_map/ppermute | solution.py:175
  8.7 0.7 copy-start.5
  17.1 14.0 %collective-permute-start.8 = (bf16[384,512]{1,0:T(8,128)(2,1)S(1)}, bf16[384,512]{1,0:T(8,128)(2,1)}, u32[]{:S(2)}, u32[]{:S(2)}) collective-permute-start(bf16[384,512]{1,0:T(8,128)(2,1)S(1)} %get-tuple-element.25), channel_id=1, source_target_pairs={{1,16},{5,20},{9,17},{13,21},{16,8},{20,12},{24,9},{28,13},{3,18},... | collective-permute-start | bytes 1179656 | tf_op jit(solution)/shard_map/ppermute | solution.py:175
  18.4 25.3 %collective-permute-start.3 = (bf16[768,512]{1,0:T(8,128)(2,1)}, bf16[768,512]{1,0:T(8,128)(2,1)}, u32[]{:S(2)}, u32[]{:S(2)}) collective-permute-start(bf16[768,512]{1,0:T(8,128)(2,1)} %collective-permute-done.refs_2_), channel_id=1, source_target_pairs={{1,5},{5,1},{9,13},{13,9},{16,20},{20,16},{24,28},{28,24},{3,7},{7... | collective-permute-start | bytes 2359304 | tf_op jit(solution)/shard_map/ppermute | solution.py:175
  20.0 18.6 %collective-permute-start.6 = (bf16[384,512]{1,0:T(8,128)(2,1)S(1)}, bf16[384,512]{1,0:T(8,128)(2,1)}, u32[]{:S(2)}, u32[]{:S(2)}) collective-permute-start(bf16[384,512]{1,0:T(8,128)(2,1)S(1)} %collective-permute-done.4.refs_0_), channel_id=1, source_target_pairs={{8,0},{9,1},{12,4},{13,5},{16,24},{17,25},{20,28},{21,29},{10,2},{... | collective-permute-start | bytes 1179656 | tf_op jit(solution)/shard_map/ppermute | solution.py:175
  31.1 11.2 %collective-permute-start.10 = (bf16[384,512]{1,0:T(8,128)(2,1)}, bf16[384,512]{1,0:T(8,128)(2,1)}, u32[]{:S(2)}, u32[]{:S(2)}) collective-permute-start(bf16[384,512]{1,0:T(8,128)(2,1)} %collective-permute-done.8.refs_0_), channel_id=1, source_target_pairs={{8,0},{9,1},{12,4},{13,5},{16,24},{17,25},{20,28},{21,29},{10,2},{... | collective-permute-start | bytes 1179656 | tf_op jit(solution)/shard_map/ppermute | solution.py:175
  33.1 10.6 %copy-start.8 = (s32[3]{0:T(128)S(1)}, s32[3]{0:T(128)}, u32[]{:S(2)}) copy-start(s32[3]{0:T(128)} %here_lengths.1) | copy-start | bytes 40
  34.9 15.2 %collective-permute-start.5 = (bf16[384,512]{1,0:T(8,128)(2,1)S(1)}, bf16[384,512]{1,0:T(8,128)(2,1)}, u32[]{:S(2)}, u32[]{:S(2)}) collective-permute-start(bf16[384,512]{1,0:T(8,128)(2,1)S(1)} %collective-permute-done.4.refs_0_), channel_id=1, source_target_pairs={{8,12},{9,13},{12,8},{13,9},{16,20},{17,21},{20,16},{21,17},{10,14... | collective-permute-start | bytes 1179656 | tf_op jit(solution)/shard_map/ppermute | solution.py:175
  38.6 11.5 %collective-permute-start.7 = (bf16[384,512]{1,0:T(8,128)(2,1)}, bf16[384,512]{1,0:T(8,128)(2,1)}, u32[]{:S(2)}, u32[]{:S(2)}) collective-permute-start(bf16[384,512]{1,0:T(8,128)(2,1)} %collective-permute-done.6.refs_2_), channel_id=1, source_target_pairs={{0,4},{1,5},{4,0},{5,1},{24,28},{25,29},{28,24},{29,25},{2,6},{3,7... | collective-permute-start | bytes 1179656 | tf_op jit(solution)/shard_map/ppermute | solution.py:175
  40.1 15.3 %collective-permute-start.9 = (bf16[384,512]{1,0:T(8,128)(2,1)}, bf16[384,512]{1,0:T(8,128)(2,1)}, u32[]{:S(2)}, u32[]{:S(2)}) collective-permute-start(bf16[384,512]{1,0:T(8,128)(2,1)} %collective-permute-done.8.refs_0_), channel_id=1, source_target_pairs={{8,12},{9,13},{12,8},{13,9},{16,20},{17,21},{20,16},{21,17},{10,14... | collective-permute-start | bytes 1179656 | tf_op jit(solution)/shard_map/ppermute | solution.py:175
  42.3 13.1 %collective-permute-start.11 = (bf16[384,512]{1,0:T(8,128)(2,1)}, bf16[384,512]{1,0:T(8,128)(2,1)}, u32[]{:S(2)}, u32[]{:S(2)}) collective-permute-start(bf16[384,512]{1,0:T(8,128)(2,1)} %collective-permute-done.10.refs_2_), channel_id=1, source_target_pairs={{0,4},{1,5},{4,0},{5,1},{24,28},{25,29},{28,24},{29,25},{2,6},{3,7... | collective-permute-start | bytes 1179656 | tf_op jit(solution)/shard_map/ppermute | solution.py:175
  49.1 0.9 copy-start.11
  50.0 15.3 %collective-permute-start.12 = (bf16[768,512]{1,0:T(8,128)(2,1)}, bf16[768,512]{1,0:T(8,128)(2,1)}, u32[]{:S(2)}, u32[]{:S(2)}) collective-permute-start(bf16[768,512]{1,0:T(8,128)(2,1)} %get-tuple-element.27), channel_id=1, source_target_pairs={{0,1},{1,0},{4,5},{5,4},{8,9},{9,8},{12,13},{13,12},{16,17},{17,16... | collective-permute-start | bytes 2359304 | tf_op jit(solution)/shard_map/ppermute | solution.py:175
  53.4 5.1 %copy-start.9 = (bf16[384,512]{1,0:T(8,128)(2,1)}, bf16[384,512]{1,0:T(8,128)(2,1)S(1)}, u32[]{:S(2)}) copy-start(bf16[384,512]{1,0:T(8,128)(2,1)S(1)} %get-tuple-element.24.refs_1_) | copy-start | bytes 1179652
  53.4 10.6 %copy-start.6 = (s32[192]{0:T(256)S(1)}, s32[192]{0:T(256)}, u32[]{:S(2)}) copy-start(s32[192]{0:T(256)} %here_targets.1) | copy-start | bytes 2308
  53.5 11.8 %collective-permute-start.13 = (bf16[384,512]{1,0:T(8,128)(2,1)S(1)}, bf16[384,512]{1,0:T(8,128)(2,1)S(1)}, u32[]{:S(2)}, u32[]{:S(2)}) collective-permute-start(bf16[384,512]{1,0:T(8,128)(2,1)S(1)} %get-tuple-element.28), channel_id=1, source_target_pairs={{0,1},{1,0},{4,5},{5,4},{8,9},{9,8},{12,13},{13,12},{16,17},{17,16... | collective-permute-start | bytes 1179656 | tf_op jit(solution)/shard_map/ppermute | solution.py:175
  58.5 0.8 copy-start.10
  59.3 6.0 %collective-permute-start.14 = (bf16[384,512]{1,0:T(8,128)(2,1)S(1)}, bf16[384,512]{1,0:T(8,128)(2,1)S(1)}, u32[]{:S(2)}, u32[]{:S(2)}) collective-permute-start(bf16[384,512]{1,0:T(8,128)(2,1)S(1)} %get-tuple-element.29), channel_id=1, source_target_pairs={{0,1},{1,0},{4,5},{5,4},{8,9},{9,8},{12,13},{13,12},{16,17},{17,16... | collective-permute-start | bytes 1179656 | tf_op jit(solution)/shard_map/ppermute | solution.py:175
  59.3 62.5 %all-to-all-start = ((bf16[4,192,512]{2,1,0:T(8,128)(2,1)}), bf16[4,192,512]{2,1,0:T(8,128)(2,1)S(1)}, u32[]{:S(2)}, u32[]{:S(2)}) async-start(bf16[4,192,512]{2,1,0:T(8,128)(2,1)} %shard_map.55.refs_4_), calls=%async_computation | async-start | bytes 1572864 | tf_op jit(solution)/shard_map/all_to_all | solution.py:533
  64.1 1.1 collective-permute-start.1
  65.3 0.8 copy-start.14
  65.3 0.9 copy-start.12
  65.3 0.8 copy-start.13
  66.2 66.3 %copy-start.2 = (bf16[1024,512]{1,0:T(8,128)(2,1)S(1)}, bf16[1024,512]{1,0:T(8,128)(2,1)}, u32[]{:S(2)}) copy-start(bf16[1024,512]{1,0:T(8,128)(2,1)} %w_ref.1) | copy-start | bytes 3145732
  83.9 21.6 %copy-start.7 = (s32[192]{0:T(256)S(1)}, s32[192]{0:T(256)}, u32[]{:S(2)}) copy-start(s32[192]{0:T(256)} %here_targets.1) | copy-start | bytes 2308
  83.9 1.4 %collective-permute-start.15 = (f32[2,3072]{1,0:T(2,128)}, f32[2,3072]{1,0:T(2,128)S(1)}, u32[]{:S(2)}, u32[]{:S(2)}) collective-permute-start(f32[2,3072]{1,0:T(2,128)} %get-tuple-element.32.a_ref), channel_id=1, source_target_pairs={{0,1},{1,0},{4,5},{5,4},{8,9},{9,8},{12,13},{13,12},{16,17},{17,16... | collective-permute-start | bytes 73736 | tf_op jit(solution)/shard_map/ppermute | solution.py:175
  85.3 0.7 copy-start.4
  86.1 3.8 %collective-permute-start.16 = (f32[2,3072]{1,0:T(2,128)S(1)}, f32[2,3072]{1,0:T(2,128)S(1)}, u32[]{:S(2)}, u32[]{:S(2)}) collective-permute-start(f32[2,3072]{1,0:T(2,128)S(1)} %shard_map.60.refs_0_), channel_id=1, source_target_pairs={{0,4},{1,5},{4,0},{5,1},{8,12},{9,13},{12,8},{13,9},{16,20},{17,21... | collective-permute-start | bytes 73736 | tf_op jit(solution)/shard_map/ppermute | solution.py:175
  87.0 3.8 %collective-permute-start.17 = (f32[2,3072]{1,0:T(2,128)S(1)}, f32[2,3072]{1,0:T(2,128)S(1)}, u32[]{:S(2)}, u32[]{:S(2)}) collective-permute-start(f32[2,3072]{1,0:T(2,128)S(1)} %shard_map.60.refs_0_), channel_id=1, source_target_pairs={{0,8},{1,9},{4,12},{5,13},{8,0},{9,1},{12,4},{13,5},{16,24},{17,25... | collective-permute-start | bytes 73736 | tf_op jit(solution)/shard_map/ppermute | solution.py:175
  87.0 4.7 %collective-permute-start.18 = (f32[2,3072]{1,0:T(2,128)S(1)}, f32[2,3072]{1,0:T(2,128)S(1)}, u32[]{:S(2)}, u32[]{:S(2)}) collective-permute-start(f32[2,3072]{1,0:T(2,128)S(1)} %shard_map.60.refs_0_), channel_id=1, source_target_pairs={{0,12},{1,13},{4,8},{5,9},{8,4},{9,5},{12,0},{13,1},{16,28},{17,29... | collective-permute-start | bytes 73736 | tf_op jit(solution)/shard_map/ppermute | solution.py:175
  91.8 1.4 %copy-start.1 = (f32[3072,128]{1,0:T(8,128)S(1)}, f32[3072,128]{1,0:T(8,128)}, u32[]{:S(2)}) copy-start(f32[3072,128]{1,0:T(8,128)} %get-tuple-element.30.att_ref) | copy-start | bytes 4718596
  93.2 1.1 copy-start.3
  96.0 12.3 %collective-permute-start.19 = (bf16[768,128]{1,0:T(8,128)(2,1)S(1)}, bf16[768,128]{1,0:T(8,128)(2,1)S(1)}, u32[]{:S(2)}, u32[]{:S(2)}) collective-permute-start(bf16[768,128]{1,0:T(8,128)(2,1)S(1)} %get-tuple-element.33), channel_id=1, source_target_pairs={{0,0},{1,8},{4,4},{5,12},{8,16},{9,24},{12,20},{13,28},{16,1},{17,... | collective-permute-start | bytes 589832 | tf_op jit(solution)/shard_map/ppermute | solution.py:175
  100.9 17.3 %collective-permute-start.21 = (bf16[768,128]{1,0:T(8,128)(2,1)S(1)}, bf16[768,128]{1,0:T(8,128)(2,1)S(1)}, u32[]{:S(2)}, u32[]{:S(2)}) collective-permute-start(bf16[768,128]{1,0:T(8,128)(2,1)S(1)} %get-tuple-element.34), channel_id=1, source_target_pairs={{0,8},{1,16},{4,12},{5,20},{8,24},{9,0},{12,28},{13,4},{16,9},{17,... | collective-permute-start | bytes 589832 | tf_op jit(solution)/shard_map/ppermute | solution.py:175
  102.8 16.5 %collective-permute-start.23 = (bf16[768,128]{1,0:T(8,128)(2,1)S(1)}, bf16[768,128]{1,0:T(8,128)(2,1)S(1)}, u32[]{:S(2)}, u32[]{:S(2)}) collective-permute-start(bf16[768,128]{1,0:T(8,128)(2,1)S(1)} %get-tuple-element.35), channel_id=1, source_target_pairs={{0,16},{1,24},{4,20},{5,28},{8,0},{9,8},{12,4},{13,12},{16,17},{17... | collective-permute-start | bytes 589832 | tf_op jit(solution)/shard_map/ppermute | solution.py:175
  104.9 15.4 %collective-permute-start.25 = (bf16[768,128]{1,0:T(8,128)(2,1)S(1)}, bf16[768,128]{1,0:T(8,128)(2,1)S(1)}, u32[]{:S(2)}, u32[]{:S(2)}) collective-permute-start(bf16[768,128]{1,0:T(8,128)(2,1)S(1)} %get-tuple-element.36), channel_id=1, source_target_pairs={{0,24},{1,0},{4,28},{5,4},{8,8},{9,16},{12,12},{13,20},{16,25},{17... | collective-permute-start | bytes 589832 | tf_op jit(solution)/shard_map/ppermute | solution.py:175
  108.4 13.4 %collective-permute-start.20 = (bf16[768,128]{1,0:T(8,128)(2,1)S(1)}, bf16[768,128]{1,0:T(8,128)(2,1)S(1)}, u32[]{:S(2)}, u32[]{:S(2)}) collective-permute-start(bf16[768,128]{1,0:T(8,128)(2,1)S(1)} %collective-permute-done.19.refs_1_), channel_id=1, source_target_pairs={{0,4},{1,5},{4,0},{5,1},{8,12},{9,13},{12,8},{13,9},{16,20},{17,21... | collective-permute-start | bytes 589832 | tf_op jit(solution)/shard_map/ppermute | solution.py:175
  118.2 7.8 %collective-permute-start.22 = (bf16[768,128]{1,0:T(8,128)(2,1)S(1)}, bf16[768,128]{1,0:T(8,128)(2,1)S(1)}, u32[]{:S(2)}, u32[]{:S(2)}) collective-permute-start(bf16[768,128]{1,0:T(8,128)(2,1)S(1)} %collective-permute-done.21.refs_3_), channel_id=1, source_target_pairs={{0,4},{1,5},{4,0},{5,1},{8,12},{9,13},{12,8},{13,9},{16,20},{17,21... | collective-permute-start | bytes 589832 | tf_op jit(solution)/shard_map/ppermute | solution.py:175
  119.3 11.0 %collective-permute-start.24 = (bf16[768,128]{1,0:T(8,128)(2,1)S(1)}, bf16[768,128]{1,0:T(8,128)(2,1)S(1)}, u32[]{:S(2)}, u32[]{:S(2)}) collective-permute-start(bf16[768,128]{1,0:T(8,128)(2,1)S(1)} %collective-permute-done.23.refs_5_), channel_id=1, source_target_pairs={{0,4},{1,5},{4,0},{5,1},{8,12},{9,13},{12,8},{13,9},{16,20},{17,21... | collective-permute-start | bytes 589832 | tf_op jit(solution)/shard_map/ppermute | solution.py:175
  120.3 12.3 %collective-permute-start.26 = (bf16[768,128]{1,0:T(8,128)(2,1)S(1)}, bf16[768,128]{1,0:T(8,128)(2,1)S(1)}, u32[]{:S(2)}, u32[]{:S(2)}) collective-permute-start(bf16[768,128]{1,0:T(8,128)(2,1)S(1)} %collective-permute-done.25.refs_7_), channel_id=1, source_target_pairs={{0,4},{1,5},{4,0},{5,1},{8,12},{9,13},{12,8},{13,9},{16,20},{17,21... | collective-permute-start | bytes 589832 | tf_op jit(solution)/shard_map/ppermute | solution.py:175

commit v7 on v6

--- a/solution.py
+++ b/solution.py
@@ -295,8 +295,8 @@
     own = info[len(pieces)] == 0
     blocks = here_targets.shape[0]
     seq = att_ref.shape[0]
-    low = lax.broadcasted_iota(jnp.int32, (SUB, 128), 1) < DH
-    zero = jnp.zeros((SUB, 128), jnp.bfloat16)
+    low = lax.broadcasted_iota(jnp.int32, (512, 128), 1) < DH
+    zero = jnp.zeros((512, 128), jnp.bfloat16)
     for n, piece in enumerate(pieces):
         base = info[n]
 
@@ -323,16 +323,17 @@
         at = pl.ds(pl.multiple_of(q0, 256), rows)
         q = held[at, 128:256]
         total = None
-        for s in range(keys // SUB):
-            ks = pl.ds(pl.multiple_of(k0_at + s * SUB, SUB), SUB)
+        sub = min(keys, 512)
+        for s in range(keys // sub):
+            ks = pl.ds(pl.multiple_of(k0_at + s * sub, sub), sub)
             if first is not None:
-                kp = k0_at + s * SUB + lax.broadcasted_iota(jnp.int32, (1, SUB), 1)
+                kp = k0_at + s * sub + lax.broadcasted_iota(jnp.int32, (1, sub), 1)
                 ok = kp >= first
                 if causal:
                     ok = ok & (kp <= q0 + lax.broadcasted_iota(jnp.int32, (rows, 1), 0))
             v, k = held[ks, 0:128], held[ks, 256:384]
             for upper in (False, True):
-                kk, vv = (jnp.where(low, zero, m) if upper else jnp.where(low, m, zero) for m in (k, v))
+                kk, vv = (jnp.where(low[:sub], zero[:sub], m) if upper else jnp.where(low[:sub], m, zero[:sub]) for m in (k, v))
                 t = lax.dot_general(q, kk, (((1,), (1,)), ((), ())), preferred_element_type=jnp.float32)
                 w = t + t * jnp.tanh(t)
                 if first is not None:

time: 136 us -> 136 us (level)
  transfers between devices with their start and end apart: 28 -> 28, of which waited for: 13 -> 13; matrix products, arithmetic and copies ran while one was open for 3% -> 3% of each run, Pallas kernels for 25% -> 24%
where the time goes in v7:
time: 136 us; the launch traced here: 135 us
  starting transfers between devices  46 us (34%)
  waiting for transfers between devices  42.2 us (31%)
  Pallas kernels  35.6 us (26%)
  local copies, waits for them, and re-layouts  10.4 us (8%)
    ppermute x27, waiting for transfers between devices, move(): return lax.ppermute(value, ROUTE, route(rule))  42.2 us
    ppermute x27, starting transfers between devices, move(): return lax.ppermute(value, ROUTE, route(rule))  41.3 us
    pallas_call x1, Pallas kernels, attend(): pl.pallas_call(attend_kernel, out_shape=(jax.ShapeDtypeStruct((seq, 128),...  17.5 us
    pallas_call x3, Pallas kernels, project(): pl.pallas_call(functools.partial(project_kernel, len(after)), out_shape=(...  11.9 us
    unnamed x30, local copies, waits for them, and re-layouts  6.53 us
    all_to_all x1, starting transfers between devices, team_body(): lax.all_to_all(send, ('half', 'zlo'), split_axis=0, concat_axis=0, tiled=...  4.73 us
  transfers between devices with their start and end apart: 28, of which 13 were waited for; matrix products, arithmetic and copies ran while one was open for 3% of the time, Pallas kernels for 24%

profile of v7, /device:TPU:8, one launch (start us, length us, event | category | flops | bytes accessed | tf_op | source)
XLA Modules:
  0.0 134.8 jit_solution(3403683569743291826)
XLA Ops:
  0.0 2.3 %collective-permute-start = (bf16[768,512]{1,0:T(8,128)(2,1)}, bf16[768,512]{1,0:T(8,128)(2,1)}, u32[]{:S(2)}, u32[]{:S(2)}) collective-permute-start(bf16[768,512]{1,0:T(8,128)(2,1)} %refs_0_.1), channel_id=1, source_target_pairs={{0,9},{4,13},{8,1},{12,5},{17,24},{21,28},{25,16},{29,20},{2,11},{... | collective-permute-start | bytes 2359304 | tf_op jit(solution)/shard_map/ppermute | solution.py:175
  2.3 1.2 fusion.4
  3.5 1.3 collective-permute-start.4
  4.8 3.9 %collective-permute-start.2 = (bf16[768,512]{1,0:T(8,128)(2,1)}, bf16[768,512]{1,0:T(8,128)(2,1)}, u32[]{:S(2)}, u32[]{:S(2)}) collective-permute-start(bf16[768,512]{1,0:T(8,128)(2,1)} %refs_0_.1), channel_id=1, source_target_pairs={{0,4},{4,0},{8,12},{12,8},{17,21},{21,17},{25,29},{29,25},{2,6},{6... | collective-permute-start | bytes 2359304 | tf_op jit(solution)/shard_map/ppermute | solution.py:175
  8.7 0.7 copy-done.5
  9.4 1.9 %shard_map.55.refs_4_ = bf16[4,192,512]{2,1,0:T(8,128)(2,1)} custom-call(s32[1]{0:T(128)} %bitcast.8.info, s32[192]{0:T(256)S(1)} %copy-done.5, bf16[768,512]{1,0:T(8,128)(2,1)S(1)} %copy-done, bf16[768,512]{1,0:T(8,128)(2,1)S(1)} %copy-done), custom_call_target="tpu_custom_call" | custom-call | bytes 1572864 | tf_op jit(solution)/shard_map/pallas_call | solution.py:449
  11.3 5.8 %collective-permute-done.4.refs_0_ = bf16[384,512]{1,0:T(8,128)(2,1)S(1)} collective-permute-done((bf16[384,512]{1,0:T(8,128)(2,1)S(1)}, bf16[384,512]{1,0:T(8,128)(2,1)S(1)}, u32[]{:S(2)}, u32[]{:S(2)}) %collective-permute-start.4) | collective-permute-done | bytes 393248 | tf_op jit(solution)/shard_map/ppermute | solution.py:175
  17.1 1.3 collective-permute-start.8
  18.4 1.6 %collective-permute-start.3 = (bf16[768,512]{1,0:T(8,128)(2,1)}, bf16[768,512]{1,0:T(8,128)(2,1)}, u32[]{:S(2)}, u32[]{:S(2)}) collective-permute-start(bf16[768,512]{1,0:T(8,128)(2,1)} %collective-permute-done.refs_2_), channel_id=1, source_target_pairs={{1,5},{5,1},{9,13},{13,9},{16,20},{20,16},{24,28},{28,24},{3,7},{7... | collective-permute-start | bytes 2359304 | tf_op jit(solution)/shard_map/ppermute | solution.py:175
  20.0 2.0 %collective-permute-start.6 = (bf16[384,512]{1,0:T(8,128)(2,1)S(1)}, bf16[384,512]{1,0:T(8,128)(2,1)}, u32[]{:S(2)}, u32[]{:S(2)}) collective-permute-start(bf16[384,512]{1,0:T(8,128)(2,1)S(1)} %collective-permute-done.4.refs_0_), channel_id=1, source_target_pairs={{8,0},{9,1},{12,4},{13,5},{16,24},{17,25},{20,28},{21,29},{10,2},{... | collective-permute-start | bytes 1179656 | tf_op jit(solution)/shard_map/ppermute | solution.py:175
  22.0 9.1 %collective-permute-done.8.refs_0_ = bf16[384,512]{1,0:T(8,128)(2,1)} collective-permute-done((bf16[384,512]{1,0:T(8,128)(2,1)S(1)}, bf16[384,512]{1,0:T(8,128)(2,1)}, u32[]{:S(2)}, u32[]{:S(2)}) %collective-permute-start.8) | collective-permute-done | bytes 393248 | tf_op jit(solution)/shard_map/ppermute | solution.py:175
  31.1 2.0 %collective-permute-start.10 = (bf16[384,512]{1,0:T(8,128)(2,1)}, bf16[384,512]{1,0:T(8,128)(2,1)}, u32[]{:S(2)}, u32[]{:S(2)}) collective-permute-start(bf16[384,512]{1,0:T(8,128)(2,1)} %collective-permute-done.8.refs_0_), channel_id=1, source_target_pairs={{8,0},{9,1},{12,4},{13,5},{16,24},{17,25},{20,28},{21,29},{10,2},{... | collective-permute-start | bytes 1179656 | tf_op jit(solution)/shard_map/ppermute | solution.py:175
  33.1 1.7 %constant_dynamic-slice_fusion.refs_4_.refs_5_ = bf16[4,1024,256]{2,1,0:T(8,128)(2,1)S(1)} fusion(bf16[4,1024,512]{2,1,0:T(8,128)(2,1)} %param.6, s32[]{:T(128)S(6)} %select_n.52), kind=kLoop, calls=%fused_computation.15 | loop fusion | bytes 4194308 | tf_op jit(solution)/shard_map/dynamic_slice | solution.py:508
  34.9 3.7 %collective-permute-start.5 = (bf16[384,512]{1,0:T(8,128)(2,1)S(1)}, bf16[384,512]{1,0:T(8,128)(2,1)}, u32[]{:S(2)}, u32[]{:S(2)}) collective-permute-start(bf16[384,512]{1,0:T(8,128)(2,1)S(1)} %collective-permute-done.4.refs_0_), channel_id=1, source_target_pairs={{8,12},{9,13},{12,8},{13,9},{16,20},{17,21},{20,16},{21,17},{10,14... | collective-permute-start | bytes 1179656 | tf_op jit(solution)/shard_map/ppermute | solution.py:175
  38.6 1.4 %collective-permute-start.7 = (bf16[384,512]{1,0:T(8,128)(2,1)}, bf16[384,512]{1,0:T(8,128)(2,1)}, u32[]{:S(2)}, u32[]{:S(2)}) collective-permute-start(bf16[384,512]{1,0:T(8,128)(2,1)} %collective-permute-done.6.refs_2_), channel_id=1, source_target_pairs={{0,4},{1,5},{4,0},{5,1},{24,28},{25,29},{28,24},{29,25},{2,6},{3,7... | collective-permute-start | bytes 1179656 | tf_op jit(solution)/shard_map/ppermute | solution.py:175
  40.1 2.2 %collective-permute-start.9 = (bf16[384,512]{1,0:T(8,128)(2,1)}, bf16[384,512]{1,0:T(8,128)(2,1)}, u32[]{:S(2)}, u32[]{:S(2)}) collective-permute-start(bf16[384,512]{1,0:T(8,128)(2,1)} %collective-permute-done.8.refs_0_), channel_id=1, source_target_pairs={{8,12},{9,13},{12,8},{13,9},{16,20},{17,21},{20,16},{21,17},{10,14... | collective-permute-start | bytes 1179656 | tf_op jit(solution)/shard_map/ppermute | solution.py:175
  42.3 1.5 %collective-permute-start.11 = (bf16[384,512]{1,0:T(8,128)(2,1)}, bf16[384,512]{1,0:T(8,128)(2,1)}, u32[]{:S(2)}, u32[]{:S(2)}) collective-permute-start(bf16[384,512]{1,0:T(8,128)(2,1)} %collective-permute-done.10.refs_2_), channel_id=1, source_target_pairs={{0,4},{1,5},{4,0},{5,1},{24,28},{25,29},{28,24},{29,25},{2,6},{3,7... | collective-permute-start | bytes 1179656 | tf_op jit(solution)/shard_map/ppermute | solution.py:175
  43.7 5.4 %shard_map.56 = (bf16[768,512]{1,0:T(8,128)(2,1)S(1)}, bf16[768,512]{1,0:T(8,128)(2,1)}) custom-call(s32[4]{0:T(128)S(1)} %add_add_fusion.info, s32[3]{0:T(128)S(1)} %copy-done.8, bf16[768,512]{1,0:T(8,128)(2,1)S(1)} %copy-done, bf16[768,512]{1,0:T(8,128)(2,1)} %collective-permute-done.2.refs_1_, bf16[768,512]{1,0:T(8,128)(2,1)} %collective-permute-done.refs_2_, ...), custom_call_target="tpu_custom_call" | custom-call | flops 1610612736 | bytes 5242880 | tf_op jit(solution)/shard_map/pallas_call | solution.py:270
  49.1 0.9 copy-done.11
  50.1 3.3 %shard_map.57 = (bf16[384,512]{1,0:T(8,128)(2,1)S(1)}, bf16[384,512]{1,0:T(8,128)(2,1)S(1)}) custom-call(s32[4]{0:T(128)S(1)} %add_add_fusion.1.info, s32[3]{0:T(128)S(1)} %copy-done.8, bf16[384,512]{1,0:T(8,128)(2,1)S(1)} %collective-permute-done.4.refs_0_, bf16[384,512]{1,0:T(8,128)(2,1)} %collective-permute-done.5.refs_1_, ...), custom_call_target="tpu_custom_call" | custom-call | flops 805306368 | bytes 3670016 | tf_op jit(solution)/shard_map/pallas_call | solution.py:270
  54.0 1.3 collective-permute-done.9.refs_1_
  55.3 3.2 %shard_map.58 = (bf16[384,512]{1,0:T(8,128)(2,1)S(1)}, bf16[384,512]{1,0:T(8,128)(2,1)S(1)}) custom-call(s32[4]{0:T(128)S(1)} %add_add_fusion.1.info, s32[3]{0:T(128)S(1)} %copy-done.8, bf16[384,512]{1,0:T(8,128)(2,1)} %collective-permute-done.8.refs_0_, bf16[384,512]{1,0:T(8,128)(2,1)} %collective-permute-done.9.refs_1_, ...), custom_call_target="tpu_custom_call" | custom-call | flops 805306368 | bytes 3670016 | tf_op jit(solution)/shard_map/pallas_call | solution.py:270
  58.5 0.8 copy-done.10
  59.3 4.7 %all-to-all-start = ((bf16[4,192,512]{2,1,0:T(8,128)(2,1)}), bf16[4,192,512]{2,1,0:T(8,128)(2,1)S(1)}, u32[]{:S(2)}, u32[]{:S(2)}) async-start(bf16[4,192,512]{2,1,0:T(8,128)(2,1)} %shard_map.55.refs_4_), calls=%async_computation | async-start | bytes 1572864 | tf_op jit(solution)/shard_map/all_to_all | solution.py:534
  65.3 0.8 copy-done.13
  66.2 17.5 %shard_map.59 = (f32[3072,128]{1,0:T(8,128)}, bf16[3072,128]{1,0:T(8,128)(2,1)}, f32[2,3072]{1,0:T(2,128)}) custom-call(s32[7]{0:T(128)} %stack.102.info, s32[192]{0:T(256)} %here_targets.1, s32[3]{0:T(128)} %here_lengths.1, s32[195]{0:T(256)} %copy-done.14, bf16[768,512]{1,0:T(8,128)(2,1)} %copy-done.11, bf16[384,512]{1,0:T(8,128)(2,1)} %copy-done.9, ...), custom_call_target="tpu_custom_call" | custom-call | flops 2415919104 | bytes 5505024 | tf_op jit(solution)/shard_map/pallas_call | solution.py:371
  83.9 1.2 collective-permute-done.15.b_ref
  85.1 0.7 copy-done.4
  85.8 1.0 collective-permute-start.16
  86.8 2.5 %collective-permute-start.18 = (f32[2,3072]{1,0:T(2,128)S(1)}, f32[2,3072]{1,0:T(2,128)S(1)}, u32[]{:S(2)}, u32[]{:S(2)}) collective-permute-start(f32[2,3072]{1,0:T(2,128)S(1)} %shard_map.60.refs_0_), channel_id=1, source_target_pairs={{0,12},{1,13},{4,8},{5,9},{8,4},{9,5},{12,0},{13,1},{16,28},{17,29... | collective-permute-start | bytes 73736 | tf_op jit(solution)/shard_map/ppermute | solution.py:175
  89.6 1.0 collective-permute-done.17.refs_2_
  90.6 0.9 collective-permute-done.18.refs_3_
  91.5 1.4 %copy-done.1 = f32[3072,128]{1,0:T(8,128)S(1)} copy-done((f32[3072,128]{1,0:T(8,128)S(1)}, f32[3072,128]{1,0:T(8,128)}, u32[]{:S(2)}) %copy-start.1) | copy-done | bytes 1572888
  92.9 1.1 copy-done.3
  94.0 1.7 %shard_map.61 = (bf16[768,128]{1,0:T(8,128)(2,1)S(1)}, bf16[768,128]{1,0:T(8,128)(2,1)S(1)}, bf16[768,128]{1,0:T(8,128)(2,1)S(1)}, bf16[768,128]{1,0:T(8,128)(2,1)S(1)}) custom-call(s32[1]{0:T(128)} %bitcast.9.info, f32[3072,128]{1,0:T(8,128)S(1)} %copy-done.1, bf16[3072,128]{1,0:T(8,128)(2,1)S(1)} %copy-done.3, f32[2,3072]{1,0:T(2,128)S(1)} %shard_map.60.refs_0_, ...), custom_call_target="tpu_custom_call" | custom-call | flops 3145728 | bytes 3145728 | tf_op jit(solution)/shard_map/pallas_call | solution.py:423
  95.8 4.8 %collective-permute-start.19 = (bf16[768,128]{1,0:T(8,128)(2,1)S(1)}, bf16[768,128]{1,0:T(8,128)(2,1)S(1)}, u32[]{:S(2)}, u32[]{:S(2)}) collective-permute-start(bf16[768,128]{1,0:T(8,128)(2,1)S(1)} %get-tuple-element.33), channel_id=1, source_target_pairs={{0,0},{1,8},{4,4},{5,12},{8,16},{9,24},{12,20},{13,28},{16,1},{17,... | collective-permute-start | bytes 589832 | tf_op jit(solution)/shard_map/ppermute | solution.py:175
  100.6 1.9 %collective-permute-start.21 = (bf16[768,128]{1,0:T(8,128)(2,1)S(1)}, bf16[768,128]{1,0:T(8,128)(2,1)S(1)}, u32[]{:S(2)}, u32[]{:S(2)}) collective-permute-start(bf16[768,128]{1,0:T(8,128)(2,1)S(1)} %get-tuple-element.34), channel_id=1, source_target_pairs={{0,8},{1,16},{4,12},{5,20},{8,24},{9,0},{12,28},{13,4},{16,9},{17,... | collective-permute-start | bytes 589832 | tf_op jit(solution)/shard_map/ppermute | solution.py:175
  102.5 2.1 %collective-permute-start.23 = (bf16[768,128]{1,0:T(8,128)(2,1)S(1)}, bf16[768,128]{1,0:T(8,128)(2,1)S(1)}, u32[]{:S(2)}, u32[]{:S(2)}) collective-permute-start(bf16[768,128]{1,0:T(8,128)(2,1)S(1)} %get-tuple-element.35), channel_id=1, source_target_pairs={{0,16},{1,24},{4,20},{5,28},{8,0},{9,8},{12,4},{13,12},{16,17},{17... | collective-permute-start | bytes 589832 | tf_op jit(solution)/shard_map/ppermute | solution.py:175
  105.3 2.8 %collective-permute-done.19.refs_1_ = bf16[768,128]{1,0:T(8,128)(2,1)S(1)} collective-permute-done((bf16[768,128]{1,0:T(8,128)(2,1)S(1)}, bf16[768,128]{1,0:T(8,128)(2,1)S(1)}, u32[]{:S(2)}, u32[]{:S(2)}) %collective-permute-start.19) | collective-permute-done | bytes 196640 | tf_op jit(solution)/shard_map/ppermute | solution.py:175
  108.1 1.1 collective-permute-start.20
  109.2 8.8 %collective-permute-done.21.refs_3_ = bf16[768,128]{1,0:T(8,128)(2,1)S(1)} collective-permute-done((bf16[768,128]{1,0:T(8,128)(2,1)S(1)}, bf16[768,128]{1,0:T(8,128)(2,1)S(1)}, u32[]{:S(2)}, u32[]{:S(2)}) %collective-permute-start.21) | collective-permute-done | bytes 196640 | tf_op jit(solution)/shard_map/ppermute | solution.py:175
  118.0 1.1 collective-permute-start.22
  119.0 1.0 collective-permute-start.24
  120.0 1.1 collective-permute-start.26
  121.6 4.2 %collective-permute-done.22.refs_4_ = bf16[768,128]{1,0:T(8,128)(2,1)S(1)} collective-permute-done((bf16[768,128]{1,0:T(8,128)(2,1)S(1)}, bf16[768,128]{1,0:T(8,128)(2,1)S(1)}, u32[]{:S(2)}, u32[]{:S(2)}) %collective-permute-start.22) | collective-permute-done | bytes 196640 | tf_op jit(solution)/shard_map/ppermute | solution.py:175
  125.8 4.2 %collective-permute-done.24.refs_6_ = bf16[768,128]{1,0:T(8,128)(2,1)S(1)} collective-permute-done((bf16[768,128]{1,0:T(8,128)(2,1)S(1)}, bf16[768,128]{1,0:T(8,128)(2,1)S(1)}, u32[]{:S(2)}, u32[]{:S(2)}) %collective-permute-start.24) | collective-permute-done | bytes 196640 | tf_op jit(solution)/shard_map/ppermute | solution.py:175
  130.0 2.2 %collective-permute-done.26.refs_8_ = bf16[768,128]{1,0:T(8,128)(2,1)S(1)} collective-permute-done((bf16[768,128]{1,0:T(8,128)(2,1)S(1)}, bf16[768,128]{1,0:T(8,128)(2,1)S(1)}, u32[]{:S(2)}, u32[]{:S(2)}) %collective-permute-start.26) | collective-permute-done | bytes 196640 | tf_op jit(solution)/shard_map/ppermute | solution.py:175
  132.3 2.6 %shard_map.62 = bf16[768,512]{1,0:T(8,128)(2,1)} custom-call(s32[8]{0:T(128)S(1)} %stack.92.info, s32[4]{0:T(128)S(1)} %fusion.2.quarter, bf16[1024,512]{1,0:T(8,128)(2,1)S(1)} %copy-done.2, bf16[4,192,512]{2,1,0:T(8,128)(2,1)S(1)} %all-to-all-done.refs_0_, bf16[768,128]{1,0:T(8,128)(2,1)S(1)} %collective-permute-done.19.refs_1_, ...), custom_call_target="tpu_custom_call" | custom-call | flops 805306368 | bytes 8388608 | tf_op jit(solution)/shard_map/pallas_call | solution.py:485
  (59 shorter events, 3.9 us)
Async XLA Ops:
  0.0 8.7 %copy-start = (bf16[768,512]{1,0:T(8,128)(2,1)S(1)}, bf16[768,512]{1,0:T(8,128)(2,1)}, u32[]{:S(2)}) copy-start(bf16[768,512]{1,0:T(8,128)(2,1)} %refs_0_.1) | copy-start | bytes 2359300
  0.0 18.4 %collective-permute-start = (bf16[768,512]{1,0:T(8,128)(2,1)}, bf16[768,512]{1,0:T(8,128)(2,1)}, u32[]{:S(2)}, u32[]{:S(2)}) collective-permute-start(bf16[768,512]{1,0:T(8,128)(2,1)} %refs_0_.1), channel_id=1, source_target_pairs={{0,9},{4,13},{8,1},{12,5},{17,24},{21,28},{25,16},{29,20},{2,11},{... | collective-permute-start | bytes 2359304 | tf_op jit(solution)/shard_map/ppermute | solution.py:175
  3.5 13.6 %collective-permute-start.4 = (bf16[384,512]{1,0:T(8,128)(2,1)S(1)}, bf16[384,512]{1,0:T(8,128)(2,1)S(1)}, u32[]{:S(2)}, u32[]{:S(2)}) collective-permute-start(bf16[384,512]{1,0:T(8,128)(2,1)S(1)} %get-tuple-element.38), channel_id=1, source_target_pairs={{1,16},{5,20},{9,17},{13,21},{16,8},{20,12},{24,9},{28,13},{3,18},... | collective-permute-start | bytes 1179656 | tf_op jit(solution)/shard_map/ppermute | solution.py:175
  4.8 35.3 %collective-permute-start.2 = (bf16[768,512]{1,0:T(8,128)(2,1)}, bf16[768,512]{1,0:T(8,128)(2,1)}, u32[]{:S(2)}, u32[]{:S(2)}) collective-permute-start(bf16[768,512]{1,0:T(8,128)(2,1)} %refs_0_.1), channel_id=1, source_target_pairs={{0,4},{4,0},{8,12},{12,8},{17,21},{21,17},{25,29},{29,25},{2,6},{6... | collective-permute-start | bytes 2359304 | tf_op jit(solution)/shard_map/ppermute | solution.py:175
  8.7 0.7 copy-start.5
  17.1 14.0 %collective-permute-start.8 = (bf16[384,512]{1,0:T(8,128)(2,1)S(1)}, bf16[384,512]{1,0:T(8,128)(2,1)}, u32[]{:S(2)}, u32[]{:S(2)}) collective-permute-start(bf16[384,512]{1,0:T(8,128)(2,1)S(1)} %get-tuple-element.25), channel_id=1, source_target_pairs={{1,16},{5,20},{9,17},{13,21},{16,8},{20,12},{24,9},{28,13},{3,18},... | collective-permute-start | bytes 1179656 | tf_op jit(solution)/shard_map/ppermute | solution.py:175
  18.4 25.3 %collective-permute-start.3 = (bf16[768,512]{1,0:T(8,128)(2,1)}, bf16[768,512]{1,0:T(8,128)(2,1)}, u32[]{:S(2)}, u32[]{:S(2)}) collective-permute-start(bf16[768,512]{1,0:T(8,128)(2,1)} %collective-permute-done.refs_2_), channel_id=1, source_target_pairs={{1,5},{5,1},{9,13},{13,9},{16,20},{20,16},{24,28},{28,24},{3,7},{7... | collective-permute-start | bytes 2359304 | tf_op jit(solution)/shard_map/ppermute | solution.py:175
  20.0 18.6 %collective-permute-start.6 = (bf16[384,512]{1,0:T(8,128)(2,1)S(1)}, bf16[384,512]{1,0:T(8,128)(2,1)}, u32[]{:S(2)}, u32[]{:S(2)}) collective-permute-start(bf16[384,512]{1,0:T(8,128)(2,1)S(1)} %collective-permute-done.4.refs_0_), channel_id=1, source_target_pairs={{8,0},{9,1},{12,4},{13,5},{16,24},{17,25},{20,28},{21,29},{10,2},{... | collective-permute-start | bytes 1179656 | tf_op jit(solution)/shard_map/ppermute | solution.py:175
  31.1 11.2 %collective-permute-start.10 = (bf16[384,512]{1,0:T(8,128)(2,1)}, bf16[384,512]{1,0:T(8,128)(2,1)}, u32[]{:S(2)}, u32[]{:S(2)}) collective-permute-start(bf16[384,512]{1,0:T(8,128)(2,1)} %collective-permute-done.8.refs_0_), channel_id=1, source_target_pairs={{8,0},{9,1},{12,4},{13,5},{16,24},{17,25},{20,28},{21,29},{10,2},{... | collective-permute-start | bytes 1179656 | tf_op jit(solution)/shard_map/ppermute | solution.py:175
  33.1 10.6 %copy-start.8 = (s32[3]{0:T(128)S(1)}, s32[3]{0:T(128)}, u32[]{:S(2)}) copy-start(s32[3]{0:T(128)} %here_lengths.1) | copy-start | bytes 40
  34.9 15.2 %collective-permute-start.5 = (bf16[384,512]{1,0:T(8,128)(2,1)S(1)}, bf16[384,512]{1,0:T(8,128)(2,1)}, u32[]{:S(2)}, u32[]{:S(2)}) collective-permute-start(bf16[384,512]{1,0:T(8,128)(2,1)S(1)} %collective-permute-done.4.refs_0_), channel_id=1, source_target_pairs={{8,12},{9,13},{12,8},{13,9},{16,20},{17,21},{20,16},{21,17},{10,14... | collective-permute-start | bytes 1179656 | tf_op jit(solution)/shard_map/ppermute | solution.py:175
  38.6 11.5 %collective-permute-start.7 = (bf16[384,512]{1,0:T(8,128)(2,1)}, bf16[384,512]{1,0:T(8,128)(2,1)}, u32[]{:S(2)}, u32[]{:S(2)}) collective-permute-start(bf16[384,512]{1,0:T(8,128)(2,1)} %collective-permute-done.6.refs_2_), channel_id=1, source_target_pairs={{0,4},{1,5},{4,0},{5,1},{24,28},{25,29},{28,24},{29,25},{2,6},{3,7... | collective-permute-start | bytes 1179656 | tf_op jit(solution)/shard_map/ppermute | solution.py:175
  40.1 15.3 %collective-permute-start.9 = (bf16[384,512]{1,0:T(8,128)(2,1)}, bf16[384,512]{1,0:T(8,128)(2,1)}, u32[]{:S(2)}, u32[]{:S(2)}) collective-permute-start(bf16[384,512]{1,0:T(8,128)(2,1)} %collective-permute-done.8.refs_0_), channel_id=1, source_target_pairs={{8,12},{9,13},{12,8},{13,9},{16,20},{17,21},{20,16},{21,17},{10,14... | collective-permute-start | bytes 1179656 | tf_op jit(solution)/shard_map/ppermute | solution.py:175
  42.3 13.1 %collective-permute-start.11 = (bf16[384,512]{1,0:T(8,128)(2,1)}, bf16[384,512]{1,0:T(8,128)(2,1)}, u32[]{:S(2)}, u32[]{:S(2)}) collective-permute-start(bf16[384,512]{1,0:T(8,128)(2,1)} %collective-permute-done.10.refs_2_), channel_id=1, source_target_pairs={{0,4},{1,5},{4,0},{5,1},{24,28},{25,29},{28,24},{29,25},{2,6},{3,7... | collective-permute-start | bytes 1179656 | tf_op jit(solution)/shard_map/ppermute | solution.py:175
  49.1 0.9 copy-start.11
  50.0 15.3 %collective-permute-start.12 = (bf16[768,512]{1,0:T(8,128)(2,1)}, bf16[768,512]{1,0:T(8,128)(2,1)}, u32[]{:S(2)}, u32[]{:S(2)}) collective-permute-start(bf16[768,512]{1,0:T(8,128)(2,1)} %get-tuple-element.27), channel_id=1, source_target_pairs={{0,1},{1,0},{4,5},{5,4},{8,9},{9,8},{12,13},{13,12},{16,17},{17,16... | collective-permute-start | bytes 2359304 | tf_op jit(solution)/shard_map/ppermute | solution.py:175
  53.4 5.1 %copy-start.9 = (bf16[384,512]{1,0:T(8,128)(2,1)}, bf16[384,512]{1,0:T(8,128)(2,1)S(1)}, u32[]{:S(2)}) copy-start(bf16[384,512]{1,0:T(8,128)(2,1)S(1)} %get-tuple-element.24.refs_1_) | copy-start | bytes 1179652
  53.4 10.6 %copy-start.6 = (s32[192]{0:T(256)S(1)}, s32[192]{0:T(256)}, u32[]{:S(2)}) copy-start(s32[192]{0:T(256)} %here_targets.1) | copy-start | bytes 2308
  53.5 11.8 %collective-permute-start.13 = (bf16[384,512]{1,0:T(8,128)(2,1)S(1)}, bf16[384,512]{1,0:T(8,128)(2,1)S(1)}, u32[]{:S(2)}, u32[]{:S(2)}) collective-permute-start(bf16[384,512]{1,0:T(8,128)(2,1)S(1)} %get-tuple-element.28), channel_id=1, source_target_pairs={{0,1},{1,0},{4,5},{5,4},{8,9},{9,8},{12,13},{13,12},{16,17},{17,16... | collective-permute-start | bytes 1179656 | tf_op jit(solution)/shard_map/ppermute | solution.py:175
  58.5 0.8 copy-start.10
  59.3 6.0 %collective-permute-start.14 = (bf16[384,512]{1,0:T(8,128)(2,1)S(1)}, bf16[384,512]{1,0:T(8,128)(2,1)S(1)}, u32[]{:S(2)}, u32[]{:S(2)}) collective-permute-start(bf16[384,512]{1,0:T(8,128)(2,1)S(1)} %get-tuple-element.29), channel_id=1, source_target_pairs={{0,1},{1,0},{4,5},{5,4},{8,9},{9,8},{12,13},{13,12},{16,17},{17,16... | collective-permute-start | bytes 1179656 | tf_op jit(solution)/shard_map/ppermute | solution.py:175
  59.3 62.2 %all-to-all-start = ((bf16[4,192,512]{2,1,0:T(8,128)(2,1)}), bf16[4,192,512]{2,1,0:T(8,128)(2,1)S(1)}, u32[]{:S(2)}, u32[]{:S(2)}) async-start(bf16[4,192,512]{2,1,0:T(8,128)(2,1)} %shard_map.55.refs_4_), calls=%async_computation | async-start | bytes 1572864 | tf_op jit(solution)/shard_map/all_to_all | solution.py:534
  64.1 1.1 collective-permute-start.1
  65.3 0.8 copy-start.14
  65.3 0.9 copy-start.12
  65.3 0.8 copy-start.13
  66.2 66.1 %copy-start.2 = (bf16[1024,512]{1,0:T(8,128)(2,1)S(1)}, bf16[1024,512]{1,0:T(8,128)(2,1)}, u32[]{:S(2)}) copy-start(bf16[1024,512]{1,0:T(8,128)(2,1)} %w_ref.1) | copy-start | bytes 3145732
  83.7 21.6 %copy-start.7 = (s32[192]{0:T(256)S(1)}, s32[192]{0:T(256)}, u32[]{:S(2)}) copy-start(s32[192]{0:T(256)} %here_targets.1) | copy-start | bytes 2308
  83.7 1.4 %collective-permute-start.15 = (f32[2,3072]{1,0:T(2,128)}, f32[2,3072]{1,0:T(2,128)S(1)}, u32[]{:S(2)}, u32[]{:S(2)}) collective-permute-start(f32[2,3072]{1,0:T(2,128)} %get-tuple-element.32.a_ref), channel_id=1, source_target_pairs={{0,1},{1,0},{4,5},{5,4},{8,9},{9,8},{12,13},{13,12},{16,17},{17,16... | collective-permute-start | bytes 73736 | tf_op jit(solution)/shard_map/ppermute | solution.py:175
  85.1 0.7 copy-start.4
  85.8 3.8 %collective-permute-start.16 = (f32[2,3072]{1,0:T(2,128)S(1)}, f32[2,3072]{1,0:T(2,128)S(1)}, u32[]{:S(2)}, u32[]{:S(2)}) collective-permute-start(f32[2,3072]{1,0:T(2,128)S(1)} %shard_map.60.refs_0_), channel_id=1, source_target_pairs={{0,4},{1,5},{4,0},{5,1},{8,12},{9,13},{12,8},{13,9},{16,20},{17,21... | collective-permute-start | bytes 73736 | tf_op jit(solution)/shard_map/ppermute | solution.py:175
  86.8 3.8 %collective-permute-start.17 = (f32[2,3072]{1,0:T(2,128)S(1)}, f32[2,3072]{1,0:T(2,128)S(1)}, u32[]{:S(2)}, u32[]{:S(2)}) collective-permute-start(f32[2,3072]{1,0:T(2,128)S(1)} %shard_map.60.refs_0_), channel_id=1, source_target_pairs={{0,8},{1,9},{4,12},{5,13},{8,0},{9,1},{12,4},{13,5},{16,24},{17,25... | collective-permute-start | bytes 73736 | tf_op jit(solution)/shard_map/ppermute | solution.py:175
  86.8 4.7 %collective-permute-start.18 = (f32[2,3072]{1,0:T(2,128)S(1)}, f32[2,3072]{1,0:T(2,128)S(1)}, u32[]{:S(2)}, u32[]{:S(2)}) collective-permute-start(f32[2,3072]{1,0:T(2,128)S(1)} %shard_map.60.refs_0_), channel_id=1, source_target_pairs={{0,12},{1,13},{4,8},{5,9},{8,4},{9,5},{12,0},{13,1},{16,28},{17,29... | collective-permute-start | bytes 73736 | tf_op jit(solution)/shard_map/ppermute | solution.py:175
  91.5 1.4 %copy-start.1 = (f32[3072,128]{1,0:T(8,128)S(1)}, f32[3072,128]{1,0:T(8,128)}, u32[]{:S(2)}) copy-start(f32[3072,128]{1,0:T(8,128)} %get-tuple-element.30.att_ref) | copy-start | bytes 4718596
  92.9 1.1 copy-start.3
  95.8 12.3 %collective-permute-start.19 = (bf16[768,128]{1,0:T(8,128)(2,1)S(1)}, bf16[768,128]{1,0:T(8,128)(2,1)S(1)}, u32[]{:S(2)}, u32[]{:S(2)}) collective-permute-start(bf16[768,128]{1,0:T(8,128)(2,1)S(1)} %get-tuple-element.33), channel_id=1, source_target_pairs={{0,0},{1,8},{4,4},{5,12},{8,16},{9,24},{12,20},{13,28},{16,1},{17,... | collective-permute-start | bytes 589832 | tf_op jit(solution)/shard_map/ppermute | solution.py:175
  100.6 17.3 %collective-permute-start.21 = (bf16[768,128]{1,0:T(8,128)(2,1)S(1)}, bf16[768,128]{1,0:T(8,128)(2,1)S(1)}, u32[]{:S(2)}, u32[]{:S(2)}) collective-permute-start(bf16[768,128]{1,0:T(8,128)(2,1)S(1)} %get-tuple-element.34), channel_id=1, source_target_pairs={{0,8},{1,16},{4,12},{5,20},{8,24},{9,0},{12,28},{13,4},{16,9},{17,... | collective-permute-start | bytes 589832 | tf_op jit(solution)/shard_map/ppermute | solution.py:175
  102.5 16.5 %collective-permute-start.23 = (bf16[768,128]{1,0:T(8,128)(2,1)S(1)}, bf16[768,128]{1,0:T(8,128)(2,1)S(1)}, u32[]{:S(2)}, u32[]{:S(2)}) collective-permute-start(bf16[768,128]{1,0:T(8,128)(2,1)S(1)} %get-tuple-element.35), channel_id=1, source_target_pairs={{0,16},{1,24},{4,20},{5,28},{8,0},{9,8},{12,4},{13,12},{16,17},{17... | collective-permute-start | bytes 589832 | tf_op jit(solution)/shard_map/ppermute | solution.py:175
  104.6 15.4 %collective-permute-start.25 = (bf16[768,128]{1,0:T(8,128)(2,1)S(1)}, bf16[768,128]{1,0:T(8,128)(2,1)S(1)}, u32[]{:S(2)}, u32[]{:S(2)}) collective-permute-start(bf16[768,128]{1,0:T(8,128)(2,1)S(1)} %get-tuple-element.36), channel_id=1, source_target_pairs={{0,24},{1,0},{4,28},{5,4},{8,8},{9,16},{12,12},{13,20},{16,25},{17... | collective-permute-start | bytes 589832 | tf_op jit(solution)/shard_map/ppermute | solution.py:175
  108.1 13.5 %collective-permute-start.20 = (bf16[768,128]{1,0:T(8,128)(2,1)S(1)}, bf16[768,128]{1,0:T(8,128)(2,1)S(1)}, u32[]{:S(2)}, u32[]{:S(2)}) collective-permute-start(bf16[768,128]{1,0:T(8,128)(2,1)S(1)} %collective-permute-done.19.refs_1_), channel_id=1, source_target_pairs={{0,4},{1,5},{4,0},{5,1},{8,12},{9,13},{12,8},{13,9},{16,20},{17,21... | collective-permute-start | bytes 589832 | tf_op jit(solution)/shard_map/ppermute | solution.py:175
  118.0 7.8 %collective-permute-start.22 = (bf16[768,128]{1,0:T(8,128)(2,1)S(1)}, bf16[768,128]{1,0:T(8,128)(2,1)S(1)}, u32[]{:S(2)}, u32[]{:S(2)}) collective-permute-start(bf16[768,128]{1,0:T(8,128)(2,1)S(1)} %collective-permute-done.21.refs_3_), channel_id=1, source_target_pairs={{0,4},{1,5},{4,0},{5,1},{8,12},{9,13},{12,8},{13,9},{16,20},{17,21... | collective-permute-start | bytes 589832 | tf_op jit(solution)/shard_map/ppermute | solution.py:175
  119.0 11.0 %collective-permute-start.24 = (bf16[768,128]{1,0:T(8,128)(2,1)S(1)}, bf16[768,128]{1,0:T(8,128)(2,1)S(1)}, u32[]{:S(2)}, u32[]{:S(2)}) collective-permute-start(bf16[768,128]{1,0:T(8,128)(2,1)S(1)} %collective-permute-done.23.refs_5_), channel_id=1, source_target_pairs={{0,4},{1,5},{4,0},{5,1},{8,12},{9,13},{12,8},{13,9},{16,20},{17,21... | collective-permute-start | bytes 589832 | tf_op jit(solution)/shard_map/ppermute | solution.py:175
  120.0 12.3 %collective-permute-start.26 = (bf16[768,128]{1,0:T(8,128)(2,1)S(1)}, bf16[768,128]{1,0:T(8,128)(2,1)S(1)}, u32[]{:S(2)}, u32[]{:S(2)}) collective-permute-start(bf16[768,128]{1,0:T(8,128)(2,1)S(1)} %collective-permute-done.25.refs_7_), channel_id=1, source_target_pairs={{0,4},{1,5},{4,0},{5,1},{8,12},{9,13},{12,8},{13,9},{16,20},{17,21... | collective-permute-start | bytes 589832 | tf_op jit(solution)/shard_map/ppermute | solution.py:175

commit v8 on v7

--- a/solution.py
+++ b/solution.py
@@ -285,7 +285,7 @@
 
 
 TQ = 1536
-TK = 512
+TK = 1536
 SUB = 256
 DSUB = 256
 

time: 136 us -> 135 us (level)
  no operation moved by 1% of the time
where the time goes in v8:
time: 135 us
  starting transfers between devices  46 us (34%)
  waiting for transfers between devices  42.2 us (31%)
  Pallas kernels  35.5 us (26%)
  local copies, waits for them, and re-layouts  10.4 us (8%)
    ppermute x27, waiting for transfers between devices, move(): return lax.ppermute(value, ROUTE, route(rule))  42.2 us
    ppermute x27, starting transfers between devices, move(): return lax.ppermute(value, ROUTE, route(rule))  41.3 us
    pallas_call x1, Pallas kernels, attend(): pl.pallas_call(attend_kernel, out_shape=(jax.ShapeDtypeStruct((seq, 128),...  17.3 us
    pallas_call x3, Pallas kernels, project(): pl.pallas_call(functools.partial(project_kernel, len(after)), out_shape=(...  11.9 us
    unnamed x30, local copies, waits for them, and re-layouts  6.53 us
    all_to_all x1, starting transfers between devices, team_body(): lax.all_to_all(send, ('half', 'zlo'), split_axis=0, concat_axis=0, tiled=...  4.73 us
  transfers between devices with their start and end apart: 28, of which 13 were waited for; matrix products, arithmetic and copies ran while one was open for 3% of the time, Pallas kernels for 24%

profile of v8, /device:TPU:8, one launch (start us, length us, event | category | flops | bytes accessed | tf_op | source)
XLA Modules:
  0.0 134.7 jit_solution(6798382098349485430)
XLA Ops:
  0.0 2.3 %collective-permute-start = (bf16[768,512]{1,0:T(8,128)(2,1)}, bf16[768,512]{1,0:T(8,128)(2,1)}, u32[]{:S(2)}, u32[]{:S(2)}) collective-permute-start(bf16[768,512]{1,0:T(8,128)(2,1)} %refs_0_.1), channel_id=1, source_target_pairs={{0,9},{4,13},{8,1},{12,5},{17,24},{21,28},{25,16},{29,20},{2,11},{... | collective-permute-start | bytes 2359304 | tf_op jit(solution)/shard_map/ppermute | solution.py:175
  2.3 1.2 fusion.4
  3.5 1.3 collective-permute-start.4
  4.8 3.9 %collective-permute-start.2 = (bf16[768,512]{1,0:T(8,128)(2,1)}, bf16[768,512]{1,0:T(8,128)(2,1)}, u32[]{:S(2)}, u32[]{:S(2)}) collective-permute-start(bf16[768,512]{1,0:T(8,128)(2,1)} %refs_0_.1), channel_id=1, source_target_pairs={{0,4},{4,0},{8,12},{12,8},{17,21},{21,17},{25,29},{29,25},{2,6},{6... | collective-permute-start | bytes 2359304 | tf_op jit(solution)/shard_map/ppermute | solution.py:175
  8.7 0.7 copy-done.5
  9.4 1.9 %shard_map.55.refs_4_ = bf16[4,192,512]{2,1,0:T(8,128)(2,1)} custom-call(s32[1]{0:T(128)} %bitcast.8.info, s32[192]{0:T(256)S(1)} %copy-done.5, bf16[768,512]{1,0:T(8,128)(2,1)S(1)} %copy-done, bf16[768,512]{1,0:T(8,128)(2,1)S(1)} %copy-done), custom_call_target="tpu_custom_call" | custom-call | bytes 1572864 | tf_op jit(solution)/shard_map/pallas_call | solution.py:449
  11.3 5.8 %collective-permute-done.4.refs_0_ = bf16[384,512]{1,0:T(8,128)(2,1)S(1)} collective-permute-done((bf16[384,512]{1,0:T(8,128)(2,1)S(1)}, bf16[384,512]{1,0:T(8,128)(2,1)S(1)}, u32[]{:S(2)}, u32[]{:S(2)}) %collective-permute-start.4) | collective-permute-done | bytes 393248 | tf_op jit(solution)/shard_map/ppermute | solution.py:175
  17.1 1.3 collective-permute-start.8
  18.4 1.6 %collective-permute-start.3 = (bf16[768,512]{1,0:T(8,128)(2,1)}, bf16[768,512]{1,0:T(8,128)(2,1)}, u32[]{:S(2)}, u32[]{:S(2)}) collective-permute-start(bf16[768,512]{1,0:T(8,128)(2,1)} %collective-permute-done.refs_2_), channel_id=1, source_target_pairs={{1,5},{5,1},{9,13},{13,9},{16,20},{20,16},{24,28},{28,24},{3,7},{7... | collective-permute-start | bytes 2359304 | tf_op jit(solution)/shard_map/ppermute | solution.py:175
  20.0 2.0 %collective-permute-start.6 = (bf16[384,512]{1,0:T(8,128)(2,1)S(1)}, bf16[384,512]{1,0:T(8,128)(2,1)}, u32[]{:S(2)}, u32[]{:S(2)}) collective-permute-start(bf16[384,512]{1,0:T(8,128)(2,1)S(1)} %collective-permute-done.4.refs_0_), channel_id=1, source_target_pairs={{8,0},{9,1},{12,4},{13,5},{16,24},{17,25},{20,28},{21,29},{10,2},{... | collective-permute-start | bytes 1179656 | tf_op jit(solution)/shard_map/ppermute | solution.py:175
  22.0 9.1 %collective-permute-done.8.refs_0_ = bf16[384,512]{1,0:T(8,128)(2,1)} collective-permute-done((bf16[384,512]{1,0:T(8,128)(2,1)S(1)}, bf16[384,512]{1,0:T(8,128)(2,1)}, u32[]{:S(2)}, u32[]{:S(2)}) %collective-permute-start.8) | collective-permute-done | bytes 393248 | tf_op jit(solution)/shard_map/ppermute | solution.py:175
  31.1 2.0 %collective-permute-start.10 = (bf16[384,512]{1,0:T(8,128)(2,1)}, bf16[384,512]{1,0:T(8,128)(2,1)}, u32[]{:S(2)}, u32[]{:S(2)}) collective-permute-start(bf16[384,512]{1,0:T(8,128)(2,1)} %collective-permute-done.8.refs_0_), channel_id=1, source_target_pairs={{8,0},{9,1},{12,4},{13,5},{16,24},{17,25},{20,28},{21,29},{10,2},{... | collective-permute-start | bytes 1179656 | tf_op jit(solution)/shard_map/ppermute | solution.py:175
  33.1 1.7 %constant_dynamic-slice_fusion.refs_4_.refs_5_ = bf16[4,1024,256]{2,1,0:T(8,128)(2,1)S(1)} fusion(bf16[4,1024,512]{2,1,0:T(8,128)(2,1)} %param.6, s32[]{:T(128)S(6)} %select_n.52), kind=kLoop, calls=%fused_computation.15 | loop fusion | bytes 4194308 | tf_op jit(solution)/shard_map/dynamic_slice | solution.py:508
  34.9 3.7 %collective-permute-start.5 = (bf16[384,512]{1,0:T(8,128)(2,1)S(1)}, bf16[384,512]{1,0:T(8,128)(2,1)}, u32[]{:S(2)}, u32[]{:S(2)}) collective-permute-start(bf16[384,512]{1,0:T(8,128)(2,1)S(1)} %collective-permute-done.4.refs_0_), channel_id=1, source_target_pairs={{8,12},{9,13},{12,8},{13,9},{16,20},{17,21},{20,16},{21,17},{10,14... | collective-permute-start | bytes 1179656 | tf_op jit(solution)/shard_map/ppermute | solution.py:175
  38.6 1.4 %collective-permute-start.7 = (bf16[384,512]{1,0:T(8,128)(2,1)}, bf16[384,512]{1,0:T(8,128)(2,1)}, u32[]{:S(2)}, u32[]{:S(2)}) collective-permute-start(bf16[384,512]{1,0:T(8,128)(2,1)} %collective-permute-done.6.refs_2_), channel_id=1, source_target_pairs={{0,4},{1,5},{4,0},{5,1},{24,28},{25,29},{28,24},{29,25},{2,6},{3,7... | collective-permute-start | bytes 1179656 | tf_op jit(solution)/shard_map/ppermute | solution.py:175
  40.1 2.2 %collective-permute-start.9 = (bf16[384,512]{1,0:T(8,128)(2,1)}, bf16[384,512]{1,0:T(8,128)(2,1)}, u32[]{:S(2)}, u32[]{:S(2)}) collective-permute-start(bf16[384,512]{1,0:T(8,128)(2,1)} %collective-permute-done.8.refs_0_), channel_id=1, source_target_pairs={{8,12},{9,13},{12,8},{13,9},{16,20},{17,21},{20,16},{21,17},{10,14... | collective-permute-start | bytes 1179656 | tf_op jit(solution)/shard_map/ppermute | solution.py:175
  42.3 1.5 %collective-permute-start.11 = (bf16[384,512]{1,0:T(8,128)(2,1)}, bf16[384,512]{1,0:T(8,128)(2,1)}, u32[]{:S(2)}, u32[]{:S(2)}) collective-permute-start(bf16[384,512]{1,0:T(8,128)(2,1)} %collective-permute-done.10.refs_2_), channel_id=1, source_target_pairs={{0,4},{1,5},{4,0},{5,1},{24,28},{25,29},{28,24},{29,25},{2,6},{3,7... | collective-permute-start | bytes 1179656 | tf_op jit(solution)/shard_map/ppermute | solution.py:175
  43.7 5.4 %shard_map.56 = (bf16[768,512]{1,0:T(8,128)(2,1)S(1)}, bf16[768,512]{1,0:T(8,128)(2,1)}) custom-call(s32[4]{0:T(128)S(1)} %add_add_fusion.info, s32[3]{0:T(128)S(1)} %copy-done.8, bf16[768,512]{1,0:T(8,128)(2,1)S(1)} %copy-done, bf16[768,512]{1,0:T(8,128)(2,1)} %collective-permute-done.2.refs_1_, bf16[768,512]{1,0:T(8,128)(2,1)} %collective-permute-done.refs_2_, ...), custom_call_target="tpu_custom_call" | custom-call | flops 1610612736 | bytes 5242880 | tf_op jit(solution)/shard_map/pallas_call | solution.py:270
  49.1 0.9 copy-done.11
  50.1 3.3 %shard_map.57 = (bf16[384,512]{1,0:T(8,128)(2,1)S(1)}, bf16[384,512]{1,0:T(8,128)(2,1)S(1)}) custom-call(s32[4]{0:T(128)S(1)} %add_add_fusion.1.info, s32[3]{0:T(128)S(1)} %copy-done.8, bf16[384,512]{1,0:T(8,128)(2,1)S(1)} %collective-permute-done.4.refs_0_, bf16[384,512]{1,0:T(8,128)(2,1)} %collective-permute-done.5.refs_1_, ...), custom_call_target="tpu_custom_call" | custom-call | flops 805306368 | bytes 3670016 | tf_op jit(solution)/shard_map/pallas_call | solution.py:270
  54.0 1.3 collective-permute-done.9.refs_1_
  55.3 3.2 %shard_map.58 = (bf16[384,512]{1,0:T(8,128)(2,1)S(1)}, bf16[384,512]{1,0:T(8,128)(2,1)S(1)}) custom-call(s32[4]{0:T(128)S(1)} %add_add_fusion.1.info, s32[3]{0:T(128)S(1)} %copy-done.8, bf16[384,512]{1,0:T(8,128)(2,1)} %collective-permute-done.8.refs_0_, bf16[384,512]{1,0:T(8,128)(2,1)} %collective-permute-done.9.refs_1_, ...), custom_call_target="tpu_custom_call" | custom-call | flops 805306368 | bytes 3670016 | tf_op jit(solution)/shard_map/pallas_call | solution.py:270
  58.5 0.8 copy-done.10
  59.3 4.7 %all-to-all-start = ((bf16[4,192,512]{2,1,0:T(8,128)(2,1)}), bf16[4,192,512]{2,1,0:T(8,128)(2,1)S(1)}, u32[]{:S(2)}, u32[]{:S(2)}) async-start(bf16[4,192,512]{2,1,0:T(8,128)(2,1)} %shard_map.55.refs_4_), calls=%async_computation | async-start | bytes 1572864 | tf_op jit(solution)/shard_map/all_to_all | solution.py:534
  65.3 0.8 copy-done.13
  66.2 17.3 %shard_map.59 = (f32[3072,128]{1,0:T(8,128)}, bf16[3072,128]{1,0:T(8,128)(2,1)}, f32[2,3072]{1,0:T(2,128)}) custom-call(s32[7]{0:T(128)} %stack.102.info, s32[192]{0:T(256)} %here_targets.1, s32[3]{0:T(128)} %here_lengths.1, s32[195]{0:T(256)} %copy-done.14, bf16[768,512]{1,0:T(8,128)(2,1)} %copy-done.11, bf16[384,512]{1,0:T(8,128)(2,1)} %copy-done.9, ...), custom_call_target="tpu_custom_call" | custom-call | flops 2415919104 | bytes 5505024 | tf_op jit(solution)/shard_map/pallas_call | solution.py:371
  83.7 1.2 collective-permute-done.15.b_ref
  84.9 0.7 copy-done.4
  85.7 1.0 collective-permute-start.16
  86.6 2.5 %collective-permute-start.18 = (f32[2,3072]{1,0:T(2,128)S(1)}, f32[2,3072]{1,0:T(2,128)S(1)}, u32[]{:S(2)}, u32[]{:S(2)}) collective-permute-start(f32[2,3072]{1,0:T(2,128)S(1)} %shard_map.60.refs_0_), channel_id=1, source_target_pairs={{0,12},{1,13},{4,8},{5,9},{8,4},{9,5},{12,0},{13,1},{16,28},{17,29... | collective-permute-start | bytes 73736 | tf_op jit(solution)/shard_map/ppermute | solution.py:175
  89.5 1.0 collective-permute-done.17.refs_2_
  90.5 0.9 collective-permute-done.18.refs_3_
  91.4 1.4 %copy-done.1 = f32[3072,128]{1,0:T(8,128)S(1)} copy-done((f32[3072,128]{1,0:T(8,128)S(1)}, f32[3072,128]{1,0:T(8,128)}, u32[]{:S(2)}) %copy-start.1) | copy-done | bytes 1572888
  92.8 1.1 copy-done.3
  93.9 1.7 %shard_map.61 = (bf16[768,128]{1,0:T(8,128)(2,1)S(1)}, bf16[768,128]{1,0:T(8,128)(2,1)S(1)}, bf16[768,128]{1,0:T(8,128)(2,1)S(1)}, bf16[768,128]{1,0:T(8,128)(2,1)S(1)}) custom-call(s32[1]{0:T(128)} %bitcast.9.info, f32[3072,128]{1,0:T(8,128)S(1)} %copy-done.1, bf16[3072,128]{1,0:T(8,128)(2,1)S(1)} %copy-done.3, f32[2,3072]{1,0:T(2,128)S(1)} %shard_map.60.refs_0_, ...), custom_call_target="tpu_custom_call" | custom-call | flops 3145728 | bytes 3145728 | tf_op jit(solution)/shard_map/pallas_call | solution.py:423
  95.6 4.8 %collective-permute-start.19 = (bf16[768,128]{1,0:T(8,128)(2,1)S(1)}, bf16[768,128]{1,0:T(8,128)(2,1)S(1)}, u32[]{:S(2)}, u32[]{:S(2)}) collective-permute-start(bf16[768,128]{1,0:T(8,128)(2,1)S(1)} %get-tuple-element.33), channel_id=1, source_target_pairs={{0,0},{1,8},{4,4},{5,12},{8,16},{9,24},{12,20},{13,28},{16,1},{17,... | collective-permute-start | bytes 589832 | tf_op jit(solution)/shard_map/ppermute | solution.py:175
  100.5 1.9 %collective-permute-start.21 = (bf16[768,128]{1,0:T(8,128)(2,1)S(1)}, bf16[768,128]{1,0:T(8,128)(2,1)S(1)}, u32[]{:S(2)}, u32[]{:S(2)}) collective-permute-start(bf16[768,128]{1,0:T(8,128)(2,1)S(1)} %get-tuple-element.34), channel_id=1, source_target_pairs={{0,8},{1,16},{4,12},{5,20},{8,24},{9,0},{12,28},{13,4},{16,9},{17,... | collective-permute-start | bytes 589832 | tf_op jit(solution)/shard_map/ppermute | solution.py:175
  102.4 2.1 %collective-permute-start.23 = (bf16[768,128]{1,0:T(8,128)(2,1)S(1)}, bf16[768,128]{1,0:T(8,128)(2,1)S(1)}, u32[]{:S(2)}, u32[]{:S(2)}) collective-permute-start(bf16[768,128]{1,0:T(8,128)(2,1)S(1)} %get-tuple-element.35), channel_id=1, source_target_pairs={{0,16},{1,24},{4,20},{5,28},{8,0},{9,8},{12,4},{13,12},{16,17},{17... | collective-permute-start | bytes 589832 | tf_op jit(solution)/shard_map/ppermute | solution.py:175
  105.2 2.8 %collective-permute-done.19.refs_1_ = bf16[768,128]{1,0:T(8,128)(2,1)S(1)} collective-permute-done((bf16[768,128]{1,0:T(8,128)(2,1)S(1)}, bf16[768,128]{1,0:T(8,128)(2,1)S(1)}, u32[]{:S(2)}, u32[]{:S(2)}) %collective-permute-start.19) | collective-permute-done | bytes 196640 | tf_op jit(solution)/shard_map/ppermute | solution.py:175
  108.0 1.1 collective-permute-start.20
  109.0 8.8 %collective-permute-done.21.refs_3_ = bf16[768,128]{1,0:T(8,128)(2,1)S(1)} collective-permute-done((bf16[768,128]{1,0:T(8,128)(2,1)S(1)}, bf16[768,128]{1,0:T(8,128)(2,1)S(1)}, u32[]{:S(2)}, u32[]{:S(2)}) %collective-permute-start.21) | collective-permute-done | bytes 196640 | tf_op jit(solution)/shard_map/ppermute | solution.py:175
  117.8 1.1 collective-permute-start.22
  118.9 1.0 collective-permute-start.24
  119.8 1.1 collective-permute-start.26
  121.4 4.2 %collective-permute-done.22.refs_4_ = bf16[768,128]{1,0:T(8,128)(2,1)S(1)} collective-permute-done((bf16[768,128]{1,0:T(8,128)(2,1)S(1)}, bf16[768,128]{1,0:T(8,128)(2,1)S(1)}, u32[]{:S(2)}, u32[]{:S(2)}) %collective-permute-start.22) | collective-permute-done | bytes 196640 | tf_op jit(solution)/shard_map/ppermute | solution.py:175
  125.7 4.2 %collective-permute-done.24.refs_6_ = bf16[768,128]{1,0:T(8,128)(2,1)S(1)} collective-permute-done((bf16[768,128]{1,0:T(8,128)(2,1)S(1)}, bf16[768,128]{1,0:T(8,128)(2,1)S(1)}, u32[]{:S(2)}, u32[]{:S(2)}) %collective-permute-start.24) | collective-permute-done | bytes 196640 | tf_op jit(solution)/shard_map/ppermute | solution.py:175
  129.9 2.2 %collective-permute-done.26.refs_8_ = bf16[768,128]{1,0:T(8,128)(2,1)S(1)} collective-permute-done((bf16[768,128]{1,0:T(8,128)(2,1)S(1)}, bf16[768,128]{1,0:T(8,128)(2,1)S(1)}, u32[]{:S(2)}, u32[]{:S(2)}) %collective-permute-start.26) | collective-permute-done | bytes 196640 | tf_op jit(solution)/shard_map/ppermute | solution.py:175
  132.1 2.6 %shard_map.62 = bf16[768,512]{1,0:T(8,128)(2,1)} custom-call(s32[8]{0:T(128)S(1)} %stack.92.info, s32[4]{0:T(128)S(1)} %fusion.2.quarter, bf16[1024,512]{1,0:T(8,128)(2,1)S(1)} %copy-done.2, bf16[4,192,512]{2,1,0:T(8,128)(2,1)S(1)} %all-to-all-done.refs_0_, bf16[768,128]{1,0:T(8,128)(2,1)S(1)} %collective-permute-done.19.refs_1_, ...), custom_call_target="tpu_custom_call" | custom-call | flops 805306368 | bytes 8388608 | tf_op jit(solution)/shard_map/pallas_call | solution.py:485
  (59 shorter events, 3.8 us)
Async XLA Ops:
  0.0 8.7 %copy-start = (bf16[768,512]{1,0:T(8,128)(2,1)S(1)}, bf16[768,512]{1,0:T(8,128)(2,1)}, u32[]{:S(2)}) copy-start(bf16[768,512]{1,0:T(8,128)(2,1)} %refs_0_.1) | copy-start | bytes 2359300
  0.0 18.4 %collective-permute-start = (bf16[768,512]{1,0:T(8,128)(2,1)}, bf16[768,512]{1,0:T(8,128)(2,1)}, u32[]{:S(2)}, u32[]{:S(2)}) collective-permute-start(bf16[768,512]{1,0:T(8,128)(2,1)} %refs_0_.1), channel_id=1, source_target_pairs={{0,9},{4,13},{8,1},{12,5},{17,24},{21,28},{25,16},{29,20},{2,11},{... | collective-permute-start | bytes 2359304 | tf_op jit(solution)/shard_map/ppermute | solution.py:175
  3.5 13.6 %collective-permute-start.4 = (bf16[384,512]{1,0:T(8,128)(2,1)S(1)}, bf16[384,512]{1,0:T(8,128)(2,1)S(1)}, u32[]{:S(2)}, u32[]{:S(2)}) collective-permute-start(bf16[384,512]{1,0:T(8,128)(2,1)S(1)} %get-tuple-element.38), channel_id=1, source_target_pairs={{1,16},{5,20},{9,17},{13,21},{16,8},{20,12},{24,9},{28,13},{3,18},... | collective-permute-start | bytes 1179656 | tf_op jit(solution)/shard_map/ppermute | solution.py:175
  4.8 35.3 %collective-permute-start.2 = (bf16[768,512]{1,0:T(8,128)(2,1)}, bf16[768,512]{1,0:T(8,128)(2,1)}, u32[]{:S(2)}, u32[]{:S(2)}) collective-permute-start(bf16[768,512]{1,0:T(8,128)(2,1)} %refs_0_.1), channel_id=1, source_target_pairs={{0,4},{4,0},{8,12},{12,8},{17,21},{21,17},{25,29},{29,25},{2,6},{6... | collective-permute-start | bytes 2359304 | tf_op jit(solution)/shard_map/ppermute | solution.py:175
  8.7 0.7 copy-start.5
  17.1 14.0 %collective-permute-start.8 = (bf16[384,512]{1,0:T(8,128)(2,1)S(1)}, bf16[384,512]{1,0:T(8,128)(2,1)}, u32[]{:S(2)}, u32[]{:S(2)}) collective-permute-start(bf16[384,512]{1,0:T(8,128)(2,1)S(1)} %get-tuple-element.25), channel_id=1, source_target_pairs={{1,16},{5,20},{9,17},{13,21},{16,8},{20,12},{24,9},{28,13},{3,18},... | collective-permute-start | bytes 1179656 | tf_op jit(solution)/shard_map/ppermute | solution.py:175
  18.4 25.3 %collective-permute-start.3 = (bf16[768,512]{1,0:T(8,128)(2,1)}, bf16[768,512]{1,0:T(8,128)(2,1)}, u32[]{:S(2)}, u32[]{:S(2)}) collective-permute-start(bf16[768,512]{1,0:T(8,128)(2,1)} %collective-permute-done.refs_2_), channel_id=1, source_target_pairs={{1,5},{5,1},{9,13},{13,9},{16,20},{20,16},{24,28},{28,24},{3,7},{7... | collective-permute-start | bytes 2359304 | tf_op jit(solution)/shard_map/ppermute | solution.py:175
  20.0 18.6 %collective-permute-start.6 = (bf16[384,512]{1,0:T(8,128)(2,1)S(1)}, bf16[384,512]{1,0:T(8,128)(2,1)}, u32[]{:S(2)}, u32[]{:S(2)}) collective-permute-start(bf16[384,512]{1,0:T(8,128)(2,1)S(1)} %collective-permute-done.4.refs_0_), channel_id=1, source_target_pairs={{8,0},{9,1},{12,4},{13,5},{16,24},{17,25},{20,28},{21,29},{10,2},{... | collective-permute-start | bytes 1179656 | tf_op jit(solution)/shard_map/ppermute | solution.py:175
  31.1 11.2 %collective-permute-start.10 = (bf16[384,512]{1,0:T(8,128)(2,1)}, bf16[384,512]{1,0:T(8,128)(2,1)}, u32[]{:S(2)}, u32[]{:S(2)}) collective-permute-start(bf16[384,512]{1,0:T(8,128)(2,1)} %collective-permute-done.8.refs_0_), channel_id=1, source_target_pairs={{8,0},{9,1},{12,4},{13,5},{16,24},{17,25},{20,28},{21,29},{10,2},{... | collective-permute-start | bytes 1179656 | tf_op jit(solution)/shard_map/ppermute | solution.py:175
  33.1 10.6 %copy-start.8 = (s32[3]{0:T(128)S(1)}, s32[3]{0:T(128)}, u32[]{:S(2)}) copy-start(s32[3]{0:T(128)} %here_lengths.1) | copy-start | bytes 40
  34.9 15.2 %collective-permute-start.5 = (bf16[384,512]{1,0:T(8,128)(2,1)S(1)}, bf16[384,512]{1,0:T(8,128)(2,1)}, u32[]{:S(2)}, u32[]{:S(2)}) collective-permute-start(bf16[384,512]{1,0:T(8,128)(2,1)S(1)} %collective-permute-done.4.refs_0_), channel_id=1, source_target_pairs={{8,12},{9,13},{12,8},{13,9},{16,20},{17,21},{20,16},{21,17},{10,14... | collective-permute-start | bytes 1179656 | tf_op jit(solution)/shard_map/ppermute | solution.py:175
  38.6 11.5 %collective-permute-start.7 = (bf16[384,512]{1,0:T(8,128)(2,1)}, bf16[384,512]{1,0:T(8,128)(2,1)}, u32[]{:S(2)}, u32[]{:S(2)}) collective-permute-start(bf16[384,512]{1,0:T(8,128)(2,1)} %collective-permute-done.6.refs_2_), channel_id=1, source_target_pairs={{0,4},{1,5},{4,0},{5,1},{24,28},{25,29},{28,24},{29,25},{2,6},{3,7... | collective-permute-start | bytes 1179656 | tf_op jit(solution)/shard_map/ppermute | solution.py:175
  40.1 15.3 %collective-permute-start.9 = (bf16[384,512]{1,0:T(8,128)(2,1)}, bf16[384,512]{1,0:T(8,128)(2,1)}, u32[]{:S(2)}, u32[]{:S(2)}) collective-permute-start(bf16[384,512]{1,0:T(8,128)(2,1)} %collective-permute-done.8.refs_0_), channel_id=1, source_target_pairs={{8,12},{9,13},{12,8},{13,9},{16,20},{17,21},{20,16},{21,17},{10,14... | collective-permute-start | bytes 1179656 | tf_op jit(solution)/shard_map/ppermute | solution.py:175
  42.3 13.1 %collective-permute-start.11 = (bf16[384,512]{1,0:T(8,128)(2,1)}, bf16[384,512]{1,0:T(8,128)(2,1)}, u32[]{:S(2)}, u32[]{:S(2)}) collective-permute-start(bf16[384,512]{1,0:T(8,128)(2,1)} %collective-permute-done.10.refs_2_), channel_id=1, source_target_pairs={{0,4},{1,5},{4,0},{5,1},{24,28},{25,29},{28,24},{29,25},{2,6},{3,7... | collective-permute-start | bytes 1179656 | tf_op jit(solution)/shard_map/ppermute | solution.py:175
  49.1 0.9 copy-start.11
  50.0 15.3 %collective-permute-start.12 = (bf16[768,512]{1,0:T(8,128)(2,1)}, bf16[768,512]{1,0:T(8,128)(2,1)}, u32[]{:S(2)}, u32[]{:S(2)}) collective-permute-start(bf16[768,512]{1,0:T(8,128)(2,1)} %get-tuple-element.27), channel_id=1, source_target_pairs={{0,1},{1,0},{4,5},{5,4},{8,9},{9,8},{12,13},{13,12},{16,17},{17,16... | collective-permute-start | bytes 2359304 | tf_op jit(solution)/shard_map/ppermute | solution.py:175
  53.4 5.1 %copy-start.9 = (bf16[384,512]{1,0:T(8,128)(2,1)}, bf16[384,512]{1,0:T(8,128)(2,1)S(1)}, u32[]{:S(2)}) copy-start(bf16[384,512]{1,0:T(8,128)(2,1)S(1)} %get-tuple-element.24.refs_1_) | copy-start | bytes 1179652
  53.4 10.6 %copy-start.6 = (s32[192]{0:T(256)S(1)}, s32[192]{0:T(256)}, u32[]{:S(2)}) copy-start(s32[192]{0:T(256)} %here_targets.1) | copy-start | bytes 2308
  53.5 11.8 %collective-permute-start.13 = (bf16[384,512]{1,0:T(8,128)(2,1)S(1)}, bf16[384,512]{1,0:T(8,128)(2,1)S(1)}, u32[]{:S(2)}, u32[]{:S(2)}) collective-permute-start(bf16[384,512]{1,0:T(8,128)(2,1)S(1)} %get-tuple-element.28), channel_id=1, source_target_pairs={{0,1},{1,0},{4,5},{5,4},{8,9},{9,8},{12,13},{13,12},{16,17},{17,16... | collective-permute-start | bytes 1179656 | tf_op jit(solution)/shard_map/ppermute | solution.py:175
  58.5 0.8 copy-start.10
  59.3 6.0 %collective-permute-start.14 = (bf16[384,512]{1,0:T(8,128)(2,1)S(1)}, bf16[384,512]{1,0:T(8,128)(2,1)S(1)}, u32[]{:S(2)}, u32[]{:S(2)}) collective-permute-start(bf16[384,512]{1,0:T(8,128)(2,1)S(1)} %get-tuple-element.29), channel_id=1, source_target_pairs={{0,1},{1,0},{4,5},{5,4},{8,9},{9,8},{12,13},{13,12},{16,17},{17,16... | collective-permute-start | bytes 1179656 | tf_op jit(solution)/shard_map/ppermute | solution.py:175
  59.3 62.1 %all-to-all-start = ((bf16[4,192,512]{2,1,0:T(8,128)(2,1)}), bf16[4,192,512]{2,1,0:T(8,128)(2,1)S(1)}, u32[]{:S(2)}, u32[]{:S(2)}) async-start(bf16[4,192,512]{2,1,0:T(8,128)(2,1)} %shard_map.55.refs_4_), calls=%async_computation | async-start | bytes 1572864 | tf_op jit(solution)/shard_map/all_to_all | solution.py:534
  64.1 1.1 collective-permute-start.1
  65.3 0.8 copy-start.14
  65.3 0.9 copy-start.12
  65.3 0.8 copy-start.13
  66.2 65.9 %copy-start.2 = (bf16[1024,512]{1,0:T(8,128)(2,1)S(1)}, bf16[1024,512]{1,0:T(8,128)(2,1)}, u32[]{:S(2)}) copy-start(bf16[1024,512]{1,0:T(8,128)(2,1)} %w_ref.1) | copy-start | bytes 3145732
  83.5 21.6 %copy-start.7 = (s32[192]{0:T(256)S(1)}, s32[192]{0:T(256)}, u32[]{:S(2)}) copy-start(s32[192]{0:T(256)} %here_targets.1) | copy-start | bytes 2308
  83.5 1.4 %collective-permute-start.15 = (f32[2,3072]{1,0:T(2,128)}, f32[2,3072]{1,0:T(2,128)S(1)}, u32[]{:S(2)}, u32[]{:S(2)}) collective-permute-start(f32[2,3072]{1,0:T(2,128)} %get-tuple-element.32.a_ref), channel_id=1, source_target_pairs={{0,1},{1,0},{4,5},{5,4},{8,9},{9,8},{12,13},{13,12},{16,17},{17,16... | collective-permute-start | bytes 73736 | tf_op jit(solution)/shard_map/ppermute | solution.py:175
  84.9 0.7 copy-start.4
  85.7 3.8 %collective-permute-start.16 = (f32[2,3072]{1,0:T(2,128)S(1)}, f32[2,3072]{1,0:T(2,128)S(1)}, u32[]{:S(2)}, u32[]{:S(2)}) collective-permute-start(f32[2,3072]{1,0:T(2,128)S(1)} %shard_map.60.refs_0_), channel_id=1, source_target_pairs={{0,4},{1,5},{4,0},{5,1},{8,12},{9,13},{12,8},{13,9},{16,20},{17,21... | collective-permute-start | bytes 73736 | tf_op jit(solution)/shard_map/ppermute | solution.py:175
  86.6 3.8 %collective-permute-start.17 = (f32[2,3072]{1,0:T(2,128)S(1)}, f32[2,3072]{1,0:T(2,128)S(1)}, u32[]{:S(2)}, u32[]{:S(2)}) collective-permute-start(f32[2,3072]{1,0:T(2,128)S(1)} %shard_map.60.refs_0_), channel_id=1, source_target_pairs={{0,8},{1,9},{4,12},{5,13},{8,0},{9,1},{12,4},{13,5},{16,24},{17,25... | collective-permute-start | bytes 73736 | tf_op jit(solution)/shard_map/ppermute | solution.py:175
  86.6 4.7 %collective-permute-start.18 = (f32[2,3072]{1,0:T(2,128)S(1)}, f32[2,3072]{1,0:T(2,128)S(1)}, u32[]{:S(2)}, u32[]{:S(2)}) collective-permute-start(f32[2,3072]{1,0:T(2,128)S(1)} %shard_map.60.refs_0_), channel_id=1, source_target_pairs={{0,12},{1,13},{4,8},{5,9},{8,4},{9,5},{12,0},{13,1},{16,28},{17,29... | collective-permute-start | bytes 73736 | tf_op jit(solution)/shard_map/ppermute | solution.py:175
  91.4 1.4 %copy-start.1 = (f32[3072,128]{1,0:T(8,128)S(1)}, f32[3072,128]{1,0:T(8,128)}, u32[]{:S(2)}) copy-start(f32[3072,128]{1,0:T(8,128)} %get-tuple-element.30.att_ref) | copy-start | bytes 4718596
  92.8 1.1 copy-start.3
  95.6 12.3 %collective-permute-start.19 = (bf16[768,128]{1,0:T(8,128)(2,1)S(1)}, bf16[768,128]{1,0:T(8,128)(2,1)S(1)}, u32[]{:S(2)}, u32[]{:S(2)}) collective-permute-start(bf16[768,128]{1,0:T(8,128)(2,1)S(1)} %get-tuple-element.33), channel_id=1, source_target_pairs={{0,0},{1,8},{4,4},{5,12},{8,16},{9,24},{12,20},{13,28},{16,1},{17,... | collective-permute-start | bytes 589832 | tf_op jit(solution)/shard_map/ppermute | solution.py:175
  100.5 17.3 %collective-permute-start.21 = (bf16[768,128]{1,0:T(8,128)(2,1)S(1)}, bf16[768,128]{1,0:T(8,128)(2,1)S(1)}, u32[]{:S(2)}, u32[]{:S(2)}) collective-permute-start(bf16[768,128]{1,0:T(8,128)(2,1)S(1)} %get-tuple-element.34), channel_id=1, source_target_pairs={{0,8},{1,16},{4,12},{5,20},{8,24},{9,0},{12,28},{13,4},{16,9},{17,... | collective-permute-start | bytes 589832 | tf_op jit(solution)/shard_map/ppermute | solution.py:175
  102.4 16.5 %collective-permute-start.23 = (bf16[768,128]{1,0:T(8,128)(2,1)S(1)}, bf16[768,128]{1,0:T(8,128)(2,1)S(1)}, u32[]{:S(2)}, u32[]{:S(2)}) collective-permute-start(bf16[768,128]{1,0:T(8,128)(2,1)S(1)} %get-tuple-element.35), channel_id=1, source_target_pairs={{0,16},{1,24},{4,20},{5,28},{8,0},{9,8},{12,4},{13,12},{16,17},{17... | collective-permute-start | bytes 589832 | tf_op jit(solution)/shard_map/ppermute | solution.py:175
  104.5 15.4 %collective-permute-start.25 = (bf16[768,128]{1,0:T(8,128)(2,1)S(1)}, bf16[768,128]{1,0:T(8,128)(2,1)S(1)}, u32[]{:S(2)}, u32[]{:S(2)}) collective-permute-start(bf16[768,128]{1,0:T(8,128)(2,1)S(1)} %get-tuple-element.36), channel_id=1, source_target_pairs={{0,24},{1,0},{4,28},{5,4},{8,8},{9,16},{12,12},{13,20},{16,25},{17... | collective-permute-start | bytes 589832 | tf_op jit(solution)/shard_map/ppermute | solution.py:175
  108.0 13.4 %collective-permute-start.20 = (bf16[768,128]{1,0:T(8,128)(2,1)S(1)}, bf16[768,128]{1,0:T(8,128)(2,1)S(1)}, u32[]{:S(2)}, u32[]{:S(2)}) collective-permute-start(bf16[768,128]{1,0:T(8,128)(2,1)S(1)} %collective-permute-done.19.refs_1_), channel_id=1, source_target_pairs={{0,4},{1,5},{4,0},{5,1},{8,12},{9,13},{12,8},{13,9},{16,20},{17,21... | collective-permute-start | bytes 589832 | tf_op jit(solution)/shard_map/ppermute | solution.py:175
  117.8 7.8 %collective-permute-start.22 = (bf16[768,128]{1,0:T(8,128)(2,1)S(1)}, bf16[768,128]{1,0:T(8,128)(2,1)S(1)}, u32[]{:S(2)}, u32[]{:S(2)}) collective-permute-start(bf16[768,128]{1,0:T(8,128)(2,1)S(1)} %collective-permute-done.21.refs_3_), channel_id=1, source_target_pairs={{0,4},{1,5},{4,0},{5,1},{8,12},{9,13},{12,8},{13,9},{16,20},{17,21... | collective-permute-start | bytes 589832 | tf_op jit(solution)/shard_map/ppermute | solution.py:175
  118.9 11.0 %collective-permute-start.24 = (bf16[768,128]{1,0:T(8,128)(2,1)S(1)}, bf16[768,128]{1,0:T(8,128)(2,1)S(1)}, u32[]{:S(2)}, u32[]{:S(2)}) collective-permute-start(bf16[768,128]{1,0:T(8,128)(2,1)S(1)} %collective-permute-done.23.refs_5_), channel_id=1, source_target_pairs={{0,4},{1,5},{4,0},{5,1},{8,12},{9,13},{12,8},{13,9},{16,20},{17,21... | collective-permute-start | bytes 589832 | tf_op jit(solution)/shard_map/ppermute | solution.py:175
  119.8 12.3 %collective-permute-start.26 = (bf16[768,128]{1,0:T(8,128)(2,1)S(1)}, bf16[768,128]{1,0:T(8,128)(2,1)S(1)}, u32[]{:S(2)}, u32[]{:S(2)}) collective-permute-start(bf16[768,128]{1,0:T(8,128)(2,1)S(1)} %collective-permute-done.25.refs_7_), channel_id=1, source_target_pairs={{0,4},{1,5},{4,0},{5,1},{8,12},{9,13},{12,8},{13,9},{16,20},{17,21... | collective-permute-start | bytes 589832 | tf_op jit(solution)/shard_map/ppermute | solution.py:175
